TPU v7x, 32 devices: a whole 2x2x4 slice. The times are simulated.
32 devices in a mesh: grp: 2 (over x), bits: 16 (over z, y, core).
Axes of the slice: x: 2, y: 2, z: 4, core: 2. Of those that a mesh axis runs over, the one named last changes fastest.
Arguments:
- prefix: bfloat16 [128, 16, 1024], P(('grp', 'bits')), parts along dimension 0, may hold values from -6 to 6
- first_suffix: bfloat16 [8, 2, 512, 512], P('grp', None, 'bits'), parts along dimension 0, may hold values from -0.109375 to 0.109375
- pair_prefix: int32 [256, 3], P(('grp', 'bits')), parts along dimension 0, may hold values from 0 to 3
- pair_suffix: int32 [256, 3], P(('grp', 'bits')), parts along dimension 0, may hold values from 0 to 3, all different within a row
- merge_count: int32 [256], P(('grp', 'bits')), parts along dimension 0, may hold values from 1 to 3, as said below
- suffix: bfloat16 [32, 2, 512, 512], P(('grp', 'bits')), parts along dimension 0, may hold values from -0.1875 to 0.1875
- routes: int32 [256, 12], P(('grp', 'bits')), parts along dimension 0, may hold values from 0 to 15, all different within a row; in each aligned block of 8 rows (0 to 7, 8 to 15, ...) at most 8 rows name the same one
- cap: bfloat16 [2, 512, 64], replicated, may hold values from -0.0546875 to 0.0546875
Outputs:
- capped: float32 [256, 16, 128], P(('grp', 'bits')), parts along dimension 0
There are 2 independent parts, one for each index of `grp`. A program takes and returns all parts, laid end to end along the dimension named above; an argument that names none is the same for every part. Nothing has to cross between parts.
Inputs may be any that keep to these rules, and one draw needn't show every extreme that they name: `pair_suffix`: each row names 3 different lifetime-one blocks. `merge_count`: some piece has exactly 3 merges and some exactly one. `routes`: each row names 12 different suffixes; in each aligned block of 8 rows no suffix is named by more than 8 rows, a bound that some block reaches.
All inputs are finite; a program needn't handle non-finite values.
Results may differ from a plain program's by a relative error of at most 0.005.
Values may be sent and summed in bfloat16 or wider, within the bound.
No kernel may reach another device: no remote copies, remote signals or barrier semaphores. Data moves between devices by JAX's collectives and lax.ppermute only.
A program may use at most 64 MiB of HBM per device.

v0:
```python
import jax
import jax.numpy as jnp
from jax import lax
from jax.sharding import PartitionSpec as P

HIGHEST_PRECISION = lax.Precision.HIGHEST


def complex_form(blocks):
    real_part = blocks[..., 0, :, :]
    imag_part = blocks[..., 1, :, :]
    upper_half = jnp.concatenate([real_part, imag_part], axis=-1)
    lower_half = jnp.concatenate([-imag_part, real_part], axis=-1)
    return jnp.concatenate([upper_half, lower_half], axis=-2)


def on_device(prefix, first_suffix, pair_prefix, pair_suffix, merge_count, suffix, routes, cap):
    pieces = pair_prefix.shape[0]
    merges = pair_prefix.shape[1]
    held_blocks = prefix.shape[0]
    rows_piece = prefix.shape[1]
    twice_width = prefix.shape[2]
    half_width = twice_width // 2
    first_count = first_suffix.shape[0]
    listed = routes.shape[1]
    owners = lax.axis_size("bits")
    slot_count = min(pieces, max(2, (2 * pieces * listed + owners - 1) // owners))
    live_mask = lax.broadcasted_iota(jnp.int32, (pieces, merges), 1) < merge_count[:, None]
    matches = (
        pair_suffix[:, :, None] == lax.broadcasted_iota(jnp.int32, (pieces, merges, first_count), 2)
    ) & live_mask[:, :, None]
    which_block = pair_prefix[:, :, None] == lax.broadcasted_iota(
        jnp.int32, (pieces, merges, held_blocks), 2
    )
    prefix_picks = jnp.einsum(
        "ika,ikp->iap", matches.astype(jnp.float32), which_block.astype(jnp.float32)
    ).astype(jnp.bfloat16)
    selected = jnp.einsum(
        "iap,prc->airc", prefix_picks, prefix, preferred_element_type=jnp.float32
    ).astype(jnp.bfloat16)
    selected = selected.reshape(first_count, pieces * rows_piece, twice_width)
    portion = lax.all_gather(first_suffix, "bits", axis=2, tiled=True)
    count_rows = portion.shape[2]
    real_cols = lax.slice_in_dim(selected, 0, count_rows, axis=2)
    imag_cols = lax.dynamic_slice_in_dim(selected, half_width, count_rows, 2)
    left_side = jnp.concatenate([real_cols, imag_cols], axis=2)
    upper_half = jnp.concatenate([portion[:, 0], portion[:, 1]], axis=2)
    lower_half = jnp.concatenate([-portion[:, 1], portion[:, 0]], axis=2)
    right_side = jnp.concatenate([upper_half, lower_half], axis=1)
    state_rows = jnp.einsum(
        "arc,acw->rw", left_side, right_side, preferred_element_type=jnp.float32
    )
    state_rows = state_rows.astype(jnp.bfloat16).reshape(pieces, rows_piece, twice_width)
    named_by = jnp.sum(
        (routes[:, :, None] == lax.broadcasted_iota(jnp.int32, (pieces, listed, owners), 2)).astype(
            jnp.int32
        ),
        axis=1,
    )
    slot_rank = jnp.cumsum(named_by, axis=0) - named_by
    slot_hit = (
        slot_rank[:, :, None] == lax.broadcasted_iota(jnp.int32, (pieces, owners, slot_count), 2)
    ) & (named_by[:, :, None] > 0)
    dispatch = jnp.transpose(slot_hit, (1, 2, 0)).astype(jnp.bfloat16)
    outgoing = jnp.einsum(
        "dmi,irc->dmrc", dispatch, state_rows, preferred_element_type=jnp.float32
    ).astype(jnp.bfloat16)
    own_form = complex_form(suffix[0])
    cap_form = complex_form(cap)
    products = jnp.einsum(
        "smrc,cw->smrw",
        lax.all_to_all(outgoing, "bits", split_axis=0, concat_axis=0, tiled=True),
        own_form,
        preferred_element_type=jnp.float32,
    ).astype(jnp.bfloat16)
    capped_terms = jnp.einsum(
        "smrw,wv->smrv", products, cap_form, preferred_element_type=jnp.float32
    )
    returned = lax.all_to_all(
        capped_terms.astype(jnp.bfloat16), "bits", split_axis=0, concat_axis=0, tiled=True
    ).astype(capped_terms.dtype)
    return jnp.einsum(
        "dmi,dmrv->irv", dispatch.astype(jnp.float32), returned, precision=HIGHEST_PRECISION
    )


def solution(mesh):
    return jax.shard_map(
        on_device,
        mesh=mesh,
        in_specs=(
            P(("grp", "bits"), None, None),
            P("grp", None, "bits", None),
            P(("grp", "bits"), None),
            P(("grp", "bits"), None),
            P(("grp", "bits")),
            P(("grp", "bits"), None, None, None),
            P(("grp", "bits"), None),
            P(),
        ),
        out_specs=P(("grp", "bits"), None, None),
        check_vma=False,
    )
```

profile of v0, /device:TPU:0, one launch (start us, length us, event | category | flops | bytes accessed | tf_op | source)
XLA Modules:
  0.0 205.7 jit_solution(14975206516049845053)
XLA Ops:
  6.5 0.0 all-gather.2.cloned.1.call-start
  6.5 1.7 copy.52
  8.2 0.0 all-gather.2.cloned.1.call-update
  8.2 0.8 copy.47
  9.0 0.8 copy.48
  9.7 0.7 iota_compare_fusion.5
  10.5 0.2 fusion.32
  10.7 1.3 fusion.22
  12.0 0.6 copy.51
  12.6 0.8 copy.46
  13.3 0.1 convert_reduce_fusion
  13.5 49.4 %all-gather.2.cloned.1.call-done = bf16[4,2,512,512]{3,2,0,1:T(8,128)(2,1)} async-done(((bf16[4,2,32,512]{3,2,0,1:T(8,128)(2,1)}), bf16[4,2,512,512]{3,2,0,1:T(8,128)(2,1)}) %all-gather.2.cloned.1.call-update) | async-done | bytes 4194320 | tf_op jit(solution)/shard_map/all_gather | solution.py:42
  62.9 0.0 copy-start
  62.9 2.7 %slice_bitcast_fusion = (bf16[4,512,512]{2,1,0:T(8,128)(2,1)S(1)}, bf16[4,512,512]{2,1,0:T(8,128)(2,1)S(1)}) fusion(bf16[4,2,512,512]{3,2,0,1:T(8,128)(2,1)} %all-gather.2.cloned.1.call-done), kind=kLoop, calls=%fused_computation.11 | loop fusion | bytes 8388608 | tf_op jit(solution)/shard_map/squeeze | solution.py:47
  65.5 0.8 copy-done
  66.3 0.1 fusion.63
  66.4 1.3 fusion.29
  67.7 1.6 convolution_convert_fusion
  69.3 4.3 %copy.54 = bf16[16,8,16,1024]{3,2,1,0:T(8,128)(2,1)} copy(bf16[16,8,16,1024]{3,0,2,1:T(8,128)(2,1)S(1)} %convolution_convert_fusion) | data formatting | bytes 8388608 | tf_op jit(solution)/shard_map/convert_element_type | solution.py:67
  73.6 0.0 copy-start.2
  73.6 0.0 copy-start.1
  73.6 4.9 %all-to-all-start = ((bf16[16,8,16,1024]{3,2,1,0:T(8,128)(2,1)}), bf16[16,8,16,1024]{3,2,1,0:T(8,128)(2,1)}, u32[]{:S(2)}, u32[]{:S(2)}) async-start(bf16[16,8,16,1024]{3,2,1,0:T(8,128)(2,1)} %copy.54), calls=%async_computation | async-start | bytes 8388608 | tf_op jit(solution)/shard_map/all_to_all | solution.py:72
  78.5 0.0 copy-done.2
  78.5 0.1 copy.68
  78.6 0.1 copy.67
  78.8 0.0 copy-done.1
  78.8 0.1 slice_bitcast_fusion.2
  78.9 77.0 %all-to-all-done = bf16[16,8,16,1024]{3,2,1,0:T(8,128)(2,1)} async-done(((bf16[16,8,16,1024]{3,2,1,0:T(8,128)(2,1)}), bf16[16,8,16,1024]{3,2,1,0:T(8,128)(2,1)}, u32[]{:S(2)}, u32[]{:S(2)}) %all-to-all-start) | async-done | bytes 4194336 | tf_op jit(solution)/shard_map/all_to_all | solution.py:72
  155.9 7.9 %fusion.23 = bf16[16,8,16,128]{3,2,1,0:T(8,128)(2,1)S(1)} fusion(bf16[16,8,16,1024]{3,2,1,0:T(8,128)(2,1)} %all-to-all-done, bf16[512,512]{1,0:T(8,128)(2,1)S(1)} %get-tuple-element.8, bf16[512,512]{1,0:T(8,128)(2,1)S(1)} %fusion.62, bf16[512,512]{1,0:T(8,128)(2,1)S(1)} %get-tuple-element.7, bf16[512,64]{1,0:T(8,128)(2,1)S(1)} %bitcast.66, ...), kind=kOutput, calls=%fused_computation.23 | convolution fusion | flops 4843634688 | bytes 6488064 | tf_op jit(solution)/shard_map/smrw,wv->smrv/dot_general | solution.py:76
  163.8 0.1 copy.57
  164.0 33.9 %all_to_all.10 = bf16[16,8,16,128]{3,1,2,0:T(8,128)(2,1)S(1)} all-to-all(bf16[16,8,16,128]{3,1,2,0:T(8,128)(2,1)S(1)} %copy.57), channel_id=1, replica_groups=mesh['grp'=2,'bits'=16] {'bits'}, dimensions={0} | all-to-all | bytes 1048576 | tf_op jit(solution)/shard_map/all_to_all | solution.py:79
  197.9 0.4 convolution_bitcast_fusion
  198.3 0.6 copy.59
  (6 shorter events, 0.1 us)
Async XLA Ops:
  6.5 56.3 %all-gather.2.cloned.1.call-start = ((), (), s32[]{:S(2)}) async-start(), calls=%async_computation.2 | async-start | bytes 4456448 | tf_op jit(solution)/shard_map/all_gather | solution.py:42
  62.9 3.4 %copy-start = (bf16[4,2,512,512]{3,2,0,1:T(8,128)(2,1)S(1)}, bf16[4,2,512,512]{3,2,0,1:T(8,128)(2,1)}, u32[]{:S(2)}) copy-start(bf16[4,2,512,512]{3,2,0,1:T(8,128)(2,1)} %all-gather.2.cloned.1.call-done) | copy-start | bytes 12582916
  73.6 4.9 %copy-start.2 = (bf16[2,512,64]{1,2,0:T(8,128)(2,1)S(1)}, bf16[2,512,64]{1,2,0:T(8,128)(2,1)}, u32[]{:S(2)}) copy-start(bf16[2,512,64]{1,2,0:T(8,128)(2,1)} %param.15) | copy-start | bytes 393220
  73.6 5.2 %copy-start.1 = (bf16[1,2,512,512]{3,2,1,0:T(8,128)(2,1)S(1)}, bf16[1,2,512,512]{3,2,1,0:T(8,128)(2,1)}, u32[]{:S(2)}) copy-start(bf16[1,2,512,512]{3,2,1,0:T(8,128)(2,1)} %param.13) | copy-start | bytes 3145732
  73.6 82.3 %all-to-all-start = ((bf16[16,8,16,1024]{3,2,1,0:T(8,128)(2,1)}), bf16[16,8,16,1024]{3,2,1,0:T(8,128)(2,1)}, u32[]{:S(2)}, u32[]{:S(2)}) async-start(bf16[16,8,16,1024]{3,2,1,0:T(8,128)(2,1)} %copy.54), calls=%async_computation | async-start | bytes 8388608 | tf_op jit(solution)/shard_map/all_to_all | solution.py:72
Sparse Core Ops, SparseCore 0:
  9.5 53.2 all-gather.1
where the time goes:
time: 206 us
  waiting for transfers between devices  126 us (61%)
  blocking collectives  33.9 us (16%)
  between operations  13.5 us (7%)
  local copies, waits for them, and re-layouts  13.4 us (7%)
  matrix products  12.7 us (6%)
  starting transfers between devices  4.85 us (2%)
    all_to_all x1, waiting for transfers between devices, on_device(): lax.all_to_all(outgoing, 'bits', split_axis=0, concat_axis=0, tiled=True)  77 us
    all_gather x1, waiting for transfers between devices, on_device(): portion = lax.all_gather(first_suffix, 'bits', axis=2, tiled=True)  49.4 us
    all_to_all x1, blocking collectives, on_device(): lax.all_to_all(capped_terms.astype(jnp.bfloat16), 'bits', split_axis=0, c...  33.9 us
    dot_general x1, matrix products, on_device(): jnp.einsum('smrw,wv->smrv', products, cap_form, preferred_element_type=jn...  7.92 us
    unnamed x12, local copies, waits for them, and re-layouts  4.98 us
    all_to_all x1, starting transfers between devices, on_device(): lax.all_to_all(outgoing, 'bits', split_axis=0, concat_axis=0, tiled=True)  4.85 us
    convert_element_type x1, local copies, waits for them, and re-layouts, on_device(): outgoing = jnp.einsum('dmi,irc->dmrc', dispatch, state_rows, preferred_el...  4.3 us
  transfers between devices with their start and end apart: 2, of which 2 were waited for; matrix products, arithmetic and copies ran while one was open for 3% of the time, Pallas kernels for 0%

commit v1 on v0

--- a/solution.py
+++ b/solution.py
@@ -1,9 +1,16 @@
+import functools
+
 import jax
 import jax.numpy as jnp
 from jax import lax
+from jax.experimental import pallas as pl
+from jax.experimental.pallas import tpu as pltpu
 from jax.sharding import PartitionSpec as P
 
 HIGHEST_PRECISION = lax.Precision.HIGHEST
+LANES = 128
+PLANE = 4
+VMEM_BYTES = 32 * 1024 * 1024
 
 
 def complex_form(blocks):
@@ -14,7 +21,156 @@
     return jnp.concatenate([upper_half, lower_half], axis=-2)
 
 
-def on_device(prefix, first_suffix, pair_prefix, pair_suffix, merge_count, suffix, routes, cap):
+def swap(x, bit):
+    owners = lax.axis_size("bits")
+    return lax.ppermute(x, "bits", [(i, i ^ bit) for i in range(owners)])
+
+
+def pack_kernel(planes, suffix_ref, cap_ref, first_ref, plan_ref, *packs):
+    me = lax.axis_index("bits")
+    plane = me // PLANE
+    cap_real = cap_ref[0].astype(jnp.float32)
+    cap_imag = cap_ref[1].astype(jnp.float32)
+    upper = jnp.concatenate([cap_real, cap_imag], axis=1).astype(jnp.bfloat16)
+    lower = jnp.concatenate([-cap_imag, cap_real], axis=1).astype(jnp.bfloat16)
+    blocks, _, depth, width = first_ref.shape
+    part = width // planes
+    for k in range(planes):
+        there = pl.ds(pl.multiple_of((plane ^ k) * part, part), part)
+        for a in range(blocks):
+            for c in range(2):
+                packs[k][2 * a + c] = first_ref[a, c, :, there]
+        closed = jnp.dot(suffix_ref[0, there, :], upper, preferred_element_type=jnp.float32)
+        closed += jnp.dot(suffix_ref[1, there, :], lower, preferred_element_type=jnp.float32)
+        closed = closed.astype(jnp.bfloat16)
+        for c in range(part // depth):
+            packs[k][2 * blocks + c] = closed[c * depth:(c + 1) * depth]
+        packs[k][2 * blocks + part // depth] = plan_ref[...]
+
+
+def work_kernel(planes, blocks, merges, listed, plan_ref, *refs):
+    slots = planes * PLANE
+    packs, prefixes = refs[:slots], refs[slots:slots + planes]
+    outs = refs[slots + planes:slots + 2 * planes]
+    forms, closed, rows, products, state, wide, terms, sems = refs[slots + 2 * planes:]
+    me = lax.axis_index("bits")
+    depth = packs[0].shape[1]
+    part = closed.shape[1] * depth
+    held = prefixes[0].shape[0]
+    rows_piece = prefixes[0].shape[1]
+    half = prefixes[0].shape[2] // 2
+    pieces = outs[0].shape[0]
+    copies = []
+    for j in range(slots):
+        there = pl.ds(pl.multiple_of((me ^ j) * depth, depth), depth)
+        copies.append(pltpu.make_async_copy(packs[j].at[0:2 * blocks], forms.at[:, there, :], sems.at[2 * j]))
+        copies.append(
+            pltpu.make_async_copy(
+                packs[j].at[2 * blocks:2 * blocks + part // depth], closed.at[j], sems.at[2 * j + 1]
+            )
+        )
+    for k in range(planes):
+        copies.append(pltpu.make_async_copy(prefixes[k], rows.at[k], sems.at[2 * slots + k]))
+    for copy in copies:
+        copy.start()
+    for copy in copies:
+        copy.wait()
+    left = rows[...].reshape(planes * held * rows_piece, 2 * half)
+    for a in range(blocks):
+        right = jnp.concatenate([forms[2 * a], forms[2 * a + 1]], axis=1)
+        real = jnp.dot(left[:, :half], right, preferred_element_type=jnp.float32)
+        imag = jnp.dot(left[:, half:], right, preferred_element_type=jnp.float32)
+        products[a, :, :part] = real[:, :part] - imag[:, part:]
+        products[a, :, part:] = real[:, part:] + imag[:, :part]
+    for i in range(planes * pieces):
+        total = None
+        for m in range(merges):
+            row = (i // pieces * held + plan_ref[i, m]) * rows_piece
+            term = products[plan_ref[i, merges + m], pl.ds(pl.multiple_of(row, rows_piece), rows_piece), :]
+            term = jnp.where(m < plan_ref[i, 2 * merges], term, 0.0)
+            total = term if total is None else total + term
+        state[i * rows_piece:(i + 1) * rows_piece, :] = total.astype(jnp.bfloat16)
+    lane = lax.broadcasted_iota(jnp.int32, (part, LANES), 1)
+    for j in range(slots):
+        real_rows = closed[j].reshape(part, LANES)
+        turned = pltpu.roll(real_rows.astype(jnp.float32), LANES // 2, 1)
+        turned = jnp.where(lane < LANES // 2, -turned, turned)
+        wide[:part, j * LANES:(j + 1) * LANES] = real_rows
+        wide[part:, j * LANES:(j + 1) * LANES] = turned.astype(jnp.bfloat16)
+    for j in range(0, slots, 2):
+        both = jnp.dot(state[...], wide[:, j * LANES:(j + 2) * LANES], preferred_element_type=jnp.float32)
+        terms[j] = both[:, :LANES]
+        terms[j + 1] = both[:, LANES:]
+    for i in range(planes * pieces):
+        total = None
+        for k in range(listed):
+            slot = plan_ref[i, 2 * merges + 1 + k] ^ me
+            term = terms[slot, i * rows_piece:(i + 1) * rows_piece, :]
+            total = term if total is None else total + term
+        out = outs[i // pieces]
+        out[i % pieces] = total.astype(out.dtype)
+
+
+def in_planes(prefix, first_suffix, pair_prefix, pair_suffix, merge_count, suffix, routes, cap):
+    owners = lax.axis_size("bits")
+    planes = owners // PLANE
+    pieces, merges = pair_prefix.shape
+    listed = routes.shape[1]
+    held, rows_piece, twice_width = prefix.shape
+    blocks, _, depth, width = first_suffix.shape
+    part = width // planes
+    vmem = pl.BlockSpec(memory_space=pltpu.VMEM)
+    anywhere = pl.BlockSpec(memory_space=pl.ANY)
+    plan = jnp.concatenate([pair_prefix, pair_suffix, merge_count[:, None], routes], axis=1)
+    entries = plan.shape[1]
+    plan = jnp.pad(plan, ((0, depth - pieces), (0, LANES - entries))).astype(jnp.bfloat16)
+    pack = jax.ShapeDtypeStruct((2 * blocks + part // depth + 1, depth, LANES), jnp.bfloat16)
+    packs = pl.pallas_call(
+        functools.partial(pack_kernel, planes),
+        out_shape=[pack] * planes,
+        in_specs=[vmem] * 4,
+        out_specs=[vmem] * planes,
+        compiler_params=pltpu.CompilerParams(vmem_limit_bytes=VMEM_BYTES),
+        name="pack",
+    )(suffix[0], cap, first_suffix, plan)
+    packs = [packs[0]] + [swap(packs[k], k * PLANE) for k in range(1, planes)]
+    prefixes = [prefix] + [swap(prefix, k * PLANE) for k in range(1, planes)]
+    across = [swap(p, 2) for p in packs]
+    beside = [swap(p, 1) for p in packs]
+    corner = [swap(p, 1) for p in across]
+    everyone = [group[k] for k in range(planes) for group in (packs, beside, across, corner)]
+    routing = jnp.concatenate([p[-1, :pieces, :entries] for p in packs], axis=0).astype(jnp.int32)
+    slots = owners
+    rows = planes * held * rows_piece
+    state_rows = planes * pieces * rows_piece
+    outs = pl.pallas_call(
+        functools.partial(work_kernel, planes, blocks, merges, listed),
+        out_shape=[
+            jax.ShapeDtypeStruct((pieces, rows_piece, LANES), jnp.float32 if k == 0 else jnp.bfloat16)
+            for k in range(planes)
+        ],
+        in_specs=[pl.BlockSpec(memory_space=pltpu.SMEM)] + [anywhere] * (slots + planes),
+        out_specs=[vmem] * planes,
+        scratch_shapes=[
+            pltpu.VMEM((2 * blocks, width, LANES), jnp.bfloat16),
+            pltpu.VMEM((slots, part // depth, depth, LANES), jnp.bfloat16),
+            pltpu.VMEM((planes, held, rows_piece, twice_width), jnp.bfloat16),
+            pltpu.VMEM((blocks, rows, 2 * part), jnp.float32),
+            pltpu.VMEM((state_rows, 2 * part), jnp.bfloat16),
+            pltpu.VMEM((2 * part, slots * LANES), jnp.bfloat16),
+            pltpu.VMEM((slots, state_rows, LANES), jnp.float32),
+            pltpu.SemaphoreType.DMA((2 * slots + planes,)),
+        ],
+        compiler_params=pltpu.CompilerParams(vmem_limit_bytes=VMEM_BYTES),
+        name="work",
+    )(routing, *everyone, *prefixes)
+    total = outs[0]
+    for k in range(1, planes):
+        total = total + swap(outs[k], k * PLANE).astype(jnp.float32)
+    return total
+
+
+def by_owner(prefix, first_suffix, pair_prefix, pair_suffix, merge_count, suffix, routes, cap):
     pieces = pair_prefix.shape[0]
     merges = pair_prefix.shape[1]
     held_blocks = prefix.shape[0]
@@ -84,6 +240,16 @@
     )
 
 
+def on_device(*args):
+    prefix, first_suffix, cap = args[0], args[1], args[7]
+    planes = lax.axis_size("bits") // PLANE
+    width = first_suffix.shape[3]
+    depth = first_suffix.shape[2]
+    if planes & (planes - 1) == 0 and planes > 0 and width == planes * LANES and 2 * cap.shape[2] == LANES and depth % 32 == 0:
+        return in_planes(*args)
+    return by_owner(*args)
+
+
 def solution(mesh):
     return jax.shard_map(
         on_device,

time: 206 us -> 53.1 us (0.26)
  waiting for transfers between devices: 126 us -> 17.2 us
  blocking collectives: 33.9 us -> 0 us
  starting transfers between devices: 4.85 us -> 24.1 us
  between operations: 13.5 us -> 0.09 us
  matrix products: 12.7 us -> 0 us
  local copies, waits for them, and re-layouts: 13.4 us -> 2.6 us
  Pallas kernels: 0 us -> 5.51 us
  other arithmetic: 1.04 us -> 3.45 us
    all_to_all x1 -> x0, waiting for transfers between devices: 77 us -> none  [on_device(): lax.all_to_all(outgoing, 'bits', split_axis=0, concat_axis=0, tiled=True)]
    all_gather x1 -> x0, waiting for transfers between devices: 49.4 us -> none  [on_device(): portion = lax.all_gather(first_suffix, 'bits', axis=2, tiled=True)]
    all_to_all x1 -> x0, blocking collectives: 33.9 us -> none  [on_device(): lax.all_to_all(capped_terms.astype(jnp.bfloat16), 'bits', split_axis=0, c...]
    ppermute x0 -> x21, starting transfers between devices: none -> 24.1 us  [swap(): return lax.ppermute(x, 'bits', [(i, i ^ bit) for i in range(owners)])]
    ppermute x0 -> x21, waiting for transfers between devices: none -> 17.2 us  [swap(): return lax.ppermute(x, 'bits', [(i, i ^ bit) for i in range(owners)])]
    dot_general x6 -> x0, matrix products: 12.7 us -> none  [the longest x1 7.92 us: on_device(): jnp.einsum('smrw,wv->smrv', products, cap_form, preferred_element_type=jn...]
    pallas_call x0 -> x2, Pallas kernels: none -> 5.51 us  [the longest x1 4.99 us: in_planes(): pl.pallas_call(functools.partial(work_kernel, planes, blocks, merges, lis...]
    convert_element_type x3 -> x0, local copies, waits for them, and re-layouts: 5.03 us -> none  [the longest x1 4.3 us: on_device(): outgoing = jnp.einsum('dmi,irc->dmrc', dispatch, state_rows, preferred_el...]
  transfers between devices with their start and end apart: 2 -> 21, of which waited for: 2 -> 9; matrix products, arithmetic and copies ran while one was open for 3% -> 8% of each run, Pallas kernels for 0% -> 1%
where the time goes in v1:
time: 53.1 us; the launch traced here: 52.9 us
  starting transfers between devices  24.1 us (45%)
  waiting for transfers between devices  17.2 us (32%)
  Pallas kernels  5.51 us (10%)
  other arithmetic  3.45 us (6%)
  local copies, waits for them, and re-layouts  2.6 us (5%)
    ppermute x21, starting transfers between devices, swap(): return lax.ppermute(x, 'bits', [(i, i ^ bit) for i in range(owners)])  24.1 us
    ppermute x21, waiting for transfers between devices, swap(): return lax.ppermute(x, 'bits', [(i, i ^ bit) for i in range(owners)])  17.2 us
    pallas_call x1, Pallas kernels, in_planes(): pl.pallas_call(functools.partial(work_kernel, planes, blocks, merges, lis...  4.99 us
    unnamed x7, local copies, waits for them, and re-layouts  2.31 us
    another operation x3, other arithmetic  2.06 us
  transfers between devices with their start and end apart: 21, of which 9 were waited for; matrix products, arithmetic and copies ran while one was open for 8% of the time, Pallas kernels for 1%

profile of v1, /device:TPU:0, one launch (start us, length us, event | category | flops | bytes accessed | tf_op | source)
XLA Modules:
  0.0 52.9 jit_solution(11365015873709983418)
XLA Ops:
  0.0 4.0 %collective-permute-start.16 = (bf16[4,16,1024]{2,1,0:T(8,128)(2,1)}, bf16[4,16,1024]{2,1,0:T(8,128)(2,1)S(1)}, u32[]{:S(2)}, u32[]{:S(2)}) collective-permute-start(bf16[4,16,1024]{2,1,0:T(8,128)(2,1)} %refs_16_.1), channel_id=1, source_target_pairs={{0,8},{1,9},{2,10},{3,11},{4,12},{5,13},{6,14},{7,15},{8,0},{9,1},... | collective-permute-start | bytes 393224 | tf_op jit(solution)/shard_map/ppermute | solution.py:26
  4.0 1.6 %collective-permute-start.15 = (bf16[4,16,1024]{2,1,0:T(8,128)(2,1)}, bf16[4,16,1024]{2,1,0:T(8,128)(2,1)S(1)}, u32[]{:S(2)}, u32[]{:S(2)}) collective-permute-start(bf16[4,16,1024]{2,1,0:T(8,128)(2,1)} %refs_16_.1), channel_id=1, source_target_pairs={{0,4},{1,5},{2,6},{3,7},{4,0},{5,1},{6,2},{7,3},{8,12},{9,13},{10,... | collective-permute-start | bytes 393224 | tf_op jit(solution)/shard_map/ppermute | solution.py:26
  5.6 0.0 collective-permute-start.17
  5.6 0.7 %convert_bitcast_fusion = bf16[8,1]{0,1:T(2,128)(2,1)S(1)} fusion(s32[8]{0:T(128)} %param.12), kind=kLoop, calls=%fused_computation.20 | loop fusion | flops 8 | bytes 48 | tf_op jit(solution)/shard_map/broadcast_in_dim | solution.py:124
  6.3 0.7 %convert.15 = bf16[8,3]{0,1:T(4,128)(2,1)S(1)} convert(s32[8,3]{0,1:T(4,128)} %param.10) | non-fusion elementwise | flops 24 | bytes 144 | tf_op jit(solution)/shard_map/convert.2
  7.0 0.1 copy.13
  7.1 0.7 %convert.16 = bf16[8,3]{0,1:T(4,128)(2,1)S(1)} convert(s32[8,3]{0,1:T(4,128)} %param.11) | non-fusion elementwise | flops 24 | bytes 144 | tf_op jit(solution)/shard_map/convert.3
  7.7 0.1 copy.14
  7.8 0.1 copy.15
  7.9 0.7 %convert.18 = bf16[8,12]{1,0:T(8,128)(2,1)S(1)} convert(s32[8,12]{1,0:T(8,128)} %param.14) | non-fusion elementwise | flops 96 | bytes 576 | tf_op jit(solution)/shard_map/convert.5
  8.6 1.1 %copy.16.cap_ref = bf16[2,512,64]{2,1,0:T(8,128)(2,1)S(1)} copy(bf16[2,512,64]{1,2,0:T(8,128)(2,1)} %param.15) | data formatting | bytes 262144 | tf_op args[7]
  9.7 0.1 fusion.8.plan_ref
  9.8 1.2 %copy-done = bf16[1,2,512,512]{3,2,1,0:T(8,128)(2,1)S(1)} copy-done((bf16[1,2,512,512]{3,2,1,0:T(8,128)(2,1)S(1)}, bf16[1,2,512,512]{3,2,1,0:T(8,128)(2,1)}, u32[]{:S(2)}) %copy-start) | copy-done | bytes 1048600
  11.0 0.5 pack.1
  11.6 1.0 %collective-permute-start = (bf16[13,32,128]{2,1,0:T(8,128)(2,1)S(1)}, bf16[13,32,128]{2,1,0:T(8,128)(2,1)S(1)}, u32[]{:S(2)}, u32[]{:S(2)}) collective-permute-start(bf16[13,32,128]{2,1,0:T(8,128)(2,1)S(1)} %get-tuple-element.14), channel_id=1, source_target_pairs={{0,4},{1,5},{2,6},{3,7},{4,0},{5,1},{6,2},{7,3},{8,12},{9,13},{10,... | collective-permute-start | bytes 319496 | tf_op jit(solution)/shard_map/ppermute | solution.py:26
  12.5 3.5 %collective-permute-start.1 = (bf16[13,32,128]{2,1,0:T(8,128)(2,1)S(1)}, bf16[13,32,128]{2,1,0:T(8,128)(2,1)S(1)}, u32[]{:S(2)}, u32[]{:S(2)}) collective-permute-start(bf16[13,32,128]{2,1,0:T(8,128)(2,1)S(1)} %get-tuple-element.15), channel_id=1, source_target_pairs={{0,8},{1,9},{2,10},{3,11},{4,12},{5,13},{6,14},{7,15},{8,0},{9,1},... | collective-permute-start | bytes 319496 | tf_op jit(solution)/shard_map/ppermute | solution.py:26
  16.0 1.3 %collective-permute-done.refs_4_ = bf16[13,32,128]{2,1,0:T(8,128)(2,1)S(1)} collective-permute-done((bf16[13,32,128]{2,1,0:T(8,128)(2,1)S(1)}, bf16[13,32,128]{2,1,0:T(8,128)(2,1)S(1)}, u32[]{:S(2)}, u32[]{:S(2)}) %collective-permute-start) | collective-permute-done | bytes 106528 | tf_op jit(solution)/shard_map/ppermute | solution.py:26
  17.3 2.8 %collective-permute-start.2 = (bf16[13,32,128]{2,1,0:T(8,128)(2,1)S(1)}, bf16[13,32,128]{2,1,0:T(8,128)(2,1)S(1)}, u32[]{:S(2)}, u32[]{:S(2)}) collective-permute-start(bf16[13,32,128]{2,1,0:T(8,128)(2,1)S(1)} %get-tuple-element.16), channel_id=1, source_target_pairs={{0,12},{1,13},{2,14},{3,15},{4,8},{5,9},{6,10},{7,11},{8,4},{9,5},... | collective-permute-start | bytes 319496 | tf_op jit(solution)/shard_map/ppermute | solution.py:26
  20.1 2.3 %collective-permute-done.1.refs_8_ = bf16[13,32,128]{2,1,0:T(8,128)(2,1)S(1)} collective-permute-done((bf16[13,32,128]{2,1,0:T(8,128)(2,1)S(1)}, bf16[13,32,128]{2,1,0:T(8,128)(2,1)S(1)}, u32[]{:S(2)}, u32[]{:S(2)}) %collective-permute-start.1) | collective-permute-done | bytes 106528 | tf_op jit(solution)/shard_map/ppermute | solution.py:26
  22.4 1.6 %collective-permute-start.4 = (bf16[13,32,128]{2,1,0:T(8,128)(2,1)S(1)}, bf16[13,32,128]{2,1,0:T(8,128)(2,1)S(1)}, u32[]{:S(2)}, u32[]{:S(2)}) collective-permute-start(bf16[13,32,128]{2,1,0:T(8,128)(2,1)S(1)} %get-tuple-element.13.refs_0_), channel_id=1, source_target_pairs={{0,2},{1,3},{2,0},{3,1},{4,6},{5,7},{6,4},{7,5},{8,10},{9,11},{10,... | collective-permute-start | bytes 319496 | tf_op jit(solution)/shard_map/ppermute | solution.py:26
  24.0 0.0 collective-permute-done.2.refs_12_
  24.0 0.0 collective-permute-start.3
  24.0 3.1 %collective-permute-done.4.refs_2_ = bf16[13,32,128]{2,1,0:T(8,128)(2,1)S(1)} collective-permute-done((bf16[13,32,128]{2,1,0:T(8,128)(2,1)S(1)}, bf16[13,32,128]{2,1,0:T(8,128)(2,1)S(1)}, u32[]{:S(2)}, u32[]{:S(2)}) %collective-permute-start.4) | collective-permute-done | bytes 106528 | tf_op jit(solution)/shard_map/ppermute | solution.py:26
  27.1 1.8 %collective-permute-start.7 = (bf16[13,32,128]{2,1,0:T(8,128)(2,1)S(1)}, bf16[13,32,128]{2,1,0:T(8,128)(2,1)S(1)}, u32[]{:S(2)}, u32[]{:S(2)}) collective-permute-start(bf16[13,32,128]{2,1,0:T(8,128)(2,1)S(1)} %collective-permute-done.refs_4_), channel_id=1, source_target_pairs={{0,2},{1,3},{2,0},{3,1},{4,6},{5,7},{6,4},{7,5},{8,10},{9,11},{10,... | collective-permute-start | bytes 319496 | tf_op jit(solution)/shard_map/ppermute | solution.py:26
  28.9 0.0 collective-permute-done.16.refs_18_
  28.9 0.3 collective-permute-start.10
  29.2 0.3 collective-permute-start.9
  29.5 0.0 collective-permute-done.17.refs_19_
  29.5 1.7 %collective-permute-start.13 = (bf16[13,32,128]{2,1,0:T(8,128)(2,1)S(1)}, bf16[13,32,128]{2,1,0:T(8,128)(2,1)S(1)}, u32[]{:S(2)}, u32[]{:S(2)}) collective-permute-start(bf16[13,32,128]{2,1,0:T(8,128)(2,1)S(1)} %collective-permute-done.2.refs_12_), channel_id=1, source_target_pairs={{0,2},{1,3},{2,0},{3,1},{4,6},{5,7},{6,4},{7,5},{8,10},{9,11},{10,... | collective-permute-start | bytes 319496 | tf_op jit(solution)/shard_map/ppermute | solution.py:26
  31.2 1.1 %collective-permute-done.7.refs_6_ = bf16[13,32,128]{2,1,0:T(8,128)(2,1)S(1)} collective-permute-done((bf16[13,32,128]{2,1,0:T(8,128)(2,1)S(1)}, bf16[13,32,128]{2,1,0:T(8,128)(2,1)S(1)}, u32[]{:S(2)}, u32[]{:S(2)}) %collective-permute-start.7) | collective-permute-done | bytes 106528 | tf_op jit(solution)/shard_map/ppermute | solution.py:26
  32.3 0.0 collective-permute-start.12
  32.3 0.5 collective-permute-start.5
  32.8 2.0 %collective-permute-done.10.refs_10_ = bf16[13,32,128]{2,1,0:T(8,128)(2,1)S(1)} collective-permute-done((bf16[13,32,128]{2,1,0:T(8,128)(2,1)S(1)}, bf16[13,32,128]{2,1,0:T(8,128)(2,1)S(1)}, u32[]{:S(2)}, u32[]{:S(2)}) %collective-permute-start.10) | collective-permute-done | bytes 106528 | tf_op jit(solution)/shard_map/ppermute | solution.py:26
  34.8 0.0 collective-permute-done.9.refs_9_
  34.8 0.5 collective-permute-start.11
  35.3 1.3 %collective-permute-done.13.refs_14_ = bf16[13,32,128]{2,1,0:T(8,128)(2,1)S(1)} collective-permute-done((bf16[13,32,128]{2,1,0:T(8,128)(2,1)S(1)}, bf16[13,32,128]{2,1,0:T(8,128)(2,1)S(1)}, u32[]{:S(2)}, u32[]{:S(2)}) %collective-permute-start.13) | collective-permute-done | bytes 106528 | tf_op jit(solution)/shard_map/ppermute | solution.py:26
  36.6 0.0 collective-permute-start.14
  36.6 0.0 collective-permute-done.12.refs_13_
  36.6 0.0 collective-permute-done.5.refs_3_
  36.6 0.0 collective-permute-done.11.refs_11_
  36.7 1.3 %collective-permute-done.14.refs_15_ = bf16[13,32,128]{2,1,0:T(8,128)(2,1)S(1)} collective-permute-done((bf16[13,32,128]{2,1,0:T(8,128)(2,1)S(1)}, bf16[13,32,128]{2,1,0:T(8,128)(2,1)S(1)}, u32[]{:S(2)}, u32[]{:S(2)}) %collective-permute-start.14) | collective-permute-done | bytes 106528 | tf_op jit(solution)/shard_map/ppermute | solution.py:26
  37.9 5.0 %work.1 = (f32[8,16,128]{2,1,0:T(8,128)S(1)}, bf16[8,16,128]{2,1,0:T(8,128)(2,1)S(1)}, bf16[8,16,128]{2,1,0:T(8,128)(2,1)S(1)}, bf16[8,16,128]{2,1,0:T(8,128)(2,1)S(1)}) custom-call(s32[32,19]{1,0:T(8,128)S(1)} %maximum_convert_fusion.plan_ref, bf16[13,32,128]{2,1,0:T(8,128)(2,1)S(1)} %get-tuple-element.13.refs_0_, ...), custom_call_target="tpu_custom_call" | custom-call | tf_op jit(solution)/shard_map/work/pallas_call | solution.py:146
  42.9 0.2 collective-permute-start.18
  43.1 3.4 %collective-permute-start.19 = (bf16[8,16,128]{2,1,0:T(8,128)(2,1)S(1)}, bf16[8,16,128]{2,1,0:T(8,128)(2,1)S(1)}, u32[]{:S(2)}, u32[]{:S(2)}) collective-permute-start(bf16[8,16,128]{2,1,0:T(8,128)(2,1)S(1)} %get-tuple-element.19), channel_id=1, source_target_pairs={{0,8},{1,9},{2,10},{3,11},{4,12},{5,13},{6,14},{7,15},{8,0},{9,1},... | collective-permute-start | bytes 98312 | tf_op jit(solution)/shard_map/ppermute | solution.py:26
  46.5 0.8 %collective-permute-start.20 = (bf16[8,16,128]{2,1,0:T(8,128)(2,1)S(1)}, bf16[8,16,128]{2,1,0:T(8,128)(2,1)S(1)}, u32[]{:S(2)}, u32[]{:S(2)}) collective-permute-start(bf16[8,16,128]{2,1,0:T(8,128)(2,1)S(1)} %get-tuple-element.20), channel_id=1, source_target_pairs={{0,12},{1,13},{2,14},{3,15},{4,8},{5,9},{6,10},{7,11},{8,4},{9,5},... | collective-permute-start | bytes 98312 | tf_op jit(solution)/shard_map/ppermute | solution.py:26
  47.4 1.2 %collective-permute-done.19 = bf16[8,16,128]{2,1,0:T(8,128)(2,1)S(1)} collective-permute-done((bf16[8,16,128]{2,1,0:T(8,128)(2,1)S(1)}, bf16[8,16,128]{2,1,0:T(8,128)(2,1)S(1)}, u32[]{:S(2)}, u32[]{:S(2)}) %collective-permute-start.19) | collective-permute-done | bytes 32800 | tf_op jit(solution)/shard_map/ppermute | solution.py:26
  48.6 3.6 %collective-permute-done.20 = bf16[8,16,128]{2,1,0:T(8,128)(2,1)S(1)} collective-permute-done((bf16[8,16,128]{2,1,0:T(8,128)(2,1)S(1)}, bf16[8,16,128]{2,1,0:T(8,128)(2,1)S(1)}, u32[]{:S(2)}, u32[]{:S(2)}) %collective-permute-start.20) | collective-permute-done | bytes 32800 | tf_op jit(solution)/shard_map/ppermute | solution.py:26
  52.2 0.6 %convert_add_fusion = f32[8,16,128]{2,1,0:T(8,128)} fusion(bf16[8,16,128]{2,1,0:T(8,128)(2,1)S(1)} %collective-permute-done.20, bf16[8,16,128]{2,1,0:T(8,128)(2,1)S(1)} %collective-permute-done.19, f32[8,16,128]{2,1,0:T(8,128)S(1)} %get-tuple-element.17, bf16[8,16,128]{2,1,0:T(8,128)(2,1)S(1)} %collective-permute-done.18), kind=kLoop, calls=%fused_computation | loop fusion | flops 98304 | bytes 229376 | tf_op jit(solution)/shard_map/add | solution.py:169
  (17 shorter events, 0.0 us)
Async XLA Ops:
  0.0 9.8 %copy-start.1 = (bf16[4,2,32,512]{3,2,1,0:T(8,128)(2,1)S(1)}, bf16[4,2,32,512]{3,2,1,0:T(8,128)(2,1)}, u32[]{:S(2)}) copy-start(bf16[4,2,32,512]{3,2,1,0:T(8,128)(2,1)} %first_ref.1) | copy-start | bytes 786436
  0.0 28.9 %collective-permute-start.16 = (bf16[4,16,1024]{2,1,0:T(8,128)(2,1)}, bf16[4,16,1024]{2,1,0:T(8,128)(2,1)S(1)}, u32[]{:S(2)}, u32[]{:S(2)}) collective-permute-start(bf16[4,16,1024]{2,1,0:T(8,128)(2,1)} %refs_16_.1), channel_id=1, source_target_pairs={{0,8},{1,9},{2,10},{3,11},{4,12},{5,13},{6,14},{7,15},{8,0},{9,1},... | collective-permute-start | bytes 393224 | tf_op jit(solution)/shard_map/ppermute | solution.py:26
  4.0 25.2 %collective-permute-start.15 = (bf16[4,16,1024]{2,1,0:T(8,128)(2,1)}, bf16[4,16,1024]{2,1,0:T(8,128)(2,1)S(1)}, u32[]{:S(2)}, u32[]{:S(2)}) collective-permute-start(bf16[4,16,1024]{2,1,0:T(8,128)(2,1)} %refs_16_.1), channel_id=1, source_target_pairs={{0,4},{1,5},{2,6},{3,7},{4,0},{5,1},{6,2},{7,3},{8,12},{9,13},{10,... | collective-permute-start | bytes 393224 | tf_op jit(solution)/shard_map/ppermute | solution.py:26
  5.6 23.9 %collective-permute-start.17 = (bf16[4,16,1024]{2,1,0:T(8,128)(2,1)}, bf16[4,16,1024]{2,1,0:T(8,128)(2,1)S(1)}, u32[]{:S(2)}, u32[]{:S(2)}) collective-permute-start(bf16[4,16,1024]{2,1,0:T(8,128)(2,1)} %refs_16_.1), channel_id=1, source_target_pairs={{0,12},{1,13},{2,14},{3,15},{4,8},{5,9},{6,10},{7,11},{8,4},{9,5},... | collective-permute-start | bytes 393224 | tf_op jit(solution)/shard_map/ppermute | solution.py:26
  9.8 1.2 %copy-start = (bf16[1,2,512,512]{3,2,1,0:T(8,128)(2,1)S(1)}, bf16[1,2,512,512]{3,2,1,0:T(8,128)(2,1)}, u32[]{:S(2)}) copy-start(bf16[1,2,512,512]{3,2,1,0:T(8,128)(2,1)} %param.13) | copy-start | bytes 3145732
  11.0 26.9 %copy-start.2 = (bf16[4,16,1024]{2,1,0:T(8,128)(2,1)S(1)}, bf16[4,16,1024]{2,1,0:T(8,128)(2,1)}, u32[]{:S(2)}) copy-start(bf16[4,16,1024]{2,1,0:T(8,128)(2,1)} %refs_16_.1) | copy-start | bytes 393220
  11.6 5.8 %collective-permute-start = (bf16[13,32,128]{2,1,0:T(8,128)(2,1)S(1)}, bf16[13,32,128]{2,1,0:T(8,128)(2,1)S(1)}, u32[]{:S(2)}, u32[]{:S(2)}) collective-permute-start(bf16[13,32,128]{2,1,0:T(8,128)(2,1)S(1)} %get-tuple-element.14), channel_id=1, source_target_pairs={{0,4},{1,5},{2,6},{3,7},{4,0},{5,1},{6,2},{7,3},{8,12},{9,13},{10,... | collective-permute-start | bytes 319496 | tf_op jit(solution)/shard_map/ppermute | solution.py:26
  12.5 9.9 %collective-permute-start.1 = (bf16[13,32,128]{2,1,0:T(8,128)(2,1)S(1)}, bf16[13,32,128]{2,1,0:T(8,128)(2,1)S(1)}, u32[]{:S(2)}, u32[]{:S(2)}) collective-permute-start(bf16[13,32,128]{2,1,0:T(8,128)(2,1)S(1)} %get-tuple-element.15), channel_id=1, source_target_pairs={{0,8},{1,9},{2,10},{3,11},{4,12},{5,13},{6,14},{7,15},{8,0},{9,1},... | collective-permute-start | bytes 319496 | tf_op jit(solution)/shard_map/ppermute | solution.py:26
  17.3 6.7 %collective-permute-start.2 = (bf16[13,32,128]{2,1,0:T(8,128)(2,1)S(1)}, bf16[13,32,128]{2,1,0:T(8,128)(2,1)S(1)}, u32[]{:S(2)}, u32[]{:S(2)}) collective-permute-start(bf16[13,32,128]{2,1,0:T(8,128)(2,1)S(1)} %get-tuple-element.16), channel_id=1, source_target_pairs={{0,12},{1,13},{2,14},{3,15},{4,8},{5,9},{6,10},{7,11},{8,4},{9,5},... | collective-permute-start | bytes 319496 | tf_op jit(solution)/shard_map/ppermute | solution.py:26
  22.4 4.7 %collective-permute-start.4 = (bf16[13,32,128]{2,1,0:T(8,128)(2,1)S(1)}, bf16[13,32,128]{2,1,0:T(8,128)(2,1)S(1)}, u32[]{:S(2)}, u32[]{:S(2)}) collective-permute-start(bf16[13,32,128]{2,1,0:T(8,128)(2,1)S(1)} %get-tuple-element.13.refs_0_), channel_id=1, source_target_pairs={{0,2},{1,3},{2,0},{3,1},{4,6},{5,7},{6,4},{7,5},{8,10},{9,11},{10,... | collective-permute-start | bytes 319496 | tf_op jit(solution)/shard_map/ppermute | solution.py:26
  24.0 4.9 %collective-permute-start.3 = (bf16[13,32,128]{2,1,0:T(8,128)(2,1)S(1)}, bf16[13,32,128]{2,1,0:T(8,128)(2,1)S(1)}, u32[]{:S(2)}, u32[]{:S(2)}) collective-permute-start(bf16[13,32,128]{2,1,0:T(8,128)(2,1)S(1)} %get-tuple-element.13.refs_0_), channel_id=1, source_target_pairs={{0,1},{1,0},{2,3},{3,2},{4,5},{5,4},{6,7},{7,6},{8,9},{9,8},{10,11... | collective-permute-start | bytes 319496 | tf_op jit(solution)/shard_map/ppermute | solution.py:26
  27.1 5.2 %collective-permute-start.7 = (bf16[13,32,128]{2,1,0:T(8,128)(2,1)S(1)}, bf16[13,32,128]{2,1,0:T(8,128)(2,1)S(1)}, u32[]{:S(2)}, u32[]{:S(2)}) collective-permute-start(bf16[13,32,128]{2,1,0:T(8,128)(2,1)S(1)} %collective-permute-done.refs_4_), channel_id=1, source_target_pairs={{0,2},{1,3},{2,0},{3,1},{4,6},{5,7},{6,4},{7,5},{8,10},{9,11},{10,... | collective-permute-start | bytes 319496 | tf_op jit(solution)/shard_map/ppermute | solution.py:26
  28.9 3.4 %collective-permute-start.6 = (bf16[13,32,128]{2,1,0:T(8,128)(2,1)S(1)}, bf16[13,32,128]{2,1,0:T(8,128)(2,1)S(1)}, u32[]{:S(2)}, u32[]{:S(2)}) collective-permute-start(bf16[13,32,128]{2,1,0:T(8,128)(2,1)S(1)} %collective-permute-done.refs_4_), channel_id=1, source_target_pairs={{0,1},{1,0},{2,3},{3,2},{4,5},{5,4},{6,7},{7,6},{8,9},{9,8},{10,11... | collective-permute-start | bytes 319496 | tf_op jit(solution)/shard_map/ppermute | solution.py:26
  28.9 5.8 %collective-permute-start.10 = (bf16[13,32,128]{2,1,0:T(8,128)(2,1)S(1)}, bf16[13,32,128]{2,1,0:T(8,128)(2,1)S(1)}, u32[]{:S(2)}, u32[]{:S(2)}) collective-permute-start(bf16[13,32,128]{2,1,0:T(8,128)(2,1)S(1)} %collective-permute-done.1.refs_8_), channel_id=1, source_target_pairs={{0,2},{1,3},{2,0},{3,1},{4,6},{5,7},{6,4},{7,5},{8,10},{9,11},{10,... | collective-permute-start | bytes 319496 | tf_op jit(solution)/shard_map/ppermute | solution.py:26
  29.2 5.6 %collective-permute-start.9 = (bf16[13,32,128]{2,1,0:T(8,128)(2,1)S(1)}, bf16[13,32,128]{2,1,0:T(8,128)(2,1)S(1)}, u32[]{:S(2)}, u32[]{:S(2)}) collective-permute-start(bf16[13,32,128]{2,1,0:T(8,128)(2,1)S(1)} %collective-permute-done.1.refs_8_), channel_id=1, source_target_pairs={{0,1},{1,0},{2,3},{3,2},{4,5},{5,4},{6,7},{7,6},{8,9},{9,8},{10,11... | collective-permute-start | bytes 319496 | tf_op jit(solution)/shard_map/ppermute | solution.py:26
  29.5 7.1 %collective-permute-start.13 = (bf16[13,32,128]{2,1,0:T(8,128)(2,1)S(1)}, bf16[13,32,128]{2,1,0:T(8,128)(2,1)S(1)}, u32[]{:S(2)}, u32[]{:S(2)}) collective-permute-start(bf16[13,32,128]{2,1,0:T(8,128)(2,1)S(1)} %collective-permute-done.2.refs_12_), channel_id=1, source_target_pairs={{0,2},{1,3},{2,0},{3,1},{4,6},{5,7},{6,4},{7,5},{8,10},{9,11},{10,... | collective-permute-start | bytes 319496 | tf_op jit(solution)/shard_map/ppermute | solution.py:26
  32.3 4.3 %collective-permute-start.12 = (bf16[13,32,128]{2,1,0:T(8,128)(2,1)S(1)}, bf16[13,32,128]{2,1,0:T(8,128)(2,1)S(1)}, u32[]{:S(2)}, u32[]{:S(2)}) collective-permute-start(bf16[13,32,128]{2,1,0:T(8,128)(2,1)S(1)} %collective-permute-done.2.refs_12_), channel_id=1, source_target_pairs={{0,1},{1,0},{2,3},{3,2},{4,5},{5,4},{6,7},{7,6},{8,9},{9,8},{10,11... | collective-permute-start | bytes 319496 | tf_op jit(solution)/shard_map/ppermute | solution.py:26
  32.3 4.3 %collective-permute-start.5 = (bf16[13,32,128]{2,1,0:T(8,128)(2,1)S(1)}, bf16[13,32,128]{2,1,0:T(8,128)(2,1)S(1)}, u32[]{:S(2)}, u32[]{:S(2)}) collective-permute-start(bf16[13,32,128]{2,1,0:T(8,128)(2,1)S(1)} %collective-permute-done.4.refs_2_), channel_id=1, source_target_pairs={{0,1},{1,0},{2,3},{3,2},{4,5},{5,4},{6,7},{7,6},{8,9},{9,8},{10,11... | collective-permute-start | bytes 319496 | tf_op jit(solution)/shard_map/ppermute | solution.py:26
  34.8 1.9 %collective-permute-start.8 = (bf16[13,32,128]{2,1,0:T(8,128)(2,1)S(1)}, bf16[13,32,128]{2,1,0:T(8,128)(2,1)S(1)}, u32[]{:S(2)}, u32[]{:S(2)}) collective-permute-start(bf16[13,32,128]{2,1,0:T(8,128)(2,1)S(1)} %collective-permute-done.7.refs_6_), channel_id=1, source_target_pairs={{0,1},{1,0},{2,3},{3,2},{4,5},{5,4},{6,7},{7,6},{8,9},{9,8},{10,11... | collective-permute-start | bytes 319496 | tf_op jit(solution)/shard_map/ppermute | solution.py:26
  34.8 1.9 %collective-permute-start.11 = (bf16[13,32,128]{2,1,0:T(8,128)(2,1)S(1)}, bf16[13,32,128]{2,1,0:T(8,128)(2,1)S(1)}, u32[]{:S(2)}, u32[]{:S(2)}) collective-permute-start(bf16[13,32,128]{2,1,0:T(8,128)(2,1)S(1)} %collective-permute-done.10.refs_10_), channel_id=1, source_target_pairs={{0,1},{1,0},{2,3},{3,2},{4,5},{5,4},{6,7},{7,6},{8,9},{9,8},{10,11... | collective-permute-start | bytes 319496 | tf_op jit(solution)/shard_map/ppermute | solution.py:26
  36.6 1.3 %collective-permute-start.14 = (bf16[13,32,128]{2,1,0:T(8,128)(2,1)S(1)}, bf16[13,32,128]{2,1,0:T(8,128)(2,1)S(1)}, u32[]{:S(2)}, u32[]{:S(2)}) collective-permute-start(bf16[13,32,128]{2,1,0:T(8,128)(2,1)S(1)} %collective-permute-done.13.refs_14_), channel_id=1, source_target_pairs={{0,1},{1,0},{2,3},{3,2},{4,5},{5,4},{6,7},{7,6},{8,9},{9,8},{10,11... | collective-permute-start | bytes 319496 | tf_op jit(solution)/shard_map/ppermute | solution.py:26
  42.9 4.5 %collective-permute-start.18 = (bf16[8,16,128]{2,1,0:T(8,128)(2,1)S(1)}, bf16[8,16,128]{2,1,0:T(8,128)(2,1)S(1)}, u32[]{:S(2)}, u32[]{:S(2)}) collective-permute-start(bf16[8,16,128]{2,1,0:T(8,128)(2,1)S(1)} %get-tuple-element.18), channel_id=1, source_target_pairs={{0,4},{1,5},{2,6},{3,7},{4,0},{5,1},{6,2},{7,3},{8,12},{9,13},{10,... | collective-permute-start | bytes 98312 | tf_op jit(solution)/shard_map/ppermute | solution.py:26
  43.1 5.5 %collective-permute-start.19 = (bf16[8,16,128]{2,1,0:T(8,128)(2,1)S(1)}, bf16[8,16,128]{2,1,0:T(8,128)(2,1)S(1)}, u32[]{:S(2)}, u32[]{:S(2)}) collective-permute-start(bf16[8,16,128]{2,1,0:T(8,128)(2,1)S(1)} %get-tuple-element.19), channel_id=1, source_target_pairs={{0,8},{1,9},{2,10},{3,11},{4,12},{5,13},{6,14},{7,15},{8,0},{9,1},... | collective-permute-start | bytes 98312 | tf_op jit(solution)/shard_map/ppermute | solution.py:26
  46.5 5.7 %collective-permute-start.20 = (bf16[8,16,128]{2,1,0:T(8,128)(2,1)S(1)}, bf16[8,16,128]{2,1,0:T(8,128)(2,1)S(1)}, u32[]{:S(2)}, u32[]{:S(2)}) collective-permute-start(bf16[8,16,128]{2,1,0:T(8,128)(2,1)S(1)} %get-tuple-element.20), channel_id=1, source_target_pairs={{0,12},{1,13},{2,14},{3,15},{4,8},{5,9},{6,10},{7,11},{8,4},{9,5},... | collective-permute-start | bytes 98312 | tf_op jit(solution)/shard_map/ppermute | solution.py:26

commit v2 on v0

--- a/solution.py
+++ b/solution.py
@@ -1,9 +1,18 @@
+import functools
+
 import jax
 import jax.numpy as jnp
 from jax import lax
+from jax.experimental import pallas as pl
+from jax.experimental.pallas import tpu as pltpu
 from jax.sharding import PartitionSpec as P
 
 HIGHEST_PRECISION = lax.Precision.HIGHEST
+LANES = 128
+PLANE = 4
+VMEM_BYTES = 32 * 1024 * 1024
+PACK_BYTES = 60 * 1024 * 1024
+HEAD = 8
 
 
 def complex_form(blocks):
@@ -14,7 +23,245 @@
     return jnp.concatenate([upper_half, lower_half], axis=-2)
 
 
-def on_device(prefix, first_suffix, pair_prefix, pair_suffix, merge_count, suffix, routes, cap):
+def swap(x, bit):
+    owners = lax.axis_size("bits")
+    return lax.ppermute(x, "bits", [(i, i ^ bit) for i in range(owners)])
+
+
+def pack_kernel(planes, *refs):
+    sources, outs = refs[:8], refs[8:9 + planes]
+    plan, closed, *copied, sems = refs[9 + planes:]
+    suffix_ref, cap_ref, first_ref, prefix_ref, *numbers = copied
+    pair_prefix_ref, pair_suffix_ref, count_ref, routes_ref = numbers
+    plane = lax.axis_index("bits") // PLANE
+    copies = [pltpu.make_async_copy(source, ref, sems.at[n]) for n, (source, ref) in enumerate(zip(sources, copied))]
+    for copy in copies:
+        copy.start()
+    merges, pieces = pair_prefix_ref.shape
+    listed = routes_ref.shape[1]
+    plan[...] = jnp.zeros_like(plan)
+    for copy in copies[4:]:
+        copy.wait()
+    plan[:merges, :pieces] = pair_prefix_ref[...]
+    plan[merges:2 * merges, :pieces] = pair_suffix_ref[...]
+    plan[2 * merges:2 * merges + 1, :pieces] = count_ref[...]
+    plan[HEAD:HEAD + pieces, :listed] = routes_ref[...]
+    routing = plan[...].astype(jnp.float32).astype(jnp.bfloat16)
+    copies[1].wait()
+    upper = jnp.concatenate([cap_ref[0], cap_ref[1]], axis=0)
+    lower = jnp.concatenate([-cap_ref[1], cap_ref[0]], axis=0)
+    blocks, _, depth, width = first_ref.shape
+    part, span = width // 2, width // (planes // 2)
+    turned = (((1,), (1,)), ((), ()))
+    copies[0].wait()
+    both = lax.dot_general(suffix_ref[0], upper, turned, preferred_element_type=jnp.float32)
+    both += lax.dot_general(suffix_ref[1], lower, turned, preferred_element_type=jnp.float32)
+    closed[...] = both.astype(jnp.bfloat16)
+    copies[2].wait()
+    copies[3].wait()
+    held, rows_piece, twice_width = prefix_ref.shape
+    per = depth // rows_piece
+    for k in range(planes):
+        low, high = plane % 2 ^ k % 2, plane // 2 ^ k // 2
+        entries = []
+        if k < 2:
+            for a in range(blocks):
+                for c in range(2):
+                    for n in range(0, part, LANES):
+                        entries.append(first_ref[a, c, :, pl.ds(pl.multiple_of(low * part + n, LANES), LANES)])
+        for n in range(0, part, depth):
+            entries.append(closed[pl.ds(pl.multiple_of(low * part + n, depth), depth), :])
+        relayed = len(entries)
+        entries.append(routing)
+        for start in range(0, twice_width, width):
+            for n in range(0, span, LANES):
+                columns = pl.ds(pl.multiple_of(high * span + (start + n), LANES), LANES)
+                for row in range(0, held, per):
+                    entries.append(prefix_ref[row:row + per, :, columns].reshape(depth, LANES))
+        for n, entry in enumerate(entries):
+            if k == 0 and n >= relayed:
+                outs[planes][n - relayed] = entry
+            else:
+                outs[k][n] = entry
+
+
+def take_kernel(count, *refs):
+    out = refs[count]
+    for k in range(count):
+        out[k] = refs[k][:out.shape[1]]
+
+
+def take(packs, size):
+    vmem = pl.BlockSpec(memory_space=pltpu.VMEM)
+    return pl.pallas_call(
+        functools.partial(take_kernel, len(packs)),
+        out_shape=jax.ShapeDtypeStruct((len(packs), size) + packs[0].shape[1:], packs[0].dtype),
+        in_specs=[vmem] * len(packs),
+        out_specs=vmem,
+        compiler_params=pltpu.CompilerParams(vmem_limit_bytes=VMEM_BYTES),
+        cost_estimate=pl.CostEstimate(flops=0, bytes_accessed=2 ** 12, transcendentals=0),
+        name="take",
+    )(*packs)
+
+
+def state_kernel(planes, blocks, merges, pieces, rows_piece, held, *refs):
+    relays, packs = refs[:2 * PLANE], refs[2 * PLANE:2 * PLANE + planes]
+    state, plan_out, forms, products, plan, sem = refs[2 * PLANE + planes:]
+    me = lax.axis_index("bits")
+    depth = packs[0].shape[1]
+    span, twice_part = forms.shape[1:]
+    part = twice_part // 2
+    locals_ = []
+    tail = 1 + 2 * (span // LANES) * (held * rows_piece // depth)
+    for k in range(planes):
+        first = packs[k].shape[0] - tail
+        plan_out[k] = packs[k][first].astype(jnp.float32).astype(jnp.int32)
+        locals_.append(packs[k].at[first + 1:first + tail])
+    copy = pltpu.make_async_copy(plan_out, plan, sem)
+    copy.start()
+    for j in range(2 * PLANE):
+        there = pl.ds(pl.multiple_of((me ^ j) % (2 * PLANE) * depth, depth), depth)
+        for a in range(blocks):
+            for n in range(twice_part // LANES):
+                forms[a, there, n * LANES:(n + 1) * LANES] = relays[j][0, a * (twice_part // LANES) + n]
+    chunks = held * rows_piece // depth
+    rows = held * rows_piece
+    left = []
+    for c in range(2):
+        for k in range(planes):
+            columns = []
+            for n in range(span // LANES):
+                first = (c * (span // LANES) + n) * chunks
+                columns.append(locals_[k][first:first + chunks].reshape(rows, LANES))
+            left.append(jnp.concatenate(columns, axis=1))
+    left = jnp.concatenate(left, axis=0)
+    rows *= planes
+    for a in range(blocks):
+        both = jnp.dot(left, forms[a], preferred_element_type=jnp.float32)
+        products[a, :, :part] = both[:rows, :part] - both[rows:, part:]
+        products[a, :, part:] = both[:rows, part:] + both[rows:, :part]
+    copy.wait()
+    for i in range(planes * pieces):
+        k, n = divmod(i, pieces)
+        total = None
+        for m in range(merges):
+            row = pl.multiple_of((k * held + plan[k, m, n]) * rows_piece, rows_piece)
+            term = products[plan[k, merges + m, n], pl.ds(row, rows_piece), :]
+            term = jnp.where(m < plan[k, 2 * merges, n], term, 0.0)
+            total = term if total is None else total + term
+        state[i * rows_piece:(i + 1) * rows_piece, :] = total.astype(jnp.bfloat16)
+
+
+def close_kernel(planes, listed, pieces, rows_piece, plan, state, *refs):
+    slots = planes * PLANE
+    relays, outs = refs[:2 * PLANE + PLANE], refs[3 * PLANE:3 * PLANE + planes]
+    wide, terms = refs[3 * PLANE + planes:]
+    me = lax.axis_index("bits")
+    part = wide.shape[0] // 2
+    lane = lax.broadcasted_iota(jnp.int32, (part, LANES), 1)
+    for j in range(slots):
+        n, b = divmod(j, PLANE)
+        relay = relays[min(n, 2) * PLANE + b]
+        first = relay.shape[1] - part // relay.shape[2]
+        real_rows = relay[max(n - 2, 0), first:].reshape(part, LANES)
+        turned = pltpu.roll(real_rows.astype(jnp.float32), LANES // 2, 1)
+        turned = jnp.where(lane < LANES // 2, -turned, turned)
+        wide[:part, j * LANES:(j + 1) * LANES] = real_rows
+        wide[part:, j * LANES:(j + 1) * LANES] = turned.astype(jnp.bfloat16)
+    for j in range(0, slots, 2):
+        both = jnp.dot(state[...], wide[:, j * LANES:(j + 2) * LANES], preferred_element_type=jnp.float32)
+        terms[j] = both[:, :LANES]
+        terms[j + 1] = both[:, LANES:]
+    for i in range(planes * pieces):
+        k, n = divmod(i, pieces)
+        total = None
+        for m in range(listed):
+            slot = plan[k, HEAD + n, m] ^ me
+            term = terms[slot, i * rows_piece:(i + 1) * rows_piece, :]
+            total = term if total is None else total + term
+        outs[k][n] = total.astype(outs[k].dtype)
+
+
+def in_planes(prefix, first_suffix, pair_prefix, pair_suffix, merge_count, suffix, routes, cap):
+    owners = lax.axis_size("bits")
+    planes = owners // PLANE
+    pieces, merges = pair_prefix.shape
+    listed = routes.shape[1]
+    held, rows_piece, twice_width = prefix.shape
+    blocks, _, depth, width = first_suffix.shape
+    part, span = width // 2, width // (planes // 2)
+    vmem = pl.BlockSpec(memory_space=pltpu.VMEM)
+    smem = pl.BlockSpec(memory_space=pltpu.SMEM)
+    params = pltpu.CompilerParams(vmem_limit_bytes=VMEM_BYTES)
+    forms_size, closed_size = 2 * blocks * (part // LANES), part // depth
+    tail = 1 + 2 * (span // LANES) * (held * rows_piece // depth)
+    sources = (
+        suffix[0],
+        jnp.swapaxes(cap, 1, 2),
+        first_suffix,
+        prefix,
+        pair_prefix.T,
+        pair_suffix.T,
+        merge_count[None],
+        routes,
+    )
+    sizes = [forms_size + closed_size, forms_size + closed_size + tail] + [closed_size + tail] * (planes - 2) + [tail]
+    *packs, local = pl.pallas_call(
+        functools.partial(pack_kernel, planes),
+        out_shape=[jax.ShapeDtypeStruct((size, depth, LANES), jnp.bfloat16) for size in sizes],
+        in_specs=[pl.BlockSpec(memory_space=pl.ANY)] * len(sources),
+        out_specs=[vmem] * len(sizes),
+        scratch_shapes=[pltpu.VMEM((depth, LANES), jnp.int32), pltpu.VMEM((width, LANES), jnp.bfloat16)]
+        + [pltpu.VMEM(source.shape, source.dtype) for source in sources]
+        + [pltpu.SemaphoreType.DMA((len(sources),))],
+        compiler_params=pltpu.CompilerParams(vmem_limit_bytes=PACK_BYTES),
+        cost_estimate=pl.CostEstimate(flops=2 ** 20, bytes_accessed=2 ** 12, transcendentals=0),
+        name="pack",
+    )(*sources)
+    relay = packs[0][None]
+    packs = [local] + [swap(packs[k], k * PLANE) for k in range(1, planes)]
+    relays = [relay, take(packs[1:2], forms_size + closed_size), take(packs[2:], closed_size)]
+    relays = [(r, swap(r, 1), y, swap(y, 1)) for r, y in [(r, swap(r, 2)) for r in relays]]
+    rows = planes * pieces * rows_piece
+    state, plan = pl.pallas_call(
+        functools.partial(state_kernel, planes, blocks, merges, pieces, rows_piece, held),
+        out_shape=[
+            jax.ShapeDtypeStruct((rows, 2 * part), jnp.bfloat16),
+            jax.ShapeDtypeStruct((planes, depth, LANES), jnp.int32),
+        ],
+        in_specs=[vmem] * (2 * PLANE + planes),
+        out_specs=[vmem] * 2,
+        scratch_shapes=[
+            pltpu.VMEM((blocks, span, 2 * part), jnp.bfloat16),
+            pltpu.VMEM((blocks, planes * held * rows_piece, 2 * part), jnp.float32),
+            pltpu.SMEM((planes, depth, LANES), jnp.int32),
+            pltpu.SemaphoreType.DMA,
+        ],
+        compiler_params=params,
+        name="state",
+    )(*relays[0], *relays[1], *packs)
+    sums = pl.pallas_call(
+        functools.partial(close_kernel, planes, listed, pieces, rows_piece),
+        out_shape=[
+            jax.ShapeDtypeStruct((pieces, rows_piece, LANES), jnp.float32 if k == 0 else jnp.bfloat16)
+            for k in range(planes)
+        ],
+        in_specs=[smem] + [vmem] * (1 + 3 * PLANE),
+        out_specs=[vmem] * planes,
+        scratch_shapes=[
+            pltpu.VMEM((2 * part, owners * LANES), jnp.bfloat16),
+            pltpu.VMEM((owners, rows, LANES), jnp.float32),
+        ],
+        compiler_params=params,
+        name="close",
+    )(plan, state, *relays[0], *relays[1], *relays[2])
+    total = sums[0]
+    for k in range(1, planes):
+        total = total + swap(sums[k], k * PLANE).astype(jnp.float32)
+    return total
+
+
+def by_owner(prefix, first_suffix, pair_prefix, pair_suffix, merge_count, suffix, routes, cap):
     pieces = pair_prefix.shape[0]
     merges = pair_prefix.shape[1]
     held_blocks = prefix.shape[0]
@@ -84,6 +331,32 @@
     )
 
 
+def on_device(*args):
+    prefix, first_suffix, pair_prefix, routes, cap = args[0], args[1], args[2], args[6], args[7]
+    owners = lax.axis_size("bits")
+    planes = owners // PLANE
+    depth, width = first_suffix.shape[2:]
+    pieces, merges = pair_prefix.shape
+    fits = (
+        planes > 2
+        and planes & (planes - 1) == 0
+        and owners <= 256
+        and width == owners * depth
+        and width % (planes // 2 * LANES) == 0
+        and width // 2 % LANES == 0
+        and 2 * cap.shape[2] == LANES
+        and depth % 16 == 0
+        and LANES % depth == 0
+        and depth % prefix.shape[1] == 0
+        and prefix.shape[0] * prefix.shape[1] % depth == 0
+        and prefix.shape[1] % 16 == 0
+        and 2 * merges < HEAD
+        and HEAD + pieces <= depth
+        and max(pieces, routes.shape[1]) <= LANES
+    )
+    return in_planes(*args) if fits else by_owner(*args)
+
+
 def solution(mesh):
     return jax.shard_map(
         on_device,

time: 206 us -> 44.4 us (0.22)
  waiting for transfers between devices: 126 us -> 17 us
  blocking collectives: 33.9 us -> 0 us
  between operations: 13.5 us -> 0.09 us
  local copies, waits for them, and re-layouts: 13.4 us -> 0.01 us
  matrix products: 12.7 us -> 0 us
  starting transfers between devices: 4.85 us -> 17.4 us
  Pallas kernels: 0 us -> 9.08 us
    all_to_all x1 -> x0, waiting for transfers between devices: 77 us -> none  [on_device(): lax.all_to_all(outgoing, 'bits', split_axis=0, concat_axis=0, tiled=True)]
    all_gather x1 -> x0, waiting for transfers between devices: 49.4 us -> none  [on_device(): portion = lax.all_gather(first_suffix, 'bits', axis=2, tiled=True)]
    all_to_all x1 -> x0, blocking collectives: 33.9 us -> none  [on_device(): lax.all_to_all(capped_terms.astype(jnp.bfloat16), 'bits', split_axis=0, c...]
    ppermute x0 -> x15, starting transfers between devices: none -> 17.4 us  [swap(): return lax.ppermute(x, 'bits', [(i, i ^ bit) for i in range(owners)])]
    ppermute x0 -> x15, waiting for transfers between devices: none -> 17 us  [swap(): return lax.ppermute(x, 'bits', [(i, i ^ bit) for i in range(owners)])]
    dot_general x6 -> x0, matrix products: 12.7 us -> none  [the longest x1 7.92 us: on_device(): jnp.einsum('smrw,wv->smrv', products, cap_form, preferred_element_type=jn...]
    pallas_call x0 -> x5, Pallas kernels: none -> 9.08 us  [the longest x1 3.49 us: in_planes(): pl.pallas_call(functools.partial(close_kernel, planes, listed, pieces, ro...]
    convert_element_type x3 -> x0, local copies, waits for them, and re-layouts: 5.03 us -> none  [the longest x1 4.3 us: on_device(): outgoing = jnp.einsum('dmi,irc->dmrc', dispatch, state_rows, preferred_el...]
  transfers between devices with their start and end apart: 2 -> 15, of which waited for: 2 -> 5; matrix products, arithmetic and copies ran while one was open for 3% -> 0% of each run, Pallas kernels for 0% -> 6%
where the time goes in v2:
time: 44.4 us; the launch traced here: 44.2 us
  starting transfers between devices  17.4 us (39%)
  waiting for transfers between devices  17 us (38%)
  Pallas kernels  9.08 us (20%)
  other arithmetic  0.65 us (1%)
    ppermute x15, starting transfers between devices, swap(): return lax.ppermute(x, 'bits', [(i, i ^ bit) for i in range(owners)])  17.4 us
    ppermute x15, waiting for transfers between devices, swap(): return lax.ppermute(x, 'bits', [(i, i ^ bit) for i in range(owners)])  17 us
    pallas_call x1, Pallas kernels, in_planes(): pl.pallas_call(functools.partial(close_kernel, planes, listed, pieces, ro...  3.49 us
    pallas_call x1, Pallas kernels, in_planes(): pl.pallas_call(functools.partial(state_kernel, planes, blocks, merges, pi...  2.8 us
    pallas_call x1, Pallas kernels, in_planes(): pl.pallas_call(functools.partial(pack_kernel, planes), out_shape=[jax.Sha...  2.77 us
  transfers between devices with their start and end apart: 15, of which 5 were waited for; matrix products, arithmetic and copies ran while one was open for 0% of the time, Pallas kernels for 6%

profile of v2, /device:TPU:0, one launch (start us, length us, event | category | flops | bytes accessed | tf_op | source)
XLA Modules:
  0.0 44.2 jit_solution(6050084357303425820)
XLA Ops:
  0.0 2.8 %pack.1 = (bf16[24,32,128]{2,1,0:T(8,128)(2,1)}, bf16[33,32,128]{2,1,0:T(8,128)(2,1)}, bf16[17,32,128]{2,1,0:T(8,128)(2,1)}, bf16[17,32,128]{2,1,0:T(8,128)(2,1)}, bf16[9,32,128]{2,1,0:T(8,128)(2,1)}) custom-call(bf16[2,512,512]{2,1,0:T(8,128)(2,1)} %bitcast.10, bf16[2,64,512]{2,1,0:T(8,128)(2,1)} %bitcast.11, bf16[4,2,32,512]{3,2,1,0:T(8,128)(2,1)} %refs_2_.1, ...), custom_call_target="tpu_custom_call" | custom-call | flops 1048576 | bytes 4096 | tf_op jit(solution)/shard_map/pack/pallas_call | solution.py:209
  2.8 3.1 %collective-permute-start.3 = (bf16[33,32,128]{2,1,0:T(8,128)(2,1)}, bf16[33,32,128]{2,1,0:T(8,128)(2,1)S(1)}, u32[]{:S(2)}, u32[]{:S(2)}) collective-permute-start(bf16[33,32,128]{2,1,0:T(8,128)(2,1)} %get-tuple-element.17), channel_id=1, source_target_pairs={{0,4},{1,5},{2,6},{3,7},{4,0},{5,1},{6,2},{7,3},{8,12},{9,13},{10,... | collective-permute-start | bytes 811016 | tf_op jit(solution)/shard_map/ppermute | solution.py:28
  5.9 2.6 %collective-permute-start.7 = (bf16[17,32,128]{2,1,0:T(8,128)(2,1)}, bf16[17,32,128]{2,1,0:T(8,128)(2,1)S(1)}, u32[]{:S(2)}, u32[]{:S(2)}) collective-permute-start(bf16[17,32,128]{2,1,0:T(8,128)(2,1)} %get-tuple-element.19), channel_id=1, source_target_pairs={{0,8},{1,9},{2,10},{3,11},{4,12},{5,13},{6,14},{7,15},{8,0},{9,1},... | collective-permute-start | bytes 417800 | tf_op jit(solution)/shard_map/ppermute | solution.py:28
  8.5 0.0 collective-permute-start.8
  8.5 0.0 copy-start
  8.5 1.7 %collective-permute-start.1 = (bf16[1,24,32,128]{3,2,1,0:T(8,128)(2,1)}, bf16[1,24,32,128]{3,2,1,0:T(8,128)(2,1)S(1)}, u32[]{:S(2)}, u32[]{:S(2)}) collective-permute-start(bf16[1,24,32,128]{3,2,1,0:T(8,128)(2,1)} %bitcast.6), channel_id=1, source_target_pairs={{0,2},{1,3},{2,0},{3,1},{4,6},{5,7},{6,4},{7,5},{8,10},{9,11},{10,... | collective-permute-start | bytes 589832 | tf_op jit(solution)/shard_map/ppermute | solution.py:28
  10.2 5.3 %collective-permute-done.3.refs_0_.refs_9_ = bf16[33,32,128]{2,1,0:T(8,128)(2,1)S(1)} collective-permute-done((bf16[33,32,128]{2,1,0:T(8,128)(2,1)}, bf16[33,32,128]{2,1,0:T(8,128)(2,1)S(1)}, u32[]{:S(2)}, u32[]{:S(2)}) %collective-permute-start.3) | collective-permute-done | bytes 270368 | tf_op jit(solution)/shard_map/ppermute | solution.py:28
  15.6 0.0 copy-start.1
  15.6 1.7 %collective-permute-start.5 = (bf16[1,24,32,128]{3,2,1,0:T(8,128)(2,1)S(1)}, bf16[1,24,32,128]{3,2,1,0:T(8,128)(2,1)S(1)}, u32[]{:S(2)}, u32[]{:S(2)}) collective-permute-start(bf16[1,24,32,128]{3,2,1,0:T(8,128)(2,1)S(1)} %take.2.refs_4_), channel_id=1, source_target_pairs={{0,2},{1,3},{2,0},{3,1},{4,6},{5,7},{6,4},{7,5},{8,10},{9,11},{10,... | collective-permute-start | bytes 589832 | tf_op jit(solution)/shard_map/ppermute | solution.py:28
  17.3 0.0 copy-done
  17.3 0.0 collective-permute-start
  17.3 0.0 collective-permute-done.7.refs_10_.refs_0_
  17.3 3.5 %collective-permute-done.8.refs_11_.refs_1_ = bf16[17,32,128]{2,1,0:T(8,128)(2,1)S(1)} collective-permute-done((bf16[17,32,128]{2,1,0:T(8,128)(2,1)}, bf16[17,32,128]{2,1,0:T(8,128)(2,1)S(1)}, u32[]{:S(2)}, u32[]{:S(2)}) %collective-permute-start.8) | collective-permute-done | bytes 139296 | tf_op jit(solution)/shard_map/ppermute | solution.py:28
  20.8 1.6 %collective-permute-start.10 = (bf16[2,8,32,128]{3,2,1,0:T(8,128)(2,1)S(1)}, bf16[2,8,32,128]{3,2,1,0:T(8,128)(2,1)S(1)}, u32[]{:S(2)}, u32[]{:S(2)}) collective-permute-start(bf16[2,8,32,128]{3,2,1,0:T(8,128)(2,1)S(1)} %take.3.refs_8_), channel_id=1, source_target_pairs={{0,2},{1,3},{2,0},{3,1},{4,6},{5,7},{6,4},{7,5},{8,10},{9,11},{10,... | collective-permute-start | bytes 393224 | tf_op jit(solution)/shard_map/ppermute | solution.py:28
  22.4 0.0 collective-permute-done.1.refs_2_
  22.4 0.0 collective-permute-start.2
  22.4 0.5 %collective-permute-start.4 = (bf16[1,24,32,128]{3,2,1,0:T(8,128)(2,1)S(1)}, bf16[1,24,32,128]{3,2,1,0:T(8,128)(2,1)S(1)}, u32[]{:S(2)}, u32[]{:S(2)}) collective-permute-start(bf16[1,24,32,128]{3,2,1,0:T(8,128)(2,1)S(1)} %take.2.refs_4_), channel_id=1, source_target_pairs={{0,1},{1,0},{2,3},{3,2},{4,5},{5,4},{6,7},{7,6},{8,9},{9,8},{10,11... | collective-permute-start | bytes 589832 | tf_op jit(solution)/shard_map/ppermute | solution.py:28
  22.9 0.0 collective-permute-done.5.refs_6_
  22.9 0.0 collective-permute-start.6
  22.9 0.0 collective-permute-done.refs_1_
  22.9 0.5 %collective-permute-start.9 = (bf16[2,8,32,128]{3,2,1,0:T(8,128)(2,1)S(1)}, bf16[2,8,32,128]{3,2,1,0:T(8,128)(2,1)S(1)}, u32[]{:S(2)}, u32[]{:S(2)}) collective-permute-start(bf16[2,8,32,128]{3,2,1,0:T(8,128)(2,1)S(1)} %take.3.refs_8_), channel_id=1, source_target_pairs={{0,1},{1,0},{2,3},{3,2},{4,5},{5,4},{6,7},{7,6},{8,9},{9,8},{10,11... | collective-permute-start | bytes 393224 | tf_op jit(solution)/shard_map/ppermute | solution.py:28
  23.5 2.4 %collective-permute-done.10.refs_10_ = bf16[2,8,32,128]{3,2,1,0:T(8,128)(2,1)S(1)} collective-permute-done((bf16[2,8,32,128]{3,2,1,0:T(8,128)(2,1)S(1)}, bf16[2,8,32,128]{3,2,1,0:T(8,128)(2,1)S(1)}, u32[]{:S(2)}, u32[]{:S(2)}) %collective-permute-start.10) | collective-permute-done | bytes 131104 | tf_op jit(solution)/shard_map/ppermute | solution.py:28
  25.9 0.0 collective-permute-start.11
  25.9 0.0 collective-permute-done.2.refs_3_
  25.9 0.0 collective-permute-done.4.refs_5_
  25.9 0.0 collective-permute-done.6.refs_7_
  25.9 0.0 copy-done.1
  25.9 2.8 %state.1 = (bf16[512,512]{1,0:T(8,128)(2,1)S(1)}, s32[4,32,128]{2,1,0:T(8,128)S(1)}) custom-call(bf16[1,24,32,128]{3,2,1,0:T(8,128)(2,1)S(1)} %bitcast.8, bf16[1,24,32,128]{3,2,1,0:T(8,128)(2,1)S(1)} %collective-permute-done.refs_1_, bf16[1,24,32,128]{3,2,1,0:T(8,128)(2,1)S(1)} %collective-permute-done.1.refs_2_, ...), custom_call_target="tpu_custom_call" | custom-call | tf_op jit(solution)/shard_map/state/pallas_call | solution.py:226
  28.7 0.0 collective-permute-done.9.refs_9_
  28.7 0.0 collective-permute-done.11.refs_11_
  28.7 3.5 %close.1 = (f32[8,16,128]{2,1,0:T(8,128)S(1)}, bf16[8,16,128]{2,1,0:T(8,128)(2,1)S(1)}, bf16[8,16,128]{2,1,0:T(8,128)(2,1)S(1)}, bf16[8,16,128]{2,1,0:T(8,128)(2,1)S(1)}) custom-call(s32[4,32,128]{2,1,0:T(8,128)S(1)} %get-tuple-element.21.plan, bf16[512,512]{1,0:T(8,128)(2,1)S(1)} %get-tuple-element.22.state, bf16[1,24,32,128]{3,2,1,0:T(8,128)(2,1)S(1)} %bitcast.9, ...), custom_call_target="tpu_custom_call" | custom-call | tf_op jit(solution)/shard_map/close/pallas_call | solution.py:243
  32.2 0.9 %collective-permute-start.12 = (bf16[8,16,128]{2,1,0:T(8,128)(2,1)S(1)}, bf16[8,16,128]{2,1,0:T(8,128)(2,1)S(1)}, u32[]{:S(2)}, u32[]{:S(2)}) collective-permute-start(bf16[8,16,128]{2,1,0:T(8,128)(2,1)S(1)} %get-tuple-element.24), channel_id=1, source_target_pairs={{0,4},{1,5},{2,6},{3,7},{4,0},{5,1},{6,2},{7,3},{8,12},{9,13},{10,... | collective-permute-start | bytes 98312 | tf_op jit(solution)/shard_map/ppermute | solution.py:28
  33.1 4.7 %collective-permute-start.13 = (bf16[8,16,128]{2,1,0:T(8,128)(2,1)S(1)}, bf16[8,16,128]{2,1,0:T(8,128)(2,1)S(1)}, u32[]{:S(2)}, u32[]{:S(2)}) collective-permute-start(bf16[8,16,128]{2,1,0:T(8,128)(2,1)S(1)} %get-tuple-element.25), channel_id=1, source_target_pairs={{0,8},{1,9},{2,10},{3,11},{4,12},{5,13},{6,14},{7,15},{8,0},{9,1},... | collective-permute-start | bytes 98312 | tf_op jit(solution)/shard_map/ppermute | solution.py:28
  37.8 0.0 collective-permute-start.14
  37.9 0.0 collective-permute-done.12
  37.9 2.6 %collective-permute-done.13 = bf16[8,16,128]{2,1,0:T(8,128)(2,1)S(1)} collective-permute-done((bf16[8,16,128]{2,1,0:T(8,128)(2,1)S(1)}, bf16[8,16,128]{2,1,0:T(8,128)(2,1)S(1)}, u32[]{:S(2)}, u32[]{:S(2)}) %collective-permute-start.13) | collective-permute-done | bytes 32800 | tf_op jit(solution)/shard_map/ppermute | solution.py:28
  40.5 3.1 %collective-permute-done.14 = bf16[8,16,128]{2,1,0:T(8,128)(2,1)S(1)} collective-permute-done((bf16[8,16,128]{2,1,0:T(8,128)(2,1)S(1)}, bf16[8,16,128]{2,1,0:T(8,128)(2,1)S(1)}, u32[]{:S(2)}, u32[]{:S(2)}) %collective-permute-start.14) | collective-permute-done | bytes 32800 | tf_op jit(solution)/shard_map/ppermute | solution.py:28
  43.6 0.6 %convert_add_fusion = f32[8,16,128]{2,1,0:T(8,128)} fusion(bf16[8,16,128]{2,1,0:T(8,128)(2,1)S(1)} %collective-permute-done.14, bf16[8,16,128]{2,1,0:T(8,128)(2,1)S(1)} %collective-permute-done.13, f32[8,16,128]{2,1,0:T(8,128)S(1)} %get-tuple-element.23, bf16[8,16,128]{2,1,0:T(8,128)(2,1)S(1)} %collective-permute-done.12), kind=kLoop, calls=%fused_computation | loop fusion | flops 98304 | bytes 229376 | tf_op jit(solution)/shard_map/add | solution.py:260
  (2 shorter events, 0.0 us)
Async XLA Ops:
  2.8 12.8 %collective-permute-start.3 = (bf16[33,32,128]{2,1,0:T(8,128)(2,1)}, bf16[33,32,128]{2,1,0:T(8,128)(2,1)S(1)}, u32[]{:S(2)}, u32[]{:S(2)}) collective-permute-start(bf16[33,32,128]{2,1,0:T(8,128)(2,1)} %get-tuple-element.17), channel_id=1, source_target_pairs={{0,4},{1,5},{2,6},{3,7},{4,0},{5,1},{6,2},{7,3},{8,12},{9,13},{10,... | collective-permute-start | bytes 811016 | tf_op jit(solution)/shard_map/ppermute | solution.py:28
  5.9 11.5 %collective-permute-start.7 = (bf16[17,32,128]{2,1,0:T(8,128)(2,1)}, bf16[17,32,128]{2,1,0:T(8,128)(2,1)S(1)}, u32[]{:S(2)}, u32[]{:S(2)}) collective-permute-start(bf16[17,32,128]{2,1,0:T(8,128)(2,1)} %get-tuple-element.19), channel_id=1, source_target_pairs={{0,8},{1,9},{2,10},{3,11},{4,12},{5,13},{6,14},{7,15},{8,0},{9,1},... | collective-permute-start | bytes 417800 | tf_op jit(solution)/shard_map/ppermute | solution.py:28
  8.5 12.4 %collective-permute-start.8 = (bf16[17,32,128]{2,1,0:T(8,128)(2,1)}, bf16[17,32,128]{2,1,0:T(8,128)(2,1)S(1)}, u32[]{:S(2)}, u32[]{:S(2)}) collective-permute-start(bf16[17,32,128]{2,1,0:T(8,128)(2,1)} %get-tuple-element.20), channel_id=1, source_target_pairs={{0,12},{1,13},{2,14},{3,15},{4,8},{5,9},{6,10},{7,11},{8,4},{9,5},... | collective-permute-start | bytes 417800 | tf_op jit(solution)/shard_map/ppermute | solution.py:28
  8.5 8.9 %copy-start = (bf16[24,32,128]{2,1,0:T(8,128)(2,1)S(1)}, bf16[24,32,128]{2,1,0:T(8,128)(2,1)}, u32[]{:S(2)}) copy-start(bf16[24,32,128]{2,1,0:T(8,128)(2,1)} %get-tuple-element.16) | copy-start | bytes 589828
  8.5 14.0 %collective-permute-start.1 = (bf16[1,24,32,128]{3,2,1,0:T(8,128)(2,1)}, bf16[1,24,32,128]{3,2,1,0:T(8,128)(2,1)S(1)}, u32[]{:S(2)}, u32[]{:S(2)}) collective-permute-start(bf16[1,24,32,128]{3,2,1,0:T(8,128)(2,1)} %bitcast.6), channel_id=1, source_target_pairs={{0,2},{1,3},{2,0},{3,1},{4,6},{5,7},{6,4},{7,5},{8,10},{9,11},{10,... | collective-permute-start | bytes 589832 | tf_op jit(solution)/shard_map/ppermute | solution.py:28
  15.6 10.3 %copy-start.1 = (bf16[9,32,128]{2,1,0:T(8,128)(2,1)S(1)}, bf16[9,32,128]{2,1,0:T(8,128)(2,1)}, u32[]{:S(2)}) copy-start(bf16[9,32,128]{2,1,0:T(8,128)(2,1)} %get-tuple-element.18.refs_8_) | copy-start | bytes 221188
  15.6 7.4 %collective-permute-start.5 = (bf16[1,24,32,128]{3,2,1,0:T(8,128)(2,1)S(1)}, bf16[1,24,32,128]{3,2,1,0:T(8,128)(2,1)S(1)}, u32[]{:S(2)}, u32[]{:S(2)}) collective-permute-start(bf16[1,24,32,128]{3,2,1,0:T(8,128)(2,1)S(1)} %take.2.refs_4_), channel_id=1, source_target_pairs={{0,2},{1,3},{2,0},{3,1},{4,6},{5,7},{6,4},{7,5},{8,10},{9,11},{10,... | collective-permute-start | bytes 589832 | tf_op jit(solution)/shard_map/ppermute | solution.py:28
  17.3 5.6 %collective-permute-start = (bf16[1,24,32,128]{3,2,1,0:T(8,128)(2,1)S(1)}, bf16[1,24,32,128]{3,2,1,0:T(8,128)(2,1)S(1)}, u32[]{:S(2)}, u32[]{:S(2)}) collective-permute-start(bf16[1,24,32,128]{3,2,1,0:T(8,128)(2,1)S(1)} %bitcast.7), channel_id=1, source_target_pairs={{0,1},{1,0},{2,3},{3,2},{4,5},{5,4},{6,7},{7,6},{8,9},{9,8},{10,11... | collective-permute-start | bytes 589832 | tf_op jit(solution)/shard_map/ppermute | solution.py:28
  20.8 5.0 %collective-permute-start.10 = (bf16[2,8,32,128]{3,2,1,0:T(8,128)(2,1)S(1)}, bf16[2,8,32,128]{3,2,1,0:T(8,128)(2,1)S(1)}, u32[]{:S(2)}, u32[]{:S(2)}) collective-permute-start(bf16[2,8,32,128]{3,2,1,0:T(8,128)(2,1)S(1)} %take.3.refs_8_), channel_id=1, source_target_pairs={{0,2},{1,3},{2,0},{3,1},{4,6},{5,7},{6,4},{7,5},{8,10},{9,11},{10,... | collective-permute-start | bytes 393224 | tf_op jit(solution)/shard_map/ppermute | solution.py:28
  22.4 3.5 %collective-permute-start.2 = (bf16[1,24,32,128]{3,2,1,0:T(8,128)(2,1)S(1)}, bf16[1,24,32,128]{3,2,1,0:T(8,128)(2,1)S(1)}, u32[]{:S(2)}, u32[]{:S(2)}) collective-permute-start(bf16[1,24,32,128]{3,2,1,0:T(8,128)(2,1)S(1)} %collective-permute-done.1.refs_2_), channel_id=1, source_target_pairs={{0,1},{1,0},{2,3},{3,2},{4,5},{5,4},{6,7},{7,6},{8,9},{9,8},{10,11... | collective-permute-start | bytes 589832 | tf_op jit(solution)/shard_map/ppermute | solution.py:28
  22.4 3.5 %collective-permute-start.4 = (bf16[1,24,32,128]{3,2,1,0:T(8,128)(2,1)S(1)}, bf16[1,24,32,128]{3,2,1,0:T(8,128)(2,1)S(1)}, u32[]{:S(2)}, u32[]{:S(2)}) collective-permute-start(bf16[1,24,32,128]{3,2,1,0:T(8,128)(2,1)S(1)} %take.2.refs_4_), channel_id=1, source_target_pairs={{0,1},{1,0},{2,3},{3,2},{4,5},{5,4},{6,7},{7,6},{8,9},{9,8},{10,11... | collective-permute-start | bytes 589832 | tf_op jit(solution)/shard_map/ppermute | solution.py:28
  22.9 2.9 %collective-permute-start.6 = (bf16[1,24,32,128]{3,2,1,0:T(8,128)(2,1)S(1)}, bf16[1,24,32,128]{3,2,1,0:T(8,128)(2,1)S(1)}, u32[]{:S(2)}, u32[]{:S(2)}) collective-permute-start(bf16[1,24,32,128]{3,2,1,0:T(8,128)(2,1)S(1)} %collective-permute-done.5.refs_6_), channel_id=1, source_target_pairs={{0,1},{1,0},{2,3},{3,2},{4,5},{5,4},{6,7},{7,6},{8,9},{9,8},{10,11... | collective-permute-start | bytes 589832 | tf_op jit(solution)/shard_map/ppermute | solution.py:28
  22.9 5.8 %collective-permute-start.9 = (bf16[2,8,32,128]{3,2,1,0:T(8,128)(2,1)S(1)}, bf16[2,8,32,128]{3,2,1,0:T(8,128)(2,1)S(1)}, u32[]{:S(2)}, u32[]{:S(2)}) collective-permute-start(bf16[2,8,32,128]{3,2,1,0:T(8,128)(2,1)S(1)} %take.3.refs_8_), channel_id=1, source_target_pairs={{0,1},{1,0},{2,3},{3,2},{4,5},{5,4},{6,7},{7,6},{8,9},{9,8},{10,11... | collective-permute-start | bytes 393224 | tf_op jit(solution)/shard_map/ppermute | solution.py:28
  25.9 2.9 %collective-permute-start.11 = (bf16[2,8,32,128]{3,2,1,0:T(8,128)(2,1)S(1)}, bf16[2,8,32,128]{3,2,1,0:T(8,128)(2,1)S(1)}, u32[]{:S(2)}, u32[]{:S(2)}) collective-permute-start(bf16[2,8,32,128]{3,2,1,0:T(8,128)(2,1)S(1)} %collective-permute-done.10.refs_10_), channel_id=1, source_target_pairs={{0,1},{1,0},{2,3},{3,2},{4,5},{5,4},{6,7},{7,6},{8,9},{9,8},{10,11... | collective-permute-start | bytes 393224 | tf_op jit(solution)/shard_map/ppermute | solution.py:28
  32.2 5.6 %collective-permute-start.12 = (bf16[8,16,128]{2,1,0:T(8,128)(2,1)S(1)}, bf16[8,16,128]{2,1,0:T(8,128)(2,1)S(1)}, u32[]{:S(2)}, u32[]{:S(2)}) collective-permute-start(bf16[8,16,128]{2,1,0:T(8,128)(2,1)S(1)} %get-tuple-element.24), channel_id=1, source_target_pairs={{0,4},{1,5},{2,6},{3,7},{4,0},{5,1},{6,2},{7,3},{8,12},{9,13},{10,... | collective-permute-start | bytes 98312 | tf_op jit(solution)/shard_map/ppermute | solution.py:28
  33.1 7.3 %collective-permute-start.13 = (bf16[8,16,128]{2,1,0:T(8,128)(2,1)S(1)}, bf16[8,16,128]{2,1,0:T(8,128)(2,1)S(1)}, u32[]{:S(2)}, u32[]{:S(2)}) collective-permute-start(bf16[8,16,128]{2,1,0:T(8,128)(2,1)S(1)} %get-tuple-element.25), channel_id=1, source_target_pairs={{0,8},{1,9},{2,10},{3,11},{4,12},{5,13},{6,14},{7,15},{8,0},{9,1},... | collective-permute-start | bytes 98312 | tf_op jit(solution)/shard_map/ppermute | solution.py:28
  37.8 5.7 %collective-permute-start.14 = (bf16[8,16,128]{2,1,0:T(8,128)(2,1)S(1)}, bf16[8,16,128]{2,1,0:T(8,128)(2,1)S(1)}, u32[]{:S(2)}, u32[]{:S(2)}) collective-permute-start(bf16[8,16,128]{2,1,0:T(8,128)(2,1)S(1)} %get-tuple-element.26), channel_id=1, source_target_pairs={{0,12},{1,13},{2,14},{3,15},{4,8},{5,9},{6,10},{7,11},{8,4},{9,5},... | collective-permute-start | bytes 98312 | tf_op jit(solution)/shard_map/ppermute | solution.py:28

commit v3 on v2

--- a/solution.py
+++ b/solution.py
@@ -28,9 +28,13 @@
     return lax.ppermute(x, "bits", [(i, i ^ bit) for i in range(owners)])
 
 
+def after(x, others):
+    return lax.optimization_barrier((x, others))[0]
+
+
 def pack_kernel(planes, *refs):
-    sources, outs = refs[:8], refs[8:9 + planes]
-    plan, closed, *copied, sems = refs[9 + planes:]
+    sources, outs = refs[:8], refs[8:10 + planes]
+    plan, closed, *copied, sems = refs[10 + planes:]
     suffix_ref, cap_ref, first_ref, prefix_ref, *numbers = copied
     pair_prefix_ref, pair_suffix_ref, count_ref, routes_ref = numbers
     plane = lax.axis_index("bits") // PLANE
@@ -38,84 +42,119 @@
     for copy in copies:
         copy.start()
     merges, pieces = pair_prefix_ref.shape
-    listed = routes_ref.shape[1]
     plan[...] = jnp.zeros_like(plan)
     for copy in copies[4:]:
         copy.wait()
     plan[:merges, :pieces] = pair_prefix_ref[...]
     plan[merges:2 * merges, :pieces] = pair_suffix_ref[...]
     plan[2 * merges:2 * merges + 1, :pieces] = count_ref[...]
-    plan[HEAD:HEAD + pieces, :listed] = routes_ref[...]
+    lane = lax.broadcasted_iota(jnp.int32, (pieces, LANES), 1)
+    named = jnp.zeros((pieces, LANES), jnp.int32)
+    for owner in range(planes * PLANE):
+        hits = jnp.sum((routes_ref[...] == owner).astype(jnp.int32), axis=1, keepdims=True)
+        named = jnp.where(lane == owner, hits, named)
+    plan[HEAD:HEAD + pieces, :] = named
     routing = plan[...].astype(jnp.float32).astype(jnp.bfloat16)
+    blocks, _, depth, width = first_ref.shape
+    part, span = width // 2, width // (planes // 2)
+    held, rows_piece, twice_width = prefix_ref.shape
+    per = depth // rows_piece
+    firsts = 2 * blocks * (part // LANES)
+    relayed = [(firsts if k < 2 else 0) + part // depth for k in range(planes)]
+    lows = [plane % 2 ^ k % 2 for k in range(planes)]
+    copies[2].wait()
+    for k in range(2):
+        n = 0
+        for a in range(blocks):
+            for c in range(2):
+                for start in range(0, part, LANES):
+                    columns = pl.ds(pl.multiple_of(lows[k] * part + start, LANES), LANES)
+                    outs[k][n] = first_ref[a, c, :, columns]
+                    n += 1
+    copies[3].wait()
+    for k in range(planes):
+        high = plane // 2 ^ k // 2
+        tail = [routing]
+        for start in range(0, twice_width, width):
+            for n in range(0, span, LANES):
+                columns = pl.ds(pl.multiple_of(high * span + (start + n), LANES), LANES)
+                for row in range(0, held, per):
+                    tail.append(prefix_ref[row:row + per, :, columns].reshape(depth, LANES))
+        for n, entry in enumerate(tail):
+            if k < 2:
+                outs[planes + k][n] = entry
+            else:
+                outs[k][relayed[k] + n] = entry
     copies[1].wait()
     upper = jnp.concatenate([cap_ref[0], cap_ref[1]], axis=0)
     lower = jnp.concatenate([-cap_ref[1], cap_ref[0]], axis=0)
-    blocks, _, depth, width = first_ref.shape
-    part, span = width // 2, width // (planes // 2)
     turned = (((1,), (1,)), ((), ()))
     copies[0].wait()
     both = lax.dot_general(suffix_ref[0], upper, turned, preferred_element_type=jnp.float32)
     both += lax.dot_general(suffix_ref[1], lower, turned, preferred_element_type=jnp.float32)
     closed[...] = both.astype(jnp.bfloat16)
-    copies[2].wait()
-    copies[3].wait()
-    held, rows_piece, twice_width = prefix_ref.shape
-    per = depth // rows_piece
     for k in range(planes):
-        low, high = plane % 2 ^ k % 2, plane // 2 ^ k // 2
-        entries = []
-        if k < 2:
-            for a in range(blocks):
-                for c in range(2):
-                    for n in range(0, part, LANES):
-                        entries.append(first_ref[a, c, :, pl.ds(pl.multiple_of(low * part + n, LANES), LANES)])
-        for n in range(0, part, depth):
-            entries.append(closed[pl.ds(pl.multiple_of(low * part + n, depth), depth), :])
-        relayed = len(entries)
-        entries.append(routing)
-        for start in range(0, twice_width, width):
-            for n in range(0, span, LANES):
-                columns = pl.ds(pl.multiple_of(high * span + (start + n), LANES), LANES)
-                for row in range(0, held, per):
-                    entries.append(prefix_ref[row:row + per, :, columns].reshape(depth, LANES))
-        for n, entry in enumerate(entries):
-            if k == 0 and n >= relayed:
-                outs[planes][n - relayed] = entry
-            else:
-                outs[k][n] = entry
-
-
-def take_kernel(count, *refs):
-    out = refs[count]
-    for k in range(count):
-        out[k] = refs[k][:out.shape[1]]
-
-
-def take(packs, size):
+        for n in range(part // depth):
+            there = pl.ds(pl.multiple_of(lows[k] * part + n * depth, depth), depth)
+            outs[k][relayed[k] - part // depth + n] = closed[there, :]
+
+
+def own_kernel(*refs):
+    count = len(refs) // 2
+    for source, out in zip(refs[:count], refs[count:]):
+        out[...] = source[...]
+
+
+def own_copy(*arrays):
     vmem = pl.BlockSpec(memory_space=pltpu.VMEM)
     return pl.pallas_call(
-        functools.partial(take_kernel, len(packs)),
+        own_kernel,
+        out_shape=[jax.ShapeDtypeStruct(a.shape, a.dtype) for a in arrays],
+        in_specs=[vmem] * len(arrays),
+        out_specs=[vmem] * len(arrays),
+        compiler_params=pltpu.CompilerParams(vmem_limit_bytes=VMEM_BYTES),
+        cost_estimate=pl.CostEstimate(flops=0, bytes_accessed=2 ** 12, transcendentals=0),
+        name="own",
+    )(*arrays)
+
+
+def join_kernel(*refs):
+    for k, ref in enumerate(refs[:-1]):
+        refs[-1][k] = ref[:refs[-1].shape[1]]
+
+
+def join(packs, size):
+    vmem = pl.BlockSpec(memory_space=pltpu.VMEM)
+    return pl.pallas_call(
+        join_kernel,
         out_shape=jax.ShapeDtypeStruct((len(packs), size) + packs[0].shape[1:], packs[0].dtype),
         in_specs=[vmem] * len(packs),
         out_specs=vmem,
         compiler_params=pltpu.CompilerParams(vmem_limit_bytes=VMEM_BYTES),
         cost_estimate=pl.CostEstimate(flops=0, bytes_accessed=2 ** 12, transcendentals=0),
-        name="take",
+        name="join",
     )(*packs)
 
 
 def state_kernel(planes, blocks, merges, pieces, rows_piece, held, *refs):
     relays, packs = refs[:2 * PLANE], refs[2 * PLANE:2 * PLANE + planes]
-    state, plan_out, forms, products, plan, sem = refs[2 * PLANE + planes:]
+    state, named, plan_out, forms, products, plan, sem = refs[2 * PLANE + planes:]
     me = lax.axis_index("bits")
     depth = packs[0].shape[1]
     span, twice_part = forms.shape[1:]
     part = twice_part // 2
     locals_ = []
+    rows = planes * held * rows_piece
+    index = lax.broadcasted_iota(jnp.int32, (merges, LANES), 0)
     tail = 1 + 2 * (span // LANES) * (held * rows_piece // depth)
     for k in range(planes):
         first = packs[k].shape[0] - tail
-        plan_out[k] = packs[k][first].astype(jnp.float32).astype(jnp.int32)
+        numbers = packs[k][first].astype(jnp.float32)
+        named[k] = numbers[HEAD:HEAD + pieces]
+        plan_out[k] = numbers.astype(jnp.int32)
+        live = index < plan_out[k, 2 * merges:2 * merges + 1]
+        picked = plan_out[k, merges:2 * merges] * rows + (plan_out[k, :merges] + k * held) * rows_piece
+        plan_out[k, :merges] = jnp.where(live, picked, blocks * rows)
         locals_.append(packs[k].at[first + 1:first + tail])
     copy = pltpu.make_async_copy(plan_out, plan, sem)
     copy.start()
@@ -125,61 +164,68 @@
             for n in range(twice_part // LANES):
                 forms[a, there, n * LANES:(n + 1) * LANES] = relays[j][0, a * (twice_part // LANES) + n]
     chunks = held * rows_piece // depth
-    rows = held * rows_piece
     left = []
     for c in range(2):
         for k in range(planes):
             columns = []
             for n in range(span // LANES):
                 first = (c * (span // LANES) + n) * chunks
-                columns.append(locals_[k][first:first + chunks].reshape(rows, LANES))
+                columns.append(locals_[k][first:first + chunks].reshape(rows // planes, LANES))
             left.append(jnp.concatenate(columns, axis=1))
     left = jnp.concatenate(left, axis=0)
-    rows *= planes
+    products[blocks * rows:, :] = jnp.zeros((rows_piece, twice_part), jnp.float32)
     for a in range(blocks):
         both = jnp.dot(left, forms[a], preferred_element_type=jnp.float32)
-        products[a, :, :part] = both[:rows, :part] - both[rows:, part:]
-        products[a, :, part:] = both[:rows, part:] + both[rows:, :part]
+        products[a * rows:(a + 1) * rows, :part] = both[:rows, :part] - both[rows:, part:]
+        products[a * rows:(a + 1) * rows, part:] = both[:rows, part:] + both[rows:, :part]
     copy.wait()
     for i in range(planes * pieces):
         k, n = divmod(i, pieces)
         total = None
         for m in range(merges):
-            row = pl.multiple_of((k * held + plan[k, m, n]) * rows_piece, rows_piece)
-            term = products[plan[k, merges + m, n], pl.ds(row, rows_piece), :]
-            term = jnp.where(m < plan[k, 2 * merges, n], term, 0.0)
+            term = products[pl.ds(pl.multiple_of(plan[k, m, n], rows_piece), rows_piece), :]
             total = term if total is None else total + term
         state[i * rows_piece:(i + 1) * rows_piece, :] = total.astype(jnp.bfloat16)
 
 
-def close_kernel(planes, listed, pieces, rows_piece, plan, state, *refs):
-    slots = planes * PLANE
-    relays, outs = refs[:2 * PLANE + PLANE], refs[3 * PLANE:3 * PLANE + planes]
-    wide, terms = refs[3 * PLANE + planes:]
+def close(first_slot, named, state, relays, sums, wide):
     me = lax.axis_index("bits")
+    planes, pieces, _ = named.shape
     part = wide.shape[0] // 2
+    rows_piece = state.shape[0] // (planes * pieces)
     lane = lax.broadcasted_iota(jnp.int32, (part, LANES), 1)
-    for j in range(slots):
-        n, b = divmod(j, PLANE)
-        relay = relays[min(n, 2) * PLANE + b]
-        first = relay.shape[1] - part // relay.shape[2]
-        real_rows = relay[max(n - 2, 0), first:].reshape(part, LANES)
-        turned = pltpu.roll(real_rows.astype(jnp.float32), LANES // 2, 1)
-        turned = jnp.where(lane < LANES // 2, -turned, turned)
-        wide[:part, j * LANES:(j + 1) * LANES] = real_rows
-        wide[part:, j * LANES:(j + 1) * LANES] = turned.astype(jnp.bfloat16)
-    for j in range(0, slots, 2):
+    slot = 0
+    for unit in range(0, len(relays), PLANE):
+        for k in range(relays[unit].shape[0]):
+            for relay in relays[unit:unit + PLANE]:
+                first = relay.shape[1] - part // relay.shape[2]
+                real_rows = relay[k, first:].reshape(part, LANES)
+                turned = pltpu.roll(real_rows.astype(jnp.float32), LANES // 2, 1)
+                turned = jnp.where(lane < LANES // 2, -turned, turned)
+                wide[:part, slot * LANES:(slot + 1) * LANES] = real_rows
+                wide[part:, slot * LANES:(slot + 1) * LANES] = turned.astype(jnp.bfloat16)
+                slot += 1
+    for j in range(0, slot, 2):
         both = jnp.dot(state[...], wide[:, j * LANES:(j + 2) * LANES], preferred_element_type=jnp.float32)
-        terms[j] = both[:, :LANES]
-        terms[j + 1] = both[:, LANES:]
-    for i in range(planes * pieces):
-        k, n = divmod(i, pieces)
-        total = None
-        for m in range(listed):
-            slot = plan[k, HEAD + n, m] ^ me
-            term = terms[slot, i * rows_piece:(i + 1) * rows_piece, :]
-            total = term if total is None else total + term
-        outs[k][n] = total.astype(outs[k].dtype)
+        owner = (first_slot + j) ^ me
+        for i in range(planes * pieces):
+            k, n = divmod(i, pieces)
+            here = slice(i * rows_piece, (i + 1) * rows_piece)
+            add = both[here, :LANES] * named[k, n, owner] + both[here, LANES:] * named[k, n, owner ^ 1]
+            sums[here, :] = add if first_slot + j == 0 else sums[here, :] + add
+
+
+def close_first_kernel(named, state, *refs):
+    close(0, named, state, refs[:-2], *refs[-2:])
+
+
+def close_rest_kernel(planes, named, state, sums_in, *refs):
+    relays, outs = refs[:PLANE], refs[PLANE:PLANE + planes]
+    sums, wide = refs[PLANE + planes:]
+    sums[...] = sums_in[...]
+    close(2 * PLANE, named, state, relays, sums, wide)
+    for out, start in zip(outs, range(0, sums.shape[0], sums.shape[0] // planes)):
+        out[...] = sums[start:start + sums.shape[0] // planes, :].reshape(out.shape).astype(out.dtype)
 
 
 def in_planes(prefix, first_suffix, pair_prefix, pair_suffix, merge_count, suffix, routes, cap):
@@ -205,8 +251,8 @@
         merge_count[None],
         routes,
     )
-    sizes = [forms_size + closed_size, forms_size + closed_size + tail] + [closed_size + tail] * (planes - 2) + [tail]
-    *packs, local = pl.pallas_call(
+    sizes = [forms_size + closed_size] * 2 + [closed_size + tail] * (planes - 2) + [tail] * 2
+    packs = pl.pallas_call(
         functools.partial(pack_kernel, planes),
         out_shape=[jax.ShapeDtypeStruct((size, depth, LANES), jnp.bfloat16) for size in sizes],
         in_specs=[pl.BlockSpec(memory_space=pl.ANY)] * len(sources),
@@ -218,43 +264,62 @@
         cost_estimate=pl.CostEstimate(flops=2 ** 20, bytes_accessed=2 ** 12, transcendentals=0),
         name="pack",
     )(*sources)
-    relay = packs[0][None]
-    packs = [local] + [swap(packs[k], k * PLANE) for k in range(1, planes)]
-    relays = [relay, take(packs[1:2], forms_size + closed_size), take(packs[2:], closed_size)]
-    relays = [(r, swap(r, 1), y, swap(y, 1)) for r, y in [(r, swap(r, 2)) for r in relays]]
+    far = [swap(packs[k], k * PLANE) for k in range(2, planes)]
+    near = swap(packs[planes + 1], PLANE)
+    relays = [packs[0][None], swap(packs[1], PLANE)[None], join([after(far[0], near)] + far[1:], closed_size)]
+    across = [swap(r, 2) for r in relays]
+    own, local = own_copy(relays[0], packs[planes])
+    relays[0] = own
+    packs = [local, near] + far
+    beside = [swap(r, 1) for r in relays]
+    corner = [swap(across[0], 1), swap(after(across[1], beside[2]), 1)]
     rows = planes * pieces * rows_piece
-    state, plan = pl.pallas_call(
+    state, named = pl.pallas_call(
         functools.partial(state_kernel, planes, blocks, merges, pieces, rows_piece, held),
         out_shape=[
             jax.ShapeDtypeStruct((rows, 2 * part), jnp.bfloat16),
-            jax.ShapeDtypeStruct((planes, depth, LANES), jnp.int32),
+            jax.ShapeDtypeStruct((planes, pieces, LANES), jnp.float32),
         ],
         in_specs=[vmem] * (2 * PLANE + planes),
         out_specs=[vmem] * 2,
         scratch_shapes=[
+            pltpu.VMEM((planes, depth, LANES), jnp.int32),
             pltpu.VMEM((blocks, span, 2 * part), jnp.bfloat16),
-            pltpu.VMEM((blocks, planes * held * rows_piece, 2 * part), jnp.float32),
+            pltpu.VMEM(((blocks * planes * held + 1) * rows_piece, 2 * part), jnp.float32),
             pltpu.SMEM((planes, depth, LANES), jnp.int32),
             pltpu.SemaphoreType.DMA,
         ],
         compiler_params=params,
+        cost_estimate=pl.CostEstimate(flops=0, bytes_accessed=2 ** 12, transcendentals=0),
         name="state",
-    )(*relays[0], *relays[1], *packs)
+    )(*[group[n] for n in range(2) for group in (relays, beside, across, corner)], *packs)
+    corner.append(swap(after(across[2], state), 1))
+    relays = list(zip(relays, beside, across, corner))
+    early = 2 * PLANE
     sums = pl.pallas_call(
-        functools.partial(close_kernel, planes, listed, pieces, rows_piece),
+        close_first_kernel,
+        out_shape=jax.ShapeDtypeStruct((rows, LANES), jnp.float32),
+        in_specs=[smem] + [vmem] * (1 + 2 * PLANE),
+        out_specs=vmem,
+        scratch_shapes=[pltpu.VMEM((2 * part, early * LANES), jnp.bfloat16)],
+        compiler_params=params,
+        name="close_first",
+    )(named, state, *relays[0], *relays[1])
+    sums = pl.pallas_call(
+        functools.partial(close_rest_kernel, planes),
         out_shape=[
             jax.ShapeDtypeStruct((pieces, rows_piece, LANES), jnp.float32 if k == 0 else jnp.bfloat16)
             for k in range(planes)
         ],
-        in_specs=[smem] + [vmem] * (1 + 3 * PLANE),
+        in_specs=[smem] + [vmem] * (2 + PLANE),
         out_specs=[vmem] * planes,
         scratch_shapes=[
-            pltpu.VMEM((2 * part, owners * LANES), jnp.bfloat16),
-            pltpu.VMEM((owners, rows, LANES), jnp.float32),
+            pltpu.VMEM((rows, LANES), jnp.float32),
+            pltpu.VMEM((2 * part, (owners - early) * LANES), jnp.bfloat16),
         ],
         compiler_params=params,
-        name="close",
-    )(plan, state, *relays[0], *relays[1], *relays[2])
+        name="close_rest",
+    )(named, state, sums, *relays[2])
     total = sums[0]
     for k in range(1, planes):
         total = total + swap(sums[k], k * PLANE).astype(jnp.float32)
@@ -352,7 +417,7 @@
         and prefix.shape[1] % 16 == 0
         and 2 * merges < HEAD
         and HEAD + pieces <= depth
-        and max(pieces, routes.shape[1]) <= LANES
+        and max(pieces, owners) <= LANES
     )
     return in_planes(*args) if fits else by_owner(*args)
 

time: 44.4 us -> 41.1 us (0.926)
  waiting for transfers between devices: 17 us -> 13.5 us
  starting transfers between devices: 17.4 us -> 17.9 us
    ppermute x15 -> x16, waiting for transfers between devices: 17 us -> 13.5 us  [swap(): return lax.ppermute(x, 'bits', [(i, i ^ bit) for i in range(owners)])]
    ppermute x15 -> x16, starting transfers between devices: 17.4 us -> 17.9 us  [swap(): return lax.ppermute(x, 'bits', [(i, i ^ bit) for i in range(owners)])]
    pallas_call x3 -> x4, Pallas kernels: 3.51 us -> 3.37 us  [the longest x1 1.67 us: in_planes(): pl.pallas_call(functools.partial(close_rest_kernel, planes), out_shape=[j...]
  transfers between devices with their start and end apart: 15 -> 16, of which waited for: 5 -> 8; matrix products, arithmetic and copies ran while one was open for 0% -> 0% of each run, Pallas kernels for 6% -> 11%
where the time goes in v3:
time: 41.1 us; the launch traced here: 40.9 us
  starting transfers between devices  17.9 us (44%)
  waiting for transfers between devices  13.5 us (33%)
  Pallas kernels  8.79 us (21%)
  other arithmetic  0.65 us (2%)
    ppermute x16, starting transfers between devices, swap(): return lax.ppermute(x, 'bits', [(i, i ^ bit) for i in range(owners)])  17.9 us
    ppermute x16, waiting for transfers between devices, swap(): return lax.ppermute(x, 'bits', [(i, i ^ bit) for i in range(owners)])  13.5 us
    pallas_call x1, Pallas kernels, in_planes(): pl.pallas_call(functools.partial(pack_kernel, planes), out_shape=[jax.Sha...  2.81 us
    pallas_call x1, Pallas kernels, in_planes(): pl.pallas_call(functools.partial(state_kernel, planes, blocks, merges, pi...  2.61 us
    pallas_call x1, Pallas kernels, in_planes(): pl.pallas_call(functools.partial(close_rest_kernel, planes), out_shape=[j...  1.67 us
    pallas_call x1, Pallas kernels, in_planes(): pl.pallas_call(close_first_kernel, out_shape=jax.ShapeDtypeStruct((rows,...  1.67 us
  transfers between devices with their start and end apart: 16, of which 8 were waited for; matrix products, arithmetic and copies ran while one was open for 0% of the time, Pallas kernels for 11%

profile of v3, /device:TPU:0, one launch (start us, length us, event | category | flops | bytes accessed | tf_op | source)
XLA Modules:
  0.0 40.9 jit_solution(10017581828007584651)
XLA Ops:
  0.0 2.8 %pack.1 = (bf16[24,32,128]{2,1,0:T(8,128)(2,1)}, bf16[24,32,128]{2,1,0:T(8,128)(2,1)}, bf16[17,32,128]{2,1,0:T(8,128)(2,1)}, bf16[17,32,128]{2,1,0:T(8,128)(2,1)...) custom-call(bf16[2,512,512]{2,1,0:T(8,128)(2,1)} %bitcast.13, bf16[2,64,512]{2,1,0:T(8,128)(2,1)} %bitcast.14, ...), custom_call_target="tpu_custom_call" | custom-call | flops 1048576 | bytes 4096 | tf_op jit(solution)/shard_map/pack/pallas_call | solution.py:255
  2.8 3.1 %collective-permute-start.3 = (bf16[24,32,128]{2,1,0:T(8,128)(2,1)}, bf16[24,32,128]{2,1,0:T(8,128)(2,1)S(1)}, u32[]{:S(2)}, u32[]{:S(2)}) collective-permute-start(bf16[24,32,128]{2,1,0:T(8,128)(2,1)} %get-tuple-element.25), channel_id=1, source_target_pairs={{0,4},{1,5},{2,6},{3,7},{4,0},{5,1},{6,2},{7,3},{8,12},{9,13},{10,... | collective-permute-start | bytes 589832 | tf_op jit(solution)/shard_map/ppermute | solution.py:28
  5.9 2.6 %collective-permute-start.6 = (bf16[17,32,128]{2,1,0:T(8,128)(2,1)}, bf16[17,32,128]{2,1,0:T(8,128)(2,1)S(1)}, u32[]{:S(2)}, u32[]{:S(2)}) collective-permute-start(bf16[17,32,128]{2,1,0:T(8,128)(2,1)} %get-tuple-element.26), channel_id=1, source_target_pairs={{0,8},{1,9},{2,10},{3,11},{4,12},{5,13},{6,14},{7,15},{8,0},{9,1},... | collective-permute-start | bytes 417800 | tf_op jit(solution)/shard_map/ppermute | solution.py:28
  8.5 0.0 collective-permute-start.8
  8.5 0.9 %collective-permute-start.7 = (bf16[9,32,128]{2,1,0:T(8,128)(2,1)}, bf16[9,32,128]{2,1,0:T(8,128)(2,1)S(1)}, u32[]{:S(2)}, u32[]{:S(2)}) collective-permute-start(bf16[9,32,128]{2,1,0:T(8,128)(2,1)} %get-tuple-element.27), channel_id=1, source_target_pairs={{0,4},{1,5},{2,6},{3,7},{4,0},{5,1},{6,2},{7,3},{8,12},{9,13},{10,... | collective-permute-start | bytes 221192 | tf_op jit(solution)/shard_map/ppermute | solution.py:28
  9.4 1.5 %collective-permute-start.1 = (bf16[1,24,32,128]{3,2,1,0:T(8,128)(2,1)}, bf16[1,24,32,128]{3,2,1,0:T(8,128)(2,1)S(1)}, u32[]{:S(2)}, u32[]{:S(2)}) collective-permute-start(bf16[1,24,32,128]{3,2,1,0:T(8,128)(2,1)} %bitcast.11), channel_id=1, source_target_pairs={{0,2},{1,3},{2,0},{3,1},{4,6},{5,7},{6,4},{7,5},{8,10},{9,11},{10,... | collective-permute-start | bytes 589832 | tf_op jit(solution)/shard_map/ppermute | solution.py:28
  10.9 3.7 %collective-permute-done.3 = bf16[24,32,128]{2,1,0:T(8,128)(2,1)S(1)} collective-permute-done((bf16[24,32,128]{2,1,0:T(8,128)(2,1)}, bf16[24,32,128]{2,1,0:T(8,128)(2,1)S(1)}, u32[]{:S(2)}, u32[]{:S(2)}) %collective-permute-start.3) | collective-permute-done | bytes 196640 | tf_op jit(solution)/shard_map/ppermute | solution.py:28
  14.7 0.0 copy-start
  14.7 0.0 copy-start.1
  14.7 1.7 %collective-permute-start.5 = (bf16[1,24,32,128]{3,2,1,0:T(8,128)(2,1)S(1)}, bf16[1,24,32,128]{3,2,1,0:T(8,128)(2,1)S(1)}, u32[]{:S(2)}, u32[]{:S(2)}) collective-permute-start(bf16[1,24,32,128]{3,2,1,0:T(8,128)(2,1)S(1)} %bitcast.7), channel_id=1, source_target_pairs={{0,2},{1,3},{2,0},{3,1},{4,6},{5,7},{6,4},{7,5},{8,10},{9,11},{10,... | collective-permute-start | bytes 589832 | tf_op jit(solution)/shard_map/ppermute | solution.py:28
  16.3 1.7 %collective-permute-done.7.refs_9_ = bf16[9,32,128]{2,1,0:T(8,128)(2,1)S(1)} collective-permute-done((bf16[9,32,128]{2,1,0:T(8,128)(2,1)}, bf16[9,32,128]{2,1,0:T(8,128)(2,1)S(1)}, u32[]{:S(2)}, u32[]{:S(2)}) %collective-permute-start.7) | collective-permute-done | bytes 73760 | tf_op jit(solution)/shard_map/ppermute | solution.py:28
  18.0 0.8 %collective-permute-done.6.refs_0_.refs_10_ = bf16[17,32,128]{2,1,0:T(8,128)(2,1)S(1)} collective-permute-done((bf16[17,32,128]{2,1,0:T(8,128)(2,1)}, bf16[17,32,128]{2,1,0:T(8,128)(2,1)S(1)}, u32[]{:S(2)}, u32[]{:S(2)}) %collective-permute-start.6) | collective-permute-done | bytes 139296 | tf_op jit(solution)/shard_map/ppermute | solution.py:28
  18.8 1.2 %collective-permute-done.8.refs_1_.refs_11_ = bf16[17,32,128]{2,1,0:T(8,128)(2,1)S(1)} collective-permute-done((bf16[17,32,128]{2,1,0:T(8,128)(2,1)}, bf16[17,32,128]{2,1,0:T(8,128)(2,1)S(1)}, u32[]{:S(2)}, u32[]{:S(2)}) %collective-permute-start.8) | collective-permute-done | bytes 139296 | tf_op jit(solution)/shard_map/ppermute | solution.py:28
  20.1 0.1 collective-permute-start.9
  20.1 0.0 copy-done
  20.2 0.0 copy-done.1
  20.2 0.5 %collective-permute-start = (bf16[1,24,32,128]{3,2,1,0:T(8,128)(2,1)S(1)}, bf16[1,24,32,128]{3,2,1,0:T(8,128)(2,1)S(1)}, u32[]{:S(2)}, u32[]{:S(2)}) collective-permute-start(bf16[1,24,32,128]{3,2,1,0:T(8,128)(2,1)S(1)} %get-tuple-element.24.refs_0_), channel_id=1, source_target_pairs={{0,1},{1,0},{2,3},{3,2},{4,5},{5,4},{6,7},{7,6},{8,9},{9,8},{10,11... | collective-permute-start | bytes 589832 | tf_op jit(solution)/shard_map/ppermute | solution.py:28
  20.7 0.1 collective-permute-start.4
  20.8 0.0 collective-permute-done.1.refs_2_
  20.8 0.4 %collective-permute-start.2 = (bf16[1,24,32,128]{3,2,1,0:T(8,128)(2,1)S(1)}, bf16[1,24,32,128]{3,2,1,0:T(8,128)(2,1)S(1)}, u32[]{:S(2)}, u32[]{:S(2)}) collective-permute-start(bf16[1,24,32,128]{3,2,1,0:T(8,128)(2,1)S(1)} %collective-permute-done.1.refs_2_), channel_id=1, source_target_pairs={{0,1},{1,0},{2,3},{3,2},{4,5},{5,4},{6,7},{7,6},{8,9},{9,8},{10,11... | collective-permute-start | bytes 589832 | tf_op jit(solution)/shard_map/ppermute | solution.py:28
  21.3 0.2 collective-permute-done.9.refs_1_
  21.5 0.0 collective-permute-done.5.refs_6_
  21.5 0.1 collective-permute-start.10
  21.6 1.5 %collective-permute-start.11 = (bf16[2,8,32,128]{3,2,1,0:T(8,128)(2,1)S(1)}, bf16[2,8,32,128]{3,2,1,0:T(8,128)(2,1)S(1)}, u32[]{:S(2)}, u32[]{:S(2)}) collective-permute-start(bf16[2,8,32,128]{3,2,1,0:T(8,128)(2,1)S(1)} %join.1.refs_0_), channel_id=1, source_target_pairs={{0,2},{1,3},{2,0},{3,1},{4,6},{5,7},{6,4},{7,5},{8,10},{9,11},{10,... | collective-permute-start | bytes 393224 | tf_op jit(solution)/shard_map/ppermute | solution.py:28
  23.2 0.0 collective-permute-done.refs_1_
  23.2 0.0 collective-permute-done.2.refs_3_
  23.2 0.0 collective-permute-done.4.refs_5_
  23.2 0.0 collective-permute-done.10.refs_7_
  23.2 2.6 %state.1 = (bf16[512,512]{1,0:T(8,128)(2,1)S(1)}, f32[4,8,128]{2,1,0:T(8,128)S(1)}) custom-call(bf16[1,24,32,128]{3,2,1,0:T(8,128)(2,1)S(1)} %get-tuple-element.24.refs_0_, bf16[1,24,32,128]{3,2,1,0:T(8,128)(2,1)S(1)} %collective-permute-done.refs_1_, bf16[1,24,32,128]{3,2,1,0:T(8,128)(2,1)S(1)} %collective-permute-done.1.refs_2_, ...), custom_call_target="tpu_custom_call" | custom-call | bytes 4096 | tf_op jit(solution)/shard_map/state/pallas_call | solution.py:277
  25.8 1.6 %collective-permute-done.11.refs_2_ = bf16[2,8,32,128]{3,2,1,0:T(8,128)(2,1)S(1)} collective-permute-done((bf16[2,8,32,128]{3,2,1,0:T(8,128)(2,1)S(1)}, bf16[2,8,32,128]{3,2,1,0:T(8,128)(2,1)S(1)}, u32[]{:S(2)}, u32[]{:S(2)}) %collective-permute-start.11) | collective-permute-done | bytes 131104 | tf_op jit(solution)/shard_map/ppermute | solution.py:28
  27.4 0.0 collective-permute-start.12
  27.4 1.7 %close_first.1.sums_in = f32[512,128]{1,0:T(8,128)S(1)} custom-call(f32[4,8,128]{2,1,0:T(8,128)S(1)} %get-tuple-element.32.named, bf16[512,512]{1,0:T(8,128)(2,1)S(1)} %get-tuple-element.33.state, bf16[1,24,32,128]{3,2,1,0:T(8,128)(2,1)S(1)} %get-tuple-element.24.refs_0_, bf16[1,24,32,128]{3,2,1,0:T(8,128)(2,1)S(1)} %collective-permute-done.refs_1_, ...), custom_call_target="tpu_custom_call" | custom-call | tf_op jit(solution)/shard_map/close_first/pallas_call | solution.py:299
  29.1 0.0 collective-permute-done.12.refs_3_
  29.1 1.7 %close_rest.1 = (f32[8,16,128]{2,1,0:T(8,128)S(1)}, bf16[8,16,128]{2,1,0:T(8,128)(2,1)S(1)}, bf16[8,16,128]{2,1,0:T(8,128)(2,1)S(1)}, bf16[8,16,128]{2,1,0:T(8,128)(2,1)S(1)}) custom-call(f32[4,8,128]{2,1,0:T(8,128)S(1)} %get-tuple-element.32.named, bf16[512,512]{1,0:T(8,128)(2,1)S(1)} %get-tuple-element.33.state, f32[512,128]{1,0:T(8,128)S(1)} %close_first.1.sums_in, ...), custom_call_target="tpu_custom_call" | custom-call | tf_op jit(solution)/shard_map/close_rest/pallas_call | solution.py:308
  30.8 4.6 %collective-permute-start.15 = (bf16[8,16,128]{2,1,0:T(8,128)(2,1)S(1)}, bf16[8,16,128]{2,1,0:T(8,128)(2,1)S(1)}, u32[]{:S(2)}, u32[]{:S(2)}) collective-permute-start(bf16[8,16,128]{2,1,0:T(8,128)(2,1)S(1)} %get-tuple-element.38), channel_id=1, source_target_pairs={{0,12},{1,13},{2,14},{3,15},{4,8},{5,9},{6,10},{7,11},{8,4},{9,5},... | collective-permute-start | bytes 98312 | tf_op jit(solution)/shard_map/ppermute | solution.py:28
  35.4 0.0 collective-permute-start.14
  35.4 0.6 %collective-permute-start.13 = (bf16[8,16,128]{2,1,0:T(8,128)(2,1)S(1)}, bf16[8,16,128]{2,1,0:T(8,128)(2,1)S(1)}, u32[]{:S(2)}, u32[]{:S(2)}) collective-permute-start(bf16[8,16,128]{2,1,0:T(8,128)(2,1)S(1)} %get-tuple-element.36), channel_id=1, source_target_pairs={{0,4},{1,5},{2,6},{3,7},{4,0},{5,1},{6,2},{7,3},{8,12},{9,13},{10,... | collective-permute-start | bytes 98312 | tf_op jit(solution)/shard_map/ppermute | solution.py:28
  36.0 1.6 %collective-permute-done.15 = bf16[8,16,128]{2,1,0:T(8,128)(2,1)S(1)} collective-permute-done((bf16[8,16,128]{2,1,0:T(8,128)(2,1)S(1)}, bf16[8,16,128]{2,1,0:T(8,128)(2,1)S(1)}, u32[]{:S(2)}, u32[]{:S(2)}) %collective-permute-start.15) | collective-permute-done | bytes 32800 | tf_op jit(solution)/shard_map/ppermute | solution.py:28
  37.6 2.6 %collective-permute-done.14 = bf16[8,16,128]{2,1,0:T(8,128)(2,1)S(1)} collective-permute-done((bf16[8,16,128]{2,1,0:T(8,128)(2,1)S(1)}, bf16[8,16,128]{2,1,0:T(8,128)(2,1)S(1)}, u32[]{:S(2)}, u32[]{:S(2)}) %collective-permute-start.14) | collective-permute-done | bytes 32800 | tf_op jit(solution)/shard_map/ppermute | solution.py:28
  40.2 0.0 collective-permute-done.13
  40.2 0.6 %convert_add_fusion = f32[8,16,128]{2,1,0:T(8,128)} fusion(bf16[8,16,128]{2,1,0:T(8,128)(2,1)S(1)} %collective-permute-done.15, bf16[8,16,128]{2,1,0:T(8,128)(2,1)S(1)} %collective-permute-done.14, f32[8,16,128]{2,1,0:T(8,128)S(1)} %get-tuple-element.35, bf16[8,16,128]{2,1,0:T(8,128)(2,1)S(1)} %collective-permute-done.13), kind=kLoop, calls=%fused_computation | loop fusion | flops 98304 | bytes 229376 | tf_op jit(solution)/shard_map/add | solution.py:325
  (2 shorter events, 0.0 us)
Async XLA Ops:
  2.8 11.8 %collective-permute-start.3 = (bf16[24,32,128]{2,1,0:T(8,128)(2,1)}, bf16[24,32,128]{2,1,0:T(8,128)(2,1)S(1)}, u32[]{:S(2)}, u32[]{:S(2)}) collective-permute-start(bf16[24,32,128]{2,1,0:T(8,128)(2,1)} %get-tuple-element.25), channel_id=1, source_target_pairs={{0,4},{1,5},{2,6},{3,7},{4,0},{5,1},{6,2},{7,3},{8,12},{9,13},{10,... | collective-permute-start | bytes 589832 | tf_op jit(solution)/shard_map/ppermute | solution.py:28
  5.9 12.9 %collective-permute-start.6 = (bf16[17,32,128]{2,1,0:T(8,128)(2,1)}, bf16[17,32,128]{2,1,0:T(8,128)(2,1)S(1)}, u32[]{:S(2)}, u32[]{:S(2)}) collective-permute-start(bf16[17,32,128]{2,1,0:T(8,128)(2,1)} %get-tuple-element.26), channel_id=1, source_target_pairs={{0,8},{1,9},{2,10},{3,11},{4,12},{5,13},{6,14},{7,15},{8,0},{9,1},... | collective-permute-start | bytes 417800 | tf_op jit(solution)/shard_map/ppermute | solution.py:28
  8.5 11.5 %collective-permute-start.8 = (bf16[17,32,128]{2,1,0:T(8,128)(2,1)}, bf16[17,32,128]{2,1,0:T(8,128)(2,1)S(1)}, u32[]{:S(2)}, u32[]{:S(2)}) collective-permute-start(bf16[17,32,128]{2,1,0:T(8,128)(2,1)} %get-tuple-element.29), channel_id=1, source_target_pairs={{0,12},{1,13},{2,14},{3,15},{4,8},{5,9},{6,10},{7,11},{8,4},{9,5},... | collective-permute-start | bytes 417800 | tf_op jit(solution)/shard_map/ppermute | solution.py:28
  8.5 9.5 %collective-permute-start.7 = (bf16[9,32,128]{2,1,0:T(8,128)(2,1)}, bf16[9,32,128]{2,1,0:T(8,128)(2,1)S(1)}, u32[]{:S(2)}, u32[]{:S(2)}) collective-permute-start(bf16[9,32,128]{2,1,0:T(8,128)(2,1)} %get-tuple-element.27), channel_id=1, source_target_pairs={{0,4},{1,5},{2,6},{3,7},{4,0},{5,1},{6,2},{7,3},{8,12},{9,13},{10,... | collective-permute-start | bytes 221192 | tf_op jit(solution)/shard_map/ppermute | solution.py:28
  9.4 11.4 %collective-permute-start.1 = (bf16[1,24,32,128]{3,2,1,0:T(8,128)(2,1)}, bf16[1,24,32,128]{3,2,1,0:T(8,128)(2,1)S(1)}, u32[]{:S(2)}, u32[]{:S(2)}) collective-permute-start(bf16[1,24,32,128]{3,2,1,0:T(8,128)(2,1)} %bitcast.11), channel_id=1, source_target_pairs={{0,2},{1,3},{2,0},{3,1},{4,6},{5,7},{6,4},{7,5},{8,10},{9,11},{10,... | collective-permute-start | bytes 589832 | tf_op jit(solution)/shard_map/ppermute | solution.py:28
  14.7 5.5 %copy-start = (bf16[24,32,128]{2,1,0:T(8,128)(2,1)S(1)}, bf16[24,32,128]{2,1,0:T(8,128)(2,1)}, u32[]{:S(2)}) copy-start(bf16[24,32,128]{2,1,0:T(8,128)(2,1)} %get-tuple-element.22) | copy-start | bytes 589828
  14.7 5.5 %copy-start.1 = (bf16[9,32,128]{2,1,0:T(8,128)(2,1)S(1)}, bf16[9,32,128]{2,1,0:T(8,128)(2,1)}, u32[]{:S(2)}) copy-start(bf16[9,32,128]{2,1,0:T(8,128)(2,1)} %get-tuple-element.23.refs_1_) | copy-start | bytes 221188
  14.7 6.8 %collective-permute-start.5 = (bf16[1,24,32,128]{3,2,1,0:T(8,128)(2,1)S(1)}, bf16[1,24,32,128]{3,2,1,0:T(8,128)(2,1)S(1)}, u32[]{:S(2)}, u32[]{:S(2)}) collective-permute-start(bf16[1,24,32,128]{3,2,1,0:T(8,128)(2,1)S(1)} %bitcast.7), channel_id=1, source_target_pairs={{0,2},{1,3},{2,0},{3,1},{4,6},{5,7},{6,4},{7,5},{8,10},{9,11},{10,... | collective-permute-start | bytes 589832 | tf_op jit(solution)/shard_map/ppermute | solution.py:28
  20.1 1.4 %collective-permute-start.9 = (bf16[2,8,32,128]{3,2,1,0:T(8,128)(2,1)S(1)}, bf16[2,8,32,128]{3,2,1,0:T(8,128)(2,1)S(1)}, u32[]{:S(2)}, u32[]{:S(2)}) collective-permute-start(bf16[2,8,32,128]{3,2,1,0:T(8,128)(2,1)S(1)} %join.1.refs_0_), channel_id=1, source_target_pairs={{0,1},{1,0},{2,3},{3,2},{4,5},{5,4},{6,7},{7,6},{8,9},{9,8},{10,11... | collective-permute-start | bytes 393224 | tf_op jit(solution)/shard_map/ppermute | solution.py:28
  20.2 3.0 %collective-permute-start = (bf16[1,24,32,128]{3,2,1,0:T(8,128)(2,1)S(1)}, bf16[1,24,32,128]{3,2,1,0:T(8,128)(2,1)S(1)}, u32[]{:S(2)}, u32[]{:S(2)}) collective-permute-start(bf16[1,24,32,128]{3,2,1,0:T(8,128)(2,1)S(1)} %get-tuple-element.24.refs_0_), channel_id=1, source_target_pairs={{0,1},{1,0},{2,3},{3,2},{4,5},{5,4},{6,7},{7,6},{8,9},{9,8},{10,11... | collective-permute-start | bytes 589832 | tf_op jit(solution)/shard_map/ppermute | solution.py:28
  20.7 2.4 %collective-permute-start.4 = (bf16[1,24,32,128]{3,2,1,0:T(8,128)(2,1)S(1)}, bf16[1,24,32,128]{3,2,1,0:T(8,128)(2,1)S(1)}, u32[]{:S(2)}, u32[]{:S(2)}) collective-permute-start(bf16[1,24,32,128]{3,2,1,0:T(8,128)(2,1)S(1)} %bitcast.8), channel_id=1, source_target_pairs={{0,1},{1,0},{2,3},{3,2},{4,5},{5,4},{6,7},{7,6},{8,9},{9,8},{10,11... | collective-permute-start | bytes 589832 | tf_op jit(solution)/shard_map/ppermute | solution.py:28
  20.8 2.4 %collective-permute-start.2 = (bf16[1,24,32,128]{3,2,1,0:T(8,128)(2,1)S(1)}, bf16[1,24,32,128]{3,2,1,0:T(8,128)(2,1)S(1)}, u32[]{:S(2)}, u32[]{:S(2)}) collective-permute-start(bf16[1,24,32,128]{3,2,1,0:T(8,128)(2,1)S(1)} %collective-permute-done.1.refs_2_), channel_id=1, source_target_pairs={{0,1},{1,0},{2,3},{3,2},{4,5},{5,4},{6,7},{7,6},{8,9},{9,8},{10,11... | collective-permute-start | bytes 589832 | tf_op jit(solution)/shard_map/ppermute | solution.py:28
  21.5 1.7 %collective-permute-start.10 = (bf16[1,24,32,128]{3,2,1,0:T(8,128)(2,1)S(1)}, bf16[1,24,32,128]{3,2,1,0:T(8,128)(2,1)S(1)}, u32[]{:S(2)}, u32[]{:S(2)}) collective-permute-start(bf16[1,24,32,128]{3,2,1,0:T(8,128)(2,1)S(1)} %collective-permute-done.5.refs_6_), channel_id=1, source_target_pairs={{0,1},{1,0},{2,3},{3,2},{4,5},{5,4},{6,7},{7,6},{8,9},{9,8},{10,11... | collective-permute-start | bytes 589832 | tf_op jit(solution)/shard_map/ppermute | solution.py:28
  21.6 5.8 %collective-permute-start.11 = (bf16[2,8,32,128]{3,2,1,0:T(8,128)(2,1)S(1)}, bf16[2,8,32,128]{3,2,1,0:T(8,128)(2,1)S(1)}, u32[]{:S(2)}, u32[]{:S(2)}) collective-permute-start(bf16[2,8,32,128]{3,2,1,0:T(8,128)(2,1)S(1)} %join.1.refs_0_), channel_id=1, source_target_pairs={{0,2},{1,3},{2,0},{3,1},{4,6},{5,7},{6,4},{7,5},{8,10},{9,11},{10,... | collective-permute-start | bytes 393224 | tf_op jit(solution)/shard_map/ppermute | solution.py:28
  27.4 1.7 %collective-permute-start.12 = (bf16[2,8,32,128]{3,2,1,0:T(8,128)(2,1)S(1)}, bf16[2,8,32,128]{3,2,1,0:T(8,128)(2,1)S(1)}, u32[]{:S(2)}, u32[]{:S(2)}) collective-permute-start(bf16[2,8,32,128]{3,2,1,0:T(8,128)(2,1)S(1)} %collective-permute-done.11.refs_2_), channel_id=1, source_target_pairs={{0,1},{1,0},{2,3},{3,2},{4,5},{5,4},{6,7},{7,6},{8,9},{9,8},{10,11... | collective-permute-start | bytes 393224 | tf_op jit(solution)/shard_map/ppermute | solution.py:28
  30.8 6.9 %collective-permute-start.15 = (bf16[8,16,128]{2,1,0:T(8,128)(2,1)S(1)}, bf16[8,16,128]{2,1,0:T(8,128)(2,1)S(1)}, u32[]{:S(2)}, u32[]{:S(2)}) collective-permute-start(bf16[8,16,128]{2,1,0:T(8,128)(2,1)S(1)} %get-tuple-element.38), channel_id=1, source_target_pairs={{0,12},{1,13},{2,14},{3,15},{4,8},{5,9},{6,10},{7,11},{8,4},{9,5},... | collective-permute-start | bytes 98312 | tf_op jit(solution)/shard_map/ppermute | solution.py:28
  35.4 4.8 %collective-permute-start.14 = (bf16[8,16,128]{2,1,0:T(8,128)(2,1)S(1)}, bf16[8,16,128]{2,1,0:T(8,128)(2,1)S(1)}, u32[]{:S(2)}, u32[]{:S(2)}) collective-permute-start(bf16[8,16,128]{2,1,0:T(8,128)(2,1)S(1)} %get-tuple-element.37), channel_id=1, source_target_pairs={{0,8},{1,9},{2,10},{3,11},{4,12},{5,13},{6,14},{7,15},{8,0},{9,1},... | collective-permute-start | bytes 98312 | tf_op jit(solution)/shard_map/ppermute | solution.py:28
  35.4 4.8 %collective-permute-start.13 = (bf16[8,16,128]{2,1,0:T(8,128)(2,1)S(1)}, bf16[8,16,128]{2,1,0:T(8,128)(2,1)S(1)}, u32[]{:S(2)}, u32[]{:S(2)}) collective-permute-start(bf16[8,16,128]{2,1,0:T(8,128)(2,1)S(1)} %get-tuple-element.36), channel_id=1, source_target_pairs={{0,4},{1,5},{2,6},{3,7},{4,0},{5,1},{6,2},{7,3},{8,12},{9,13},{10,... | collective-permute-start | bytes 98312 | tf_op jit(solution)/shard_map/ppermute | solution.py:28

commit v4 on v3

--- a/solution.py
+++ b/solution.py
@@ -48,13 +48,16 @@
     plan[:merges, :pieces] = pair_prefix_ref[...]
     plan[merges:2 * merges, :pieces] = pair_suffix_ref[...]
     plan[2 * merges:2 * merges + 1, :pieces] = count_ref[...]
+    me = lax.axis_index("bits")
     lane = lax.broadcasted_iota(jnp.int32, (pieces, LANES), 1)
-    named = jnp.zeros((pieces, LANES), jnp.int32)
-    for owner in range(planes * PLANE):
-        hits = jnp.sum((routes_ref[...] == owner).astype(jnp.int32), axis=1, keepdims=True)
-        named = jnp.where(lane == owner, hits, named)
-    plan[HEAD:HEAD + pieces, :] = named
-    routing = plan[...].astype(jnp.float32).astype(jnp.bfloat16)
+    named = [jnp.zeros((pieces, LANES), jnp.int32)] * planes
+    for slot in range(planes * PLANE):
+        hits = jnp.sum((routes_ref[...] == slot ^ me).astype(jnp.int32), axis=1, keepdims=True)
+        named = [jnp.where(lane == slot ^ k * PLANE, hits, there) for k, there in enumerate(named)]
+    routing = []
+    for k in range(planes):
+        plan[HEAD:HEAD + pieces, :] = named[k]
+        routing.append(plan[...].astype(jnp.float32).astype(jnp.bfloat16))
     blocks, _, depth, width = first_ref.shape
     part, span = width // 2, width // (planes // 2)
     held, rows_piece, twice_width = prefix_ref.shape
@@ -74,7 +77,7 @@
     copies[3].wait()
     for k in range(planes):
         high = plane // 2 ^ k // 2
-        tail = [routing]
+        tail = [routing[k]]
         for start in range(0, twice_width, width):
             for n in range(0, span, LANES):
                 columns = pl.ds(pl.multiple_of(high * span + (start + n), LANES), LANES)
@@ -150,7 +153,9 @@
     for k in range(planes):
         first = packs[k].shape[0] - tail
         numbers = packs[k][first].astype(jnp.float32)
-        named[k] = numbers[HEAD:HEAD + pieces]
+        for n in range(pieces):
+            here = slice((k * pieces + n) * rows_piece, (k * pieces + n + 1) * rows_piece)
+            named[here, :] = jnp.broadcast_to(numbers[HEAD + n:HEAD + n + 1], (rows_piece, LANES))
         plan_out[k] = numbers.astype(jnp.int32)
         live = index < plan_out[k, 2 * merges:2 * merges + 1]
         picked = plan_out[k, merges:2 * merges] * rows + (plan_out[k, :merges] + k * held) * rows_piece
@@ -188,42 +193,41 @@
         state[i * rows_piece:(i + 1) * rows_piece, :] = total.astype(jnp.bfloat16)
 
 
-def close(first_slot, named, state, relays, sums, wide):
-    me = lax.axis_index("bits")
-    planes, pieces, _ = named.shape
-    part = wide.shape[0] // 2
-    rows_piece = state.shape[0] // (planes * pieces)
+def close(order, named, state, relays, sums, wide):
+    part, rows = wide.shape[0] // 2, state.shape[0]
     lane = lax.broadcasted_iota(jnp.int32, (part, LANES), 1)
     slot = 0
-    for unit in range(0, len(relays), PLANE):
-        for k in range(relays[unit].shape[0]):
-            for relay in relays[unit:unit + PLANE]:
-                first = relay.shape[1] - part // relay.shape[2]
-                real_rows = relay[k, first:].reshape(part, LANES)
-                turned = pltpu.roll(real_rows.astype(jnp.float32), LANES // 2, 1)
-                turned = jnp.where(lane < LANES // 2, -turned, turned)
-                wide[:part, slot * LANES:(slot + 1) * LANES] = real_rows
-                wide[part:, slot * LANES:(slot + 1) * LANES] = turned.astype(jnp.bfloat16)
-                slot += 1
+    for relay in relays:
+        for k in range(relay.shape[0]):
+            first = relay.shape[1] - part // relay.shape[2]
+            real_rows = relay[k, first:].reshape(part, LANES)
+            turned = pltpu.roll(real_rows.astype(jnp.float32), LANES // 2, 1)
+            turned = jnp.where(lane < LANES // 2, -turned, turned)
+            wide[:part, slot * LANES:(slot + 1) * LANES] = real_rows
+            wide[part:, slot * LANES:(slot + 1) * LANES] = turned.astype(jnp.bfloat16)
+            slot += 1
     for j in range(0, slot, 2):
         both = jnp.dot(state[...], wide[:, j * LANES:(j + 2) * LANES], preferred_element_type=jnp.float32)
-        owner = (first_slot + j) ^ me
-        for i in range(planes * pieces):
-            k, n = divmod(i, pieces)
-            here = slice(i * rows_piece, (i + 1) * rows_piece)
-            add = both[here, :LANES] * named[k, n, owner] + both[here, LANES:] * named[k, n, owner ^ 1]
-            sums[here, :] = add if first_slot + j == 0 else sums[here, :] + add
+        for side, slot in enumerate(order[j:j + 2]):
+            factor = jnp.broadcast_to(named[:, slot:slot + 1], (rows, LANES))
+            add = both[:, side * LANES:(side + 1) * LANES] * factor
+            sums[...] = add if slot == 0 else sums[...] + add
 
 
 def close_first_kernel(named, state, *refs):
-    close(0, named, state, refs[:-2], *refs[-2:])
-
-
-def close_rest_kernel(planes, named, state, sums_in, *refs):
-    relays, outs = refs[:PLANE], refs[PLANE:PLANE + planes]
-    sums, wide = refs[PLANE + planes:]
+    close(range(2 * PLANE), named, state, refs[:-2], *refs[-2:])
+
+
+def close_more_kernel(order, named, state, sums_in, *refs):
+    relays, sums, wide = refs[:-2], refs[-2], refs[-1]
     sums[...] = sums_in[...]
-    close(2 * PLANE, named, state, relays, sums, wide)
+    close(order, named, state, relays, sums, wide)
+
+
+def close_last_kernel(planes, order, named, state, sums_in, relay, *refs):
+    outs, sums, wide = refs[:planes], refs[planes], refs[planes + 1]
+    sums[...] = sums_in[...]
+    close(order, named, state, [relay], sums, wide)
     for out, start in zip(outs, range(0, sums.shape[0], sums.shape[0] // planes)):
         out[...] = sums[start:start + sums.shape[0] // planes, :].reshape(out.shape).astype(out.dtype)
 
@@ -237,7 +241,6 @@
     blocks, _, depth, width = first_suffix.shape
     part, span = width // 2, width // (planes // 2)
     vmem = pl.BlockSpec(memory_space=pltpu.VMEM)
-    smem = pl.BlockSpec(memory_space=pltpu.SMEM)
     params = pltpu.CompilerParams(vmem_limit_bytes=VMEM_BYTES)
     forms_size, closed_size = 2 * blocks * (part // LANES), part // depth
     tail = 1 + 2 * (span // LANES) * (held * rows_piece // depth)
@@ -267,18 +270,19 @@
     far = [swap(packs[k], k * PLANE) for k in range(2, planes)]
     near = swap(packs[planes + 1], PLANE)
     relays = [packs[0][None], swap(packs[1], PLANE)[None], join([after(far[0], near)] + far[1:], closed_size)]
-    across = [swap(r, 2) for r in relays]
     own, local = own_copy(relays[0], packs[planes])
+    across = [swap(r, 2) for r in relays[:2]]
     relays[0] = own
     packs = [local, near] + far
     beside = [swap(r, 1) for r in relays]
-    corner = [swap(across[0], 1), swap(after(across[1], beside[2]), 1)]
+    corner = [swap(y, 1) for y in across]
+    across.append(swap(relays[2], 2))
     rows = planes * pieces * rows_piece
     state, named = pl.pallas_call(
         functools.partial(state_kernel, planes, blocks, merges, pieces, rows_piece, held),
         out_shape=[
             jax.ShapeDtypeStruct((rows, 2 * part), jnp.bfloat16),
-            jax.ShapeDtypeStruct((planes, pieces, LANES), jnp.float32),
+            jax.ShapeDtypeStruct((rows, LANES), jnp.float32),
         ],
         in_specs=[vmem] * (2 * PLANE + planes),
         out_specs=[vmem] * 2,
@@ -293,33 +297,46 @@
         cost_estimate=pl.CostEstimate(flops=0, bytes_accessed=2 ** 12, transcendentals=0),
         name="state",
     )(*[group[n] for n in range(2) for group in (relays, beside, across, corner)], *packs)
-    corner.append(swap(after(across[2], state), 1))
-    relays = list(zip(relays, beside, across, corner))
     early = 2 * PLANE
+    tiny = pl.CostEstimate(flops=0, bytes_accessed=2 ** 12, transcendentals=0)
     sums = pl.pallas_call(
         close_first_kernel,
         out_shape=jax.ShapeDtypeStruct((rows, LANES), jnp.float32),
-        in_specs=[smem] + [vmem] * (1 + 2 * PLANE),
+        in_specs=[vmem] * (2 + early),
         out_specs=vmem,
         scratch_shapes=[pltpu.VMEM((2 * part, early * LANES), jnp.bfloat16)],
         compiler_params=params,
+        cost_estimate=tiny,
         name="close_first",
-    )(named, state, *relays[0], *relays[1])
+    )(named, state, *[group[n] for n in range(2) for group in (relays, beside, across, corner)])
+    corner.append(swap(across[2], 1))
+    far_slots = range(early, owners, PLANE)
+    order = [k + n for n in (0, 1, 2) for k in far_slots]
     sums = pl.pallas_call(
-        functools.partial(close_rest_kernel, planes),
+        functools.partial(close_more_kernel, order),
+        out_shape=jax.ShapeDtypeStruct((rows, LANES), jnp.float32),
+        in_specs=[vmem] * (3 + 3),
+        out_specs=vmem,
+        scratch_shapes=[pltpu.VMEM((2 * part, len(order) * LANES), jnp.bfloat16)],
+        compiler_params=params,
+        name="close_more",
+    )(named, state, sums, relays[2], beside[2], across[2])
+    order = [k + 3 for k in far_slots]
+    sums = pl.pallas_call(
+        functools.partial(close_last_kernel, planes, order),
         out_shape=[
             jax.ShapeDtypeStruct((pieces, rows_piece, LANES), jnp.float32 if k == 0 else jnp.bfloat16)
             for k in range(planes)
         ],
-        in_specs=[smem] + [vmem] * (2 + PLANE),
+        in_specs=[vmem] * 4,
         out_specs=[vmem] * planes,
         scratch_shapes=[
             pltpu.VMEM((rows, LANES), jnp.float32),
-            pltpu.VMEM((2 * part, (owners - early) * LANES), jnp.bfloat16),
+            pltpu.VMEM((2 * part, len(order) * LANES), jnp.bfloat16),
         ],
         compiler_params=params,
-        name="close_rest",
-    )(named, state, sums, *relays[2])
+        name="close_last",
+    )(named, state, sums, corner[2])
     total = sums[0]
     for k in range(1, planes):
         total = total + swap(sums[k], k * PLANE).astype(jnp.float32)

time: 41.1 us -> 40.2 us (0.978)
  local copies, waits for them, and re-layouts: 0.01 us -> 1.81 us
  Pallas kernels: 8.79 us -> 7.41 us
  waiting for transfers between devices: 13.5 us -> 12.2 us
    unnamed x4, local copies, waits for them, and re-layouts: 0.01 us -> 1.81 us
    ppermute x16, waiting for transfers between devices: 13.5 us -> 12.2 us  [swap(): return lax.ppermute(x, 'bits', [(i, i ^ bit) for i in range(owners)])]
    pallas_call x1, Pallas kernels: 1.67 us -> 0.88 us  [in_planes(): pl.pallas_call(close_first_kernel, out_shape=jax.ShapeDtypeStruct((rows,...]
    pallas_call x1 -> x2, Pallas kernels: 1.67 us -> 1.07 us  [the longest x1 0.68 us: in_planes(): pl.pallas_call(functools.partial(close_more_kernel, order), out_shape=jax...]
  transfers between devices with their start and end apart: 16 -> 16, of which waited for: 8 -> 5; matrix products, arithmetic and copies ran while one was open for 0% -> 0% of each run, Pallas kernels for 11% -> 11%
where the time goes in v4:
time: 40.2 us; the launch traced here: 40 us
  starting transfers between devices  17.8 us (44%)
  waiting for transfers between devices  12.2 us (30%)
  Pallas kernels  7.41 us (18%)
  local copies, waits for them, and re-layouts  1.81 us (5%)
  other arithmetic  0.65 us (2%)
    ppermute x16, starting transfers between devices, swap(): return lax.ppermute(x, 'bits', [(i, i ^ bit) for i in range(owners)])  17.8 us
    ppermute x16, waiting for transfers between devices, swap(): return lax.ppermute(x, 'bits', [(i, i ^ bit) for i in range(owners)])  12.2 us
    pallas_call x1, Pallas kernels, in_planes(): pl.pallas_call(functools.partial(pack_kernel, planes), out_shape=[jax.Sha...  2.81 us
    pallas_call x1, Pallas kernels, in_planes(): pl.pallas_call(functools.partial(state_kernel, planes, blocks, merges, pi...  2.62 us
    unnamed x4, local copies, waits for them, and re-layouts  1.81 us
    pallas_call x1, Pallas kernels, in_planes(): pl.pallas_call(close_first_kernel, out_shape=jax.ShapeDtypeStruct((rows,...  0.88 us
  transfers between devices with their start and end apart: 16, of which 5 were waited for; matrix products, arithmetic and copies ran while one was open for 0% of the time, Pallas kernels for 11%

profile of v4, /device:TPU:0, one launch (start us, length us, event | category | flops | bytes accessed | tf_op | source)
XLA Modules:
  0.0 40.0 jit_solution(4572045801010615535)
XLA Ops:
  0.0 2.8 %pack.1 = (bf16[24,32,128]{2,1,0:T(8,128)(2,1)}, bf16[24,32,128]{2,1,0:T(8,128)(2,1)}, bf16[17,32,128]{2,1,0:T(8,128)(2,1)}, bf16[17,32,128]{2,1,0:T(8,128)(2,1)...) custom-call(bf16[2,512,512]{2,1,0:T(8,128)(2,1)} %bitcast.13, bf16[2,64,512]{2,1,0:T(8,128)(2,1)} %bitcast.14, ...), custom_call_target="tpu_custom_call" | custom-call | flops 1048576 | bytes 4096 | tf_op jit(solution)/shard_map/pack/pallas_call | solution.py:258
  2.8 3.1 %collective-permute-start.3 = (bf16[24,32,128]{2,1,0:T(8,128)(2,1)}, bf16[24,32,128]{2,1,0:T(8,128)(2,1)S(1)}, u32[]{:S(2)}, u32[]{:S(2)}) collective-permute-start(bf16[24,32,128]{2,1,0:T(8,128)(2,1)} %get-tuple-element.23), channel_id=1, source_target_pairs={{0,4},{1,5},{2,6},{3,7},{4,0},{5,1},{6,2},{7,3},{8,12},{9,13},{10,... | collective-permute-start | bytes 589832 | tf_op jit(solution)/shard_map/ppermute | solution.py:28
  5.9 2.6 %collective-permute-start.8 = (bf16[17,32,128]{2,1,0:T(8,128)(2,1)}, bf16[17,32,128]{2,1,0:T(8,128)(2,1)S(1)}, u32[]{:S(2)}, u32[]{:S(2)}) collective-permute-start(bf16[17,32,128]{2,1,0:T(8,128)(2,1)} %get-tuple-element.26), channel_id=1, source_target_pairs={{0,8},{1,9},{2,10},{3,11},{4,12},{5,13},{6,14},{7,15},{8,0},{9,1},... | collective-permute-start | bytes 417800 | tf_op jit(solution)/shard_map/ppermute | solution.py:28
  8.5 0.4 %collective-permute-start.7 = (bf16[9,32,128]{2,1,0:T(8,128)(2,1)}, bf16[9,32,128]{2,1,0:T(8,128)(2,1)S(1)}, u32[]{:S(2)}, u32[]{:S(2)}) collective-permute-start(bf16[9,32,128]{2,1,0:T(8,128)(2,1)} %get-tuple-element.25), channel_id=1, source_target_pairs={{0,4},{1,5},{2,6},{3,7},{4,0},{5,1},{6,2},{7,3},{8,12},{9,13},{10,... | collective-permute-start | bytes 221192 | tf_op jit(solution)/shard_map/ppermute | solution.py:28
  8.9 1.4 %collective-permute-start.9 = (bf16[17,32,128]{2,1,0:T(8,128)(2,1)}, bf16[17,32,128]{2,1,0:T(8,128)(2,1)S(1)}, u32[]{:S(2)}, u32[]{:S(2)}) collective-permute-start(bf16[17,32,128]{2,1,0:T(8,128)(2,1)} %get-tuple-element.27), channel_id=1, source_target_pairs={{0,12},{1,13},{2,14},{3,15},{4,8},{5,9},{6,10},{7,11},{8,4},{9,5},... | collective-permute-start | bytes 417800 | tf_op jit(solution)/shard_map/ppermute | solution.py:28
  10.3 1.5 %collective-permute-start.1 = (bf16[1,24,32,128]{3,2,1,0:T(8,128)(2,1)}, bf16[1,24,32,128]{3,2,1,0:T(8,128)(2,1)S(1)}, u32[]{:S(2)}, u32[]{:S(2)}) collective-permute-start(bf16[1,24,32,128]{3,2,1,0:T(8,128)(2,1)} %bitcast.11), channel_id=1, source_target_pairs={{0,2},{1,3},{2,0},{3,1},{4,6},{5,7},{6,4},{7,5},{8,10},{9,11},{10,... | collective-permute-start | bytes 589832 | tf_op jit(solution)/shard_map/ppermute | solution.py:28
  11.8 3.0 %collective-permute-done.3 = bf16[24,32,128]{2,1,0:T(8,128)(2,1)S(1)} collective-permute-done((bf16[24,32,128]{2,1,0:T(8,128)(2,1)}, bf16[24,32,128]{2,1,0:T(8,128)(2,1)S(1)}, u32[]{:S(2)}, u32[]{:S(2)}) %collective-permute-start.3) | collective-permute-done | bytes 196640 | tf_op jit(solution)/shard_map/ppermute | solution.py:28
  14.8 1.7 %collective-permute-start.5 = (bf16[1,24,32,128]{3,2,1,0:T(8,128)(2,1)S(1)}, bf16[1,24,32,128]{3,2,1,0:T(8,128)(2,1)S(1)}, u32[]{:S(2)}, u32[]{:S(2)}) collective-permute-start(bf16[1,24,32,128]{3,2,1,0:T(8,128)(2,1)S(1)} %bitcast.7), channel_id=1, source_target_pairs={{0,2},{1,3},{2,0},{3,1},{4,6},{5,7},{6,4},{7,5},{8,10},{9,11},{10,... | collective-permute-start | bytes 589832 | tf_op jit(solution)/shard_map/ppermute | solution.py:28
  16.5 0.0 copy-start
  16.5 0.9 %copy-done = bf16[24,32,128]{2,1,0:T(8,128)(2,1)S(1)} copy-done((bf16[24,32,128]{2,1,0:T(8,128)(2,1)S(1)}, bf16[24,32,128]{2,1,0:T(8,128)(2,1)}, u32[]{:S(2)}) %copy-start) | copy-done | bytes 196632
  17.4 0.0 copy-start.1
  17.4 0.9 %copy-done.1 = bf16[9,32,128]{2,1,0:T(8,128)(2,1)S(1)} copy-done((bf16[9,32,128]{2,1,0:T(8,128)(2,1)S(1)}, bf16[9,32,128]{2,1,0:T(8,128)(2,1)}, u32[]{:S(2)}) %copy-start.1) | copy-done | bytes 73752
  18.3 0.0 collective-permute-done.7.refs_9_
  18.3 0.1 collective-permute-start
  18.4 0.0 collective-permute-done.8.refs_10_.refs_0_
  18.4 2.4 %collective-permute-done.9.refs_11_.refs_1_ = bf16[17,32,128]{2,1,0:T(8,128)(2,1)S(1)} collective-permute-done((bf16[17,32,128]{2,1,0:T(8,128)(2,1)}, bf16[17,32,128]{2,1,0:T(8,128)(2,1)S(1)}, u32[]{:S(2)}, u32[]{:S(2)}) %collective-permute-start.9) | collective-permute-done | bytes 139296 | tf_op jit(solution)/shard_map/ppermute | solution.py:28
  20.8 1.6 %collective-permute-start.11 = (bf16[2,8,32,128]{3,2,1,0:T(8,128)(2,1)S(1)}, bf16[2,8,32,128]{3,2,1,0:T(8,128)(2,1)S(1)}, u32[]{:S(2)}, u32[]{:S(2)}) collective-permute-start(bf16[2,8,32,128]{3,2,1,0:T(8,128)(2,1)S(1)} %join.1.refs_0_), channel_id=1, source_target_pairs={{0,2},{1,3},{2,0},{3,1},{4,6},{5,7},{6,4},{7,5},{8,10},{9,11},{10,... | collective-permute-start | bytes 393224 | tf_op jit(solution)/shard_map/ppermute | solution.py:28
  22.4 0.0 collective-permute-start.4
  22.4 0.0 collective-permute-done.1.refs_2_
  22.4 0.5 %collective-permute-start.2 = (bf16[1,24,32,128]{3,2,1,0:T(8,128)(2,1)S(1)}, bf16[1,24,32,128]{3,2,1,0:T(8,128)(2,1)S(1)}, u32[]{:S(2)}, u32[]{:S(2)}) collective-permute-start(bf16[1,24,32,128]{3,2,1,0:T(8,128)(2,1)S(1)} %collective-permute-done.1.refs_2_), channel_id=1, source_target_pairs={{0,1},{1,0},{2,3},{3,2},{4,5},{5,4},{6,7},{7,6},{8,9},{9,8},{10,11... | collective-permute-start | bytes 589832 | tf_op jit(solution)/shard_map/ppermute | solution.py:28
  22.9 0.0 collective-permute-done.5.refs_6_
  22.9 0.1 collective-permute-start.6
  23.0 0.0 collective-permute-done.refs_1_
  23.0 0.4 %collective-permute-start.10 = (bf16[2,8,32,128]{3,2,1,0:T(8,128)(2,1)S(1)}, bf16[2,8,32,128]{3,2,1,0:T(8,128)(2,1)S(1)}, u32[]{:S(2)}, u32[]{:S(2)}) collective-permute-start(bf16[2,8,32,128]{3,2,1,0:T(8,128)(2,1)S(1)} %join.1.refs_0_), channel_id=1, source_target_pairs={{0,1},{1,0},{2,3},{3,2},{4,5},{5,4},{6,7},{7,6},{8,9},{9,8},{10,11... | collective-permute-start | bytes 393224 | tf_op jit(solution)/shard_map/ppermute | solution.py:28
  23.5 2.4 %collective-permute-done.11.refs_2_ = bf16[2,8,32,128]{3,2,1,0:T(8,128)(2,1)S(1)} collective-permute-done((bf16[2,8,32,128]{3,2,1,0:T(8,128)(2,1)S(1)}, bf16[2,8,32,128]{3,2,1,0:T(8,128)(2,1)S(1)}, u32[]{:S(2)}, u32[]{:S(2)}) %collective-permute-start.11) | collective-permute-done | bytes 131104 | tf_op jit(solution)/shard_map/ppermute | solution.py:28
  25.9 0.0 collective-permute-start.12
  25.9 0.0 collective-permute-done.2.refs_3_
  25.9 0.0 collective-permute-done.4.refs_5_
  25.9 0.0 collective-permute-done.6.refs_7_
  25.9 2.6 %state.1 = (bf16[512,512]{1,0:T(8,128)(2,1)S(1)}, f32[512,128]{1,0:T(8,128)S(1)}) custom-call(bf16[1,24,32,128]{3,2,1,0:T(8,128)(2,1)S(1)} %get-tuple-element.22.refs_0_, bf16[1,24,32,128]{3,2,1,0:T(8,128)(2,1)S(1)} %collective-permute-done.refs_1_, bf16[1,24,32,128]{3,2,1,0:T(8,128)(2,1)S(1)} %collective-permute-done.1.refs_2_, ...), custom_call_target="tpu_custom_call" | custom-call | bytes 4096 | tf_op jit(solution)/shard_map/state/pallas_call | solution.py:281
  28.5 0.9 %close_first.1.sums_in = f32[512,128]{1,0:T(8,128)S(1)} custom-call(f32[512,128]{1,0:T(8,128)S(1)} %get-tuple-element.28.named, bf16[512,512]{1,0:T(8,128)(2,1)S(1)} %get-tuple-element.29.state, bf16[1,24,32,128]{3,2,1,0:T(8,128)(2,1)S(1)} %get-tuple-element.22.refs_0_, bf16[1,24,32,128]{3,2,1,0:T(8,128)(2,1)S(1)} %collective-permute-done.refs_1_, ...), custom_call_target="tpu_custom_call" | custom-call | bytes 4096 | tf_op jit(solution)/shard_map/close_first/pallas_call | solution.py:302
  29.4 0.0 collective-permute-done.10.refs_1_
  29.4 0.7 %close_more.1.sums_in = f32[512,128]{1,0:T(8,128)S(1)} custom-call(f32[512,128]{1,0:T(8,128)S(1)} %get-tuple-element.28.named, bf16[512,512]{1,0:T(8,128)(2,1)S(1)} %get-tuple-element.29.state, f32[512,128]{1,0:T(8,128)S(1)} %close_first.1.sums_in, bf16[2,8,32,128]{3,2,1,0:T(8,128)(2,1)S(1)} %join.1.refs_0_, ...), custom_call_target="tpu_custom_call" | custom-call | tf_op jit(solution)/shard_map/close_more/pallas_call | solution.py:315
  30.1 0.0 collective-permute-done.12.relay
  30.1 0.4 close_last.1
  30.5 1.0 %collective-permute-start.13 = (bf16[8,16,128]{2,1,0:T(8,128)(2,1)S(1)}, bf16[8,16,128]{2,1,0:T(8,128)(2,1)S(1)}, u32[]{:S(2)}, u32[]{:S(2)}) collective-permute-start(bf16[8,16,128]{2,1,0:T(8,128)(2,1)S(1)} %get-tuple-element.32), channel_id=1, source_target_pairs={{0,4},{1,5},{2,6},{3,7},{4,0},{5,1},{6,2},{7,3},{8,12},{9,13},{10,... | collective-permute-start | bytes 98312 | tf_op jit(solution)/shard_map/ppermute | solution.py:28
  31.5 2.1 %collective-permute-start.14 = (bf16[8,16,128]{2,1,0:T(8,128)(2,1)S(1)}, bf16[8,16,128]{2,1,0:T(8,128)(2,1)S(1)}, u32[]{:S(2)}, u32[]{:S(2)}) collective-permute-start(bf16[8,16,128]{2,1,0:T(8,128)(2,1)S(1)} %get-tuple-element.33), channel_id=1, source_target_pairs={{0,8},{1,9},{2,10},{3,11},{4,12},{5,13},{6,14},{7,15},{8,0},{9,1},... | collective-permute-start | bytes 98312 | tf_op jit(solution)/shard_map/ppermute | solution.py:28
  33.6 1.3 %collective-permute-start.15 = (bf16[8,16,128]{2,1,0:T(8,128)(2,1)S(1)}, bf16[8,16,128]{2,1,0:T(8,128)(2,1)S(1)}, u32[]{:S(2)}, u32[]{:S(2)}) collective-permute-start(bf16[8,16,128]{2,1,0:T(8,128)(2,1)S(1)} %get-tuple-element.34), channel_id=1, source_target_pairs={{0,12},{1,13},{2,14},{3,15},{4,8},{5,9},{6,10},{7,11},{8,4},{9,5},... | collective-permute-start | bytes 98312 | tf_op jit(solution)/shard_map/ppermute | solution.py:28
  35.0 0.0 collective-permute-done.13
  35.0 2.0 %collective-permute-done.14 = bf16[8,16,128]{2,1,0:T(8,128)(2,1)S(1)} collective-permute-done((bf16[8,16,128]{2,1,0:T(8,128)(2,1)S(1)}, bf16[8,16,128]{2,1,0:T(8,128)(2,1)S(1)}, u32[]{:S(2)}, u32[]{:S(2)}) %collective-permute-start.14) | collective-permute-done | bytes 32800 | tf_op jit(solution)/shard_map/ppermute | solution.py:28
  36.9 2.4 %collective-permute-done.15 = bf16[8,16,128]{2,1,0:T(8,128)(2,1)S(1)} collective-permute-done((bf16[8,16,128]{2,1,0:T(8,128)(2,1)S(1)}, bf16[8,16,128]{2,1,0:T(8,128)(2,1)S(1)}, u32[]{:S(2)}, u32[]{:S(2)}) %collective-permute-start.15) | collective-permute-done | bytes 32800 | tf_op jit(solution)/shard_map/ppermute | solution.py:28
  39.3 0.6 %convert_add_fusion = f32[8,16,128]{2,1,0:T(8,128)} fusion(bf16[8,16,128]{2,1,0:T(8,128)(2,1)S(1)} %collective-permute-done.15, bf16[8,16,128]{2,1,0:T(8,128)(2,1)S(1)} %collective-permute-done.14, f32[8,16,128]{2,1,0:T(8,128)S(1)} %get-tuple-element.31, bf16[8,16,128]{2,1,0:T(8,128)(2,1)S(1)} %collective-permute-done.13), kind=kLoop, calls=%fused_computation | loop fusion | flops 98304 | bytes 229376 | tf_op jit(solution)/shard_map/add | solution.py:342
  (2 shorter events, 0.0 us)
Async XLA Ops:
  2.8 12.0 %collective-permute-start.3 = (bf16[24,32,128]{2,1,0:T(8,128)(2,1)}, bf16[24,32,128]{2,1,0:T(8,128)(2,1)S(1)}, u32[]{:S(2)}, u32[]{:S(2)}) collective-permute-start(bf16[24,32,128]{2,1,0:T(8,128)(2,1)} %get-tuple-element.23), channel_id=1, source_target_pairs={{0,4},{1,5},{2,6},{3,7},{4,0},{5,1},{6,2},{7,3},{8,12},{9,13},{10,... | collective-permute-start | bytes 589832 | tf_op jit(solution)/shard_map/ppermute | solution.py:28
  5.9 12.5 %collective-permute-start.8 = (bf16[17,32,128]{2,1,0:T(8,128)(2,1)}, bf16[17,32,128]{2,1,0:T(8,128)(2,1)S(1)}, u32[]{:S(2)}, u32[]{:S(2)}) collective-permute-start(bf16[17,32,128]{2,1,0:T(8,128)(2,1)} %get-tuple-element.26), channel_id=1, source_target_pairs={{0,8},{1,9},{2,10},{3,11},{4,12},{5,13},{6,14},{7,15},{8,0},{9,1},... | collective-permute-start | bytes 417800 | tf_op jit(solution)/shard_map/ppermute | solution.py:28
  8.5 9.8 %collective-permute-start.7 = (bf16[9,32,128]{2,1,0:T(8,128)(2,1)}, bf16[9,32,128]{2,1,0:T(8,128)(2,1)S(1)}, u32[]{:S(2)}, u32[]{:S(2)}) collective-permute-start(bf16[9,32,128]{2,1,0:T(8,128)(2,1)} %get-tuple-element.25), channel_id=1, source_target_pairs={{0,4},{1,5},{2,6},{3,7},{4,0},{5,1},{6,2},{7,3},{8,12},{9,13},{10,... | collective-permute-start | bytes 221192 | tf_op jit(solution)/shard_map/ppermute | solution.py:28
  8.9 11.9 %collective-permute-start.9 = (bf16[17,32,128]{2,1,0:T(8,128)(2,1)}, bf16[17,32,128]{2,1,0:T(8,128)(2,1)S(1)}, u32[]{:S(2)}, u32[]{:S(2)}) collective-permute-start(bf16[17,32,128]{2,1,0:T(8,128)(2,1)} %get-tuple-element.27), channel_id=1, source_target_pairs={{0,12},{1,13},{2,14},{3,15},{4,8},{5,9},{6,10},{7,11},{8,4},{9,5},... | collective-permute-start | bytes 417800 | tf_op jit(solution)/shard_map/ppermute | solution.py:28
  10.3 12.1 %collective-permute-start.1 = (bf16[1,24,32,128]{3,2,1,0:T(8,128)(2,1)}, bf16[1,24,32,128]{3,2,1,0:T(8,128)(2,1)S(1)}, u32[]{:S(2)}, u32[]{:S(2)}) collective-permute-start(bf16[1,24,32,128]{3,2,1,0:T(8,128)(2,1)} %bitcast.11), channel_id=1, source_target_pairs={{0,2},{1,3},{2,0},{3,1},{4,6},{5,7},{6,4},{7,5},{8,10},{9,11},{10,... | collective-permute-start | bytes 589832 | tf_op jit(solution)/shard_map/ppermute | solution.py:28
  14.8 8.1 %collective-permute-start.5 = (bf16[1,24,32,128]{3,2,1,0:T(8,128)(2,1)S(1)}, bf16[1,24,32,128]{3,2,1,0:T(8,128)(2,1)S(1)}, u32[]{:S(2)}, u32[]{:S(2)}) collective-permute-start(bf16[1,24,32,128]{3,2,1,0:T(8,128)(2,1)S(1)} %bitcast.7), channel_id=1, source_target_pairs={{0,2},{1,3},{2,0},{3,1},{4,6},{5,7},{6,4},{7,5},{8,10},{9,11},{10,... | collective-permute-start | bytes 589832 | tf_op jit(solution)/shard_map/ppermute | solution.py:28
  16.5 0.9 %copy-start = (bf16[24,32,128]{2,1,0:T(8,128)(2,1)S(1)}, bf16[24,32,128]{2,1,0:T(8,128)(2,1)}, u32[]{:S(2)}) copy-start(bf16[24,32,128]{2,1,0:T(8,128)(2,1)} %get-tuple-element.20) | copy-start | bytes 589828
  17.4 0.9 %copy-start.1 = (bf16[9,32,128]{2,1,0:T(8,128)(2,1)S(1)}, bf16[9,32,128]{2,1,0:T(8,128)(2,1)}, u32[]{:S(2)}) copy-start(bf16[9,32,128]{2,1,0:T(8,128)(2,1)} %get-tuple-element.21.refs_1_) | copy-start | bytes 221188
  18.3 4.7 %collective-permute-start = (bf16[1,24,32,128]{3,2,1,0:T(8,128)(2,1)S(1)}, bf16[1,24,32,128]{3,2,1,0:T(8,128)(2,1)S(1)}, u32[]{:S(2)}, u32[]{:S(2)}) collective-permute-start(bf16[1,24,32,128]{3,2,1,0:T(8,128)(2,1)S(1)} %get-tuple-element.22.refs_0_), channel_id=1, source_target_pairs={{0,1},{1,0},{2,3},{3,2},{4,5},{5,4},{6,7},{7,6},{8,9},{9,8},{10,11... | collective-permute-start | bytes 589832 | tf_op jit(solution)/shard_map/ppermute | solution.py:28
  20.8 5.0 %collective-permute-start.11 = (bf16[2,8,32,128]{3,2,1,0:T(8,128)(2,1)S(1)}, bf16[2,8,32,128]{3,2,1,0:T(8,128)(2,1)S(1)}, u32[]{:S(2)}, u32[]{:S(2)}) collective-permute-start(bf16[2,8,32,128]{3,2,1,0:T(8,128)(2,1)S(1)} %join.1.refs_0_), channel_id=1, source_target_pairs={{0,2},{1,3},{2,0},{3,1},{4,6},{5,7},{6,4},{7,5},{8,10},{9,11},{10,... | collective-permute-start | bytes 393224 | tf_op jit(solution)/shard_map/ppermute | solution.py:28
  22.4 3.5 %collective-permute-start.4 = (bf16[1,24,32,128]{3,2,1,0:T(8,128)(2,1)S(1)}, bf16[1,24,32,128]{3,2,1,0:T(8,128)(2,1)S(1)}, u32[]{:S(2)}, u32[]{:S(2)}) collective-permute-start(bf16[1,24,32,128]{3,2,1,0:T(8,128)(2,1)S(1)} %bitcast.8), channel_id=1, source_target_pairs={{0,1},{1,0},{2,3},{3,2},{4,5},{5,4},{6,7},{7,6},{8,9},{9,8},{10,11... | collective-permute-start | bytes 589832 | tf_op jit(solution)/shard_map/ppermute | solution.py:28
  22.4 3.4 %collective-permute-start.2 = (bf16[1,24,32,128]{3,2,1,0:T(8,128)(2,1)S(1)}, bf16[1,24,32,128]{3,2,1,0:T(8,128)(2,1)S(1)}, u32[]{:S(2)}, u32[]{:S(2)}) collective-permute-start(bf16[1,24,32,128]{3,2,1,0:T(8,128)(2,1)S(1)} %collective-permute-done.1.refs_2_), channel_id=1, source_target_pairs={{0,1},{1,0},{2,3},{3,2},{4,5},{5,4},{6,7},{7,6},{8,9},{9,8},{10,11... | collective-permute-start | bytes 589832 | tf_op jit(solution)/shard_map/ppermute | solution.py:28
  22.9 2.9 %collective-permute-start.6 = (bf16[1,24,32,128]{3,2,1,0:T(8,128)(2,1)S(1)}, bf16[1,24,32,128]{3,2,1,0:T(8,128)(2,1)S(1)}, u32[]{:S(2)}, u32[]{:S(2)}) collective-permute-start(bf16[1,24,32,128]{3,2,1,0:T(8,128)(2,1)S(1)} %collective-permute-done.5.refs_6_), channel_id=1, source_target_pairs={{0,1},{1,0},{2,3},{3,2},{4,5},{5,4},{6,7},{7,6},{8,9},{9,8},{10,11... | collective-permute-start | bytes 589832 | tf_op jit(solution)/shard_map/ppermute | solution.py:28
  23.0 6.4 %collective-permute-start.10 = (bf16[2,8,32,128]{3,2,1,0:T(8,128)(2,1)S(1)}, bf16[2,8,32,128]{3,2,1,0:T(8,128)(2,1)S(1)}, u32[]{:S(2)}, u32[]{:S(2)}) collective-permute-start(bf16[2,8,32,128]{3,2,1,0:T(8,128)(2,1)S(1)} %join.1.refs_0_), channel_id=1, source_target_pairs={{0,1},{1,0},{2,3},{3,2},{4,5},{5,4},{6,7},{7,6},{8,9},{9,8},{10,11... | collective-permute-start | bytes 393224 | tf_op jit(solution)/shard_map/ppermute | solution.py:28
  25.9 4.2 %collective-permute-start.12 = (bf16[2,8,32,128]{3,2,1,0:T(8,128)(2,1)S(1)}, bf16[2,8,32,128]{3,2,1,0:T(8,128)(2,1)S(1)}, u32[]{:S(2)}, u32[]{:S(2)}) collective-permute-start(bf16[2,8,32,128]{3,2,1,0:T(8,128)(2,1)S(1)} %collective-permute-done.11.refs_2_), channel_id=1, source_target_pairs={{0,1},{1,0},{2,3},{3,2},{4,5},{5,4},{6,7},{7,6},{8,9},{9,8},{10,11... | collective-permute-start | bytes 393224 | tf_op jit(solution)/shard_map/ppermute | solution.py:28
  30.5 4.5 %collective-permute-start.13 = (bf16[8,16,128]{2,1,0:T(8,128)(2,1)S(1)}, bf16[8,16,128]{2,1,0:T(8,128)(2,1)S(1)}, u32[]{:S(2)}, u32[]{:S(2)}) collective-permute-start(bf16[8,16,128]{2,1,0:T(8,128)(2,1)S(1)} %get-tuple-element.32), channel_id=1, source_target_pairs={{0,4},{1,5},{2,6},{3,7},{4,0},{5,1},{6,2},{7,3},{8,12},{9,13},{10,... | collective-permute-start | bytes 98312 | tf_op jit(solution)/shard_map/ppermute | solution.py:28
  31.5 5.4 %collective-permute-start.14 = (bf16[8,16,128]{2,1,0:T(8,128)(2,1)S(1)}, bf16[8,16,128]{2,1,0:T(8,128)(2,1)S(1)}, u32[]{:S(2)}, u32[]{:S(2)}) collective-permute-start(bf16[8,16,128]{2,1,0:T(8,128)(2,1)S(1)} %get-tuple-element.33), channel_id=1, source_target_pairs={{0,8},{1,9},{2,10},{3,11},{4,12},{5,13},{6,14},{7,15},{8,0},{9,1},... | collective-permute-start | bytes 98312 | tf_op jit(solution)/shard_map/ppermute | solution.py:28
  33.6 5.7 %collective-permute-start.15 = (bf16[8,16,128]{2,1,0:T(8,128)(2,1)S(1)}, bf16[8,16,128]{2,1,0:T(8,128)(2,1)S(1)}, u32[]{:S(2)}, u32[]{:S(2)}) collective-permute-start(bf16[8,16,128]{2,1,0:T(8,128)(2,1)S(1)} %get-tuple-element.34), channel_id=1, source_target_pairs={{0,12},{1,13},{2,14},{3,15},{4,8},{5,9},{6,10},{7,11},{8,4},{9,5},... | collective-permute-start | bytes 98312 | tf_op jit(solution)/shard_map/ppermute | solution.py:28

commit v5 on v4

--- a/solution.py
+++ b/solution.py
@@ -12,7 +12,6 @@
 PLANE = 4
 VMEM_BYTES = 32 * 1024 * 1024
 PACK_BYTES = 60 * 1024 * 1024
-HEAD = 8
 
 
 def complex_form(blocks):
@@ -42,25 +41,30 @@
     for copy in copies:
         copy.start()
     merges, pieces = pair_prefix_ref.shape
-    plan[...] = jnp.zeros_like(plan)
+    blocks, held, slots = first_ref.shape[0], prefix_ref.shape[0], planes * PLANE
     for copy in copies[4:]:
         copy.wait()
-    plan[:merges, :pieces] = pair_prefix_ref[...]
-    plan[merges:2 * merges, :pieces] = pair_suffix_ref[...]
-    plan[2 * merges:2 * merges + 1, :pieces] = count_ref[...]
     me = lax.axis_index("bits")
     lane = lax.broadcasted_iota(jnp.int32, (pieces, LANES), 1)
     named = [jnp.zeros((pieces, LANES), jnp.int32)] * planes
-    for slot in range(planes * PLANE):
+    for slot in range(slots):
         hits = jnp.sum((routes_ref[...] == slot ^ me).astype(jnp.int32), axis=1, keepdims=True)
         named = [jnp.where(lane == slot ^ k * PLANE, hits, there) for k, there in enumerate(named)]
+    own_lane = lax.broadcasted_iota(jnp.int32, (pieces, pieces), 0) == lax.broadcasted_iota(jnp.int32, (pieces, pieces), 1)
+    picks = jnp.zeros((pieces, LANES), jnp.int32)
+    for m in range(merges):
+        pick = pair_suffix_ref[m:m + 1, :] * held + pair_prefix_ref[m:m + 1, :]
+        pick = jnp.where(m < count_ref[...], slots + pick, -1)
+        pick = jnp.sum(jnp.where(own_lane, jnp.broadcast_to(pick, (pieces, pieces)), 0), axis=1, keepdims=True)
+        picks += (lane == pick).astype(jnp.int32)
+    plan[...] = jnp.zeros_like(plan)
     routing = []
     for k in range(planes):
-        plan[HEAD:HEAD + pieces, :] = named[k]
-        routing.append(plan[...].astype(jnp.float32).astype(jnp.bfloat16))
+        plan[:pieces, :] = (named[k] + picks).astype(jnp.float32)
+        routing.append(plan[...].astype(jnp.bfloat16))
     blocks, _, depth, width = first_ref.shape
     part, span = width // 2, width // (planes // 2)
-    held, rows_piece, twice_width = prefix_ref.shape
+    rows_piece, twice_width = prefix_ref.shape[1:]
     per = depth // rows_piece
     firsts = 2 * blocks * (part // LANES)
     relayed = [(firsts if k < 2 else 0) + part // depth for k in range(planes)]
@@ -139,58 +143,60 @@
     )(*packs)
 
 
-def state_kernel(planes, blocks, merges, pieces, rows_piece, held, *refs):
+def state_kernel(planes, blocks, pieces, rows_piece, held, *refs):
     relays, packs = refs[:2 * PLANE], refs[2 * PLANE:2 * PLANE + planes]
-    state, named, plan_out, forms, products, plan, sem = refs[2 * PLANE + planes:]
+    state, named, forms, high, low = refs[2 * PLANE + planes:]
     me = lax.axis_index("bits")
     depth = packs[0].shape[1]
     span, twice_part = forms.shape[1:]
     part = twice_part // 2
+    rows = held * rows_piece
     locals_ = []
-    rows = planes * held * rows_piece
-    index = lax.broadcasted_iota(jnp.int32, (merges, LANES), 0)
-    tail = 1 + 2 * (span // LANES) * (held * rows_piece // depth)
+    tail = 1 + 2 * (span // LANES) * (rows // depth)
     for k in range(planes):
         first = packs[k].shape[0] - tail
         numbers = packs[k][first].astype(jnp.float32)
         for n in range(pieces):
             here = slice((k * pieces + n) * rows_piece, (k * pieces + n + 1) * rows_piece)
-            named[here, :] = jnp.broadcast_to(numbers[HEAD + n:HEAD + n + 1], (rows_piece, LANES))
-        plan_out[k] = numbers.astype(jnp.int32)
-        live = index < plan_out[k, 2 * merges:2 * merges + 1]
-        picked = plan_out[k, merges:2 * merges] * rows + (plan_out[k, :merges] + k * held) * rows_piece
-        plan_out[k, :merges] = jnp.where(live, picked, blocks * rows)
+            named[here, :] = jnp.broadcast_to(numbers[n:n + 1], (rows_piece, LANES))
         locals_.append(packs[k].at[first + 1:first + tail])
-    copy = pltpu.make_async_copy(plan_out, plan, sem)
-    copy.start()
+    wide = (LANES, blocks * rows)
+    spread = lax.broadcasted_iota(jnp.int32, wide, 0) - planes * PLANE == lax.broadcasted_iota(jnp.int32, wide, 1) // rows_piece
+    spread = spread.astype(jnp.float32).astype(jnp.bfloat16)
+    wide = (planes * pieces * rows_piece, blocks * rows)
+    same_row = lax.broadcasted_iota(jnp.int32, wide, 0) % rows_piece == lax.broadcasted_iota(jnp.int32, wide, 1) % rows_piece
+    picks = jnp.dot(named[...].astype(jnp.bfloat16), spread, preferred_element_type=jnp.float32)
+    picks = jnp.where(same_row, picks, 0.0).astype(jnp.bfloat16)
     for j in range(2 * PLANE):
         there = pl.ds(pl.multiple_of((me ^ j) % (2 * PLANE) * depth, depth), depth)
         for a in range(blocks):
             for n in range(twice_part // LANES):
                 forms[a, there, n * LANES:(n + 1) * LANES] = relays[j][0, a * (twice_part // LANES) + n]
-    chunks = held * rows_piece // depth
+    chunks = rows // depth
     left = []
     for c in range(2):
         for k in range(planes):
             columns = []
             for n in range(span // LANES):
                 first = (c * (span // LANES) + n) * chunks
-                columns.append(locals_[k][first:first + chunks].reshape(rows // planes, LANES))
+                columns.append(locals_[k][first:first + chunks].reshape(rows, LANES))
             left.append(jnp.concatenate(columns, axis=1))
     left = jnp.concatenate(left, axis=0)
-    products[blocks * rows:, :] = jnp.zeros((rows_piece, twice_part), jnp.float32)
     for a in range(blocks):
         both = jnp.dot(left, forms[a], preferred_element_type=jnp.float32)
-        products[a * rows:(a + 1) * rows, :part] = both[:rows, :part] - both[rows:, part:]
-        products[a * rows:(a + 1) * rows, part:] = both[:rows, part:] + both[rows:, :part]
-    copy.wait()
-    for i in range(planes * pieces):
-        k, n = divmod(i, pieces)
-        total = None
-        for m in range(merges):
-            term = products[pl.ds(pl.multiple_of(plan[k, m, n], rows_piece), rows_piece), :]
-            total = term if total is None else total + term
-        state[i * rows_piece:(i + 1) * rows_piece, :] = total.astype(jnp.bfloat16)
+        real, imag = both[:planes * rows], both[planes * rows:]
+        product = jnp.concatenate([real[:, :part] - imag[:, part:], real[:, part:] + imag[:, :part]], axis=1)
+        rounded = product.astype(jnp.bfloat16)
+        rest = (product - rounded.astype(jnp.float32)).astype(jnp.bfloat16)
+        for k in range(planes):
+            high[k, a * rows:(a + 1) * rows, :] = rounded[k * rows:(k + 1) * rows]
+            low[k, a * rows:(a + 1) * rows, :] = rest[k * rows:(k + 1) * rows]
+    size = pieces * rows_piece
+    for k in range(planes):
+        pick = picks[k * size:(k + 1) * size]
+        total = jnp.dot(pick, high[k], preferred_element_type=jnp.float32)
+        total += jnp.dot(pick, low[k], preferred_element_type=jnp.float32)
+        state[k * size:(k + 1) * size, :] = total.astype(jnp.bfloat16)
 
 
 def close(order, named, state, relays, sums, wide):
@@ -260,7 +266,7 @@
         out_shape=[jax.ShapeDtypeStruct((size, depth, LANES), jnp.bfloat16) for size in sizes],
         in_specs=[pl.BlockSpec(memory_space=pl.ANY)] * len(sources),
         out_specs=[vmem] * len(sizes),
-        scratch_shapes=[pltpu.VMEM((depth, LANES), jnp.int32), pltpu.VMEM((width, LANES), jnp.bfloat16)]
+        scratch_shapes=[pltpu.VMEM((depth, LANES), jnp.float32), pltpu.VMEM((width, LANES), jnp.bfloat16)]
         + [pltpu.VMEM(source.shape, source.dtype) for source in sources]
         + [pltpu.SemaphoreType.DMA((len(sources),))],
         compiler_params=pltpu.CompilerParams(vmem_limit_bytes=PACK_BYTES),
@@ -279,7 +285,7 @@
     across.append(swap(relays[2], 2))
     rows = planes * pieces * rows_piece
     state, named = pl.pallas_call(
-        functools.partial(state_kernel, planes, blocks, merges, pieces, rows_piece, held),
+        functools.partial(state_kernel, planes, blocks, pieces, rows_piece, held),
         out_shape=[
             jax.ShapeDtypeStruct((rows, 2 * part), jnp.bfloat16),
             jax.ShapeDtypeStruct((rows, LANES), jnp.float32),
@@ -287,11 +293,9 @@
         in_specs=[vmem] * (2 * PLANE + planes),
         out_specs=[vmem] * 2,
         scratch_shapes=[
-            pltpu.VMEM((planes, depth, LANES), jnp.int32),
             pltpu.VMEM((blocks, span, 2 * part), jnp.bfloat16),
-            pltpu.VMEM(((blocks * planes * held + 1) * rows_piece, 2 * part), jnp.float32),
-            pltpu.SMEM((planes, depth, LANES), jnp.int32),
-            pltpu.SemaphoreType.DMA,
+            pltpu.VMEM((planes, blocks * held * rows_piece, 2 * part), jnp.bfloat16),
+            pltpu.VMEM((planes, blocks * held * rows_piece, 2 * part), jnp.bfloat16),
         ],
         compiler_params=params,
         cost_estimate=pl.CostEstimate(flops=0, bytes_accessed=2 ** 12, transcendentals=0),
@@ -418,7 +422,7 @@
     owners = lax.axis_size("bits")
     planes = owners // PLANE
     depth, width = first_suffix.shape[2:]
-    pieces, merges = pair_prefix.shape
+    pieces = pair_prefix.shape[0]
     fits = (
         planes > 2
         and planes & (planes - 1) == 0
@@ -432,9 +436,8 @@
         and depth % prefix.shape[1] == 0
         and prefix.shape[0] * prefix.shape[1] % depth == 0
         and prefix.shape[1] % 16 == 0
-        and 2 * merges < HEAD
-        and HEAD + pieces <= depth
-        and max(pieces, owners) <= LANES
+        and pieces <= min(depth, LANES)
+        and owners + first_suffix.shape[0] * prefix.shape[0] <= LANES
     )
     return in_planes(*args) if fits else by_owner(*args)
 

time: 40.2 us -> 39 us (0.970)
  Pallas kernels: 7.41 us -> 6.21 us
    pallas_call x1, Pallas kernels: 2.62 us -> 1.42 us  [in_planes(): pl.pallas_call(functools.partial(state_kernel, planes, blocks, pieces, ro...]
  transfers between devices with their start and end apart: 16 -> 16, of which waited for: 5 -> 5; matrix products, arithmetic and copies ran while one was open for 0% -> 0% of each run, Pallas kernels for 11% -> 8%
where the time goes in v5:
time: 39 us; the launch traced here: 38.8 us
  starting transfers between devices  17.8 us (46%)
  waiting for transfers between devices  12.2 us (31%)
  Pallas kernels  6.21 us (16%)
  local copies, waits for them, and re-layouts  1.81 us (5%)
  other arithmetic  0.65 us (2%)
    ppermute x16, starting transfers between devices, swap(): return lax.ppermute(x, 'bits', [(i, i ^ bit) for i in range(owners)])  17.8 us
    ppermute x16, waiting for transfers between devices, swap(): return lax.ppermute(x, 'bits', [(i, i ^ bit) for i in range(owners)])  12.2 us
    pallas_call x1, Pallas kernels, in_planes(): pl.pallas_call(functools.partial(pack_kernel, planes), out_shape=[jax.Sha...  2.82 us
    unnamed x4, local copies, waits for them, and re-layouts  1.81 us
    pallas_call x1, Pallas kernels, in_planes(): pl.pallas_call(functools.partial(state_kernel, planes, blocks, pieces, ro...  1.42 us
    pallas_call x1, Pallas kernels, in_planes(): pl.pallas_call(close_first_kernel, out_shape=jax.ShapeDtypeStruct((rows,...  0.88 us
  transfers between devices with their start and end apart: 16, of which 5 were waited for; matrix products, arithmetic and copies ran while one was open for 0% of the time, Pallas kernels for 8%

profile of v5, /device:TPU:0, one launch (start us, length us, event | category | flops | bytes accessed | tf_op | source)
XLA Modules:
  0.0 38.8 jit_solution(14298450584501312701)
XLA Ops:
  0.0 2.8 %pack.1 = (bf16[24,32,128]{2,1,0:T(8,128)(2,1)}, bf16[24,32,128]{2,1,0:T(8,128)(2,1)}, bf16[17,32,128]{2,1,0:T(8,128)(2,1)}, bf16[17,32,128]{2,1,0:T(8,128)(2,1)...) custom-call(bf16[2,512,512]{2,1,0:T(8,128)(2,1)} %bitcast.13, bf16[2,64,512]{2,1,0:T(8,128)(2,1)} %bitcast.14, ...), custom_call_target="tpu_custom_call" | custom-call | flops 1048576 | bytes 4096 | tf_op jit(solution)/shard_map/pack/pallas_call | solution.py:264
  2.8 3.1 %collective-permute-start.3 = (bf16[24,32,128]{2,1,0:T(8,128)(2,1)}, bf16[24,32,128]{2,1,0:T(8,128)(2,1)S(1)}, u32[]{:S(2)}, u32[]{:S(2)}) collective-permute-start(bf16[24,32,128]{2,1,0:T(8,128)(2,1)} %get-tuple-element.23), channel_id=1, source_target_pairs={{0,4},{1,5},{2,6},{3,7},{4,0},{5,1},{6,2},{7,3},{8,12},{9,13},{10,... | collective-permute-start | bytes 589832 | tf_op jit(solution)/shard_map/ppermute | solution.py:27
  5.9 2.6 %collective-permute-start.8 = (bf16[17,32,128]{2,1,0:T(8,128)(2,1)}, bf16[17,32,128]{2,1,0:T(8,128)(2,1)S(1)}, u32[]{:S(2)}, u32[]{:S(2)}) collective-permute-start(bf16[17,32,128]{2,1,0:T(8,128)(2,1)} %get-tuple-element.26), channel_id=1, source_target_pairs={{0,8},{1,9},{2,10},{3,11},{4,12},{5,13},{6,14},{7,15},{8,0},{9,1},... | collective-permute-start | bytes 417800 | tf_op jit(solution)/shard_map/ppermute | solution.py:27
  8.5 0.4 %collective-permute-start.7 = (bf16[9,32,128]{2,1,0:T(8,128)(2,1)}, bf16[9,32,128]{2,1,0:T(8,128)(2,1)S(1)}, u32[]{:S(2)}, u32[]{:S(2)}) collective-permute-start(bf16[9,32,128]{2,1,0:T(8,128)(2,1)} %get-tuple-element.25), channel_id=1, source_target_pairs={{0,4},{1,5},{2,6},{3,7},{4,0},{5,1},{6,2},{7,3},{8,12},{9,13},{10,... | collective-permute-start | bytes 221192 | tf_op jit(solution)/shard_map/ppermute | solution.py:27
  9.0 1.4 %collective-permute-start.9 = (bf16[17,32,128]{2,1,0:T(8,128)(2,1)}, bf16[17,32,128]{2,1,0:T(8,128)(2,1)S(1)}, u32[]{:S(2)}, u32[]{:S(2)}) collective-permute-start(bf16[17,32,128]{2,1,0:T(8,128)(2,1)} %get-tuple-element.27), channel_id=1, source_target_pairs={{0,12},{1,13},{2,14},{3,15},{4,8},{5,9},{6,10},{7,11},{8,4},{9,5},... | collective-permute-start | bytes 417800 | tf_op jit(solution)/shard_map/ppermute | solution.py:27
  10.3 1.5 %collective-permute-start.1 = (bf16[1,24,32,128]{3,2,1,0:T(8,128)(2,1)}, bf16[1,24,32,128]{3,2,1,0:T(8,128)(2,1)S(1)}, u32[]{:S(2)}, u32[]{:S(2)}) collective-permute-start(bf16[1,24,32,128]{3,2,1,0:T(8,128)(2,1)} %bitcast.11), channel_id=1, source_target_pairs={{0,2},{1,3},{2,0},{3,1},{4,6},{5,7},{6,4},{7,5},{8,10},{9,11},{10,... | collective-permute-start | bytes 589832 | tf_op jit(solution)/shard_map/ppermute | solution.py:27
  11.8 3.0 %collective-permute-done.3 = bf16[24,32,128]{2,1,0:T(8,128)(2,1)S(1)} collective-permute-done((bf16[24,32,128]{2,1,0:T(8,128)(2,1)}, bf16[24,32,128]{2,1,0:T(8,128)(2,1)S(1)}, u32[]{:S(2)}, u32[]{:S(2)}) %collective-permute-start.3) | collective-permute-done | bytes 196640 | tf_op jit(solution)/shard_map/ppermute | solution.py:27
  14.8 1.7 %collective-permute-start.5 = (bf16[1,24,32,128]{3,2,1,0:T(8,128)(2,1)S(1)}, bf16[1,24,32,128]{3,2,1,0:T(8,128)(2,1)S(1)}, u32[]{:S(2)}, u32[]{:S(2)}) collective-permute-start(bf16[1,24,32,128]{3,2,1,0:T(8,128)(2,1)S(1)} %bitcast.7), channel_id=1, source_target_pairs={{0,2},{1,3},{2,0},{3,1},{4,6},{5,7},{6,4},{7,5},{8,10},{9,11},{10,... | collective-permute-start | bytes 589832 | tf_op jit(solution)/shard_map/ppermute | solution.py:27
  16.5 0.0 copy-start
  16.5 0.9 %copy-done = bf16[24,32,128]{2,1,0:T(8,128)(2,1)S(1)} copy-done((bf16[24,32,128]{2,1,0:T(8,128)(2,1)S(1)}, bf16[24,32,128]{2,1,0:T(8,128)(2,1)}, u32[]{:S(2)}) %copy-start) | copy-done | bytes 196632
  17.4 0.0 copy-start.1
  17.4 0.9 %copy-done.1 = bf16[9,32,128]{2,1,0:T(8,128)(2,1)S(1)} copy-done((bf16[9,32,128]{2,1,0:T(8,128)(2,1)S(1)}, bf16[9,32,128]{2,1,0:T(8,128)(2,1)}, u32[]{:S(2)}) %copy-start.1) | copy-done | bytes 73752
  18.3 0.0 collective-permute-done.7.refs_9_
  18.3 0.1 collective-permute-start
  18.4 0.0 collective-permute-done.8.refs_10_.refs_0_
  18.4 2.4 %collective-permute-done.9.refs_11_.refs_1_ = bf16[17,32,128]{2,1,0:T(8,128)(2,1)S(1)} collective-permute-done((bf16[17,32,128]{2,1,0:T(8,128)(2,1)}, bf16[17,32,128]{2,1,0:T(8,128)(2,1)S(1)}, u32[]{:S(2)}, u32[]{:S(2)}) %collective-permute-start.9) | collective-permute-done | bytes 139296 | tf_op jit(solution)/shard_map/ppermute | solution.py:27
  20.8 1.6 %collective-permute-start.11 = (bf16[2,8,32,128]{3,2,1,0:T(8,128)(2,1)S(1)}, bf16[2,8,32,128]{3,2,1,0:T(8,128)(2,1)S(1)}, u32[]{:S(2)}, u32[]{:S(2)}) collective-permute-start(bf16[2,8,32,128]{3,2,1,0:T(8,128)(2,1)S(1)} %join.1.refs_0_), channel_id=1, source_target_pairs={{0,2},{1,3},{2,0},{3,1},{4,6},{5,7},{6,4},{7,5},{8,10},{9,11},{10,... | collective-permute-start | bytes 393224 | tf_op jit(solution)/shard_map/ppermute | solution.py:27
  22.4 0.0 collective-permute-start.4
  22.4 0.0 collective-permute-done.1.refs_2_
  22.4 0.5 %collective-permute-start.2 = (bf16[1,24,32,128]{3,2,1,0:T(8,128)(2,1)S(1)}, bf16[1,24,32,128]{3,2,1,0:T(8,128)(2,1)S(1)}, u32[]{:S(2)}, u32[]{:S(2)}) collective-permute-start(bf16[1,24,32,128]{3,2,1,0:T(8,128)(2,1)S(1)} %collective-permute-done.1.refs_2_), channel_id=1, source_target_pairs={{0,1},{1,0},{2,3},{3,2},{4,5},{5,4},{6,7},{7,6},{8,9},{9,8},{10,11... | collective-permute-start | bytes 589832 | tf_op jit(solution)/shard_map/ppermute | solution.py:27
  22.9 0.0 collective-permute-done.5.refs_6_
  22.9 0.1 collective-permute-start.6
  23.0 0.0 collective-permute-done.refs_1_
  23.0 0.4 %collective-permute-start.10 = (bf16[2,8,32,128]{3,2,1,0:T(8,128)(2,1)S(1)}, bf16[2,8,32,128]{3,2,1,0:T(8,128)(2,1)S(1)}, u32[]{:S(2)}, u32[]{:S(2)}) collective-permute-start(bf16[2,8,32,128]{3,2,1,0:T(8,128)(2,1)S(1)} %join.1.refs_0_), channel_id=1, source_target_pairs={{0,1},{1,0},{2,3},{3,2},{4,5},{5,4},{6,7},{7,6},{8,9},{9,8},{10,11... | collective-permute-start | bytes 393224 | tf_op jit(solution)/shard_map/ppermute | solution.py:27
  23.4 2.4 %collective-permute-done.11.refs_2_ = bf16[2,8,32,128]{3,2,1,0:T(8,128)(2,1)S(1)} collective-permute-done((bf16[2,8,32,128]{3,2,1,0:T(8,128)(2,1)S(1)}, bf16[2,8,32,128]{3,2,1,0:T(8,128)(2,1)S(1)}, u32[]{:S(2)}, u32[]{:S(2)}) %collective-permute-start.11) | collective-permute-done | bytes 131104 | tf_op jit(solution)/shard_map/ppermute | solution.py:27
  25.9 0.0 collective-permute-start.12
  25.9 0.0 collective-permute-done.2.refs_3_
  25.9 0.0 collective-permute-done.4.refs_5_
  25.9 0.0 collective-permute-done.6.refs_7_
  25.9 1.4 %state.1 = (bf16[512,512]{1,0:T(8,128)(2,1)S(1)}, f32[512,128]{1,0:T(8,128)S(1)}) custom-call(bf16[1,24,32,128]{3,2,1,0:T(8,128)(2,1)S(1)} %get-tuple-element.22.refs_0_, bf16[1,24,32,128]{3,2,1,0:T(8,128)(2,1)S(1)} %collective-permute-done.refs_1_, bf16[1,24,32,128]{3,2,1,0:T(8,128)(2,1)S(1)} %collective-permute-done.1.refs_2_, ...), custom_call_target="tpu_custom_call" | custom-call | bytes 4096 | tf_op jit(solution)/shard_map/state/pallas_call | solution.py:287
  27.3 0.9 %close_first.1.sums_in = f32[512,128]{1,0:T(8,128)S(1)} custom-call(f32[512,128]{1,0:T(8,128)S(1)} %get-tuple-element.28.named, bf16[512,512]{1,0:T(8,128)(2,1)S(1)} %get-tuple-element.29.state, bf16[1,24,32,128]{3,2,1,0:T(8,128)(2,1)S(1)} %get-tuple-element.22.refs_0_, bf16[1,24,32,128]{3,2,1,0:T(8,128)(2,1)S(1)} %collective-permute-done.refs_1_, ...), custom_call_target="tpu_custom_call" | custom-call | bytes 4096 | tf_op jit(solution)/shard_map/close_first/pallas_call | solution.py:306
  28.2 0.0 collective-permute-done.10.refs_1_
  28.2 0.7 %close_more.1.sums_in = f32[512,128]{1,0:T(8,128)S(1)} custom-call(f32[512,128]{1,0:T(8,128)S(1)} %get-tuple-element.28.named, bf16[512,512]{1,0:T(8,128)(2,1)S(1)} %get-tuple-element.29.state, f32[512,128]{1,0:T(8,128)S(1)} %close_first.1.sums_in, bf16[2,8,32,128]{3,2,1,0:T(8,128)(2,1)S(1)} %join.1.refs_0_, ...), custom_call_target="tpu_custom_call" | custom-call | tf_op jit(solution)/shard_map/close_more/pallas_call | solution.py:319
  28.9 0.0 collective-permute-done.12.relay
  28.9 0.4 %close_last.1 = (f32[8,16,128]{2,1,0:T(8,128)S(1)}, bf16[8,16,128]{2,1,0:T(8,128)(2,1)S(1)}, bf16[8,16,128]{2,1,0:T(8,128)(2,1)S(1)}, bf16[8,16,128]{2,1,0:T(8,128)(2,1)S(1)}) custom-call(f32[512,128]{1,0:T(8,128)S(1)} %get-tuple-element.28.named, bf16[512,512]{1,0:T(8,128)(2,1)S(1)} %get-tuple-element.29.state, f32[512,128]{1,0:T(8,128)S(1)} %close_more.1.sums_in, ...), custom_call_target="tpu_custom_call" | custom-call | tf_op jit(solution)/shard_map/close_last/pallas_call | solution.py:329
  29.3 1.0 %collective-permute-start.13 = (bf16[8,16,128]{2,1,0:T(8,128)(2,1)S(1)}, bf16[8,16,128]{2,1,0:T(8,128)(2,1)S(1)}, u32[]{:S(2)}, u32[]{:S(2)}) collective-permute-start(bf16[8,16,128]{2,1,0:T(8,128)(2,1)S(1)} %get-tuple-element.32), channel_id=1, source_target_pairs={{0,4},{1,5},{2,6},{3,7},{4,0},{5,1},{6,2},{7,3},{8,12},{9,13},{10,... | collective-permute-start | bytes 98312 | tf_op jit(solution)/shard_map/ppermute | solution.py:27
  30.3 2.1 %collective-permute-start.14 = (bf16[8,16,128]{2,1,0:T(8,128)(2,1)S(1)}, bf16[8,16,128]{2,1,0:T(8,128)(2,1)S(1)}, u32[]{:S(2)}, u32[]{:S(2)}) collective-permute-start(bf16[8,16,128]{2,1,0:T(8,128)(2,1)S(1)} %get-tuple-element.33), channel_id=1, source_target_pairs={{0,8},{1,9},{2,10},{3,11},{4,12},{5,13},{6,14},{7,15},{8,0},{9,1},... | collective-permute-start | bytes 98312 | tf_op jit(solution)/shard_map/ppermute | solution.py:27
  32.4 1.3 %collective-permute-start.15 = (bf16[8,16,128]{2,1,0:T(8,128)(2,1)S(1)}, bf16[8,16,128]{2,1,0:T(8,128)(2,1)S(1)}, u32[]{:S(2)}, u32[]{:S(2)}) collective-permute-start(bf16[8,16,128]{2,1,0:T(8,128)(2,1)S(1)} %get-tuple-element.34), channel_id=1, source_target_pairs={{0,12},{1,13},{2,14},{3,15},{4,8},{5,9},{6,10},{7,11},{8,4},{9,5},... | collective-permute-start | bytes 98312 | tf_op jit(solution)/shard_map/ppermute | solution.py:27
  33.8 0.0 collective-permute-done.13
  33.8 2.0 %collective-permute-done.14 = bf16[8,16,128]{2,1,0:T(8,128)(2,1)S(1)} collective-permute-done((bf16[8,16,128]{2,1,0:T(8,128)(2,1)S(1)}, bf16[8,16,128]{2,1,0:T(8,128)(2,1)S(1)}, u32[]{:S(2)}, u32[]{:S(2)}) %collective-permute-start.14) | collective-permute-done | bytes 32800 | tf_op jit(solution)/shard_map/ppermute | solution.py:27
  35.7 2.4 %collective-permute-done.15 = bf16[8,16,128]{2,1,0:T(8,128)(2,1)S(1)} collective-permute-done((bf16[8,16,128]{2,1,0:T(8,128)(2,1)S(1)}, bf16[8,16,128]{2,1,0:T(8,128)(2,1)S(1)}, u32[]{:S(2)}, u32[]{:S(2)}) %collective-permute-start.15) | collective-permute-done | bytes 32800 | tf_op jit(solution)/shard_map/ppermute | solution.py:27
  38.1 0.6 %convert_add_fusion = f32[8,16,128]{2,1,0:T(8,128)} fusion(bf16[8,16,128]{2,1,0:T(8,128)(2,1)S(1)} %collective-permute-done.15, bf16[8,16,128]{2,1,0:T(8,128)(2,1)S(1)} %collective-permute-done.14, f32[8,16,128]{2,1,0:T(8,128)S(1)} %get-tuple-element.31, bf16[8,16,128]{2,1,0:T(8,128)(2,1)S(1)} %collective-permute-done.13), kind=kLoop, calls=%fused_computation | loop fusion | flops 98304 | bytes 229376 | tf_op jit(solution)/shard_map/add | solution.py:346
  (2 shorter events, 0.0 us)
Async XLA Ops:
  2.8 12.0 %collective-permute-start.3 = (bf16[24,32,128]{2,1,0:T(8,128)(2,1)}, bf16[24,32,128]{2,1,0:T(8,128)(2,1)S(1)}, u32[]{:S(2)}, u32[]{:S(2)}) collective-permute-start(bf16[24,32,128]{2,1,0:T(8,128)(2,1)} %get-tuple-element.23), channel_id=1, source_target_pairs={{0,4},{1,5},{2,6},{3,7},{4,0},{5,1},{6,2},{7,3},{8,12},{9,13},{10,... | collective-permute-start | bytes 589832 | tf_op jit(solution)/shard_map/ppermute | solution.py:27
  5.9 12.5 %collective-permute-start.8 = (bf16[17,32,128]{2,1,0:T(8,128)(2,1)}, bf16[17,32,128]{2,1,0:T(8,128)(2,1)S(1)}, u32[]{:S(2)}, u32[]{:S(2)}) collective-permute-start(bf16[17,32,128]{2,1,0:T(8,128)(2,1)} %get-tuple-element.26), channel_id=1, source_target_pairs={{0,8},{1,9},{2,10},{3,11},{4,12},{5,13},{6,14},{7,15},{8,0},{9,1},... | collective-permute-start | bytes 417800 | tf_op jit(solution)/shard_map/ppermute | solution.py:27
  8.5 9.8 %collective-permute-start.7 = (bf16[9,32,128]{2,1,0:T(8,128)(2,1)}, bf16[9,32,128]{2,1,0:T(8,128)(2,1)S(1)}, u32[]{:S(2)}, u32[]{:S(2)}) collective-permute-start(bf16[9,32,128]{2,1,0:T(8,128)(2,1)} %get-tuple-element.25), channel_id=1, source_target_pairs={{0,4},{1,5},{2,6},{3,7},{4,0},{5,1},{6,2},{7,3},{8,12},{9,13},{10,... | collective-permute-start | bytes 221192 | tf_op jit(solution)/shard_map/ppermute | solution.py:27
  9.0 11.9 %collective-permute-start.9 = (bf16[17,32,128]{2,1,0:T(8,128)(2,1)}, bf16[17,32,128]{2,1,0:T(8,128)(2,1)S(1)}, u32[]{:S(2)}, u32[]{:S(2)}) collective-permute-start(bf16[17,32,128]{2,1,0:T(8,128)(2,1)} %get-tuple-element.27), channel_id=1, source_target_pairs={{0,12},{1,13},{2,14},{3,15},{4,8},{5,9},{6,10},{7,11},{8,4},{9,5},... | collective-permute-start | bytes 417800 | tf_op jit(solution)/shard_map/ppermute | solution.py:27
  10.3 12.1 %collective-permute-start.1 = (bf16[1,24,32,128]{3,2,1,0:T(8,128)(2,1)}, bf16[1,24,32,128]{3,2,1,0:T(8,128)(2,1)S(1)}, u32[]{:S(2)}, u32[]{:S(2)}) collective-permute-start(bf16[1,24,32,128]{3,2,1,0:T(8,128)(2,1)} %bitcast.11), channel_id=1, source_target_pairs={{0,2},{1,3},{2,0},{3,1},{4,6},{5,7},{6,4},{7,5},{8,10},{9,11},{10,... | collective-permute-start | bytes 589832 | tf_op jit(solution)/shard_map/ppermute | solution.py:27
  14.8 8.1 %collective-permute-start.5 = (bf16[1,24,32,128]{3,2,1,0:T(8,128)(2,1)S(1)}, bf16[1,24,32,128]{3,2,1,0:T(8,128)(2,1)S(1)}, u32[]{:S(2)}, u32[]{:S(2)}) collective-permute-start(bf16[1,24,32,128]{3,2,1,0:T(8,128)(2,1)S(1)} %bitcast.7), channel_id=1, source_target_pairs={{0,2},{1,3},{2,0},{3,1},{4,6},{5,7},{6,4},{7,5},{8,10},{9,11},{10,... | collective-permute-start | bytes 589832 | tf_op jit(solution)/shard_map/ppermute | solution.py:27
  16.5 0.9 %copy-start = (bf16[24,32,128]{2,1,0:T(8,128)(2,1)S(1)}, bf16[24,32,128]{2,1,0:T(8,128)(2,1)}, u32[]{:S(2)}) copy-start(bf16[24,32,128]{2,1,0:T(8,128)(2,1)} %get-tuple-element.20) | copy-start | bytes 589828
  17.4 0.9 %copy-start.1 = (bf16[9,32,128]{2,1,0:T(8,128)(2,1)S(1)}, bf16[9,32,128]{2,1,0:T(8,128)(2,1)}, u32[]{:S(2)}) copy-start(bf16[9,32,128]{2,1,0:T(8,128)(2,1)} %get-tuple-element.21.refs_1_) | copy-start | bytes 221188
  18.3 4.7 %collective-permute-start = (bf16[1,24,32,128]{3,2,1,0:T(8,128)(2,1)S(1)}, bf16[1,24,32,128]{3,2,1,0:T(8,128)(2,1)S(1)}, u32[]{:S(2)}, u32[]{:S(2)}) collective-permute-start(bf16[1,24,32,128]{3,2,1,0:T(8,128)(2,1)S(1)} %get-tuple-element.22.refs_0_), channel_id=1, source_target_pairs={{0,1},{1,0},{2,3},{3,2},{4,5},{5,4},{6,7},{7,6},{8,9},{9,8},{10,11... | collective-permute-start | bytes 589832 | tf_op jit(solution)/shard_map/ppermute | solution.py:27
  20.8 5.0 %collective-permute-start.11 = (bf16[2,8,32,128]{3,2,1,0:T(8,128)(2,1)S(1)}, bf16[2,8,32,128]{3,2,1,0:T(8,128)(2,1)S(1)}, u32[]{:S(2)}, u32[]{:S(2)}) collective-permute-start(bf16[2,8,32,128]{3,2,1,0:T(8,128)(2,1)S(1)} %join.1.refs_0_), channel_id=1, source_target_pairs={{0,2},{1,3},{2,0},{3,1},{4,6},{5,7},{6,4},{7,5},{8,10},{9,11},{10,... | collective-permute-start | bytes 393224 | tf_op jit(solution)/shard_map/ppermute | solution.py:27
  22.4 3.5 %collective-permute-start.4 = (bf16[1,24,32,128]{3,2,1,0:T(8,128)(2,1)S(1)}, bf16[1,24,32,128]{3,2,1,0:T(8,128)(2,1)S(1)}, u32[]{:S(2)}, u32[]{:S(2)}) collective-permute-start(bf16[1,24,32,128]{3,2,1,0:T(8,128)(2,1)S(1)} %bitcast.8), channel_id=1, source_target_pairs={{0,1},{1,0},{2,3},{3,2},{4,5},{5,4},{6,7},{7,6},{8,9},{9,8},{10,11... | collective-permute-start | bytes 589832 | tf_op jit(solution)/shard_map/ppermute | solution.py:27
  22.4 3.4 %collective-permute-start.2 = (bf16[1,24,32,128]{3,2,1,0:T(8,128)(2,1)S(1)}, bf16[1,24,32,128]{3,2,1,0:T(8,128)(2,1)S(1)}, u32[]{:S(2)}, u32[]{:S(2)}) collective-permute-start(bf16[1,24,32,128]{3,2,1,0:T(8,128)(2,1)S(1)} %collective-permute-done.1.refs_2_), channel_id=1, source_target_pairs={{0,1},{1,0},{2,3},{3,2},{4,5},{5,4},{6,7},{7,6},{8,9},{9,8},{10,11... | collective-permute-start | bytes 589832 | tf_op jit(solution)/shard_map/ppermute | solution.py:27
  22.9 2.9 %collective-permute-start.6 = (bf16[1,24,32,128]{3,2,1,0:T(8,128)(2,1)S(1)}, bf16[1,24,32,128]{3,2,1,0:T(8,128)(2,1)S(1)}, u32[]{:S(2)}, u32[]{:S(2)}) collective-permute-start(bf16[1,24,32,128]{3,2,1,0:T(8,128)(2,1)S(1)} %collective-permute-done.5.refs_6_), channel_id=1, source_target_pairs={{0,1},{1,0},{2,3},{3,2},{4,5},{5,4},{6,7},{7,6},{8,9},{9,8},{10,11... | collective-permute-start | bytes 589832 | tf_op jit(solution)/shard_map/ppermute | solution.py:27
  23.0 5.2 %collective-permute-start.10 = (bf16[2,8,32,128]{3,2,1,0:T(8,128)(2,1)S(1)}, bf16[2,8,32,128]{3,2,1,0:T(8,128)(2,1)S(1)}, u32[]{:S(2)}, u32[]{:S(2)}) collective-permute-start(bf16[2,8,32,128]{3,2,1,0:T(8,128)(2,1)S(1)} %join.1.refs_0_), channel_id=1, source_target_pairs={{0,1},{1,0},{2,3},{3,2},{4,5},{5,4},{6,7},{7,6},{8,9},{9,8},{10,11... | collective-permute-start | bytes 393224 | tf_op jit(solution)/shard_map/ppermute | solution.py:27
  25.9 3.0 %collective-permute-start.12 = (bf16[2,8,32,128]{3,2,1,0:T(8,128)(2,1)S(1)}, bf16[2,8,32,128]{3,2,1,0:T(8,128)(2,1)S(1)}, u32[]{:S(2)}, u32[]{:S(2)}) collective-permute-start(bf16[2,8,32,128]{3,2,1,0:T(8,128)(2,1)S(1)} %collective-permute-done.11.refs_2_), channel_id=1, source_target_pairs={{0,1},{1,0},{2,3},{3,2},{4,5},{5,4},{6,7},{7,6},{8,9},{9,8},{10,11... | collective-permute-start | bytes 393224 | tf_op jit(solution)/shard_map/ppermute | solution.py:27
  29.3 4.5 %collective-permute-start.13 = (bf16[8,16,128]{2,1,0:T(8,128)(2,1)S(1)}, bf16[8,16,128]{2,1,0:T(8,128)(2,1)S(1)}, u32[]{:S(2)}, u32[]{:S(2)}) collective-permute-start(bf16[8,16,128]{2,1,0:T(8,128)(2,1)S(1)} %get-tuple-element.32), channel_id=1, source_target_pairs={{0,4},{1,5},{2,6},{3,7},{4,0},{5,1},{6,2},{7,3},{8,12},{9,13},{10,... | collective-permute-start | bytes 98312 | tf_op jit(solution)/shard_map/ppermute | solution.py:27
  30.3 5.4 %collective-permute-start.14 = (bf16[8,16,128]{2,1,0:T(8,128)(2,1)S(1)}, bf16[8,16,128]{2,1,0:T(8,128)(2,1)S(1)}, u32[]{:S(2)}, u32[]{:S(2)}) collective-permute-start(bf16[8,16,128]{2,1,0:T(8,128)(2,1)S(1)} %get-tuple-element.33), channel_id=1, source_target_pairs={{0,8},{1,9},{2,10},{3,11},{4,12},{5,13},{6,14},{7,15},{8,0},{9,1},... | collective-permute-start | bytes 98312 | tf_op jit(solution)/shard_map/ppermute | solution.py:27
  32.4 5.7 %collective-permute-start.15 = (bf16[8,16,128]{2,1,0:T(8,128)(2,1)S(1)}, bf16[8,16,128]{2,1,0:T(8,128)(2,1)S(1)}, u32[]{:S(2)}, u32[]{:S(2)}) collective-permute-start(bf16[8,16,128]{2,1,0:T(8,128)(2,1)S(1)} %get-tuple-element.34), channel_id=1, source_target_pairs={{0,12},{1,13},{2,14},{3,15},{4,8},{5,9},{6,10},{7,11},{8,4},{9,5},... | collective-permute-start | bytes 98312 | tf_op jit(solution)/shard_map/ppermute | solution.py:27

commit v6 on v5

--- a/solution.py
+++ b/solution.py
@@ -143,9 +143,10 @@
     )(*packs)
 
 
-def state_kernel(planes, blocks, pieces, rows_piece, held, *refs):
+def front_kernel(planes, slots, order, blocks, pieces, rows_piece, held, *refs):
     relays, packs = refs[:2 * PLANE], refs[2 * PLANE:2 * PLANE + planes]
-    state, named, forms, high, low = refs[2 * PLANE + planes:]
+    closing = refs[2 * PLANE + planes:-7]
+    state, named, sums, forms, high, low, wide = refs[-7:]
     me = lax.axis_index("bits")
     depth = packs[0].shape[1]
     span, twice_part = forms.shape[1:]
@@ -160,11 +161,11 @@
             here = slice((k * pieces + n) * rows_piece, (k * pieces + n + 1) * rows_piece)
             named[here, :] = jnp.broadcast_to(numbers[n:n + 1], (rows_piece, LANES))
         locals_.append(packs[k].at[first + 1:first + tail])
-    wide = (LANES, blocks * rows)
-    spread = lax.broadcasted_iota(jnp.int32, wide, 0) - planes * PLANE == lax.broadcasted_iota(jnp.int32, wide, 1) // rows_piece
+    shape = (LANES, blocks * rows)
+    spread = lax.broadcasted_iota(jnp.int32, shape, 0) - slots == lax.broadcasted_iota(jnp.int32, shape, 1) // rows_piece
     spread = spread.astype(jnp.float32).astype(jnp.bfloat16)
-    wide = (planes * pieces * rows_piece, blocks * rows)
-    same_row = lax.broadcasted_iota(jnp.int32, wide, 0) % rows_piece == lax.broadcasted_iota(jnp.int32, wide, 1) % rows_piece
+    shape = (planes * pieces * rows_piece, blocks * rows)
+    same_row = lax.broadcasted_iota(jnp.int32, shape, 0) % rows_piece == lax.broadcasted_iota(jnp.int32, shape, 1) % rows_piece
     picks = jnp.dot(named[...].astype(jnp.bfloat16), spread, preferred_element_type=jnp.float32)
     picks = jnp.where(same_row, picks, 0.0).astype(jnp.bfloat16)
     for j in range(2 * PLANE):
@@ -197,6 +198,7 @@
         total = jnp.dot(pick, high[k], preferred_element_type=jnp.float32)
         total += jnp.dot(pick, low[k], preferred_element_type=jnp.float32)
         state[k * size:(k + 1) * size, :] = total.astype(jnp.bfloat16)
+    close(order, named, state, relays + closing, sums, wide)
 
 
 def close(order, named, state, relays, sums, wide):
@@ -220,29 +222,19 @@
             sums[...] = add if slot == 0 else sums[...] + add
 
 
-def close_first_kernel(named, state, *refs):
-    close(range(2 * PLANE), named, state, refs[:-2], *refs[-2:])
-
-
-def close_more_kernel(order, named, state, sums_in, *refs):
-    relays, sums, wide = refs[:-2], refs[-2], refs[-1]
-    sums[...] = sums_in[...]
-    close(order, named, state, relays, sums, wide)
-
-
-def close_last_kernel(planes, order, named, state, sums_in, relay, *refs):
-    outs, sums, wide = refs[:planes], refs[planes], refs[planes + 1]
+def last_kernel(order, named, state, sums_in, relay, *refs):
+    *outs, sums, wide = refs
     sums[...] = sums_in[...]
     close(order, named, state, [relay], sums, wide)
-    for out, start in zip(outs, range(0, sums.shape[0], sums.shape[0] // planes)):
-        out[...] = sums[start:start + sums.shape[0] // planes, :].reshape(out.shape).astype(out.dtype)
+    size = sums.shape[0] // len(outs)
+    for k, out in enumerate(outs):
+        out[...] = sums[k * size:(k + 1) * size, :].reshape(out.shape).astype(out.dtype)
 
 
 def in_planes(prefix, first_suffix, pair_prefix, pair_suffix, merge_count, suffix, routes, cap):
     owners = lax.axis_size("bits")
     planes = owners // PLANE
-    pieces, merges = pair_prefix.shape
-    listed = routes.shape[1]
+    pieces = pair_prefix.shape[0]
     held, rows_piece, twice_width = prefix.shape
     blocks, _, depth, width = first_suffix.shape
     part, span = width // 2, width // (planes // 2)
@@ -283,67 +275,55 @@
     beside = [swap(r, 1) for r in relays]
     corner = [swap(y, 1) for y in across]
     across.append(swap(relays[2], 2))
-    rows = planes * pieces * rows_piece
-    state, named = pl.pallas_call(
-        functools.partial(state_kernel, planes, blocks, pieces, rows_piece, held),
-        out_shape=[
-            jax.ShapeDtypeStruct((rows, 2 * part), jnp.bfloat16),
-            jax.ShapeDtypeStruct((rows, LANES), jnp.float32),
-        ],
-        in_specs=[vmem] * (2 * PLANE + planes),
-        out_specs=[vmem] * 2,
-        scratch_shapes=[
-            pltpu.VMEM((blocks, span, 2 * part), jnp.bfloat16),
-            pltpu.VMEM((planes, blocks * held * rows_piece, 2 * part), jnp.bfloat16),
-            pltpu.VMEM((planes, blocks * held * rows_piece, 2 * part), jnp.bfloat16),
-        ],
-        compiler_params=params,
-        cost_estimate=pl.CostEstimate(flops=0, bytes_accessed=2 ** 12, transcendentals=0),
-        name="state",
-    )(*[group[n] for n in range(2) for group in (relays, beside, across, corner)], *packs)
+    corner.append(swap(across[2], 1))
     early = 2 * PLANE
+    far_slots = range(early, owners, PLANE)
+    order = list(range(early)) + [k + n for n in (0, 1, 2) for k in far_slots]
+    last = [k + 3 for k in far_slots]
+    relays = [group[n] for n in range(2) for group in (relays, beside, across, corner)] + [relays[2], beside[2], across[2]]
     tiny = pl.CostEstimate(flops=0, bytes_accessed=2 ** 12, transcendentals=0)
-    sums = pl.pallas_call(
-        close_first_kernel,
-        out_shape=jax.ShapeDtypeStruct((rows, LANES), jnp.float32),
-        in_specs=[vmem] * (2 + early),
-        out_specs=vmem,
-        scratch_shapes=[pltpu.VMEM((2 * part, early * LANES), jnp.bfloat16)],
-        compiler_params=params,
-        cost_estimate=tiny,
-        name="close_first",
-    )(named, state, *[group[n] for n in range(2) for group in (relays, beside, across, corner)])
-    corner.append(swap(across[2], 1))
-    far_slots = range(early, owners, PLANE)
-    order = [k + n for n in (0, 1, 2) for k in far_slots]
-    sums = pl.pallas_call(
-        functools.partial(close_more_kernel, order),
-        out_shape=jax.ShapeDtypeStruct((rows, LANES), jnp.float32),
-        in_specs=[vmem] * (3 + 3),
-        out_specs=vmem,
-        scratch_shapes=[pltpu.VMEM((2 * part, len(order) * LANES), jnp.bfloat16)],
-        compiler_params=params,
-        name="close_more",
-    )(named, state, sums, relays[2], beside[2], across[2])
-    order = [k + 3 for k in far_slots]
-    sums = pl.pallas_call(
-        functools.partial(close_last_kernel, planes, order),
-        out_shape=[
-            jax.ShapeDtypeStruct((pieces, rows_piece, LANES), jnp.float32 if k == 0 else jnp.bfloat16)
-            for k in range(planes)
-        ],
-        in_specs=[vmem] * 4,
-        out_specs=[vmem] * planes,
-        scratch_shapes=[
-            pltpu.VMEM((rows, LANES), jnp.float32),
-            pltpu.VMEM((2 * part, len(order) * LANES), jnp.bfloat16),
-        ],
-        compiler_params=params,
-        name="close_last",
-    )(named, state, sums, corner[2])
-    total = sums[0]
+
+    def sums_of(chosen, dtype):
+        count = len(chosen)
+        rows = count * pieces * rows_piece
+        operands = relays[:early] + [packs[k] for k in chosen] + relays[early:]
+        state, named, sums = pl.pallas_call(
+            functools.partial(front_kernel, count, owners, order, blocks, pieces, rows_piece, held),
+            out_shape=[
+                jax.ShapeDtypeStruct((rows, 2 * part), jnp.bfloat16),
+                jax.ShapeDtypeStruct((rows, LANES), jnp.float32),
+                jax.ShapeDtypeStruct((rows, LANES), jnp.float32),
+            ],
+            in_specs=[vmem] * len(operands),
+            out_specs=[vmem] * 3,
+            scratch_shapes=[
+                pltpu.VMEM((blocks, span, 2 * part), jnp.bfloat16),
+                pltpu.VMEM((count, blocks * held * rows_piece, 2 * part), jnp.bfloat16),
+                pltpu.VMEM((count, blocks * held * rows_piece, 2 * part), jnp.bfloat16),
+                pltpu.VMEM((2 * part, len(order) * LANES), jnp.bfloat16),
+            ],
+            compiler_params=params,
+            cost_estimate=tiny,
+            name="front",
+        )(*operands)
+        return pl.pallas_call(
+            functools.partial(last_kernel, last),
+            out_shape=[jax.ShapeDtypeStruct((pieces, rows_piece, LANES), dtype)] * count,
+            in_specs=[vmem] * 4,
+            out_specs=[vmem] * count,
+            scratch_shapes=[
+                pltpu.VMEM((rows, LANES), jnp.float32),
+                pltpu.VMEM((2 * part, len(last) * LANES), jnp.bfloat16),
+            ],
+            compiler_params=params,
+            cost_estimate=tiny,
+            name="last",
+        )(named, state, sums, corner[2])
+
+    sent = sums_of(range(1, planes), jnp.bfloat16)
+    total = sums_of([0], jnp.float32)[0]
     for k in range(1, planes):
-        total = total + swap(sums[k], k * PLANE).astype(jnp.float32)
+        total = total + swap(sent[k - 1], k * PLANE).astype(jnp.float32)
     return total
 
 

time: 39 us -> 37 us (0.949)
  waiting for transfers between devices: 12.2 us -> 9.56 us
  Pallas kernels: 6.21 us -> 6.84 us
    ppermute x16, waiting for transfers between devices: 12.2 us -> 9.56 us  [swap(): return lax.ppermute(x, 'bits', [(i, i ^ bit) for i in range(owners)])]
    pallas_call x4, Pallas kernels: 3.37 us -> 3.99 us  [the longest x2 3.33 us: sums_of(): pl.pallas_call(functools.partial(front_kernel, count, owners, order, bloc...]
  transfers between devices with their start and end apart: 16 -> 16, of which waited for: 5 -> 4; matrix products, arithmetic and copies ran while one was open for 0% -> 0% of each run, Pallas kernels for 8% -> 10%
where the time goes in v6:
time: 37 us; the launch traced here: 36.8 us
  starting transfers between devices  17.8 us (48%)
  waiting for transfers between devices  9.56 us (26%)
  Pallas kernels  6.84 us (18%)
  local copies, waits for them, and re-layouts  1.81 us (5%)
  other arithmetic  0.65 us (2%)
    ppermute x16, starting transfers between devices, swap(): return lax.ppermute(x, 'bits', [(i, i ^ bit) for i in range(owners)])  17.8 us
    ppermute x16, waiting for transfers between devices, swap(): return lax.ppermute(x, 'bits', [(i, i ^ bit) for i in range(owners)])  9.56 us
    pallas_call x2, Pallas kernels, sums_of(): pl.pallas_call(functools.partial(front_kernel, count, owners, order, bloc...  3.33 us
    pallas_call x1, Pallas kernels, in_planes(): pl.pallas_call(functools.partial(pack_kernel, planes), out_shape=[jax.Sha...  2.82 us
    unnamed x4, local copies, waits for them, and re-layouts  1.81 us
  transfers between devices with their start and end apart: 16, of which 4 were waited for; matrix products, arithmetic and copies ran while one was open for 0% of the time, Pallas kernels for 10%

profile of v6, /device:TPU:0, one launch (start us, length us, event | category | flops | bytes accessed | tf_op | source)
XLA Modules:
  0.0 36.8 jit_solution(14412637896503157852)
XLA Ops:
  0.0 2.8 %pack.1 = (bf16[24,32,128]{2,1,0:T(8,128)(2,1)}, bf16[24,32,128]{2,1,0:T(8,128)(2,1)}, bf16[17,32,128]{2,1,0:T(8,128)(2,1)}, bf16[17,32,128]{2,1,0:T(8,128)(2,1)...) custom-call(bf16[2,512,512]{2,1,0:T(8,128)(2,1)} %bitcast.13, bf16[2,64,512]{2,1,0:T(8,128)(2,1)} %bitcast.14, ...), custom_call_target="tpu_custom_call" | custom-call | flops 1048576 | bytes 4096 | tf_op jit(solution)/shard_map/pack/pallas_call | solution.py:256
  2.8 3.1 %collective-permute-start.3 = (bf16[24,32,128]{2,1,0:T(8,128)(2,1)}, bf16[24,32,128]{2,1,0:T(8,128)(2,1)S(1)}, u32[]{:S(2)}, u32[]{:S(2)}) collective-permute-start(bf16[24,32,128]{2,1,0:T(8,128)(2,1)} %get-tuple-element.26), channel_id=1, source_target_pairs={{0,4},{1,5},{2,6},{3,7},{4,0},{5,1},{6,2},{7,3},{8,12},{9,13},{10,... | collective-permute-start | bytes 589832 | tf_op jit(solution)/shard_map/ppermute | solution.py:27
  6.0 0.1 collective-permute-start.8
  6.0 2.9 %collective-permute-start.7 = (bf16[17,32,128]{2,1,0:T(8,128)(2,1)}, bf16[17,32,128]{2,1,0:T(8,128)(2,1)S(1)}, u32[]{:S(2)}, u32[]{:S(2)}) collective-permute-start(bf16[17,32,128]{2,1,0:T(8,128)(2,1)} %get-tuple-element.28), channel_id=1, source_target_pairs={{0,8},{1,9},{2,10},{3,11},{4,12},{5,13},{6,14},{7,15},{8,0},{9,1},... | collective-permute-start | bytes 417800 | tf_op jit(solution)/shard_map/ppermute | solution.py:27
  9.0 1.4 %collective-permute-start.9 = (bf16[17,32,128]{2,1,0:T(8,128)(2,1)}, bf16[17,32,128]{2,1,0:T(8,128)(2,1)S(1)}, u32[]{:S(2)}, u32[]{:S(2)}) collective-permute-start(bf16[17,32,128]{2,1,0:T(8,128)(2,1)} %get-tuple-element.31), channel_id=1, source_target_pairs={{0,12},{1,13},{2,14},{3,15},{4,8},{5,9},{6,10},{7,11},{8,4},{9,5},... | collective-permute-start | bytes 417800 | tf_op jit(solution)/shard_map/ppermute | solution.py:27
  10.3 1.5 %collective-permute-start.1 = (bf16[1,24,32,128]{3,2,1,0:T(8,128)(2,1)}, bf16[1,24,32,128]{3,2,1,0:T(8,128)(2,1)S(1)}, u32[]{:S(2)}, u32[]{:S(2)}) collective-permute-start(bf16[1,24,32,128]{3,2,1,0:T(8,128)(2,1)} %bitcast.11), channel_id=1, source_target_pairs={{0,2},{1,3},{2,0},{3,1},{4,6},{5,7},{6,4},{7,5},{8,10},{9,11},{10,... | collective-permute-start | bytes 589832 | tf_op jit(solution)/shard_map/ppermute | solution.py:27
  11.9 3.0 %collective-permute-done.3 = bf16[24,32,128]{2,1,0:T(8,128)(2,1)S(1)} collective-permute-done((bf16[24,32,128]{2,1,0:T(8,128)(2,1)}, bf16[24,32,128]{2,1,0:T(8,128)(2,1)S(1)}, u32[]{:S(2)}, u32[]{:S(2)}) %collective-permute-start.3) | collective-permute-done | bytes 196640 | tf_op jit(solution)/shard_map/ppermute | solution.py:27
  14.8 1.7 %collective-permute-start.5 = (bf16[1,24,32,128]{3,2,1,0:T(8,128)(2,1)S(1)}, bf16[1,24,32,128]{3,2,1,0:T(8,128)(2,1)S(1)}, u32[]{:S(2)}, u32[]{:S(2)}) collective-permute-start(bf16[1,24,32,128]{3,2,1,0:T(8,128)(2,1)S(1)} %bitcast.7), channel_id=1, source_target_pairs={{0,2},{1,3},{2,0},{3,1},{4,6},{5,7},{6,4},{7,5},{8,10},{9,11},{10,... | collective-permute-start | bytes 589832 | tf_op jit(solution)/shard_map/ppermute | solution.py:27
  16.5 0.0 copy-start
  16.5 0.9 %copy-done = bf16[24,32,128]{2,1,0:T(8,128)(2,1)S(1)} copy-done((bf16[24,32,128]{2,1,0:T(8,128)(2,1)S(1)}, bf16[24,32,128]{2,1,0:T(8,128)(2,1)}, u32[]{:S(2)}) %copy-start) | copy-done | bytes 196632
  17.4 0.0 copy-start.1
  17.4 0.9 %copy-done.1 = bf16[9,32,128]{2,1,0:T(8,128)(2,1)S(1)} copy-done((bf16[9,32,128]{2,1,0:T(8,128)(2,1)S(1)}, bf16[9,32,128]{2,1,0:T(8,128)(2,1)}, u32[]{:S(2)}) %copy-start.1) | copy-done | bytes 73752
  18.3 0.0 collective-permute-done.8.refs_8_
  18.3 0.1 collective-permute-start
  18.4 0.0 collective-permute-done.7.refs_0_.refs_9_
  18.4 2.4 %collective-permute-done.9.refs_1_.refs_10_ = bf16[17,32,128]{2,1,0:T(8,128)(2,1)S(1)} collective-permute-done((bf16[17,32,128]{2,1,0:T(8,128)(2,1)}, bf16[17,32,128]{2,1,0:T(8,128)(2,1)S(1)}, u32[]{:S(2)}, u32[]{:S(2)}) %collective-permute-start.9) | collective-permute-done | bytes 139296 | tf_op jit(solution)/shard_map/ppermute | solution.py:27
  20.9 1.6 %collective-permute-start.11 = (bf16[2,8,32,128]{3,2,1,0:T(8,128)(2,1)S(1)}, bf16[2,8,32,128]{3,2,1,0:T(8,128)(2,1)S(1)}, u32[]{:S(2)}, u32[]{:S(2)}) collective-permute-start(bf16[2,8,32,128]{3,2,1,0:T(8,128)(2,1)S(1)} %join.1.refs_9_.refs_11_), channel_id=1, source_target_pairs={{0,2},{1,3},{2,0},{3,1},{4,6},{5,7},{6,4},{7,5},{8,10},{9,11},{10,... | collective-permute-start | bytes 393224 | tf_op jit(solution)/shard_map/ppermute | solution.py:27
  22.5 0.0 collective-permute-start.4
  22.5 0.0 collective-permute-done.1.refs_2_
  22.5 0.5 %collective-permute-start.2 = (bf16[1,24,32,128]{3,2,1,0:T(8,128)(2,1)S(1)}, bf16[1,24,32,128]{3,2,1,0:T(8,128)(2,1)S(1)}, u32[]{:S(2)}, u32[]{:S(2)}) collective-permute-start(bf16[1,24,32,128]{3,2,1,0:T(8,128)(2,1)S(1)} %collective-permute-done.1.refs_2_), channel_id=1, source_target_pairs={{0,1},{1,0},{2,3},{3,2},{4,5},{5,4},{6,7},{7,6},{8,9},{9,8},{10,11... | collective-permute-start | bytes 589832 | tf_op jit(solution)/shard_map/ppermute | solution.py:27
  23.0 0.0 collective-permute-done.5.refs_6_
  23.0 0.1 collective-permute-start.6
  23.1 0.0 collective-permute-done.refs_1_
  23.1 0.4 %collective-permute-start.10 = (bf16[2,8,32,128]{3,2,1,0:T(8,128)(2,1)S(1)}, bf16[2,8,32,128]{3,2,1,0:T(8,128)(2,1)S(1)}, u32[]{:S(2)}, u32[]{:S(2)}) collective-permute-start(bf16[2,8,32,128]{3,2,1,0:T(8,128)(2,1)S(1)} %join.1.refs_9_.refs_11_), channel_id=1, source_target_pairs={{0,1},{1,0},{2,3},{3,2},{4,5},{5,4},{6,7},{7,6},{8,9},{9,8},{10,11... | collective-permute-start | bytes 393224 | tf_op jit(solution)/shard_map/ppermute | solution.py:27
  23.5 2.4 %collective-permute-done.11.refs_11_.refs_13_ = bf16[2,8,32,128]{3,2,1,0:T(8,128)(2,1)S(1)} collective-permute-done((bf16[2,8,32,128]{3,2,1,0:T(8,128)(2,1)S(1)}, bf16[2,8,32,128]{3,2,1,0:T(8,128)(2,1)S(1)}, u32[]{:S(2)}, u32[]{:S(2)}) %collective-permute-start.11) | collective-permute-done | bytes 131104 | tf_op jit(solution)/shard_map/ppermute | solution.py:27
  25.9 0.0 collective-permute-start.12
  25.9 0.0 collective-permute-done.10.refs_10_.refs_12_
  25.9 0.0 collective-permute-done.2.refs_3_
  25.9 0.0 collective-permute-done.4.refs_5_
  25.9 0.0 collective-permute-done.6.refs_7_
  26.0 2.1 %front.3 = (bf16[384,512]{1,0:T(8,128)(2,1)S(1)}, f32[384,128]{1,0:T(8,128)S(1)}, f32[384,128]{1,0:T(8,128)S(1)}) custom-call(bf16[1,24,32,128]{3,2,1,0:T(8,128)(2,1)S(1)} %get-tuple-element.25.refs_0_, bf16[1,24,32,128]{3,2,1,0:T(8,128)(2,1)S(1)} %collective-permute-done.refs_1_, bf16[1,24,32,128]{3,2,1,0:T(8,128)(2,1)S(1)} %collective-permute-done.1.refs_2_, ...), custom_call_target="tpu_custom_call" | custom-call | bytes 4096 | tf_op jit(solution)/shard_map/front/pallas_call | solution.py:290
  28.1 0.0 collective-permute-done.12.relay
  28.1 0.4 last.3
  28.5 2.7 %collective-permute-start.15 = (bf16[8,16,128]{2,1,0:T(8,128)(2,1)S(1)}, bf16[8,16,128]{2,1,0:T(8,128)(2,1)S(1)}, u32[]{:S(2)}, u32[]{:S(2)}) collective-permute-start(bf16[8,16,128]{2,1,0:T(8,128)(2,1)S(1)} %get-tuple-element.40), channel_id=1, source_target_pairs={{0,12},{1,13},{2,14},{3,15},{4,8},{5,9},{6,10},{7,11},{8,4},{9,5},... | collective-permute-start | bytes 98312 | tf_op jit(solution)/shard_map/ppermute | solution.py:27
  31.1 0.7 %collective-permute-start.14 = (bf16[8,16,128]{2,1,0:T(8,128)(2,1)S(1)}, bf16[8,16,128]{2,1,0:T(8,128)(2,1)S(1)}, u32[]{:S(2)}, u32[]{:S(2)}) collective-permute-start(bf16[8,16,128]{2,1,0:T(8,128)(2,1)S(1)} %get-tuple-element.39), channel_id=1, source_target_pairs={{0,8},{1,9},{2,10},{3,11},{4,12},{5,13},{6,14},{7,15},{8,0},{9,1},... | collective-permute-start | bytes 98312 | tf_op jit(solution)/shard_map/ppermute | solution.py:27
  31.8 1.1 %collective-permute-start.13 = (bf16[8,16,128]{2,1,0:T(8,128)(2,1)S(1)}, bf16[8,16,128]{2,1,0:T(8,128)(2,1)S(1)}, u32[]{:S(2)}, u32[]{:S(2)}) collective-permute-start(bf16[8,16,128]{2,1,0:T(8,128)(2,1)S(1)} %get-tuple-element.38), channel_id=1, source_target_pairs={{0,4},{1,5},{2,6},{3,7},{4,0},{5,1},{6,2},{7,3},{8,12},{9,13},{10,... | collective-permute-start | bytes 98312 | tf_op jit(solution)/shard_map/ppermute | solution.py:27
  32.9 1.2 %front.2 = (bf16[128,512]{1,0:T(8,128)(2,1)S(1)}, f32[128,128]{1,0:T(8,128)S(1)}, f32[128,128]{1,0:T(8,128)S(1)}) custom-call(bf16[1,24,32,128]{3,2,1,0:T(8,128)(2,1)S(1)} %get-tuple-element.25.refs_0_, bf16[1,24,32,128]{3,2,1,0:T(8,128)(2,1)S(1)} %collective-permute-done.refs_1_, bf16[1,24,32,128]{3,2,1,0:T(8,128)(2,1)S(1)} %collective-permute-done.1.refs_2_, ...), custom_call_target="tpu_custom_call" | custom-call | bytes 4096 | tf_op jit(solution)/shard_map/front/pallas_call | solution.py:290
  34.1 0.3 last.2
  34.4 0.0 collective-permute-done.15
  34.4 1.7 %collective-permute-done.14 = bf16[8,16,128]{2,1,0:T(8,128)(2,1)S(1)} collective-permute-done((bf16[8,16,128]{2,1,0:T(8,128)(2,1)S(1)}, bf16[8,16,128]{2,1,0:T(8,128)(2,1)S(1)}, u32[]{:S(2)}, u32[]{:S(2)}) %collective-permute-start.14) | collective-permute-done | bytes 32800 | tf_op jit(solution)/shard_map/ppermute | solution.py:27
  36.1 0.0 collective-permute-done.13
  36.1 0.6 %convert_add_fusion = f32[8,16,128]{2,1,0:T(8,128)} fusion(bf16[8,16,128]{2,1,0:T(8,128)(2,1)S(1)} %collective-permute-done.15, bf16[8,16,128]{2,1,0:T(8,128)(2,1)S(1)} %collective-permute-done.14, f32[8,16,128]{2,1,0:T(8,128)S(1)} %last.2, bf16[8,16,128]{2,1,0:T(8,128)(2,1)S(1)} %collective-permute-done.13), kind=kLoop, calls=%fused_computation | loop fusion | flops 98304 | bytes 229376 | tf_op jit(solution)/shard_map/add | solution.py:326
  (2 shorter events, 0.0 us)
Async XLA Ops:
  2.8 12.0 %collective-permute-start.3 = (bf16[24,32,128]{2,1,0:T(8,128)(2,1)}, bf16[24,32,128]{2,1,0:T(8,128)(2,1)S(1)}, u32[]{:S(2)}, u32[]{:S(2)}) collective-permute-start(bf16[24,32,128]{2,1,0:T(8,128)(2,1)} %get-tuple-element.26), channel_id=1, source_target_pairs={{0,4},{1,5},{2,6},{3,7},{4,0},{5,1},{6,2},{7,3},{8,12},{9,13},{10,... | collective-permute-start | bytes 589832 | tf_op jit(solution)/shard_map/ppermute | solution.py:27
  6.0 12.4 %collective-permute-start.8 = (bf16[9,32,128]{2,1,0:T(8,128)(2,1)}, bf16[9,32,128]{2,1,0:T(8,128)(2,1)S(1)}, u32[]{:S(2)}, u32[]{:S(2)}) collective-permute-start(bf16[9,32,128]{2,1,0:T(8,128)(2,1)} %get-tuple-element.29), channel_id=1, source_target_pairs={{0,4},{1,5},{2,6},{3,7},{4,0},{5,1},{6,2},{7,3},{8,12},{9,13},{10,... | collective-permute-start | bytes 221192 | tf_op jit(solution)/shard_map/ppermute | solution.py:27
  6.0 12.4 %collective-permute-start.7 = (bf16[17,32,128]{2,1,0:T(8,128)(2,1)}, bf16[17,32,128]{2,1,0:T(8,128)(2,1)S(1)}, u32[]{:S(2)}, u32[]{:S(2)}) collective-permute-start(bf16[17,32,128]{2,1,0:T(8,128)(2,1)} %get-tuple-element.28), channel_id=1, source_target_pairs={{0,8},{1,9},{2,10},{3,11},{4,12},{5,13},{6,14},{7,15},{8,0},{9,1},... | collective-permute-start | bytes 417800 | tf_op jit(solution)/shard_map/ppermute | solution.py:27
  9.0 11.9 %collective-permute-start.9 = (bf16[17,32,128]{2,1,0:T(8,128)(2,1)}, bf16[17,32,128]{2,1,0:T(8,128)(2,1)S(1)}, u32[]{:S(2)}, u32[]{:S(2)}) collective-permute-start(bf16[17,32,128]{2,1,0:T(8,128)(2,1)} %get-tuple-element.31), channel_id=1, source_target_pairs={{0,12},{1,13},{2,14},{3,15},{4,8},{5,9},{6,10},{7,11},{8,4},{9,5},... | collective-permute-start | bytes 417800 | tf_op jit(solution)/shard_map/ppermute | solution.py:27
  10.3 12.1 %collective-permute-start.1 = (bf16[1,24,32,128]{3,2,1,0:T(8,128)(2,1)}, bf16[1,24,32,128]{3,2,1,0:T(8,128)(2,1)S(1)}, u32[]{:S(2)}, u32[]{:S(2)}) collective-permute-start(bf16[1,24,32,128]{3,2,1,0:T(8,128)(2,1)} %bitcast.11), channel_id=1, source_target_pairs={{0,2},{1,3},{2,0},{3,1},{4,6},{5,7},{6,4},{7,5},{8,10},{9,11},{10,... | collective-permute-start | bytes 589832 | tf_op jit(solution)/shard_map/ppermute | solution.py:27
  14.8 8.2 %collective-permute-start.5 = (bf16[1,24,32,128]{3,2,1,0:T(8,128)(2,1)S(1)}, bf16[1,24,32,128]{3,2,1,0:T(8,128)(2,1)S(1)}, u32[]{:S(2)}, u32[]{:S(2)}) collective-permute-start(bf16[1,24,32,128]{3,2,1,0:T(8,128)(2,1)S(1)} %bitcast.7), channel_id=1, source_target_pairs={{0,2},{1,3},{2,0},{3,1},{4,6},{5,7},{6,4},{7,5},{8,10},{9,11},{10,... | collective-permute-start | bytes 589832 | tf_op jit(solution)/shard_map/ppermute | solution.py:27
  16.5 0.9 %copy-start = (bf16[24,32,128]{2,1,0:T(8,128)(2,1)S(1)}, bf16[24,32,128]{2,1,0:T(8,128)(2,1)}, u32[]{:S(2)}) copy-start(bf16[24,32,128]{2,1,0:T(8,128)(2,1)} %get-tuple-element.23) | copy-start | bytes 589828
  17.4 0.9 %copy-start.1 = (bf16[9,32,128]{2,1,0:T(8,128)(2,1)S(1)}, bf16[9,32,128]{2,1,0:T(8,128)(2,1)}, u32[]{:S(2)}) copy-start(bf16[9,32,128]{2,1,0:T(8,128)(2,1)} %get-tuple-element.24.refs_1_) | copy-start | bytes 221188
  18.3 4.7 %collective-permute-start = (bf16[1,24,32,128]{3,2,1,0:T(8,128)(2,1)S(1)}, bf16[1,24,32,128]{3,2,1,0:T(8,128)(2,1)S(1)}, u32[]{:S(2)}, u32[]{:S(2)}) collective-permute-start(bf16[1,24,32,128]{3,2,1,0:T(8,128)(2,1)S(1)} %get-tuple-element.25.refs_0_), channel_id=1, source_target_pairs={{0,1},{1,0},{2,3},{3,2},{4,5},{5,4},{6,7},{7,6},{8,9},{9,8},{10,11... | collective-permute-start | bytes 589832 | tf_op jit(solution)/shard_map/ppermute | solution.py:27
  20.9 5.0 %collective-permute-start.11 = (bf16[2,8,32,128]{3,2,1,0:T(8,128)(2,1)S(1)}, bf16[2,8,32,128]{3,2,1,0:T(8,128)(2,1)S(1)}, u32[]{:S(2)}, u32[]{:S(2)}) collective-permute-start(bf16[2,8,32,128]{3,2,1,0:T(8,128)(2,1)S(1)} %join.1.refs_9_.refs_11_), channel_id=1, source_target_pairs={{0,2},{1,3},{2,0},{3,1},{4,6},{5,7},{6,4},{7,5},{8,10},{9,11},{10,... | collective-permute-start | bytes 393224 | tf_op jit(solution)/shard_map/ppermute | solution.py:27
  22.5 3.5 %collective-permute-start.4 = (bf16[1,24,32,128]{3,2,1,0:T(8,128)(2,1)S(1)}, bf16[1,24,32,128]{3,2,1,0:T(8,128)(2,1)S(1)}, u32[]{:S(2)}, u32[]{:S(2)}) collective-permute-start(bf16[1,24,32,128]{3,2,1,0:T(8,128)(2,1)S(1)} %bitcast.8), channel_id=1, source_target_pairs={{0,1},{1,0},{2,3},{3,2},{4,5},{5,4},{6,7},{7,6},{8,9},{9,8},{10,11... | collective-permute-start | bytes 589832 | tf_op jit(solution)/shard_map/ppermute | solution.py:27
  22.5 3.4 %collective-permute-start.2 = (bf16[1,24,32,128]{3,2,1,0:T(8,128)(2,1)S(1)}, bf16[1,24,32,128]{3,2,1,0:T(8,128)(2,1)S(1)}, u32[]{:S(2)}, u32[]{:S(2)}) collective-permute-start(bf16[1,24,32,128]{3,2,1,0:T(8,128)(2,1)S(1)} %collective-permute-done.1.refs_2_), channel_id=1, source_target_pairs={{0,1},{1,0},{2,3},{3,2},{4,5},{5,4},{6,7},{7,6},{8,9},{9,8},{10,11... | collective-permute-start | bytes 589832 | tf_op jit(solution)/shard_map/ppermute | solution.py:27
  23.0 3.0 %collective-permute-start.6 = (bf16[1,24,32,128]{3,2,1,0:T(8,128)(2,1)S(1)}, bf16[1,24,32,128]{3,2,1,0:T(8,128)(2,1)S(1)}, u32[]{:S(2)}, u32[]{:S(2)}) collective-permute-start(bf16[1,24,32,128]{3,2,1,0:T(8,128)(2,1)S(1)} %collective-permute-done.5.refs_6_), channel_id=1, source_target_pairs={{0,1},{1,0},{2,3},{3,2},{4,5},{5,4},{6,7},{7,6},{8,9},{9,8},{10,11... | collective-permute-start | bytes 589832 | tf_op jit(solution)/shard_map/ppermute | solution.py:27
  23.1 2.9 %collective-permute-start.10 = (bf16[2,8,32,128]{3,2,1,0:T(8,128)(2,1)S(1)}, bf16[2,8,32,128]{3,2,1,0:T(8,128)(2,1)S(1)}, u32[]{:S(2)}, u32[]{:S(2)}) collective-permute-start(bf16[2,8,32,128]{3,2,1,0:T(8,128)(2,1)S(1)} %join.1.refs_9_.refs_11_), channel_id=1, source_target_pairs={{0,1},{1,0},{2,3},{3,2},{4,5},{5,4},{6,7},{7,6},{8,9},{9,8},{10,11... | collective-permute-start | bytes 393224 | tf_op jit(solution)/shard_map/ppermute | solution.py:27
  25.9 2.2 %collective-permute-start.12 = (bf16[2,8,32,128]{3,2,1,0:T(8,128)(2,1)S(1)}, bf16[2,8,32,128]{3,2,1,0:T(8,128)(2,1)S(1)}, u32[]{:S(2)}, u32[]{:S(2)}) collective-permute-start(bf16[2,8,32,128]{3,2,1,0:T(8,128)(2,1)S(1)} %collective-permute-done.11.refs_11_.refs_13_), channel_id=1, source_target_pairs={{0,1},{1,0},{2,3},{3,2},{4,5},{5,4},{6,7},{7,6},{8,9},{9,8},{10,11... | collective-permute-start | bytes 393224 | tf_op jit(solution)/shard_map/ppermute | solution.py:27
  28.5 6.0 %collective-permute-start.15 = (bf16[8,16,128]{2,1,0:T(8,128)(2,1)S(1)}, bf16[8,16,128]{2,1,0:T(8,128)(2,1)S(1)}, u32[]{:S(2)}, u32[]{:S(2)}) collective-permute-start(bf16[8,16,128]{2,1,0:T(8,128)(2,1)S(1)} %get-tuple-element.40), channel_id=1, source_target_pairs={{0,12},{1,13},{2,14},{3,15},{4,8},{5,9},{6,10},{7,11},{8,4},{9,5},... | collective-permute-start | bytes 98312 | tf_op jit(solution)/shard_map/ppermute | solution.py:27
  31.1 5.0 %collective-permute-start.14 = (bf16[8,16,128]{2,1,0:T(8,128)(2,1)S(1)}, bf16[8,16,128]{2,1,0:T(8,128)(2,1)S(1)}, u32[]{:S(2)}, u32[]{:S(2)}) collective-permute-start(bf16[8,16,128]{2,1,0:T(8,128)(2,1)S(1)} %get-tuple-element.39), channel_id=1, source_target_pairs={{0,8},{1,9},{2,10},{3,11},{4,12},{5,13},{6,14},{7,15},{8,0},{9,1},... | collective-permute-start | bytes 98312 | tf_op jit(solution)/shard_map/ppermute | solution.py:27
  31.8 4.3 %collective-permute-start.13 = (bf16[8,16,128]{2,1,0:T(8,128)(2,1)S(1)}, bf16[8,16,128]{2,1,0:T(8,128)(2,1)S(1)}, u32[]{:S(2)}, u32[]{:S(2)}) collective-permute-start(bf16[8,16,128]{2,1,0:T(8,128)(2,1)S(1)} %get-tuple-element.38), channel_id=1, source_target_pairs={{0,4},{1,5},{2,6},{3,7},{4,0},{5,1},{6,2},{7,3},{8,12},{9,13},{10,... | collective-permute-start | bytes 98312 | tf_op jit(solution)/shard_map/ppermute | solution.py:27

commit v7 on v6

--- a/solution.py
+++ b/solution.py
@@ -11,6 +11,7 @@
 LANES = 128
 PLANE = 4
 VMEM_BYTES = 32 * 1024 * 1024
+HEAD = 16
 PACK_BYTES = 60 * 1024 * 1024
 
 
@@ -31,20 +32,37 @@
     return lax.optimization_barrier((x, others))[0]
 
 
-def pack_kernel(planes, *refs):
-    sources, outs = refs[:8], refs[8:10 + planes]
-    plan, closed, *copied, sems = refs[10 + planes:]
-    suffix_ref, cap_ref, first_ref, prefix_ref, *numbers = copied
-    pair_prefix_ref, pair_suffix_ref, count_ref, routes_ref = numbers
-    plane = lax.axis_index("bits") // PLANE
-    copies = [pltpu.make_async_copy(source, ref, sems.at[n]) for n, (source, ref) in enumerate(zip(sources, copied))]
-    for copy in copies:
+def pack_kernel(planes, merges, held, *refs):
+    sources, outs, stages, copied = refs[:8], refs[8:10 + planes], refs[10 + planes:12 + 2 * planes], refs[12 + 2 * planes:-1]
+    sems = refs[-1]
+    first_ref, prefix_ref, suffix_ref, cap_ref, pair_prefix_ref, pair_suffix_ref, count_ref, routes_ref = copied
+    width = suffix_ref.shape[1]
+    rows, twice_width = prefix_ref.shape
+    part, span, slots = width // 2, width // (planes // 2), planes * PLANE
+    me = lax.axis_index("bits")
+    plane = me // PLANE
+    inward = [pltpu.make_async_copy(source, ref, sems.at[n]) for n, (source, ref) in enumerate(zip(sources, copied))]
+    for copy in inward:
         copy.start()
-    merges, pieces = pair_prefix_ref.shape
-    blocks, held, slots = first_ref.shape[0], prefix_ref.shape[0], planes * PLANE
-    for copy in copies[4:]:
+    outward = []
+
+    def send(k, row, size):
+        there = pl.ds(row, size)
+        sem = sems.at[len(sources) + len(outward)]
+        outward.append(pltpu.make_async_copy(stages[k].at[there, :], outs[k].at[there, :], sem))
+        outward[-1].start()
+
+    lows = [plane % 2 ^ k % 2 for k in range(planes)]
+    firsts = [first_ref.shape[0] * (part // LANES) if k < 2 else 0 for k in range(planes)]
+    inward[0].wait()
+    for k in range(2):
+        for n in range(part // LANES):
+            columns = pl.ds(pl.multiple_of(lows[k] * part + n * LANES, LANES), LANES)
+            stages[k][n * first_ref.shape[0]:(n + 1) * first_ref.shape[0], :] = first_ref[:, columns]
+        send(k, 0, firsts[k])
+    for copy in inward[4:]:
         copy.wait()
-    me = lax.axis_index("bits")
+    pieces = routes_ref.shape[0]
     lane = lax.broadcasted_iota(jnp.int32, (pieces, LANES), 1)
     named = [jnp.zeros((pieces, LANES), jnp.int32)] * planes
     for slot in range(slots):
@@ -57,53 +75,35 @@
         pick = jnp.where(m < count_ref[...], slots + pick, -1)
         pick = jnp.sum(jnp.where(own_lane, jnp.broadcast_to(pick, (pieces, pieces)), 0), axis=1, keepdims=True)
         picks += (lane == pick).astype(jnp.int32)
-    plan[...] = jnp.zeros_like(plan)
-    routing = []
+    inward[1].wait()
     for k in range(planes):
-        plan[:pieces, :] = (named[k] + picks).astype(jnp.float32)
-        routing.append(plan[...].astype(jnp.bfloat16))
-    blocks, _, depth, width = first_ref.shape
-    part, span = width // 2, width // (planes // 2)
-    rows_piece, twice_width = prefix_ref.shape[1:]
-    per = depth // rows_piece
-    firsts = 2 * blocks * (part // LANES)
-    relayed = [(firsts if k < 2 else 0) + part // depth for k in range(planes)]
-    lows = [plane % 2 ^ k % 2 for k in range(planes)]
-    copies[2].wait()
-    for k in range(2):
-        n = 0
-        for a in range(blocks):
-            for c in range(2):
-                for start in range(0, part, LANES):
-                    columns = pl.ds(pl.multiple_of(lows[k] * part + start, LANES), LANES)
-                    outs[k][n] = first_ref[a, c, :, columns]
-                    n += 1
-    copies[3].wait()
-    for k in range(planes):
-        high = plane // 2 ^ k // 2
-        tail = [routing[k]]
-        for start in range(0, twice_width, width):
+        message, start = (planes + k, 0) if k < 2 else (k, part)
+        stage, high = stages[message], plane // 2 ^ k // 2
+        rest = jnp.zeros((HEAD - pieces, LANES), jnp.float32)
+        routing = jnp.concatenate([(named[k] + picks).astype(jnp.float32), rest], axis=0)
+        stage[start:start + HEAD, :] = routing.astype(jnp.bfloat16)
+        row = start + HEAD
+        for side in range(0, twice_width, width):
             for n in range(0, span, LANES):
-                columns = pl.ds(pl.multiple_of(high * span + (start + n), LANES), LANES)
-                for row in range(0, held, per):
-                    tail.append(prefix_ref[row:row + per, :, columns].reshape(depth, LANES))
-        for n, entry in enumerate(tail):
-            if k < 2:
-                outs[planes + k][n] = entry
-            else:
-                outs[k][relayed[k] + n] = entry
-    copies[1].wait()
+                columns = pl.ds(pl.multiple_of(high * span + (side + n), LANES), LANES)
+                stage[row:row + rows, :] = prefix_ref[:, columns]
+                row += rows
+        send(message, start, row - start)
+    inward[3].wait()
     upper = jnp.concatenate([cap_ref[0], cap_ref[1]], axis=0)
     lower = jnp.concatenate([-cap_ref[1], cap_ref[0]], axis=0)
     turned = (((1,), (1,)), ((), ()))
-    copies[0].wait()
-    both = lax.dot_general(suffix_ref[0], upper, turned, preferred_element_type=jnp.float32)
-    both += lax.dot_general(suffix_ref[1], lower, turned, preferred_element_type=jnp.float32)
-    closed[...] = both.astype(jnp.bfloat16)
-    for k in range(planes):
-        for n in range(part // depth):
-            there = pl.ds(pl.multiple_of(lows[k] * part + n * depth, depth), depth)
-            outs[k][relayed[k] - part // depth + n] = closed[there, :]
+    inward[2].wait()
+    for low in range(2):
+        there = pl.ds(pl.multiple_of((plane % 2 ^ low) * part, part), part)
+        both = lax.dot_general(suffix_ref[0, there, :], upper, turned, preferred_element_type=jnp.float32)
+        both += lax.dot_general(suffix_ref[1, there, :], lower, turned, preferred_element_type=jnp.float32)
+        both = both.astype(jnp.bfloat16)
+        for k in range(low, planes, 2):
+            stages[k][firsts[k]:firsts[k] + part, :] = both
+            send(k, firsts[k], part)
+    for copy in outward:
+        copy.wait()
 
 
 def own_kernel(*refs):
@@ -148,19 +148,19 @@
     closing = refs[2 * PLANE + planes:-7]
     state, named, sums, forms, high, low, wide = refs[-7:]
     me = lax.axis_index("bits")
-    depth = packs[0].shape[1]
     span, twice_part = forms.shape[1:]
+    depth = span // (2 * PLANE)
     part = twice_part // 2
     rows = held * rows_piece
     locals_ = []
-    tail = 1 + 2 * (span // LANES) * (rows // depth)
+    tail = HEAD + 2 * (span // LANES) * rows
     for k in range(planes):
         first = packs[k].shape[0] - tail
-        numbers = packs[k][first].astype(jnp.float32)
+        numbers = packs[k][first:first + HEAD].astype(jnp.float32)
         for n in range(pieces):
             here = slice((k * pieces + n) * rows_piece, (k * pieces + n + 1) * rows_piece)
             named[here, :] = jnp.broadcast_to(numbers[n:n + 1], (rows_piece, LANES))
-        locals_.append(packs[k].at[first + 1:first + tail])
+        locals_.append(packs[k].at[first + HEAD:first + tail])
     shape = (LANES, blocks * rows)
     spread = lax.broadcasted_iota(jnp.int32, shape, 0) - slots == lax.broadcasted_iota(jnp.int32, shape, 1) // rows_piece
     spread = spread.astype(jnp.float32).astype(jnp.bfloat16)
@@ -171,16 +171,18 @@
     for j in range(2 * PLANE):
         there = pl.ds(pl.multiple_of((me ^ j) % (2 * PLANE) * depth, depth), depth)
         for a in range(blocks):
-            for n in range(twice_part // LANES):
-                forms[a, there, n * LANES:(n + 1) * LANES] = relays[j][0, a * (twice_part // LANES) + n]
-    chunks = rows // depth
+            for c in range(2):
+                for n in range(part // LANES):
+                    row = ((n * blocks + a) * 2 + c) * depth
+                    columns = slice(c * part + n * LANES, c * part + (n + 1) * LANES)
+                    forms[a, there, columns] = relays[j][0, row:row + depth, :]
     left = []
     for c in range(2):
         for k in range(planes):
             columns = []
             for n in range(span // LANES):
-                first = (c * (span // LANES) + n) * chunks
-                columns.append(locals_[k][first:first + chunks].reshape(rows, LANES))
+                first = (c * (span // LANES) + n) * rows
+                columns.append(locals_[k][first:first + rows])
             left.append(jnp.concatenate(columns, axis=1))
     left = jnp.concatenate(left, axis=0)
     for a in range(blocks):
@@ -207,8 +209,7 @@
     slot = 0
     for relay in relays:
         for k in range(relay.shape[0]):
-            first = relay.shape[1] - part // relay.shape[2]
-            real_rows = relay[k, first:].reshape(part, LANES)
+            real_rows = relay[k, relay.shape[1] - part:]
             turned = pltpu.roll(real_rows.astype(jnp.float32), LANES // 2, 1)
             turned = jnp.where(lane < LANES // 2, -turned, turned)
             wide[:part, slot * LANES:(slot + 1) * LANES] = real_rows
@@ -240,34 +241,35 @@
     part, span = width // 2, width // (planes // 2)
     vmem = pl.BlockSpec(memory_space=pltpu.VMEM)
     params = pltpu.CompilerParams(vmem_limit_bytes=VMEM_BYTES)
-    forms_size, closed_size = 2 * blocks * (part // LANES), part // depth
-    tail = 1 + 2 * (span // LANES) * (held * rows_piece // depth)
+    relayed = blocks * 2 * depth * (part // LANES) + part
+    tail = HEAD + 2 * (span // LANES) * held * rows_piece
     sources = (
+        first_suffix.reshape(blocks * 2 * depth, width),
+        prefix.reshape(held * rows_piece, twice_width),
         suffix[0],
         jnp.swapaxes(cap, 1, 2),
-        first_suffix,
-        prefix,
         pair_prefix.T,
         pair_suffix.T,
         merge_count[None],
         routes,
     )
-    sizes = [forms_size + closed_size] * 2 + [closed_size + tail] * (planes - 2) + [tail] * 2
+    sizes = [relayed] * 2 + [part + tail] * (planes - 2) + [tail] * 2
+    anywhere = pl.BlockSpec(memory_space=pl.ANY)
     packs = pl.pallas_call(
-        functools.partial(pack_kernel, planes),
-        out_shape=[jax.ShapeDtypeStruct((size, depth, LANES), jnp.bfloat16) for size in sizes],
-        in_specs=[pl.BlockSpec(memory_space=pl.ANY)] * len(sources),
-        out_specs=[vmem] * len(sizes),
-        scratch_shapes=[pltpu.VMEM((depth, LANES), jnp.float32), pltpu.VMEM((width, LANES), jnp.bfloat16)]
+        functools.partial(pack_kernel, planes, pair_prefix.shape[1], held),
+        out_shape=[jax.ShapeDtypeStruct((size, LANES), jnp.bfloat16) for size in sizes],
+        in_specs=[anywhere] * len(sources),
+        out_specs=[anywhere] * len(sizes),
+        scratch_shapes=[pltpu.VMEM((size, LANES), jnp.bfloat16) for size in sizes]
         + [pltpu.VMEM(source.shape, source.dtype) for source in sources]
-        + [pltpu.SemaphoreType.DMA((len(sources),))],
+        + [pltpu.SemaphoreType.DMA((len(sources) + 2 + 2 * planes,))],
         compiler_params=pltpu.CompilerParams(vmem_limit_bytes=PACK_BYTES),
         cost_estimate=pl.CostEstimate(flops=2 ** 20, bytes_accessed=2 ** 12, transcendentals=0),
         name="pack",
     )(*sources)
     far = [swap(packs[k], k * PLANE) for k in range(2, planes)]
     near = swap(packs[planes + 1], PLANE)
-    relays = [packs[0][None], swap(packs[1], PLANE)[None], join([after(far[0], near)] + far[1:], closed_size)]
+    relays = [packs[0][None], swap(packs[1], PLANE)[None], join([after(far[0], near)] + far[1:], part)]
     own, local = own_copy(relays[0], packs[planes])
     across = [swap(r, 2) for r in relays[:2]]
     relays[0] = own
@@ -412,11 +414,8 @@
         and width // 2 % LANES == 0
         and 2 * cap.shape[2] == LANES
         and depth % 16 == 0
-        and LANES % depth == 0
-        and depth % prefix.shape[1] == 0
-        and prefix.shape[0] * prefix.shape[1] % depth == 0
         and prefix.shape[1] % 16 == 0
-        and pieces <= min(depth, LANES)
+        and pieces <= HEAD
         and owners + first_suffix.shape[0] * prefix.shape[0] <= LANES
     )
     return in_planes(*args) if fits else by_owner(*args)

time: 37 us -> 36.5 us (0.986)
  waiting for transfers between devices: 9.56 us -> 9.18 us
    ppermute x16, waiting for transfers between devices: 9.56 us -> 9.18 us  [swap(): return lax.ppermute(x, 'bits', [(i, i ^ bit) for i in range(owners)])]
where the time goes in v7:
time: 36.5 us; the launch traced here: 36.3 us
  starting transfers between devices  17.8 us (49%)
  waiting for transfers between devices  9.18 us (25%)
  Pallas kernels  6.73 us (18%)
  local copies, waits for them, and re-layouts  1.81 us (5%)
  other arithmetic  0.65 us (2%)
    ppermute x16, starting transfers between devices, swap(): return lax.ppermute(x, 'bits', [(i, i ^ bit) for i in range(owners)])  17.8 us
    ppermute x16, waiting for transfers between devices, swap(): return lax.ppermute(x, 'bits', [(i, i ^ bit) for i in range(owners)])  9.18 us
    pallas_call x2, Pallas kernels, sums_of(): pl.pallas_call(functools.partial(front_kernel, count, owners, order, bloc...  3.35 us
    pallas_call x1, Pallas kernels, in_planes(): pl.pallas_call(functools.partial(pack_kernel, planes, pair_prefix.shape[1...  2.69 us
    unnamed x4, local copies, waits for them, and re-layouts  1.81 us
  transfers between devices with their start and end apart: 16, of which 4 were waited for; matrix products, arithmetic and copies ran while one was open for 0% of the time, Pallas kernels for 10%

profile of v7, /device:TPU:0, one launch (start us, length us, event | category | flops | bytes accessed | tf_op | source)
XLA Modules:
  0.0 36.3 jit_solution(14502568866413122581)
XLA Ops:
  0.0 2.7 %pack.1 = (bf16[768,128]{1,0:T(8,128)(2,1)}, bf16[768,128]{1,0:T(8,128)(2,1)}, bf16[528,128]{1,0:T(8,128)(2,1)}, bf16[528,128]{1,0:T(8,128)(2,1)}, bf16[272,128]{1,0:T(8,128)(2,1)}, /*index=5*/bf16[272,128]{1,0:T(8,128)(2,1)}) custom-call(bf16[256,512]{1,0:T(8,128)(2,1)} %bitcast.16, bf16[64,1024]{1,0:T(8,128)(2,1)} %bitcast.17, ...), custom_call_target="tpu_custom_call" | custom-call | flops 1048576 | bytes 4096 | tf_op jit(solution)/shard_map/pack/pallas_call | solution.py:258
  2.7 3.1 %collective-permute-start.3 = (bf16[768,128]{1,0:T(8,128)(2,1)}, bf16[768,128]{1,0:T(8,128)(2,1)S(1)}, u32[]{:S(2)}, u32[]{:S(2)}) collective-permute-start(bf16[768,128]{1,0:T(8,128)(2,1)} %get-tuple-element.26), channel_id=1, source_target_pairs={{0,4},{1,5},{2,6},{3,7},{4,0},{5,1},{6,2},{7,3},{8,12},{9,13},{10,... | collective-permute-start | bytes 589832 | tf_op jit(solution)/shard_map/ppermute | solution.py:28
  5.8 0.1 collective-permute-start.8
  5.9 3.0 %collective-permute-start.7 = (bf16[528,128]{1,0:T(8,128)(2,1)}, bf16[528,128]{1,0:T(8,128)(2,1)S(1)}, u32[]{:S(2)}, u32[]{:S(2)}) collective-permute-start(bf16[528,128]{1,0:T(8,128)(2,1)} %get-tuple-element.28), channel_id=1, source_target_pairs={{0,8},{1,9},{2,10},{3,11},{4,12},{5,13},{6,14},{7,15},{8,0},{9,1},... | collective-permute-start | bytes 405512 | tf_op jit(solution)/shard_map/ppermute | solution.py:28
  8.8 1.3 %collective-permute-start.9 = (bf16[528,128]{1,0:T(8,128)(2,1)}, bf16[528,128]{1,0:T(8,128)(2,1)S(1)}, u32[]{:S(2)}, u32[]{:S(2)}) collective-permute-start(bf16[528,128]{1,0:T(8,128)(2,1)} %get-tuple-element.31), channel_id=1, source_target_pairs={{0,12},{1,13},{2,14},{3,15},{4,8},{5,9},{6,10},{7,11},{8,4},{9,5},... | collective-permute-start | bytes 405512 | tf_op jit(solution)/shard_map/ppermute | solution.py:28
  10.2 1.5 %collective-permute-start.1 = (bf16[1,768,128]{2,1,0:T(8,128)(2,1)}, bf16[1,768,128]{2,1,0:T(8,128)(2,1)S(1)}, u32[]{:S(2)}, u32[]{:S(2)}) collective-permute-start(bf16[1,768,128]{2,1,0:T(8,128)(2,1)} %bitcast.13), channel_id=1, source_target_pairs={{0,2},{1,3},{2,0},{3,1},{4,6},{5,7},{6,4},{7,5},{8,10},{9,11},{10,... | collective-permute-start | bytes 589832 | tf_op jit(solution)/shard_map/ppermute | solution.py:28
  11.7 2.8 %collective-permute-done.3 = bf16[768,128]{1,0:T(8,128)(2,1)S(1)} collective-permute-done((bf16[768,128]{1,0:T(8,128)(2,1)}, bf16[768,128]{1,0:T(8,128)(2,1)S(1)}, u32[]{:S(2)}, u32[]{:S(2)}) %collective-permute-start.3) | collective-permute-done | bytes 196640 | tf_op jit(solution)/shard_map/ppermute | solution.py:28
  14.5 1.7 %collective-permute-start.5 = (bf16[1,768,128]{2,1,0:T(8,128)(2,1)S(1)}, bf16[1,768,128]{2,1,0:T(8,128)(2,1)S(1)}, u32[]{:S(2)}, u32[]{:S(2)}) collective-permute-start(bf16[1,768,128]{2,1,0:T(8,128)(2,1)S(1)} %bitcast.9), channel_id=1, source_target_pairs={{0,2},{1,3},{2,0},{3,1},{4,6},{5,7},{6,4},{7,5},{8,10},{9,11},{10,... | collective-permute-start | bytes 589832 | tf_op jit(solution)/shard_map/ppermute | solution.py:28
  16.2 0.0 copy-start
  16.2 0.9 %copy-done = bf16[768,128]{1,0:T(8,128)(2,1)S(1)} copy-done((bf16[768,128]{1,0:T(8,128)(2,1)S(1)}, bf16[768,128]{1,0:T(8,128)(2,1)}, u32[]{:S(2)}) %copy-start) | copy-done | bytes 196632
  17.2 0.0 copy-start.1
  17.2 0.9 %copy-done.1 = bf16[272,128]{1,0:T(8,128)(2,1)S(1)} copy-done((bf16[272,128]{1,0:T(8,128)(2,1)S(1)}, bf16[272,128]{1,0:T(8,128)(2,1)}, u32[]{:S(2)}) %copy-start.1) | copy-done | bytes 69656
  18.1 0.0 collective-permute-done.8.refs_8_
  18.1 0.1 collective-permute-start
  18.2 0.0 collective-permute-done.7.refs_0_.refs_9_
  18.2 2.3 %collective-permute-done.9.refs_1_.refs_10_ = bf16[528,128]{1,0:T(8,128)(2,1)S(1)} collective-permute-done((bf16[528,128]{1,0:T(8,128)(2,1)}, bf16[528,128]{1,0:T(8,128)(2,1)S(1)}, u32[]{:S(2)}, u32[]{:S(2)}) %collective-permute-start.9) | collective-permute-done | bytes 135200 | tf_op jit(solution)/shard_map/ppermute | solution.py:28
  20.5 1.6 %collective-permute-start.11 = (bf16[2,256,128]{2,1,0:T(8,128)(2,1)S(1)}, bf16[2,256,128]{2,1,0:T(8,128)(2,1)S(1)}, u32[]{:S(2)}, u32[]{:S(2)}) collective-permute-start(bf16[2,256,128]{2,1,0:T(8,128)(2,1)S(1)} %join.1.refs_9_.refs_11_), channel_id=1, source_target_pairs={{0,2},{1,3},{2,0},{3,1},{4,6},{5,7},{6,4},{7,5},{8,10},{9,11},{10,... | collective-permute-start | bytes 393224 | tf_op jit(solution)/shard_map/ppermute | solution.py:28
  22.1 0.0 collective-permute-start.4
  22.1 0.0 collective-permute-done.1.refs_2_
  22.1 0.5 %collective-permute-start.2 = (bf16[1,768,128]{2,1,0:T(8,128)(2,1)S(1)}, bf16[1,768,128]{2,1,0:T(8,128)(2,1)S(1)}, u32[]{:S(2)}, u32[]{:S(2)}) collective-permute-start(bf16[1,768,128]{2,1,0:T(8,128)(2,1)S(1)} %collective-permute-done.1.refs_2_), channel_id=1, source_target_pairs={{0,1},{1,0},{2,3},{3,2},{4,5},{5,4},{6,7},{7,6},{8,9},{9,8},{10,11... | collective-permute-start | bytes 589832 | tf_op jit(solution)/shard_map/ppermute | solution.py:28
  22.6 0.0 collective-permute-done.5.refs_6_
  22.6 0.1 collective-permute-start.6
  22.7 0.0 collective-permute-done.refs_1_
  22.7 0.4 %collective-permute-start.10 = (bf16[2,256,128]{2,1,0:T(8,128)(2,1)S(1)}, bf16[2,256,128]{2,1,0:T(8,128)(2,1)S(1)}, u32[]{:S(2)}, u32[]{:S(2)}) collective-permute-start(bf16[2,256,128]{2,1,0:T(8,128)(2,1)S(1)} %join.1.refs_9_.refs_11_), channel_id=1, source_target_pairs={{0,1},{1,0},{2,3},{3,2},{4,5},{5,4},{6,7},{7,6},{8,9},{9,8},{10,11... | collective-permute-start | bytes 393224 | tf_op jit(solution)/shard_map/ppermute | solution.py:28
  23.1 2.4 %collective-permute-done.11.refs_11_.refs_13_ = bf16[2,256,128]{2,1,0:T(8,128)(2,1)S(1)} collective-permute-done((bf16[2,256,128]{2,1,0:T(8,128)(2,1)S(1)}, bf16[2,256,128]{2,1,0:T(8,128)(2,1)S(1)}, u32[]{:S(2)}, u32[]{:S(2)}) %collective-permute-start.11) | collective-permute-done | bytes 131104 | tf_op jit(solution)/shard_map/ppermute | solution.py:28
  25.5 0.0 collective-permute-start.12
  25.5 0.0 collective-permute-done.10.refs_10_.refs_12_
  25.5 0.0 collective-permute-done.2.refs_3_
  25.5 0.0 collective-permute-done.4.refs_5_
  25.5 0.0 collective-permute-done.6.refs_7_
  25.6 2.1 %front.3 = (bf16[384,512]{1,0:T(8,128)(2,1)S(1)}, f32[384,128]{1,0:T(8,128)S(1)}, f32[384,128]{1,0:T(8,128)S(1)}) custom-call(bf16[1,768,128]{2,1,0:T(8,128)(2,1)S(1)} %get-tuple-element.25.refs_0_, bf16[1,768,128]{2,1,0:T(8,128)(2,1)S(1)} %collective-permute-done.refs_1_, bf16[1,768,128]{2,1,0:T(8,128)(2,1)S(1)} %collective-permute-done.1.refs_2_, ...), custom_call_target="tpu_custom_call" | custom-call | bytes 4096 | tf_op jit(solution)/shard_map/front/pallas_call | solution.py:292
  27.7 0.0 collective-permute-done.12.relay
  27.7 0.4 %last.3 = (bf16[8,16,128]{2,1,0:T(8,128)(2,1)S(1)}, bf16[8,16,128]{2,1,0:T(8,128)(2,1)S(1)}, bf16[8,16,128]{2,1,0:T(8,128)(2,1)S(1)}) custom-call(f32[384,128]{1,0:T(8,128)S(1)} %get-tuple-element.35.named, bf16[384,512]{1,0:T(8,128)(2,1)S(1)} %get-tuple-element.36.state, f32[384,128]{1,0:T(8,128)S(1)} %get-tuple-element.37.sums_in, ...), custom_call_target="tpu_custom_call" | custom-call | bytes 4096 | tf_op jit(solution)/shard_map/last/pallas_call | solution.py:311
  28.1 2.6 %collective-permute-start.15 = (bf16[8,16,128]{2,1,0:T(8,128)(2,1)S(1)}, bf16[8,16,128]{2,1,0:T(8,128)(2,1)S(1)}, u32[]{:S(2)}, u32[]{:S(2)}) collective-permute-start(bf16[8,16,128]{2,1,0:T(8,128)(2,1)S(1)} %get-tuple-element.40), channel_id=1, source_target_pairs={{0,12},{1,13},{2,14},{3,15},{4,8},{5,9},{6,10},{7,11},{8,4},{9,5},... | collective-permute-start | bytes 98312 | tf_op jit(solution)/shard_map/ppermute | solution.py:28
  30.7 0.6 %collective-permute-start.14 = (bf16[8,16,128]{2,1,0:T(8,128)(2,1)S(1)}, bf16[8,16,128]{2,1,0:T(8,128)(2,1)S(1)}, u32[]{:S(2)}, u32[]{:S(2)}) collective-permute-start(bf16[8,16,128]{2,1,0:T(8,128)(2,1)S(1)} %get-tuple-element.39), channel_id=1, source_target_pairs={{0,8},{1,9},{2,10},{3,11},{4,12},{5,13},{6,14},{7,15},{8,0},{9,1},... | collective-permute-start | bytes 98312 | tf_op jit(solution)/shard_map/ppermute | solution.py:28
  31.3 1.2 %collective-permute-start.13 = (bf16[8,16,128]{2,1,0:T(8,128)(2,1)S(1)}, bf16[8,16,128]{2,1,0:T(8,128)(2,1)S(1)}, u32[]{:S(2)}, u32[]{:S(2)}) collective-permute-start(bf16[8,16,128]{2,1,0:T(8,128)(2,1)S(1)} %get-tuple-element.38), channel_id=1, source_target_pairs={{0,4},{1,5},{2,6},{3,7},{4,0},{5,1},{6,2},{7,3},{8,12},{9,13},{10,... | collective-permute-start | bytes 98312 | tf_op jit(solution)/shard_map/ppermute | solution.py:28
  32.5 1.2 %front.2 = (bf16[128,512]{1,0:T(8,128)(2,1)S(1)}, f32[128,128]{1,0:T(8,128)S(1)}, f32[128,128]{1,0:T(8,128)S(1)}) custom-call(bf16[1,768,128]{2,1,0:T(8,128)(2,1)S(1)} %get-tuple-element.25.refs_0_, bf16[1,768,128]{2,1,0:T(8,128)(2,1)S(1)} %collective-permute-done.refs_1_, bf16[1,768,128]{2,1,0:T(8,128)(2,1)S(1)} %collective-permute-done.1.refs_2_, ...), custom_call_target="tpu_custom_call" | custom-call | bytes 4096 | tf_op jit(solution)/shard_map/front/pallas_call | solution.py:292
  33.8 0.3 last.2
  34.0 0.0 collective-permute-done.15
  34.1 1.6 %collective-permute-done.14 = bf16[8,16,128]{2,1,0:T(8,128)(2,1)S(1)} collective-permute-done((bf16[8,16,128]{2,1,0:T(8,128)(2,1)S(1)}, bf16[8,16,128]{2,1,0:T(8,128)(2,1)S(1)}, u32[]{:S(2)}, u32[]{:S(2)}) %collective-permute-start.14) | collective-permute-done | bytes 32800 | tf_op jit(solution)/shard_map/ppermute | solution.py:28
  35.6 0.0 collective-permute-done.13
  35.6 0.6 %convert_add_fusion = f32[8,16,128]{2,1,0:T(8,128)} fusion(bf16[8,16,128]{2,1,0:T(8,128)(2,1)S(1)} %collective-permute-done.15, bf16[8,16,128]{2,1,0:T(8,128)(2,1)S(1)} %collective-permute-done.14, f32[8,16,128]{2,1,0:T(8,128)S(1)} %last.2, bf16[8,16,128]{2,1,0:T(8,128)(2,1)S(1)} %collective-permute-done.13), kind=kLoop, calls=%fused_computation | loop fusion | flops 98304 | bytes 229376 | tf_op jit(solution)/shard_map/add | solution.py:328
  (2 shorter events, 0.0 us)
Async XLA Ops:
  2.7 11.8 %collective-permute-start.3 = (bf16[768,128]{1,0:T(8,128)(2,1)}, bf16[768,128]{1,0:T(8,128)(2,1)S(1)}, u32[]{:S(2)}, u32[]{:S(2)}) collective-permute-start(bf16[768,128]{1,0:T(8,128)(2,1)} %get-tuple-element.26), channel_id=1, source_target_pairs={{0,4},{1,5},{2,6},{3,7},{4,0},{5,1},{6,2},{7,3},{8,12},{9,13},{10,... | collective-permute-start | bytes 589832 | tf_op jit(solution)/shard_map/ppermute | solution.py:28
  5.8 12.3 %collective-permute-start.8 = (bf16[272,128]{1,0:T(8,128)(2,1)}, bf16[272,128]{1,0:T(8,128)(2,1)S(1)}, u32[]{:S(2)}, u32[]{:S(2)}) collective-permute-start(bf16[272,128]{1,0:T(8,128)(2,1)} %get-tuple-element.29), channel_id=1, source_target_pairs={{0,4},{1,5},{2,6},{3,7},{4,0},{5,1},{6,2},{7,3},{8,12},{9,13},{10,... | collective-permute-start | bytes 208904 | tf_op jit(solution)/shard_map/ppermute | solution.py:28
  5.9 12.3 %collective-permute-start.7 = (bf16[528,128]{1,0:T(8,128)(2,1)}, bf16[528,128]{1,0:T(8,128)(2,1)S(1)}, u32[]{:S(2)}, u32[]{:S(2)}) collective-permute-start(bf16[528,128]{1,0:T(8,128)(2,1)} %get-tuple-element.28), channel_id=1, source_target_pairs={{0,8},{1,9},{2,10},{3,11},{4,12},{5,13},{6,14},{7,15},{8,0},{9,1},... | collective-permute-start | bytes 405512 | tf_op jit(solution)/shard_map/ppermute | solution.py:28
  8.8 11.6 %collective-permute-start.9 = (bf16[528,128]{1,0:T(8,128)(2,1)}, bf16[528,128]{1,0:T(8,128)(2,1)S(1)}, u32[]{:S(2)}, u32[]{:S(2)}) collective-permute-start(bf16[528,128]{1,0:T(8,128)(2,1)} %get-tuple-element.31), channel_id=1, source_target_pairs={{0,12},{1,13},{2,14},{3,15},{4,8},{5,9},{6,10},{7,11},{8,4},{9,5},... | collective-permute-start | bytes 405512 | tf_op jit(solution)/shard_map/ppermute | solution.py:28
  10.2 11.9 %collective-permute-start.1 = (bf16[1,768,128]{2,1,0:T(8,128)(2,1)}, bf16[1,768,128]{2,1,0:T(8,128)(2,1)S(1)}, u32[]{:S(2)}, u32[]{:S(2)}) collective-permute-start(bf16[1,768,128]{2,1,0:T(8,128)(2,1)} %bitcast.13), channel_id=1, source_target_pairs={{0,2},{1,3},{2,0},{3,1},{4,6},{5,7},{6,4},{7,5},{8,10},{9,11},{10,... | collective-permute-start | bytes 589832 | tf_op jit(solution)/shard_map/ppermute | solution.py:28
  14.5 8.1 %collective-permute-start.5 = (bf16[1,768,128]{2,1,0:T(8,128)(2,1)S(1)}, bf16[1,768,128]{2,1,0:T(8,128)(2,1)S(1)}, u32[]{:S(2)}, u32[]{:S(2)}) collective-permute-start(bf16[1,768,128]{2,1,0:T(8,128)(2,1)S(1)} %bitcast.9), channel_id=1, source_target_pairs={{0,2},{1,3},{2,0},{3,1},{4,6},{5,7},{6,4},{7,5},{8,10},{9,11},{10,... | collective-permute-start | bytes 589832 | tf_op jit(solution)/shard_map/ppermute | solution.py:28
  16.2 0.9 %copy-start = (bf16[768,128]{1,0:T(8,128)(2,1)S(1)}, bf16[768,128]{1,0:T(8,128)(2,1)}, u32[]{:S(2)}) copy-start(bf16[768,128]{1,0:T(8,128)(2,1)} %get-tuple-element.23) | copy-start | bytes 589828
  17.2 0.9 %copy-start.1 = (bf16[272,128]{1,0:T(8,128)(2,1)S(1)}, bf16[272,128]{1,0:T(8,128)(2,1)}, u32[]{:S(2)}) copy-start(bf16[272,128]{1,0:T(8,128)(2,1)} %get-tuple-element.24.refs_1_) | copy-start | bytes 208900
  18.1 4.6 %collective-permute-start = (bf16[1,768,128]{2,1,0:T(8,128)(2,1)S(1)}, bf16[1,768,128]{2,1,0:T(8,128)(2,1)S(1)}, u32[]{:S(2)}, u32[]{:S(2)}) collective-permute-start(bf16[1,768,128]{2,1,0:T(8,128)(2,1)S(1)} %get-tuple-element.25.refs_0_), channel_id=1, source_target_pairs={{0,1},{1,0},{2,3},{3,2},{4,5},{5,4},{6,7},{7,6},{8,9},{9,8},{10,11... | collective-permute-start | bytes 589832 | tf_op jit(solution)/shard_map/ppermute | solution.py:28
  20.5 5.0 %collective-permute-start.11 = (bf16[2,256,128]{2,1,0:T(8,128)(2,1)S(1)}, bf16[2,256,128]{2,1,0:T(8,128)(2,1)S(1)}, u32[]{:S(2)}, u32[]{:S(2)}) collective-permute-start(bf16[2,256,128]{2,1,0:T(8,128)(2,1)S(1)} %join.1.refs_9_.refs_11_), channel_id=1, source_target_pairs={{0,2},{1,3},{2,0},{3,1},{4,6},{5,7},{6,4},{7,5},{8,10},{9,11},{10,... | collective-permute-start | bytes 393224 | tf_op jit(solution)/shard_map/ppermute | solution.py:28
  22.1 3.5 %collective-permute-start.4 = (bf16[1,768,128]{2,1,0:T(8,128)(2,1)S(1)}, bf16[1,768,128]{2,1,0:T(8,128)(2,1)S(1)}, u32[]{:S(2)}, u32[]{:S(2)}) collective-permute-start(bf16[1,768,128]{2,1,0:T(8,128)(2,1)S(1)} %bitcast.10), channel_id=1, source_target_pairs={{0,1},{1,0},{2,3},{3,2},{4,5},{5,4},{6,7},{7,6},{8,9},{9,8},{10,11... | collective-permute-start | bytes 589832 | tf_op jit(solution)/shard_map/ppermute | solution.py:28
  22.1 3.4 %collective-permute-start.2 = (bf16[1,768,128]{2,1,0:T(8,128)(2,1)S(1)}, bf16[1,768,128]{2,1,0:T(8,128)(2,1)S(1)}, u32[]{:S(2)}, u32[]{:S(2)}) collective-permute-start(bf16[1,768,128]{2,1,0:T(8,128)(2,1)S(1)} %collective-permute-done.1.refs_2_), channel_id=1, source_target_pairs={{0,1},{1,0},{2,3},{3,2},{4,5},{5,4},{6,7},{7,6},{8,9},{9,8},{10,11... | collective-permute-start | bytes 589832 | tf_op jit(solution)/shard_map/ppermute | solution.py:28
  22.6 2.9 %collective-permute-start.6 = (bf16[1,768,128]{2,1,0:T(8,128)(2,1)S(1)}, bf16[1,768,128]{2,1,0:T(8,128)(2,1)S(1)}, u32[]{:S(2)}, u32[]{:S(2)}) collective-permute-start(bf16[1,768,128]{2,1,0:T(8,128)(2,1)S(1)} %collective-permute-done.5.refs_6_), channel_id=1, source_target_pairs={{0,1},{1,0},{2,3},{3,2},{4,5},{5,4},{6,7},{7,6},{8,9},{9,8},{10,11... | collective-permute-start | bytes 589832 | tf_op jit(solution)/shard_map/ppermute | solution.py:28
  22.7 2.9 %collective-permute-start.10 = (bf16[2,256,128]{2,1,0:T(8,128)(2,1)S(1)}, bf16[2,256,128]{2,1,0:T(8,128)(2,1)S(1)}, u32[]{:S(2)}, u32[]{:S(2)}) collective-permute-start(bf16[2,256,128]{2,1,0:T(8,128)(2,1)S(1)} %join.1.refs_9_.refs_11_), channel_id=1, source_target_pairs={{0,1},{1,0},{2,3},{3,2},{4,5},{5,4},{6,7},{7,6},{8,9},{9,8},{10,11... | collective-permute-start | bytes 393224 | tf_op jit(solution)/shard_map/ppermute | solution.py:28
  25.5 2.2 %collective-permute-start.12 = (bf16[2,256,128]{2,1,0:T(8,128)(2,1)S(1)}, bf16[2,256,128]{2,1,0:T(8,128)(2,1)S(1)}, u32[]{:S(2)}, u32[]{:S(2)}) collective-permute-start(bf16[2,256,128]{2,1,0:T(8,128)(2,1)S(1)} %collective-permute-done.11.refs_11_.refs_13_), channel_id=1, source_target_pairs={{0,1},{1,0},{2,3},{3,2},{4,5},{5,4},{6,7},{7,6},{8,9},{9,8},{10,11... | collective-permute-start | bytes 393224 | tf_op jit(solution)/shard_map/ppermute | solution.py:28
  28.1 6.0 %collective-permute-start.15 = (bf16[8,16,128]{2,1,0:T(8,128)(2,1)S(1)}, bf16[8,16,128]{2,1,0:T(8,128)(2,1)S(1)}, u32[]{:S(2)}, u32[]{:S(2)}) collective-permute-start(bf16[8,16,128]{2,1,0:T(8,128)(2,1)S(1)} %get-tuple-element.40), channel_id=1, source_target_pairs={{0,12},{1,13},{2,14},{3,15},{4,8},{5,9},{6,10},{7,11},{8,4},{9,5},... | collective-permute-start | bytes 98312 | tf_op jit(solution)/shard_map/ppermute | solution.py:28
  30.7 5.0 %collective-permute-start.14 = (bf16[8,16,128]{2,1,0:T(8,128)(2,1)S(1)}, bf16[8,16,128]{2,1,0:T(8,128)(2,1)S(1)}, u32[]{:S(2)}, u32[]{:S(2)}) collective-permute-start(bf16[8,16,128]{2,1,0:T(8,128)(2,1)S(1)} %get-tuple-element.39), channel_id=1, source_target_pairs={{0,8},{1,9},{2,10},{3,11},{4,12},{5,13},{6,14},{7,15},{8,0},{9,1},... | collective-permute-start | bytes 98312 | tf_op jit(solution)/shard_map/ppermute | solution.py:28
  31.3 4.3 %collective-permute-start.13 = (bf16[8,16,128]{2,1,0:T(8,128)(2,1)S(1)}, bf16[8,16,128]{2,1,0:T(8,128)(2,1)S(1)}, u32[]{:S(2)}, u32[]{:S(2)}) collective-permute-start(bf16[8,16,128]{2,1,0:T(8,128)(2,1)S(1)} %get-tuple-element.38), channel_id=1, source_target_pairs={{0,4},{1,5},{2,6},{3,7},{4,0},{5,1},{6,2},{7,3},{8,12},{9,13},{10,... | collective-permute-start | bytes 98312 | tf_op jit(solution)/shard_map/ppermute | solution.py:28

commit v8 on v7

--- a/solution.py
+++ b/solution.py
@@ -68,6 +68,8 @@
     for slot in range(slots):
         hits = jnp.sum((routes_ref[...] == slot ^ me).astype(jnp.int32), axis=1, keepdims=True)
         named = [jnp.where(lane == slot ^ k * PLANE, hits, there) for k, there in enumerate(named)]
+        handed_on = 2 * slots + (slot ^ (planes - 1) * PLANE)
+        named[planes // 2] = jnp.where(lane == handed_on, hits, named[planes // 2])
     own_lane = lax.broadcasted_iota(jnp.int32, (pieces, pieces), 0) == lax.broadcasted_iota(jnp.int32, (pieces, pieces), 1)
     picks = jnp.zeros((pieces, LANES), jnp.int32)
     for m in range(merges):
@@ -76,7 +78,7 @@
         pick = jnp.sum(jnp.where(own_lane, jnp.broadcast_to(pick, (pieces, pieces)), 0), axis=1, keepdims=True)
         picks += (lane == pick).astype(jnp.int32)
     inward[1].wait()
-    for k in range(planes):
+    for k in range(planes - 1):
         message, start = (planes + k, 0) if k < 2 else (k, part)
         stage, high = stages[message], plane // 2 ^ k // 2
         rest = jnp.zeros((HEAD - pieces, LANES), jnp.float32)
@@ -126,24 +128,30 @@
 
 
 def join_kernel(*refs):
-    for k, ref in enumerate(refs[:-1]):
-        refs[-1][k] = ref[:refs[-1].shape[1]]
+    *packs, group, rest = refs
+    size = group.shape[1]
+    for k, pack in enumerate(packs):
+        group[k] = pack[:size]
+    rest[...] = packs[0][size:]
 
 
 def join(packs, size):
     vmem = pl.BlockSpec(memory_space=pltpu.VMEM)
     return pl.pallas_call(
         join_kernel,
-        out_shape=jax.ShapeDtypeStruct((len(packs), size) + packs[0].shape[1:], packs[0].dtype),
+        out_shape=[
+            jax.ShapeDtypeStruct((len(packs), size) + packs[0].shape[1:], packs[0].dtype),
+            jax.ShapeDtypeStruct((packs[0].shape[0] - size,) + packs[0].shape[1:], packs[0].dtype),
+        ],
         in_specs=[vmem] * len(packs),
-        out_specs=vmem,
+        out_specs=[vmem] * 2,
         compiler_params=pltpu.CompilerParams(vmem_limit_bytes=VMEM_BYTES),
         cost_estimate=pl.CostEstimate(flops=0, bytes_accessed=2 ** 12, transcendentals=0),
         name="join",
     )(*packs)
 
 
-def front_kernel(planes, slots, order, blocks, pieces, rows_piece, held, *refs):
+def front_kernel(planes, handed_on, slots, order, blocks, pieces, rows_piece, held, *refs):
     relays, packs = refs[:2 * PLANE], refs[2 * PLANE:2 * PLANE + planes]
     closing = refs[2 * PLANE + planes:-7]
     state, named, sums, forms, high, low, wide = refs[-7:]
@@ -157,6 +165,9 @@
     for k in range(planes):
         first = packs[k].shape[0] - tail
         numbers = packs[k][first:first + HEAD].astype(jnp.float32)
+        if k == handed_on:
+            lane = lax.broadcasted_iota(jnp.int32, numbers.shape, 1)
+            numbers = jnp.where(lane < slots, pltpu.roll(numbers, LANES - 2 * slots, 1), numbers)
         for n in range(pieces):
             here = slice((k * pieces + n) * rows_piece, (k * pieces + n + 1) * rows_piece)
             named[here, :] = jnp.broadcast_to(numbers[n:n + 1], (rows_piece, LANES))
@@ -206,14 +217,14 @@
 def close(order, named, state, relays, sums, wide):
     part, rows = wide.shape[0] // 2, state.shape[0]
     lane = lax.broadcasted_iota(jnp.int32, (part, LANES), 1)
+    sign = jnp.where(lane < LANES // 2, -1.0, 1.0).astype(jnp.bfloat16)
     slot = 0
     for relay in relays:
         for k in range(relay.shape[0]):
             real_rows = relay[k, relay.shape[1] - part:]
-            turned = pltpu.roll(real_rows.astype(jnp.float32), LANES // 2, 1)
-            turned = jnp.where(lane < LANES // 2, -turned, turned)
+            turned = pltpu.roll(real_rows, LANES // 2, 1) * sign
             wide[:part, slot * LANES:(slot + 1) * LANES] = real_rows
-            wide[part:, slot * LANES:(slot + 1) * LANES] = turned.astype(jnp.bfloat16)
+            wide[part:, slot * LANES:(slot + 1) * LANES] = turned
             slot += 1
     for j in range(0, slot, 2):
         both = jnp.dot(state[...], wide[:, j * LANES:(j + 2) * LANES], preferred_element_type=jnp.float32)
@@ -253,7 +264,7 @@
         merge_count[None],
         routes,
     )
-    sizes = [relayed] * 2 + [part + tail] * (planes - 2) + [tail] * 2
+    sizes = [relayed] * 2 + [part + tail, part] + [tail] * 2
     anywhere = pl.BlockSpec(memory_space=pl.ANY)
     packs = pl.pallas_call(
         functools.partial(pack_kernel, planes, pair_prefix.shape[1], held),
@@ -262,22 +273,23 @@
         out_specs=[anywhere] * len(sizes),
         scratch_shapes=[pltpu.VMEM((size, LANES), jnp.bfloat16) for size in sizes]
         + [pltpu.VMEM(source.shape, source.dtype) for source in sources]
-        + [pltpu.SemaphoreType.DMA((len(sources) + 2 + 2 * planes,))],
+        + [pltpu.SemaphoreType.DMA((len(sources) + 1 + 2 * planes,))],
         compiler_params=pltpu.CompilerParams(vmem_limit_bytes=PACK_BYTES),
         cost_estimate=pl.CostEstimate(flops=2 ** 20, bytes_accessed=2 ** 12, transcendentals=0),
         name="pack",
     )(*sources)
     far = [swap(packs[k], k * PLANE) for k in range(2, planes)]
     near = swap(packs[planes + 1], PLANE)
-    relays = [packs[0][None], swap(packs[1], PLANE)[None], join([after(far[0], near)] + far[1:], part)]
+    group, rest = join(far, part)
+    handed = swap(rest, PLANE)
+    relays = [packs[0][None], swap(packs[1], PLANE)[None], group]
     own, local = own_copy(relays[0], packs[planes])
-    across = [swap(r, 2) for r in relays[:2]]
+    across = [swap(r, 2) for r in relays]
     relays[0] = own
-    packs = [local, near] + far
-    beside = [swap(r, 1) for r in relays]
-    corner = [swap(y, 1) for y in across]
-    across.append(swap(relays[2], 2))
-    corner.append(swap(across[2], 1))
+    packs = [local, near, far[0], handed]
+    beside = [swap(relays[0], 1), None, swap(after(relays[2], near), 1)]
+    beside[1] = swap(after(relays[1], beside[2]), 1)
+    corner = [swap(across[0], 1), swap(after(across[1], handed), 1), swap(across[2], 1)]
     early = 2 * PLANE
     far_slots = range(early, owners, PLANE)
     order = list(range(early)) + [k + n for n in (0, 1, 2) for k in far_slots]
@@ -290,7 +302,7 @@
         rows = count * pieces * rows_piece
         operands = relays[:early] + [packs[k] for k in chosen] + relays[early:]
         state, named, sums = pl.pallas_call(
-            functools.partial(front_kernel, count, owners, order, blocks, pieces, rows_piece, held),
+            functools.partial(front_kernel, count, list(chosen).index(planes - 1) if planes - 1 in chosen else None, owners, order, blocks, pieces, rows_piece, held),
             out_shape=[
                 jax.ShapeDtypeStruct((rows, 2 * part), jnp.bfloat16),
                 jax.ShapeDtypeStruct((rows, LANES), jnp.float32),
@@ -406,9 +418,8 @@
     depth, width = first_suffix.shape[2:]
     pieces = pair_prefix.shape[0]
     fits = (
-        planes > 2
-        and planes & (planes - 1) == 0
-        and owners <= 256
+        planes == 4
+        and owners == planes * PLANE
         and width == owners * depth
         and width % (planes // 2 * LANES) == 0
         and width // 2 % LANES == 0
@@ -416,7 +427,8 @@
         and depth % 16 == 0
         and prefix.shape[1] % 16 == 0
         and pieces <= HEAD
-        and owners + first_suffix.shape[0] * prefix.shape[0] <= LANES
+        and first_suffix.shape[0] * prefix.shape[0] <= owners
+        and 3 * owners <= LANES
     )
     return in_planes(*args) if fits else by_owner(*args)
 

time: 36.5 us -> 36 us (0.986)
  local copies, waits for them, and re-layouts: 1.81 us -> 0.89 us
  waiting for transfers between devices: 9.18 us -> 9.61 us
    unnamed x4, local copies, waits for them, and re-layouts: 1.81 us -> 0.89 us
    ppermute x16 -> x17, waiting for transfers between devices: 9.18 us -> 9.61 us  [swap(): return lax.ppermute(x, 'bits', [(i, i ^ bit) for i in range(owners)])]
    ppermute x16 -> x17, starting transfers between devices: 17.8 us -> 18 us  [swap(): return lax.ppermute(x, 'bits', [(i, i ^ bit) for i in range(owners)])]
  transfers between devices with their start and end apart: 16 -> 17, of which waited for: 4 -> 9; matrix products, arithmetic and copies ran while one was open for 0% -> 0% of each run, Pallas kernels for 10% -> 10%
where the time goes in v8:
time: 36 us; the launch traced here: 35.9 us
  starting transfers between devices  18 us (50%)
  waiting for transfers between devices  9.61 us (27%)
  Pallas kernels  6.65 us (18%)
  local copies, waits for them, and re-layouts  0.89 us (2%)
  other arithmetic  0.65 us (2%)
    ppermute x17, starting transfers between devices, swap(): return lax.ppermute(x, 'bits', [(i, i ^ bit) for i in range(owners)])  18 us
    ppermute x17, waiting for transfers between devices, swap(): return lax.ppermute(x, 'bits', [(i, i ^ bit) for i in range(owners)])  9.61 us
    pallas_call x2, Pallas kernels, sums_of(): pl.pallas_call(functools.partial(front_kernel, count, list(chosen).index(...  3.3 us
    pallas_call x1, Pallas kernels, in_planes(): pl.pallas_call(functools.partial(pack_kernel, planes, pair_prefix.shape[1...  2.68 us
    unnamed x4, local copies, waits for them, and re-layouts  0.89 us
  transfers between devices with their start and end apart: 17, of which 9 were waited for; matrix products, arithmetic and copies ran while one was open for 0% of the time, Pallas kernels for 10%

profile of v8, /device:TPU:0, one launch (start us, length us, event | category | flops | bytes accessed | tf_op | source)
XLA Modules:
  0.0 35.9 jit_solution(5005224555875916180)
XLA Ops:
  0.0 2.7 %pack.1 = (bf16[768,128]{1,0:T(8,128)(2,1)}, bf16[768,128]{1,0:T(8,128)(2,1)}, bf16[528,128]{1,0:T(8,128)(2,1)}, bf16[256,128]{1,0:T(8,128)(2,1)}, bf16[272,128]{1,0:T(8,128)(2,1)}, /*index=5*/bf16[272,128]{1,0:T(8,128)(2,1)}) custom-call(bf16[256,512]{1,0:T(8,128)(2,1)} %bitcast.16, bf16[64,1024]{1,0:T(8,128)(2,1)} %bitcast.17, ...), custom_call_target="tpu_custom_call" | custom-call | flops 1048576 | bytes 4096 | tf_op jit(solution)/shard_map/pack/pallas_call | solution.py:269
  2.7 0.0 copy-start
  2.7 3.1 %collective-permute-start.3 = (bf16[768,128]{1,0:T(8,128)(2,1)}, bf16[768,128]{1,0:T(8,128)(2,1)S(1)}, u32[]{:S(2)}, u32[]{:S(2)}) collective-permute-start(bf16[768,128]{1,0:T(8,128)(2,1)} %get-tuple-element.30), channel_id=1, source_target_pairs={{0,4},{1,5},{2,6},{3,7},{4,0},{5,1},{6,2},{7,3},{8,12},{9,13},{10,... | collective-permute-start | bytes 589832 | tf_op jit(solution)/shard_map/ppermute | solution.py:28
  5.8 2.6 %collective-permute-start.4 = (bf16[528,128]{1,0:T(8,128)(2,1)}, bf16[528,128]{1,0:T(8,128)(2,1)S(1)}, u32[]{:S(2)}, u32[]{:S(2)}) collective-permute-start(bf16[528,128]{1,0:T(8,128)(2,1)} %get-tuple-element.31), channel_id=1, source_target_pairs={{0,8},{1,9},{2,10},{3,11},{4,12},{5,13},{6,14},{7,15},{8,0},{9,1},... | collective-permute-start | bytes 405512 | tf_op jit(solution)/shard_map/ppermute | solution.py:28
  8.4 0.5 %collective-permute-start.6 = (bf16[272,128]{1,0:T(8,128)(2,1)}, bf16[272,128]{1,0:T(8,128)(2,1)S(1)}, u32[]{:S(2)}, u32[]{:S(2)}) collective-permute-start(bf16[272,128]{1,0:T(8,128)(2,1)} %get-tuple-element.34), channel_id=1, source_target_pairs={{0,4},{1,5},{2,6},{3,7},{4,0},{5,1},{6,2},{7,3},{8,12},{9,13},{10,... | collective-permute-start | bytes 208904 | tf_op jit(solution)/shard_map/ppermute | solution.py:28
  8.8 1.4 %collective-permute-start.5 = (bf16[256,128]{1,0:T(8,128)(2,1)}, bf16[256,128]{1,0:T(8,128)(2,1)S(1)}, u32[]{:S(2)}, u32[]{:S(2)}) collective-permute-start(bf16[256,128]{1,0:T(8,128)(2,1)} %get-tuple-element.32), channel_id=1, source_target_pairs={{0,12},{1,13},{2,14},{3,15},{4,8},{5,9},{6,10},{7,11},{8,4},{9,5},... | collective-permute-start | bytes 196616 | tf_op jit(solution)/shard_map/ppermute | solution.py:28
  10.2 1.5 %collective-permute-start.1 = (bf16[1,768,128]{2,1,0:T(8,128)(2,1)}, bf16[1,768,128]{2,1,0:T(8,128)(2,1)S(1)}, u32[]{:S(2)}, u32[]{:S(2)}) collective-permute-start(bf16[1,768,128]{2,1,0:T(8,128)(2,1)} %bitcast.13), channel_id=1, source_target_pairs={{0,2},{1,3},{2,0},{3,1},{4,6},{5,7},{6,4},{7,5},{8,10},{9,11},{10,... | collective-permute-start | bytes 589832 | tf_op jit(solution)/shard_map/ppermute | solution.py:28
  11.7 2.8 %collective-permute-done.3 = bf16[768,128]{1,0:T(8,128)(2,1)S(1)} collective-permute-done((bf16[768,128]{1,0:T(8,128)(2,1)}, bf16[768,128]{1,0:T(8,128)(2,1)S(1)}, u32[]{:S(2)}, u32[]{:S(2)}) %collective-permute-start.3) | collective-permute-done | bytes 196640 | tf_op jit(solution)/shard_map/ppermute | solution.py:28
  14.5 1.7 %collective-permute-start.9 = (bf16[1,768,128]{2,1,0:T(8,128)(2,1)S(1)}, bf16[1,768,128]{2,1,0:T(8,128)(2,1)S(1)}, u32[]{:S(2)}, u32[]{:S(2)}) collective-permute-start(bf16[1,768,128]{2,1,0:T(8,128)(2,1)S(1)} %bitcast.9), channel_id=1, source_target_pairs={{0,2},{1,3},{2,0},{3,1},{4,6},{5,7},{6,4},{7,5},{8,10},{9,11},{10,... | collective-permute-start | bytes 589832 | tf_op jit(solution)/shard_map/ppermute | solution.py:28
  16.2 2.6 %collective-permute-done.5.refs_1_ = bf16[256,128]{1,0:T(8,128)(2,1)S(1)} collective-permute-done((bf16[256,128]{1,0:T(8,128)(2,1)}, bf16[256,128]{1,0:T(8,128)(2,1)S(1)}, u32[]{:S(2)}, u32[]{:S(2)}) %collective-permute-start.5) | collective-permute-done | bytes 65568 | tf_op jit(solution)/shard_map/ppermute | solution.py:28
  18.9 0.0 collective-permute-done.4.refs_0_.refs_9_
  18.9 0.0 collective-permute-done.6.refs_8_
  18.9 0.1 collective-permute-start.7
  19.0 0.1 collective-permute-start.10
  19.1 1.6 %collective-permute-start.12 = (bf16[2,256,128]{2,1,0:T(8,128)(2,1)S(1)}, bf16[2,256,128]{2,1,0:T(8,128)(2,1)S(1)}, u32[]{:S(2)}, u32[]{:S(2)}) collective-permute-start(bf16[2,256,128]{2,1,0:T(8,128)(2,1)S(1)} %get-tuple-element.35.refs_9_.refs_11_), channel_id=1, source_target_pairs={{0,2},{1,3},{2,0},{3,1},{4,6},{5,7},{6,4},{7,5},{8,10},{9,11},{10,... | collective-permute-start | bytes 393224 | tf_op jit(solution)/shard_map/ppermute | solution.py:28
  20.6 0.0 copy-done
  20.7 0.0 copy-start.1
  20.7 0.9 %copy-done.1 = bf16[272,128]{1,0:T(8,128)(2,1)S(1)} copy-done((bf16[272,128]{1,0:T(8,128)(2,1)S(1)}, bf16[272,128]{1,0:T(8,128)(2,1)}, u32[]{:S(2)}) %copy-start.1) | copy-done | bytes 69656
  21.6 0.0 collective-permute-done.1.refs_2_
  21.6 0.1 collective-permute-start
  21.7 0.0 collective-permute-done.7.refs_10_.refs_12_
  21.7 0.4 %collective-permute-start.2 = (bf16[1,768,128]{2,1,0:T(8,128)(2,1)S(1)}, bf16[1,768,128]{2,1,0:T(8,128)(2,1)S(1)}, u32[]{:S(2)}, u32[]{:S(2)}) collective-permute-start(bf16[1,768,128]{2,1,0:T(8,128)(2,1)S(1)} %collective-permute-done.1.refs_2_), channel_id=1, source_target_pairs={{0,1},{1,0},{2,3},{3,2},{4,5},{5,4},{6,7},{7,6},{8,9},{9,8},{10,11... | collective-permute-start | bytes 589832 | tf_op jit(solution)/shard_map/ppermute | solution.py:28
  22.1 1.4 %collective-permute-done.10.refs_10_ = bf16[272,128]{1,0:T(8,128)(2,1)S(1)} collective-permute-done((bf16[272,128]{1,0:T(8,128)(2,1)S(1)}, bf16[272,128]{1,0:T(8,128)(2,1)S(1)}, u32[]{:S(2)}, u32[]{:S(2)}) %collective-permute-start.10) | collective-permute-done | bytes 69664 | tf_op jit(solution)/shard_map/ppermute | solution.py:28
  23.6 0.0 collective-permute-start.8
  23.6 0.0 collective-permute-done.9.refs_6_
  23.6 0.5 %collective-permute-start.11 = (bf16[1,768,128]{2,1,0:T(8,128)(2,1)S(1)}, bf16[1,768,128]{2,1,0:T(8,128)(2,1)S(1)}, u32[]{:S(2)}, u32[]{:S(2)}) collective-permute-start(bf16[1,768,128]{2,1,0:T(8,128)(2,1)S(1)} %collective-permute-done.9.refs_6_), channel_id=1, source_target_pairs={{0,1},{1,0},{2,3},{3,2},{4,5},{5,4},{6,7},{7,6},{8,9},{9,8},{10,11... | collective-permute-start | bytes 589832 | tf_op jit(solution)/shard_map/ppermute | solution.py:28
  24.1 0.8 %collective-permute-done.12.refs_11_.refs_13_ = bf16[2,256,128]{2,1,0:T(8,128)(2,1)S(1)} collective-permute-done((bf16[2,256,128]{2,1,0:T(8,128)(2,1)S(1)}, bf16[2,256,128]{2,1,0:T(8,128)(2,1)S(1)}, u32[]{:S(2)}, u32[]{:S(2)}) %collective-permute-start.12) | collective-permute-done | bytes 131104 | tf_op jit(solution)/shard_map/ppermute | solution.py:28
  24.9 0.0 collective-permute-start.13
  24.9 0.0 collective-permute-done.refs_1_
  24.9 0.0 collective-permute-done.2.refs_3_
  24.9 0.1 collective-permute-done.8.refs_5_
  25.0 0.3 collective-permute-done.11.refs_7_
  25.3 2.1 %front.3 = (bf16[384,512]{1,0:T(8,128)(2,1)S(1)}, f32[384,128]{1,0:T(8,128)S(1)}, f32[384,128]{1,0:T(8,128)S(1)}) custom-call(bf16[1,768,128]{2,1,0:T(8,128)(2,1)S(1)} %get-tuple-element.29.refs_0_, bf16[1,768,128]{2,1,0:T(8,128)(2,1)S(1)} %collective-permute-done.refs_1_, bf16[1,768,128]{2,1,0:T(8,128)(2,1)S(1)} %collective-permute-done.1.refs_2_, ...), custom_call_target="tpu_custom_call" | custom-call | bytes 4096 | tf_op jit(solution)/shard_map/front/pallas_call | solution.py:304
  27.4 0.0 collective-permute-done.13.relay
  27.5 0.4 %last.3 = (bf16[8,16,128]{2,1,0:T(8,128)(2,1)S(1)}, bf16[8,16,128]{2,1,0:T(8,128)(2,1)S(1)}, bf16[8,16,128]{2,1,0:T(8,128)(2,1)S(1)}) custom-call(f32[384,128]{1,0:T(8,128)S(1)} %get-tuple-element.43.named, bf16[384,512]{1,0:T(8,128)(2,1)S(1)} %get-tuple-element.44.state, f32[384,128]{1,0:T(8,128)S(1)} %get-tuple-element.45.sums_in, ...), custom_call_target="tpu_custom_call" | custom-call | bytes 4096 | tf_op jit(solution)/shard_map/last/pallas_call | solution.py:323
  27.8 2.2 %collective-permute-start.16 = (bf16[8,16,128]{2,1,0:T(8,128)(2,1)S(1)}, bf16[8,16,128]{2,1,0:T(8,128)(2,1)S(1)}, u32[]{:S(2)}, u32[]{:S(2)}) collective-permute-start(bf16[8,16,128]{2,1,0:T(8,128)(2,1)S(1)} %get-tuple-element.48), channel_id=1, source_target_pairs={{0,12},{1,13},{2,14},{3,15},{4,8},{5,9},{6,10},{7,11},{8,4},{9,5},... | collective-permute-start | bytes 98312 | tf_op jit(solution)/shard_map/ppermute | solution.py:28
  30.0 0.7 %collective-permute-start.15 = (bf16[8,16,128]{2,1,0:T(8,128)(2,1)S(1)}, bf16[8,16,128]{2,1,0:T(8,128)(2,1)S(1)}, u32[]{:S(2)}, u32[]{:S(2)}) collective-permute-start(bf16[8,16,128]{2,1,0:T(8,128)(2,1)S(1)} %get-tuple-element.47), channel_id=1, source_target_pairs={{0,8},{1,9},{2,10},{3,11},{4,12},{5,13},{6,14},{7,15},{8,0},{9,1},... | collective-permute-start | bytes 98312 | tf_op jit(solution)/shard_map/ppermute | solution.py:28
  30.7 1.5 %collective-permute-start.14 = (bf16[8,16,128]{2,1,0:T(8,128)(2,1)S(1)}, bf16[8,16,128]{2,1,0:T(8,128)(2,1)S(1)}, u32[]{:S(2)}, u32[]{:S(2)}) collective-permute-start(bf16[8,16,128]{2,1,0:T(8,128)(2,1)S(1)} %get-tuple-element.46), channel_id=1, source_target_pairs={{0,4},{1,5},{2,6},{3,7},{4,0},{5,1},{6,2},{7,3},{8,12},{9,13},{10,... | collective-permute-start | bytes 98312 | tf_op jit(solution)/shard_map/ppermute | solution.py:28
  32.3 1.2 %front.2 = (bf16[128,512]{1,0:T(8,128)(2,1)S(1)}, f32[128,128]{1,0:T(8,128)S(1)}, f32[128,128]{1,0:T(8,128)S(1)}) custom-call(bf16[1,768,128]{2,1,0:T(8,128)(2,1)S(1)} %get-tuple-element.29.refs_0_, bf16[1,768,128]{2,1,0:T(8,128)(2,1)S(1)} %collective-permute-done.refs_1_, bf16[1,768,128]{2,1,0:T(8,128)(2,1)S(1)} %collective-permute-done.1.refs_2_, ...), custom_call_target="tpu_custom_call" | custom-call | bytes 4096 | tf_op jit(solution)/shard_map/front/pallas_call | solution.py:304
  33.4 0.3 last.2
  33.7 0.2 collective-permute-done.16
  33.9 1.0 %collective-permute-done.15 = bf16[8,16,128]{2,1,0:T(8,128)(2,1)S(1)} collective-permute-done((bf16[8,16,128]{2,1,0:T(8,128)(2,1)S(1)}, bf16[8,16,128]{2,1,0:T(8,128)(2,1)S(1)}, u32[]{:S(2)}, u32[]{:S(2)}) %collective-permute-start.15) | collective-permute-done | bytes 32800 | tf_op jit(solution)/shard_map/ppermute | solution.py:28
  34.9 0.3 collective-permute-done.14
  35.2 0.6 %convert_add_fusion = f32[8,16,128]{2,1,0:T(8,128)} fusion(bf16[8,16,128]{2,1,0:T(8,128)(2,1)S(1)} %collective-permute-done.16, bf16[8,16,128]{2,1,0:T(8,128)(2,1)S(1)} %collective-permute-done.15, f32[8,16,128]{2,1,0:T(8,128)S(1)} %last.2, bf16[8,16,128]{2,1,0:T(8,128)(2,1)S(1)} %collective-permute-done.14), kind=kLoop, calls=%fused_computation | loop fusion | flops 98304 | bytes 229376 | tf_op jit(solution)/shard_map/add | solution.py:340
  (2 shorter events, 0.0 us)
Async XLA Ops:
  2.7 18.0 %copy-start = (bf16[768,128]{1,0:T(8,128)(2,1)S(1)}, bf16[768,128]{1,0:T(8,128)(2,1)}, u32[]{:S(2)}) copy-start(bf16[768,128]{1,0:T(8,128)(2,1)} %get-tuple-element.27) | copy-start | bytes 589828
  2.7 11.8 %collective-permute-start.3 = (bf16[768,128]{1,0:T(8,128)(2,1)}, bf16[768,128]{1,0:T(8,128)(2,1)S(1)}, u32[]{:S(2)}, u32[]{:S(2)}) collective-permute-start(bf16[768,128]{1,0:T(8,128)(2,1)} %get-tuple-element.30), channel_id=1, source_target_pairs={{0,4},{1,5},{2,6},{3,7},{4,0},{5,1},{6,2},{7,3},{8,12},{9,13},{10,... | collective-permute-start | bytes 589832 | tf_op jit(solution)/shard_map/ppermute | solution.py:28
  5.8 13.1 %collective-permute-start.4 = (bf16[528,128]{1,0:T(8,128)(2,1)}, bf16[528,128]{1,0:T(8,128)(2,1)S(1)}, u32[]{:S(2)}, u32[]{:S(2)}) collective-permute-start(bf16[528,128]{1,0:T(8,128)(2,1)} %get-tuple-element.31), channel_id=1, source_target_pairs={{0,8},{1,9},{2,10},{3,11},{4,12},{5,13},{6,14},{7,15},{8,0},{9,1},... | collective-permute-start | bytes 405512 | tf_op jit(solution)/shard_map/ppermute | solution.py:28
  8.4 10.5 %collective-permute-start.6 = (bf16[272,128]{1,0:T(8,128)(2,1)}, bf16[272,128]{1,0:T(8,128)(2,1)S(1)}, u32[]{:S(2)}, u32[]{:S(2)}) collective-permute-start(bf16[272,128]{1,0:T(8,128)(2,1)} %get-tuple-element.34), channel_id=1, source_target_pairs={{0,4},{1,5},{2,6},{3,7},{4,0},{5,1},{6,2},{7,3},{8,12},{9,13},{10,... | collective-permute-start | bytes 208904 | tf_op jit(solution)/shard_map/ppermute | solution.py:28
  8.8 10.1 %collective-permute-start.5 = (bf16[256,128]{1,0:T(8,128)(2,1)}, bf16[256,128]{1,0:T(8,128)(2,1)S(1)}, u32[]{:S(2)}, u32[]{:S(2)}) collective-permute-start(bf16[256,128]{1,0:T(8,128)(2,1)} %get-tuple-element.32), channel_id=1, source_target_pairs={{0,12},{1,13},{2,14},{3,15},{4,8},{5,9},{6,10},{7,11},{8,4},{9,5},... | collective-permute-start | bytes 196616 | tf_op jit(solution)/shard_map/ppermute | solution.py:28
  10.2 11.4 %collective-permute-start.1 = (bf16[1,768,128]{2,1,0:T(8,128)(2,1)}, bf16[1,768,128]{2,1,0:T(8,128)(2,1)S(1)}, u32[]{:S(2)}, u32[]{:S(2)}) collective-permute-start(bf16[1,768,128]{2,1,0:T(8,128)(2,1)} %bitcast.13), channel_id=1, source_target_pairs={{0,2},{1,3},{2,0},{3,1},{4,6},{5,7},{6,4},{7,5},{8,10},{9,11},{10,... | collective-permute-start | bytes 589832 | tf_op jit(solution)/shard_map/ppermute | solution.py:28
  14.5 9.1 %collective-permute-start.9 = (bf16[1,768,128]{2,1,0:T(8,128)(2,1)S(1)}, bf16[1,768,128]{2,1,0:T(8,128)(2,1)S(1)}, u32[]{:S(2)}, u32[]{:S(2)}) collective-permute-start(bf16[1,768,128]{2,1,0:T(8,128)(2,1)S(1)} %bitcast.9), channel_id=1, source_target_pairs={{0,2},{1,3},{2,0},{3,1},{4,6},{5,7},{6,4},{7,5},{8,10},{9,11},{10,... | collective-permute-start | bytes 589832 | tf_op jit(solution)/shard_map/ppermute | solution.py:28
  18.9 2.8 %collective-permute-start.7 = (bf16[2,256,128]{2,1,0:T(8,128)(2,1)S(1)}, bf16[2,256,128]{2,1,0:T(8,128)(2,1)S(1)}, u32[]{:S(2)}, u32[]{:S(2)}) collective-permute-start(bf16[2,256,128]{2,1,0:T(8,128)(2,1)S(1)} %get-tuple-element.35.refs_9_.refs_11_), channel_id=1, source_target_pairs={{0,1},{1,0},{2,3},{3,2},{4,5},{5,4},{6,7},{7,6},{8,9},{9,8},{10,11... | collective-permute-start | bytes 393224 | tf_op jit(solution)/shard_map/ppermute | solution.py:28
  19.0 4.6 %collective-permute-start.10 = (bf16[272,128]{1,0:T(8,128)(2,1)S(1)}, bf16[272,128]{1,0:T(8,128)(2,1)S(1)}, u32[]{:S(2)}, u32[]{:S(2)}) collective-permute-start(bf16[272,128]{1,0:T(8,128)(2,1)S(1)} %get-tuple-element.37), channel_id=1, source_target_pairs={{0,4},{1,5},{2,6},{3,7},{4,0},{5,1},{6,2},{7,3},{8,12},{9,13},{10,... | collective-permute-start | bytes 208904 | tf_op jit(solution)/shard_map/ppermute | solution.py:28
  19.1 5.8 %collective-permute-start.12 = (bf16[2,256,128]{2,1,0:T(8,128)(2,1)S(1)}, bf16[2,256,128]{2,1,0:T(8,128)(2,1)S(1)}, u32[]{:S(2)}, u32[]{:S(2)}) collective-permute-start(bf16[2,256,128]{2,1,0:T(8,128)(2,1)S(1)} %get-tuple-element.35.refs_9_.refs_11_), channel_id=1, source_target_pairs={{0,2},{1,3},{2,0},{3,1},{4,6},{5,7},{6,4},{7,5},{8,10},{9,11},{10,... | collective-permute-start | bytes 393224 | tf_op jit(solution)/shard_map/ppermute | solution.py:28
  20.7 0.9 %copy-start.1 = (bf16[272,128]{1,0:T(8,128)(2,1)S(1)}, bf16[272,128]{1,0:T(8,128)(2,1)}, u32[]{:S(2)}) copy-start(bf16[272,128]{1,0:T(8,128)(2,1)} %get-tuple-element.28.refs_1_) | copy-start | bytes 208900
  21.6 3.3 %collective-permute-start = (bf16[1,768,128]{2,1,0:T(8,128)(2,1)S(1)}, bf16[1,768,128]{2,1,0:T(8,128)(2,1)S(1)}, u32[]{:S(2)}, u32[]{:S(2)}) collective-permute-start(bf16[1,768,128]{2,1,0:T(8,128)(2,1)S(1)} %get-tuple-element.29.refs_0_), channel_id=1, source_target_pairs={{0,1},{1,0},{2,3},{3,2},{4,5},{5,4},{6,7},{7,6},{8,9},{9,8},{10,11... | collective-permute-start | bytes 589832 | tf_op jit(solution)/shard_map/ppermute | solution.py:28
  21.7 3.2 %collective-permute-start.2 = (bf16[1,768,128]{2,1,0:T(8,128)(2,1)S(1)}, bf16[1,768,128]{2,1,0:T(8,128)(2,1)S(1)}, u32[]{:S(2)}, u32[]{:S(2)}) collective-permute-start(bf16[1,768,128]{2,1,0:T(8,128)(2,1)S(1)} %collective-permute-done.1.refs_2_), channel_id=1, source_target_pairs={{0,1},{1,0},{2,3},{3,2},{4,5},{5,4},{6,7},{7,6},{8,9},{9,8},{10,11... | collective-permute-start | bytes 589832 | tf_op jit(solution)/shard_map/ppermute | solution.py:28
  23.6 1.4 %collective-permute-start.8 = (bf16[1,768,128]{2,1,0:T(8,128)(2,1)S(1)}, bf16[1,768,128]{2,1,0:T(8,128)(2,1)S(1)}, u32[]{:S(2)}, u32[]{:S(2)}) collective-permute-start(bf16[1,768,128]{2,1,0:T(8,128)(2,1)S(1)} %bitcast.10), channel_id=1, source_target_pairs={{0,1},{1,0},{2,3},{3,2},{4,5},{5,4},{6,7},{7,6},{8,9},{9,8},{10,11... | collective-permute-start | bytes 589832 | tf_op jit(solution)/shard_map/ppermute | solution.py:28
  23.6 1.7 %collective-permute-start.11 = (bf16[1,768,128]{2,1,0:T(8,128)(2,1)S(1)}, bf16[1,768,128]{2,1,0:T(8,128)(2,1)S(1)}, u32[]{:S(2)}, u32[]{:S(2)}) collective-permute-start(bf16[1,768,128]{2,1,0:T(8,128)(2,1)S(1)} %collective-permute-done.9.refs_6_), channel_id=1, source_target_pairs={{0,1},{1,0},{2,3},{3,2},{4,5},{5,4},{6,7},{7,6},{8,9},{9,8},{10,11... | collective-permute-start | bytes 589832 | tf_op jit(solution)/shard_map/ppermute | solution.py:28
  24.9 2.6 %collective-permute-start.13 = (bf16[2,256,128]{2,1,0:T(8,128)(2,1)S(1)}, bf16[2,256,128]{2,1,0:T(8,128)(2,1)S(1)}, u32[]{:S(2)}, u32[]{:S(2)}) collective-permute-start(bf16[2,256,128]{2,1,0:T(8,128)(2,1)S(1)} %collective-permute-done.12.refs_11_.refs_13_), channel_id=1, source_target_pairs={{0,1},{1,0},{2,3},{3,2},{4,5},{5,4},{6,7},{7,6},{8,9},{9,8},{10,11... | collective-permute-start | bytes 393224 | tf_op jit(solution)/shard_map/ppermute | solution.py:28
  27.8 6.1 %collective-permute-start.16 = (bf16[8,16,128]{2,1,0:T(8,128)(2,1)S(1)}, bf16[8,16,128]{2,1,0:T(8,128)(2,1)S(1)}, u32[]{:S(2)}, u32[]{:S(2)}) collective-permute-start(bf16[8,16,128]{2,1,0:T(8,128)(2,1)S(1)} %get-tuple-element.48), channel_id=1, source_target_pairs={{0,12},{1,13},{2,14},{3,15},{4,8},{5,9},{6,10},{7,11},{8,4},{9,5},... | collective-permute-start | bytes 98312 | tf_op jit(solution)/shard_map/ppermute | solution.py:28
  30.0 4.9 %collective-permute-start.15 = (bf16[8,16,128]{2,1,0:T(8,128)(2,1)S(1)}, bf16[8,16,128]{2,1,0:T(8,128)(2,1)S(1)}, u32[]{:S(2)}, u32[]{:S(2)}) collective-permute-start(bf16[8,16,128]{2,1,0:T(8,128)(2,1)S(1)} %get-tuple-element.47), channel_id=1, source_target_pairs={{0,8},{1,9},{2,10},{3,11},{4,12},{5,13},{6,14},{7,15},{8,0},{9,1},... | collective-permute-start | bytes 98312 | tf_op jit(solution)/shard_map/ppermute | solution.py:28
  30.7 4.5 %collective-permute-start.14 = (bf16[8,16,128]{2,1,0:T(8,128)(2,1)S(1)}, bf16[8,16,128]{2,1,0:T(8,128)(2,1)S(1)}, u32[]{:S(2)}, u32[]{:S(2)}) collective-permute-start(bf16[8,16,128]{2,1,0:T(8,128)(2,1)S(1)} %get-tuple-element.46), channel_id=1, source_target_pairs={{0,4},{1,5},{2,6},{3,7},{4,0},{5,1},{6,2},{7,3},{8,12},{9,13},{10,... | collective-permute-start | bytes 98312 | tf_op jit(solution)/shard_map/ppermute | solution.py:28

commit v9 on v8

--- a/solution.py
+++ b/solution.py
@@ -287,8 +287,8 @@
     across = [swap(r, 2) for r in relays]
     relays[0] = own
     packs = [local, near, far[0], handed]
-    beside = [swap(relays[0], 1), None, swap(after(relays[2], near), 1)]
-    beside[1] = swap(after(relays[1], beside[2]), 1)
+    far_beside = swap(after(relays[2], near), 1)
+    beside = [swap(after(relays[0], far_beside), 1), swap(relays[1], 1), far_beside]
     corner = [swap(across[0], 1), swap(after(across[1], handed), 1), swap(across[2], 1)]
     early = 2 * PLANE
     far_slots = range(early, owners, PLANE)

time: 36 us -> 36 us (level)
  no operation moved by 1% of the time
where the time goes in v9:
time: 36 us; the launch traced here: 35.8 us
  starting transfers between devices  18 us (50%)
  waiting for transfers between devices  9.59 us (27%)
  Pallas kernels  6.62 us (18%)
  local copies, waits for them, and re-layouts  0.89 us (2%)
  other arithmetic  0.65 us (2%)
    ppermute x17, starting transfers between devices, swap(): return lax.ppermute(x, 'bits', [(i, i ^ bit) for i in range(owners)])  18 us
    ppermute x17, waiting for transfers between devices, swap(): return lax.ppermute(x, 'bits', [(i, i ^ bit) for i in range(owners)])  9.59 us
    pallas_call x2, Pallas kernels, sums_of(): pl.pallas_call(functools.partial(front_kernel, count, list(chosen).index(...  3.27 us
    pallas_call x1, Pallas kernels, in_planes(): pl.pallas_call(functools.partial(pack_kernel, planes, pair_prefix.shape[1...  2.68 us
    unnamed x4, local copies, waits for them, and re-layouts  0.89 us
  transfers between devices with their start and end apart: 17, of which 9 were waited for; matrix products, arithmetic and copies ran while one was open for 0% of the time, Pallas kernels for 10%

profile of v9, /device:TPU:0, one launch (start us, length us, event | category | flops | bytes accessed | tf_op | source)
XLA Modules:
  0.0 35.8 jit_solution(7231618319923080600)
XLA Ops:
  0.0 2.7 %pack.1 = (bf16[768,128]{1,0:T(8,128)(2,1)}, bf16[768,128]{1,0:T(8,128)(2,1)}, bf16[528,128]{1,0:T(8,128)(2,1)}, bf16[256,128]{1,0:T(8,128)(2,1)}, bf16[272,128]{1,0:T(8,128)(2,1)}, /*index=5*/bf16[272,128]{1,0:T(8,128)(2,1)}) custom-call(bf16[256,512]{1,0:T(8,128)(2,1)} %bitcast.16, bf16[64,1024]{1,0:T(8,128)(2,1)} %bitcast.17, ...), custom_call_target="tpu_custom_call" | custom-call | flops 1048576 | bytes 4096 | tf_op jit(solution)/shard_map/pack/pallas_call | solution.py:269
  2.7 0.0 copy-start
  2.7 3.1 %collective-permute-start.7 = (bf16[768,128]{1,0:T(8,128)(2,1)}, bf16[768,128]{1,0:T(8,128)(2,1)S(1)}, u32[]{:S(2)}, u32[]{:S(2)}) collective-permute-start(bf16[768,128]{1,0:T(8,128)(2,1)} %get-tuple-element.36), channel_id=1, source_target_pairs={{0,4},{1,5},{2,6},{3,7},{4,0},{5,1},{6,2},{7,3},{8,12},{9,13},{10,... | collective-permute-start | bytes 589832 | tf_op jit(solution)/shard_map/ppermute | solution.py:28
  5.8 2.6 %collective-permute-start = (bf16[528,128]{1,0:T(8,128)(2,1)}, bf16[528,128]{1,0:T(8,128)(2,1)S(1)}, u32[]{:S(2)}, u32[]{:S(2)}) collective-permute-start(bf16[528,128]{1,0:T(8,128)(2,1)} %get-tuple-element.30), channel_id=1, source_target_pairs={{0,8},{1,9},{2,10},{3,11},{4,12},{5,13},{6,14},{7,15},{8,0},{9,1},... | collective-permute-start | bytes 405512 | tf_op jit(solution)/shard_map/ppermute | solution.py:28
  8.4 0.5 %collective-permute-start.2 = (bf16[272,128]{1,0:T(8,128)(2,1)}, bf16[272,128]{1,0:T(8,128)(2,1)S(1)}, u32[]{:S(2)}, u32[]{:S(2)}) collective-permute-start(bf16[272,128]{1,0:T(8,128)(2,1)} %get-tuple-element.33), channel_id=1, source_target_pairs={{0,4},{1,5},{2,6},{3,7},{4,0},{5,1},{6,2},{7,3},{8,12},{9,13},{10,... | collective-permute-start | bytes 208904 | tf_op jit(solution)/shard_map/ppermute | solution.py:28
  8.8 1.4 %collective-permute-start.1 = (bf16[256,128]{1,0:T(8,128)(2,1)}, bf16[256,128]{1,0:T(8,128)(2,1)S(1)}, u32[]{:S(2)}, u32[]{:S(2)}) collective-permute-start(bf16[256,128]{1,0:T(8,128)(2,1)} %get-tuple-element.31), channel_id=1, source_target_pairs={{0,12},{1,13},{2,14},{3,15},{4,8},{5,9},{6,10},{7,11},{8,4},{9,5},... | collective-permute-start | bytes 196616 | tf_op jit(solution)/shard_map/ppermute | solution.py:28
  10.2 1.5 %collective-permute-start.5 = (bf16[1,768,128]{2,1,0:T(8,128)(2,1)}, bf16[1,768,128]{2,1,0:T(8,128)(2,1)S(1)}, u32[]{:S(2)}, u32[]{:S(2)}) collective-permute-start(bf16[1,768,128]{2,1,0:T(8,128)(2,1)} %bitcast.13), channel_id=1, source_target_pairs={{0,2},{1,3},{2,0},{3,1},{4,6},{5,7},{6,4},{7,5},{8,10},{9,11},{10,... | collective-permute-start | bytes 589832 | tf_op jit(solution)/shard_map/ppermute | solution.py:28
  11.7 2.8 %collective-permute-done.7 = bf16[768,128]{1,0:T(8,128)(2,1)S(1)} collective-permute-done((bf16[768,128]{1,0:T(8,128)(2,1)}, bf16[768,128]{1,0:T(8,128)(2,1)S(1)}, u32[]{:S(2)}, u32[]{:S(2)}) %collective-permute-start.7) | collective-permute-done | bytes 196640 | tf_op jit(solution)/shard_map/ppermute | solution.py:28
  14.5 1.7 %collective-permute-start.9 = (bf16[1,768,128]{2,1,0:T(8,128)(2,1)S(1)}, bf16[1,768,128]{2,1,0:T(8,128)(2,1)S(1)}, u32[]{:S(2)}, u32[]{:S(2)}) collective-permute-start(bf16[1,768,128]{2,1,0:T(8,128)(2,1)S(1)} %bitcast.9), channel_id=1, source_target_pairs={{0,2},{1,3},{2,0},{3,1},{4,6},{5,7},{6,4},{7,5},{8,10},{9,11},{10,... | collective-permute-start | bytes 589832 | tf_op jit(solution)/shard_map/ppermute | solution.py:28
  16.2 2.6 %collective-permute-done.1.refs_1_ = bf16[256,128]{1,0:T(8,128)(2,1)S(1)} collective-permute-done((bf16[256,128]{1,0:T(8,128)(2,1)}, bf16[256,128]{1,0:T(8,128)(2,1)S(1)}, u32[]{:S(2)}, u32[]{:S(2)}) %collective-permute-start.1) | collective-permute-done | bytes 65568 | tf_op jit(solution)/shard_map/ppermute | solution.py:28
  18.9 0.0 collective-permute-done.refs_0_.refs_9_
  18.9 0.0 collective-permute-done.2.refs_8_
  18.9 0.1 collective-permute-start.3
  19.0 0.1 collective-permute-start.10
  19.1 1.6 %collective-permute-start.12 = (bf16[2,256,128]{2,1,0:T(8,128)(2,1)S(1)}, bf16[2,256,128]{2,1,0:T(8,128)(2,1)S(1)}, u32[]{:S(2)}, u32[]{:S(2)}) collective-permute-start(bf16[2,256,128]{2,1,0:T(8,128)(2,1)S(1)} %get-tuple-element.34.refs_9_.refs_11_), channel_id=1, source_target_pairs={{0,2},{1,3},{2,0},{3,1},{4,6},{5,7},{6,4},{7,5},{8,10},{9,11},{10,... | collective-permute-start | bytes 393224 | tf_op jit(solution)/shard_map/ppermute | solution.py:28
  20.6 0.0 copy-done
  20.7 0.0 copy-start.1
  20.7 0.9 %copy-done.1 = bf16[272,128]{1,0:T(8,128)(2,1)S(1)} copy-done((bf16[272,128]{1,0:T(8,128)(2,1)S(1)}, bf16[272,128]{1,0:T(8,128)(2,1)}, u32[]{:S(2)}) %copy-start.1) | copy-done | bytes 69656
  21.6 0.0 collective-permute-done.5.refs_2_
  21.6 0.1 collective-permute-start.8
  21.7 0.0 collective-permute-done.3.refs_10_.refs_12_
  21.7 0.4 %collective-permute-start.6 = (bf16[1,768,128]{2,1,0:T(8,128)(2,1)S(1)}, bf16[1,768,128]{2,1,0:T(8,128)(2,1)S(1)}, u32[]{:S(2)}, u32[]{:S(2)}) collective-permute-start(bf16[1,768,128]{2,1,0:T(8,128)(2,1)S(1)} %collective-permute-done.5.refs_2_), channel_id=1, source_target_pairs={{0,1},{1,0},{2,3},{3,2},{4,5},{5,4},{6,7},{7,6},{8,9},{9,8},{10,11... | collective-permute-start | bytes 589832 | tf_op jit(solution)/shard_map/ppermute | solution.py:28
  22.1 1.4 %collective-permute-done.10.refs_10_ = bf16[272,128]{1,0:T(8,128)(2,1)S(1)} collective-permute-done((bf16[272,128]{1,0:T(8,128)(2,1)S(1)}, bf16[272,128]{1,0:T(8,128)(2,1)S(1)}, u32[]{:S(2)}, u32[]{:S(2)}) %collective-permute-start.10) | collective-permute-done | bytes 69664 | tf_op jit(solution)/shard_map/ppermute | solution.py:28
  23.6 0.0 collective-permute-start.4
  23.6 0.0 collective-permute-done.9.refs_6_
  23.6 0.5 %collective-permute-start.11 = (bf16[1,768,128]{2,1,0:T(8,128)(2,1)S(1)}, bf16[1,768,128]{2,1,0:T(8,128)(2,1)S(1)}, u32[]{:S(2)}, u32[]{:S(2)}) collective-permute-start(bf16[1,768,128]{2,1,0:T(8,128)(2,1)S(1)} %collective-permute-done.9.refs_6_), channel_id=1, source_target_pairs={{0,1},{1,0},{2,3},{3,2},{4,5},{5,4},{6,7},{7,6},{8,9},{9,8},{10,11... | collective-permute-start | bytes 589832 | tf_op jit(solution)/shard_map/ppermute | solution.py:28
  24.1 0.8 %collective-permute-done.12.refs_11_.refs_13_ = bf16[2,256,128]{2,1,0:T(8,128)(2,1)S(1)} collective-permute-done((bf16[2,256,128]{2,1,0:T(8,128)(2,1)S(1)}, bf16[2,256,128]{2,1,0:T(8,128)(2,1)S(1)}, u32[]{:S(2)}, u32[]{:S(2)}) %collective-permute-start.12) | collective-permute-done | bytes 131104 | tf_op jit(solution)/shard_map/ppermute | solution.py:28
  24.9 0.0 collective-permute-start.13
  24.9 0.0 collective-permute-done.6.refs_3_
  24.9 0.0 collective-permute-done.8.refs_5_
  24.9 0.1 collective-permute-done.4.refs_1_
  25.0 0.3 collective-permute-done.11.refs_7_
  25.3 2.1 %front.3 = (bf16[384,512]{1,0:T(8,128)(2,1)S(1)}, f32[384,128]{1,0:T(8,128)S(1)}, f32[384,128]{1,0:T(8,128)S(1)}) custom-call(bf16[1,768,128]{2,1,0:T(8,128)(2,1)S(1)} %get-tuple-element.35.refs_0_, bf16[1,768,128]{2,1,0:T(8,128)(2,1)S(1)} %collective-permute-done.4.refs_1_, bf16[1,768,128]{2,1,0:T(8,128)(2,1)S(1)} %collective-permute-done.5.refs_2_, ...), custom_call_target="tpu_custom_call" | custom-call | bytes 4096 | tf_op jit(solution)/shard_map/front/pallas_call | solution.py:304
  27.4 0.0 collective-permute-done.13.relay
  27.4 0.4 last.3
  27.8 2.2 %collective-permute-start.16 = (bf16[8,16,128]{2,1,0:T(8,128)(2,1)S(1)}, bf16[8,16,128]{2,1,0:T(8,128)(2,1)S(1)}, u32[]{:S(2)}, u32[]{:S(2)}) collective-permute-start(bf16[8,16,128]{2,1,0:T(8,128)(2,1)S(1)} %get-tuple-element.48), channel_id=1, source_target_pairs={{0,12},{1,13},{2,14},{3,15},{4,8},{5,9},{6,10},{7,11},{8,4},{9,5},... | collective-permute-start | bytes 98312 | tf_op jit(solution)/shard_map/ppermute | solution.py:28
  30.0 0.7 %collective-permute-start.15 = (bf16[8,16,128]{2,1,0:T(8,128)(2,1)S(1)}, bf16[8,16,128]{2,1,0:T(8,128)(2,1)S(1)}, u32[]{:S(2)}, u32[]{:S(2)}) collective-permute-start(bf16[8,16,128]{2,1,0:T(8,128)(2,1)S(1)} %get-tuple-element.47), channel_id=1, source_target_pairs={{0,8},{1,9},{2,10},{3,11},{4,12},{5,13},{6,14},{7,15},{8,0},{9,1},... | collective-permute-start | bytes 98312 | tf_op jit(solution)/shard_map/ppermute | solution.py:28
  30.7 1.5 %collective-permute-start.14 = (bf16[8,16,128]{2,1,0:T(8,128)(2,1)S(1)}, bf16[8,16,128]{2,1,0:T(8,128)(2,1)S(1)}, u32[]{:S(2)}, u32[]{:S(2)}) collective-permute-start(bf16[8,16,128]{2,1,0:T(8,128)(2,1)S(1)} %get-tuple-element.46), channel_id=1, source_target_pairs={{0,4},{1,5},{2,6},{3,7},{4,0},{5,1},{6,2},{7,3},{8,12},{9,13},{10,... | collective-permute-start | bytes 98312 | tf_op jit(solution)/shard_map/ppermute | solution.py:28
  32.2 1.2 %front.2 = (bf16[128,512]{1,0:T(8,128)(2,1)S(1)}, f32[128,128]{1,0:T(8,128)S(1)}, f32[128,128]{1,0:T(8,128)S(1)}) custom-call(bf16[1,768,128]{2,1,0:T(8,128)(2,1)S(1)} %get-tuple-element.35.refs_0_, bf16[1,768,128]{2,1,0:T(8,128)(2,1)S(1)} %collective-permute-done.4.refs_1_, bf16[1,768,128]{2,1,0:T(8,128)(2,1)S(1)} %collective-permute-done.5.refs_2_, ...), custom_call_target="tpu_custom_call" | custom-call | bytes 4096 | tf_op jit(solution)/shard_map/front/pallas_call | solution.py:304
  33.4 0.3 last.2
  33.7 0.2 collective-permute-done.16
  33.9 1.0 %collective-permute-done.15 = bf16[8,16,128]{2,1,0:T(8,128)(2,1)S(1)} collective-permute-done((bf16[8,16,128]{2,1,0:T(8,128)(2,1)S(1)}, bf16[8,16,128]{2,1,0:T(8,128)(2,1)S(1)}, u32[]{:S(2)}, u32[]{:S(2)}) %collective-permute-start.15) | collective-permute-done | bytes 32800 | tf_op jit(solution)/shard_map/ppermute | solution.py:28
  34.9 0.3 collective-permute-done.14
  35.2 0.6 %convert_add_fusion = f32[8,16,128]{2,1,0:T(8,128)} fusion(bf16[8,16,128]{2,1,0:T(8,128)(2,1)S(1)} %collective-permute-done.16, bf16[8,16,128]{2,1,0:T(8,128)(2,1)S(1)} %collective-permute-done.15, f32[8,16,128]{2,1,0:T(8,128)S(1)} %last.2, bf16[8,16,128]{2,1,0:T(8,128)(2,1)S(1)} %collective-permute-done.14), kind=kLoop, calls=%fused_computation | loop fusion | flops 98304 | bytes 229376 | tf_op jit(solution)/shard_map/add | solution.py:340
  (2 shorter events, 0.0 us)
Async XLA Ops:
  2.7 18.0 %copy-start = (bf16[768,128]{1,0:T(8,128)(2,1)S(1)}, bf16[768,128]{1,0:T(8,128)(2,1)}, u32[]{:S(2)}) copy-start(bf16[768,128]{1,0:T(8,128)(2,1)} %get-tuple-element.27) | copy-start | bytes 589828
  2.7 11.8 %collective-permute-start.7 = (bf16[768,128]{1,0:T(8,128)(2,1)}, bf16[768,128]{1,0:T(8,128)(2,1)S(1)}, u32[]{:S(2)}, u32[]{:S(2)}) collective-permute-start(bf16[768,128]{1,0:T(8,128)(2,1)} %get-tuple-element.36), channel_id=1, source_target_pairs={{0,4},{1,5},{2,6},{3,7},{4,0},{5,1},{6,2},{7,3},{8,12},{9,13},{10,... | collective-permute-start | bytes 589832 | tf_op jit(solution)/shard_map/ppermute | solution.py:28
  5.8 13.1 %collective-permute-start = (bf16[528,128]{1,0:T(8,128)(2,1)}, bf16[528,128]{1,0:T(8,128)(2,1)S(1)}, u32[]{:S(2)}, u32[]{:S(2)}) collective-permute-start(bf16[528,128]{1,0:T(8,128)(2,1)} %get-tuple-element.30), channel_id=1, source_target_pairs={{0,8},{1,9},{2,10},{3,11},{4,12},{5,13},{6,14},{7,15},{8,0},{9,1},... | collective-permute-start | bytes 405512 | tf_op jit(solution)/shard_map/ppermute | solution.py:28
  8.4 10.5 %collective-permute-start.2 = (bf16[272,128]{1,0:T(8,128)(2,1)}, bf16[272,128]{1,0:T(8,128)(2,1)S(1)}, u32[]{:S(2)}, u32[]{:S(2)}) collective-permute-start(bf16[272,128]{1,0:T(8,128)(2,1)} %get-tuple-element.33), channel_id=1, source_target_pairs={{0,4},{1,5},{2,6},{3,7},{4,0},{5,1},{6,2},{7,3},{8,12},{9,13},{10,... | collective-permute-start | bytes 208904 | tf_op jit(solution)/shard_map/ppermute | solution.py:28
  8.8 10.1 %collective-permute-start.1 = (bf16[256,128]{1,0:T(8,128)(2,1)}, bf16[256,128]{1,0:T(8,128)(2,1)S(1)}, u32[]{:S(2)}, u32[]{:S(2)}) collective-permute-start(bf16[256,128]{1,0:T(8,128)(2,1)} %get-tuple-element.31), channel_id=1, source_target_pairs={{0,12},{1,13},{2,14},{3,15},{4,8},{5,9},{6,10},{7,11},{8,4},{9,5},... | collective-permute-start | bytes 196616 | tf_op jit(solution)/shard_map/ppermute | solution.py:28
  10.2 11.4 %collective-permute-start.5 = (bf16[1,768,128]{2,1,0:T(8,128)(2,1)}, bf16[1,768,128]{2,1,0:T(8,128)(2,1)S(1)}, u32[]{:S(2)}, u32[]{:S(2)}) collective-permute-start(bf16[1,768,128]{2,1,0:T(8,128)(2,1)} %bitcast.13), channel_id=1, source_target_pairs={{0,2},{1,3},{2,0},{3,1},{4,6},{5,7},{6,4},{7,5},{8,10},{9,11},{10,... | collective-permute-start | bytes 589832 | tf_op jit(solution)/shard_map/ppermute | solution.py:28
  14.5 9.1 %collective-permute-start.9 = (bf16[1,768,128]{2,1,0:T(8,128)(2,1)S(1)}, bf16[1,768,128]{2,1,0:T(8,128)(2,1)S(1)}, u32[]{:S(2)}, u32[]{:S(2)}) collective-permute-start(bf16[1,768,128]{2,1,0:T(8,128)(2,1)S(1)} %bitcast.9), channel_id=1, source_target_pairs={{0,2},{1,3},{2,0},{3,1},{4,6},{5,7},{6,4},{7,5},{8,10},{9,11},{10,... | collective-permute-start | bytes 589832 | tf_op jit(solution)/shard_map/ppermute | solution.py:28
  18.9 2.8 %collective-permute-start.3 = (bf16[2,256,128]{2,1,0:T(8,128)(2,1)S(1)}, bf16[2,256,128]{2,1,0:T(8,128)(2,1)S(1)}, u32[]{:S(2)}, u32[]{:S(2)}) collective-permute-start(bf16[2,256,128]{2,1,0:T(8,128)(2,1)S(1)} %get-tuple-element.34.refs_9_.refs_11_), channel_id=1, source_target_pairs={{0,1},{1,0},{2,3},{3,2},{4,5},{5,4},{6,7},{7,6},{8,9},{9,8},{10,11... | collective-permute-start | bytes 393224 | tf_op jit(solution)/shard_map/ppermute | solution.py:28
  19.0 4.6 %collective-permute-start.10 = (bf16[272,128]{1,0:T(8,128)(2,1)S(1)}, bf16[272,128]{1,0:T(8,128)(2,1)S(1)}, u32[]{:S(2)}, u32[]{:S(2)}) collective-permute-start(bf16[272,128]{1,0:T(8,128)(2,1)S(1)} %get-tuple-element.37), channel_id=1, source_target_pairs={{0,4},{1,5},{2,6},{3,7},{4,0},{5,1},{6,2},{7,3},{8,12},{9,13},{10,... | collective-permute-start | bytes 208904 | tf_op jit(solution)/shard_map/ppermute | solution.py:28
  19.1 5.8 %collective-permute-start.12 = (bf16[2,256,128]{2,1,0:T(8,128)(2,1)S(1)}, bf16[2,256,128]{2,1,0:T(8,128)(2,1)S(1)}, u32[]{:S(2)}, u32[]{:S(2)}) collective-permute-start(bf16[2,256,128]{2,1,0:T(8,128)(2,1)S(1)} %get-tuple-element.34.refs_9_.refs_11_), channel_id=1, source_target_pairs={{0,2},{1,3},{2,0},{3,1},{4,6},{5,7},{6,4},{7,5},{8,10},{9,11},{10,... | collective-permute-start | bytes 393224 | tf_op jit(solution)/shard_map/ppermute | solution.py:28
  20.7 0.9 %copy-start.1 = (bf16[272,128]{1,0:T(8,128)(2,1)S(1)}, bf16[272,128]{1,0:T(8,128)(2,1)}, u32[]{:S(2)}) copy-start(bf16[272,128]{1,0:T(8,128)(2,1)} %get-tuple-element.28.refs_1_) | copy-start | bytes 208900
  21.6 3.3 %collective-permute-start.8 = (bf16[1,768,128]{2,1,0:T(8,128)(2,1)S(1)}, bf16[1,768,128]{2,1,0:T(8,128)(2,1)S(1)}, u32[]{:S(2)}, u32[]{:S(2)}) collective-permute-start(bf16[1,768,128]{2,1,0:T(8,128)(2,1)S(1)} %bitcast.10), channel_id=1, source_target_pairs={{0,1},{1,0},{2,3},{3,2},{4,5},{5,4},{6,7},{7,6},{8,9},{9,8},{10,11... | collective-permute-start | bytes 589832 | tf_op jit(solution)/shard_map/ppermute | solution.py:28
  21.7 3.2 %collective-permute-start.6 = (bf16[1,768,128]{2,1,0:T(8,128)(2,1)S(1)}, bf16[1,768,128]{2,1,0:T(8,128)(2,1)S(1)}, u32[]{:S(2)}, u32[]{:S(2)}) collective-permute-start(bf16[1,768,128]{2,1,0:T(8,128)(2,1)S(1)} %collective-permute-done.5.refs_2_), channel_id=1, source_target_pairs={{0,1},{1,0},{2,3},{3,2},{4,5},{5,4},{6,7},{7,6},{8,9},{9,8},{10,11... | collective-permute-start | bytes 589832 | tf_op jit(solution)/shard_map/ppermute | solution.py:28
  23.6 1.4 %collective-permute-start.4 = (bf16[1,768,128]{2,1,0:T(8,128)(2,1)S(1)}, bf16[1,768,128]{2,1,0:T(8,128)(2,1)S(1)}, u32[]{:S(2)}, u32[]{:S(2)}) collective-permute-start(bf16[1,768,128]{2,1,0:T(8,128)(2,1)S(1)} %get-tuple-element.35.refs_0_), channel_id=1, source_target_pairs={{0,1},{1,0},{2,3},{3,2},{4,5},{5,4},{6,7},{7,6},{8,9},{9,8},{10,11... | collective-permute-start | bytes 589832 | tf_op jit(solution)/shard_map/ppermute | solution.py:28
  23.6 1.7 %collective-permute-start.11 = (bf16[1,768,128]{2,1,0:T(8,128)(2,1)S(1)}, bf16[1,768,128]{2,1,0:T(8,128)(2,1)S(1)}, u32[]{:S(2)}, u32[]{:S(2)}) collective-permute-start(bf16[1,768,128]{2,1,0:T(8,128)(2,1)S(1)} %collective-permute-done.9.refs_6_), channel_id=1, source_target_pairs={{0,1},{1,0},{2,3},{3,2},{4,5},{5,4},{6,7},{7,6},{8,9},{9,8},{10,11... | collective-permute-start | bytes 589832 | tf_op jit(solution)/shard_map/ppermute | solution.py:28
  24.9 2.5 %collective-permute-start.13 = (bf16[2,256,128]{2,1,0:T(8,128)(2,1)S(1)}, bf16[2,256,128]{2,1,0:T(8,128)(2,1)S(1)}, u32[]{:S(2)}, u32[]{:S(2)}) collective-permute-start(bf16[2,256,128]{2,1,0:T(8,128)(2,1)S(1)} %collective-permute-done.12.refs_11_.refs_13_), channel_id=1, source_target_pairs={{0,1},{1,0},{2,3},{3,2},{4,5},{5,4},{6,7},{7,6},{8,9},{9,8},{10,11... | collective-permute-start | bytes 393224 | tf_op jit(solution)/shard_map/ppermute | solution.py:28
  27.8 6.1 %collective-permute-start.16 = (bf16[8,16,128]{2,1,0:T(8,128)(2,1)S(1)}, bf16[8,16,128]{2,1,0:T(8,128)(2,1)S(1)}, u32[]{:S(2)}, u32[]{:S(2)}) collective-permute-start(bf16[8,16,128]{2,1,0:T(8,128)(2,1)S(1)} %get-tuple-element.48), channel_id=1, source_target_pairs={{0,12},{1,13},{2,14},{3,15},{4,8},{5,9},{6,10},{7,11},{8,4},{9,5},... | collective-permute-start | bytes 98312 | tf_op jit(solution)/shard_map/ppermute | solution.py:28
  30.0 4.9 %collective-permute-start.15 = (bf16[8,16,128]{2,1,0:T(8,128)(2,1)S(1)}, bf16[8,16,128]{2,1,0:T(8,128)(2,1)S(1)}, u32[]{:S(2)}, u32[]{:S(2)}) collective-permute-start(bf16[8,16,128]{2,1,0:T(8,128)(2,1)S(1)} %get-tuple-element.47), channel_id=1, source_target_pairs={{0,8},{1,9},{2,10},{3,11},{4,12},{5,13},{6,14},{7,15},{8,0},{9,1},... | collective-permute-start | bytes 98312 | tf_op jit(solution)/shard_map/ppermute | solution.py:28
  30.7 4.5 %collective-permute-start.14 = (bf16[8,16,128]{2,1,0:T(8,128)(2,1)S(1)}, bf16[8,16,128]{2,1,0:T(8,128)(2,1)S(1)}, u32[]{:S(2)}, u32[]{:S(2)}) collective-permute-start(bf16[8,16,128]{2,1,0:T(8,128)(2,1)S(1)} %get-tuple-element.46), channel_id=1, source_target_pairs={{0,4},{1,5},{2,6},{3,7},{4,0},{5,1},{6,2},{7,3},{8,12},{9,13},{10,... | collective-permute-start | bytes 98312 | tf_op jit(solution)/shard_map/ppermute | solution.py:28

commit v10 on v8

--- a/solution.py
+++ b/solution.py
@@ -153,8 +153,8 @@
 
 def front_kernel(planes, handed_on, slots, order, blocks, pieces, rows_piece, held, *refs):
     relays, packs = refs[:2 * PLANE], refs[2 * PLANE:2 * PLANE + planes]
-    closing = refs[2 * PLANE + planes:-7]
-    state, named, sums, forms, high, low, wide = refs[-7:]
+    closing = refs[2 * PLANE + planes:-6]
+    state, named, sums, forms, parts, wide = refs[-6:]
     me = lax.axis_index("bits")
     span, twice_part = forms.shape[1:]
     depth = span // (2 * PLANE)
@@ -203,13 +203,12 @@
         rounded = product.astype(jnp.bfloat16)
         rest = (product - rounded.astype(jnp.float32)).astype(jnp.bfloat16)
         for k in range(planes):
-            high[k, a * rows:(a + 1) * rows, :] = rounded[k * rows:(k + 1) * rows]
-            low[k, a * rows:(a + 1) * rows, :] = rest[k * rows:(k + 1) * rows]
+            parts[k, a * rows:(a + 1) * rows, :] = rounded[k * rows:(k + 1) * rows]
+            parts[k, (blocks + a) * rows:(blocks + a + 1) * rows, :] = rest[k * rows:(k + 1) * rows]
     size = pieces * rows_piece
     for k in range(planes):
         pick = picks[k * size:(k + 1) * size]
-        total = jnp.dot(pick, high[k], preferred_element_type=jnp.float32)
-        total += jnp.dot(pick, low[k], preferred_element_type=jnp.float32)
+        total = jnp.dot(jnp.concatenate([pick, pick], axis=1), parts[k], preferred_element_type=jnp.float32)
         state[k * size:(k + 1) * size, :] = total.astype(jnp.bfloat16)
     close(order, named, state, relays + closing, sums, wide)
 
@@ -226,9 +225,9 @@
             wide[:part, slot * LANES:(slot + 1) * LANES] = real_rows
             wide[part:, slot * LANES:(slot + 1) * LANES] = turned
             slot += 1
-    for j in range(0, slot, 2):
-        both = jnp.dot(state[...], wide[:, j * LANES:(j + 2) * LANES], preferred_element_type=jnp.float32)
-        for side, slot in enumerate(order[j:j + 2]):
+    for j in range(0, len(order), 4):
+        both = jnp.dot(state[...], wide[:, j * LANES:min(j + 4, len(order)) * LANES], preferred_element_type=jnp.float32)
+        for side, slot in enumerate(order[j:j + 4]):
             factor = jnp.broadcast_to(named[:, slot:slot + 1], (rows, LANES))
             add = both[:, side * LANES:(side + 1) * LANES] * factor
             sums[...] = add if slot == 0 else sums[...] + add
@@ -312,8 +311,7 @@
             out_specs=[vmem] * 3,
             scratch_shapes=[
                 pltpu.VMEM((blocks, span, 2 * part), jnp.bfloat16),
-                pltpu.VMEM((count, blocks * held * rows_piece, 2 * part), jnp.bfloat16),
-                pltpu.VMEM((count, blocks * held * rows_piece, 2 * part), jnp.bfloat16),
+                pltpu.VMEM((count, 2 * blocks * held * rows_piece, 2 * part), jnp.bfloat16),
                 pltpu.VMEM((2 * part, len(order) * LANES), jnp.bfloat16),
             ],
             compiler_params=params,

time: 36 us -> 36.1 us (level)
  no operation moved by 1% of the time
where the time goes in v10:
time: 36.1 us; the launch traced here: 35.9 us
  starting transfers between devices  18 us (50%)
  waiting for transfers between devices  9.61 us (27%)
  Pallas kernels  6.69 us (19%)
  local copies, waits for them, and re-layouts  0.89 us (2%)
  other arithmetic  0.65 us (2%)
    ppermute x17, starting transfers between devices, swap(): return lax.ppermute(x, 'bits', [(i, i ^ bit) for i in range(owners)])  18 us
    ppermute x17, waiting for transfers between devices, swap(): return lax.ppermute(x, 'bits', [(i, i ^ bit) for i in range(owners)])  9.61 us
    pallas_call x2, Pallas kernels, sums_of(): pl.pallas_call(functools.partial(front_kernel, count, list(chosen).index(...  3.33 us
    pallas_call x1, Pallas kernels, in_planes(): pl.pallas_call(functools.partial(pack_kernel, planes, pair_prefix.shape[1...  2.68 us
    unnamed x4, local copies, waits for them, and re-layouts  0.89 us
  transfers between devices with their start and end apart: 17, of which 9 were waited for; matrix products, arithmetic and copies ran while one was open for 0% of the time, Pallas kernels for 10%

profile of v10, /device:TPU:0, one launch (start us, length us, event | category | flops | bytes accessed | tf_op | source)
XLA Modules:
  0.0 35.9 jit_solution(136250837005207135)
XLA Ops:
  0.0 2.7 %pack.1 = (bf16[768,128]{1,0:T(8,128)(2,1)}, bf16[768,128]{1,0:T(8,128)(2,1)}, bf16[528,128]{1,0:T(8,128)(2,1)}, bf16[256,128]{1,0:T(8,128)(2,1)}, bf16[272,128]{1,0:T(8,128)(2,1)}, /*index=5*/bf16[272,128]{1,0:T(8,128)(2,1)}) custom-call(bf16[256,512]{1,0:T(8,128)(2,1)} %bitcast.16, bf16[64,1024]{1,0:T(8,128)(2,1)} %bitcast.17, ...), custom_call_target="tpu_custom_call" | custom-call | flops 1048576 | bytes 4096 | tf_op jit(solution)/shard_map/pack/pallas_call | solution.py:268
  2.7 0.0 copy-start
  2.7 3.1 %collective-permute-start.3 = (bf16[768,128]{1,0:T(8,128)(2,1)}, bf16[768,128]{1,0:T(8,128)(2,1)S(1)}, u32[]{:S(2)}, u32[]{:S(2)}) collective-permute-start(bf16[768,128]{1,0:T(8,128)(2,1)} %get-tuple-element.30), channel_id=1, source_target_pairs={{0,4},{1,5},{2,6},{3,7},{4,0},{5,1},{6,2},{7,3},{8,12},{9,13},{10,... | collective-permute-start | bytes 589832 | tf_op jit(solution)/shard_map/ppermute | solution.py:28
  5.8 2.6 %collective-permute-start.4 = (bf16[528,128]{1,0:T(8,128)(2,1)}, bf16[528,128]{1,0:T(8,128)(2,1)S(1)}, u32[]{:S(2)}, u32[]{:S(2)}) collective-permute-start(bf16[528,128]{1,0:T(8,128)(2,1)} %get-tuple-element.31), channel_id=1, source_target_pairs={{0,8},{1,9},{2,10},{3,11},{4,12},{5,13},{6,14},{7,15},{8,0},{9,1},... | collective-permute-start | bytes 405512 | tf_op jit(solution)/shard_map/ppermute | solution.py:28
  8.4 0.5 %collective-permute-start.6 = (bf16[272,128]{1,0:T(8,128)(2,1)}, bf16[272,128]{1,0:T(8,128)(2,1)S(1)}, u32[]{:S(2)}, u32[]{:S(2)}) collective-permute-start(bf16[272,128]{1,0:T(8,128)(2,1)} %get-tuple-element.34), channel_id=1, source_target_pairs={{0,4},{1,5},{2,6},{3,7},{4,0},{5,1},{6,2},{7,3},{8,12},{9,13},{10,... | collective-permute-start | bytes 208904 | tf_op jit(solution)/shard_map/ppermute | solution.py:28
  8.8 1.4 %collective-permute-start.5 = (bf16[256,128]{1,0:T(8,128)(2,1)}, bf16[256,128]{1,0:T(8,128)(2,1)S(1)}, u32[]{:S(2)}, u32[]{:S(2)}) collective-permute-start(bf16[256,128]{1,0:T(8,128)(2,1)} %get-tuple-element.32), channel_id=1, source_target_pairs={{0,12},{1,13},{2,14},{3,15},{4,8},{5,9},{6,10},{7,11},{8,4},{9,5},... | collective-permute-start | bytes 196616 | tf_op jit(solution)/shard_map/ppermute | solution.py:28
  10.2 1.5 %collective-permute-start.1 = (bf16[1,768,128]{2,1,0:T(8,128)(2,1)}, bf16[1,768,128]{2,1,0:T(8,128)(2,1)S(1)}, u32[]{:S(2)}, u32[]{:S(2)}) collective-permute-start(bf16[1,768,128]{2,1,0:T(8,128)(2,1)} %bitcast.13), channel_id=1, source_target_pairs={{0,2},{1,3},{2,0},{3,1},{4,6},{5,7},{6,4},{7,5},{8,10},{9,11},{10,... | collective-permute-start | bytes 589832 | tf_op jit(solution)/shard_map/ppermute | solution.py:28
  11.7 2.8 %collective-permute-done.3 = bf16[768,128]{1,0:T(8,128)(2,1)S(1)} collective-permute-done((bf16[768,128]{1,0:T(8,128)(2,1)}, bf16[768,128]{1,0:T(8,128)(2,1)S(1)}, u32[]{:S(2)}, u32[]{:S(2)}) %collective-permute-start.3) | collective-permute-done | bytes 196640 | tf_op jit(solution)/shard_map/ppermute | solution.py:28
  14.5 1.7 %collective-permute-start.9 = (bf16[1,768,128]{2,1,0:T(8,128)(2,1)S(1)}, bf16[1,768,128]{2,1,0:T(8,128)(2,1)S(1)}, u32[]{:S(2)}, u32[]{:S(2)}) collective-permute-start(bf16[1,768,128]{2,1,0:T(8,128)(2,1)S(1)} %bitcast.9), channel_id=1, source_target_pairs={{0,2},{1,3},{2,0},{3,1},{4,6},{5,7},{6,4},{7,5},{8,10},{9,11},{10,... | collective-permute-start | bytes 589832 | tf_op jit(solution)/shard_map/ppermute | solution.py:28
  16.2 2.6 %collective-permute-done.5.refs_1_ = bf16[256,128]{1,0:T(8,128)(2,1)S(1)} collective-permute-done((bf16[256,128]{1,0:T(8,128)(2,1)}, bf16[256,128]{1,0:T(8,128)(2,1)S(1)}, u32[]{:S(2)}, u32[]{:S(2)}) %collective-permute-start.5) | collective-permute-done | bytes 65568 | tf_op jit(solution)/shard_map/ppermute | solution.py:28
  18.9 0.0 collective-permute-done.4.refs_0_.refs_9_
  18.9 0.0 collective-permute-done.6.refs_8_
  18.9 0.1 collective-permute-start.7
  19.0 0.1 collective-permute-start.10
  19.1 1.6 %collective-permute-start.12 = (bf16[2,256,128]{2,1,0:T(8,128)(2,1)S(1)}, bf16[2,256,128]{2,1,0:T(8,128)(2,1)S(1)}, u32[]{:S(2)}, u32[]{:S(2)}) collective-permute-start(bf16[2,256,128]{2,1,0:T(8,128)(2,1)S(1)} %get-tuple-element.35.refs_9_.refs_11_), channel_id=1, source_target_pairs={{0,2},{1,3},{2,0},{3,1},{4,6},{5,7},{6,4},{7,5},{8,10},{9,11},{10,... | collective-permute-start | bytes 393224 | tf_op jit(solution)/shard_map/ppermute | solution.py:28
  20.6 0.0 copy-done
  20.7 0.0 copy-start.1
  20.7 0.9 %copy-done.1 = bf16[272,128]{1,0:T(8,128)(2,1)S(1)} copy-done((bf16[272,128]{1,0:T(8,128)(2,1)S(1)}, bf16[272,128]{1,0:T(8,128)(2,1)}, u32[]{:S(2)}) %copy-start.1) | copy-done | bytes 69656
  21.6 0.0 collective-permute-done.1.refs_2_
  21.6 0.1 collective-permute-start
  21.7 0.0 collective-permute-done.7.refs_10_.refs_12_
  21.7 0.4 %collective-permute-start.2 = (bf16[1,768,128]{2,1,0:T(8,128)(2,1)S(1)}, bf16[1,768,128]{2,1,0:T(8,128)(2,1)S(1)}, u32[]{:S(2)}, u32[]{:S(2)}) collective-permute-start(bf16[1,768,128]{2,1,0:T(8,128)(2,1)S(1)} %collective-permute-done.1.refs_2_), channel_id=1, source_target_pairs={{0,1},{1,0},{2,3},{3,2},{4,5},{5,4},{6,7},{7,6},{8,9},{9,8},{10,11... | collective-permute-start | bytes 589832 | tf_op jit(solution)/shard_map/ppermute | solution.py:28
  22.1 1.4 %collective-permute-done.10.refs_10_ = bf16[272,128]{1,0:T(8,128)(2,1)S(1)} collective-permute-done((bf16[272,128]{1,0:T(8,128)(2,1)S(1)}, bf16[272,128]{1,0:T(8,128)(2,1)S(1)}, u32[]{:S(2)}, u32[]{:S(2)}) %collective-permute-start.10) | collective-permute-done | bytes 69664 | tf_op jit(solution)/shard_map/ppermute | solution.py:28
  23.6 0.0 collective-permute-start.8
  23.6 0.0 collective-permute-done.9.refs_6_
  23.6 0.5 %collective-permute-start.11 = (bf16[1,768,128]{2,1,0:T(8,128)(2,1)S(1)}, bf16[1,768,128]{2,1,0:T(8,128)(2,1)S(1)}, u32[]{:S(2)}, u32[]{:S(2)}) collective-permute-start(bf16[1,768,128]{2,1,0:T(8,128)(2,1)S(1)} %collective-permute-done.9.refs_6_), channel_id=1, source_target_pairs={{0,1},{1,0},{2,3},{3,2},{4,5},{5,4},{6,7},{7,6},{8,9},{9,8},{10,11... | collective-permute-start | bytes 589832 | tf_op jit(solution)/shard_map/ppermute | solution.py:28
  24.1 0.8 %collective-permute-done.12.refs_11_.refs_13_ = bf16[2,256,128]{2,1,0:T(8,128)(2,1)S(1)} collective-permute-done((bf16[2,256,128]{2,1,0:T(8,128)(2,1)S(1)}, bf16[2,256,128]{2,1,0:T(8,128)(2,1)S(1)}, u32[]{:S(2)}, u32[]{:S(2)}) %collective-permute-start.12) | collective-permute-done | bytes 131104 | tf_op jit(solution)/shard_map/ppermute | solution.py:28
  24.9 0.0 collective-permute-start.13
  24.9 0.0 collective-permute-done.refs_1_
  24.9 0.0 collective-permute-done.2.refs_3_
  24.9 0.1 collective-permute-done.8.refs_5_
  25.0 0.3 collective-permute-done.11.refs_7_
  25.3 2.2 %front.3 = (bf16[384,512]{1,0:T(8,128)(2,1)S(1)}, f32[384,128]{1,0:T(8,128)S(1)}, f32[384,128]{1,0:T(8,128)S(1)}) custom-call(bf16[1,768,128]{2,1,0:T(8,128)(2,1)S(1)} %get-tuple-element.29.refs_0_, bf16[1,768,128]{2,1,0:T(8,128)(2,1)S(1)} %collective-permute-done.refs_1_, bf16[1,768,128]{2,1,0:T(8,128)(2,1)S(1)} %collective-permute-done.1.refs_2_, ...), custom_call_target="tpu_custom_call" | custom-call | bytes 4096 | tf_op jit(solution)/shard_map/front/pallas_call | solution.py:303
  27.5 0.0 collective-permute-done.13.relay
  27.5 0.4 %last.3 = (bf16[8,16,128]{2,1,0:T(8,128)(2,1)S(1)}, bf16[8,16,128]{2,1,0:T(8,128)(2,1)S(1)}, bf16[8,16,128]{2,1,0:T(8,128)(2,1)S(1)}) custom-call(f32[384,128]{1,0:T(8,128)S(1)} %get-tuple-element.43.named, bf16[384,512]{1,0:T(8,128)(2,1)S(1)} %get-tuple-element.44.state, f32[384,128]{1,0:T(8,128)S(1)} %get-tuple-element.45.sums_in, ...), custom_call_target="tpu_custom_call" | custom-call | bytes 4096 | tf_op jit(solution)/shard_map/last/pallas_call | solution.py:321
  27.9 2.2 %collective-permute-start.16 = (bf16[8,16,128]{2,1,0:T(8,128)(2,1)S(1)}, bf16[8,16,128]{2,1,0:T(8,128)(2,1)S(1)}, u32[]{:S(2)}, u32[]{:S(2)}) collective-permute-start(bf16[8,16,128]{2,1,0:T(8,128)(2,1)S(1)} %get-tuple-element.48), channel_id=1, source_target_pairs={{0,12},{1,13},{2,14},{3,15},{4,8},{5,9},{6,10},{7,11},{8,4},{9,5},... | collective-permute-start | bytes 98312 | tf_op jit(solution)/shard_map/ppermute | solution.py:28
  30.1 0.7 %collective-permute-start.15 = (bf16[8,16,128]{2,1,0:T(8,128)(2,1)S(1)}, bf16[8,16,128]{2,1,0:T(8,128)(2,1)S(1)}, u32[]{:S(2)}, u32[]{:S(2)}) collective-permute-start(bf16[8,16,128]{2,1,0:T(8,128)(2,1)S(1)} %get-tuple-element.47), channel_id=1, source_target_pairs={{0,8},{1,9},{2,10},{3,11},{4,12},{5,13},{6,14},{7,15},{8,0},{9,1},... | collective-permute-start | bytes 98312 | tf_op jit(solution)/shard_map/ppermute | solution.py:28
  30.8 1.5 %collective-permute-start.14 = (bf16[8,16,128]{2,1,0:T(8,128)(2,1)S(1)}, bf16[8,16,128]{2,1,0:T(8,128)(2,1)S(1)}, u32[]{:S(2)}, u32[]{:S(2)}) collective-permute-start(bf16[8,16,128]{2,1,0:T(8,128)(2,1)S(1)} %get-tuple-element.46), channel_id=1, source_target_pairs={{0,4},{1,5},{2,6},{3,7},{4,0},{5,1},{6,2},{7,3},{8,12},{9,13},{10,... | collective-permute-start | bytes 98312 | tf_op jit(solution)/shard_map/ppermute | solution.py:28
  32.3 1.2 %front.2 = (bf16[128,512]{1,0:T(8,128)(2,1)S(1)}, f32[128,128]{1,0:T(8,128)S(1)}, f32[128,128]{1,0:T(8,128)S(1)}) custom-call(bf16[1,768,128]{2,1,0:T(8,128)(2,1)S(1)} %get-tuple-element.29.refs_0_, bf16[1,768,128]{2,1,0:T(8,128)(2,1)S(1)} %collective-permute-done.refs_1_, bf16[1,768,128]{2,1,0:T(8,128)(2,1)S(1)} %collective-permute-done.1.refs_2_, ...), custom_call_target="tpu_custom_call" | custom-call | bytes 4096 | tf_op jit(solution)/shard_map/front/pallas_call | solution.py:303
  33.5 0.3 last.2
  33.8 0.2 collective-permute-done.16
  33.9 1.0 %collective-permute-done.15 = bf16[8,16,128]{2,1,0:T(8,128)(2,1)S(1)} collective-permute-done((bf16[8,16,128]{2,1,0:T(8,128)(2,1)S(1)}, bf16[8,16,128]{2,1,0:T(8,128)(2,1)S(1)}, u32[]{:S(2)}, u32[]{:S(2)}) %collective-permute-start.15) | collective-permute-done | bytes 32800 | tf_op jit(solution)/shard_map/ppermute | solution.py:28
  35.0 0.3 collective-permute-done.14
  35.2 0.6 %convert_add_fusion = f32[8,16,128]{2,1,0:T(8,128)} fusion(bf16[8,16,128]{2,1,0:T(8,128)(2,1)S(1)} %collective-permute-done.16, bf16[8,16,128]{2,1,0:T(8,128)(2,1)S(1)} %collective-permute-done.15, f32[8,16,128]{2,1,0:T(8,128)S(1)} %last.2, bf16[8,16,128]{2,1,0:T(8,128)(2,1)S(1)} %collective-permute-done.14), kind=kLoop, calls=%fused_computation | loop fusion | flops 98304 | bytes 229376 | tf_op jit(solution)/shard_map/add | solution.py:338
  (2 shorter events, 0.0 us)
Async XLA Ops:
  2.7 18.0 %copy-start = (bf16[768,128]{1,0:T(8,128)(2,1)S(1)}, bf16[768,128]{1,0:T(8,128)(2,1)}, u32[]{:S(2)}) copy-start(bf16[768,128]{1,0:T(8,128)(2,1)} %get-tuple-element.27) | copy-start | bytes 589828
  2.7 11.8 %collective-permute-start.3 = (bf16[768,128]{1,0:T(8,128)(2,1)}, bf16[768,128]{1,0:T(8,128)(2,1)S(1)}, u32[]{:S(2)}, u32[]{:S(2)}) collective-permute-start(bf16[768,128]{1,0:T(8,128)(2,1)} %get-tuple-element.30), channel_id=1, source_target_pairs={{0,4},{1,5},{2,6},{3,7},{4,0},{5,1},{6,2},{7,3},{8,12},{9,13},{10,... | collective-permute-start | bytes 589832 | tf_op jit(solution)/shard_map/ppermute | solution.py:28
  5.8 13.1 %collective-permute-start.4 = (bf16[528,128]{1,0:T(8,128)(2,1)}, bf16[528,128]{1,0:T(8,128)(2,1)S(1)}, u32[]{:S(2)}, u32[]{:S(2)}) collective-permute-start(bf16[528,128]{1,0:T(8,128)(2,1)} %get-tuple-element.31), channel_id=1, source_target_pairs={{0,8},{1,9},{2,10},{3,11},{4,12},{5,13},{6,14},{7,15},{8,0},{9,1},... | collective-permute-start | bytes 405512 | tf_op jit(solution)/shard_map/ppermute | solution.py:28
  8.4 10.5 %collective-permute-start.6 = (bf16[272,128]{1,0:T(8,128)(2,1)}, bf16[272,128]{1,0:T(8,128)(2,1)S(1)}, u32[]{:S(2)}, u32[]{:S(2)}) collective-permute-start(bf16[272,128]{1,0:T(8,128)(2,1)} %get-tuple-element.34), channel_id=1, source_target_pairs={{0,4},{1,5},{2,6},{3,7},{4,0},{5,1},{6,2},{7,3},{8,12},{9,13},{10,... | collective-permute-start | bytes 208904 | tf_op jit(solution)/shard_map/ppermute | solution.py:28
  8.8 10.1 %collective-permute-start.5 = (bf16[256,128]{1,0:T(8,128)(2,1)}, bf16[256,128]{1,0:T(8,128)(2,1)S(1)}, u32[]{:S(2)}, u32[]{:S(2)}) collective-permute-start(bf16[256,128]{1,0:T(8,128)(2,1)} %get-tuple-element.32), channel_id=1, source_target_pairs={{0,12},{1,13},{2,14},{3,15},{4,8},{5,9},{6,10},{7,11},{8,4},{9,5},... | collective-permute-start | bytes 196616 | tf_op jit(solution)/shard_map/ppermute | solution.py:28
  10.2 11.4 %collective-permute-start.1 = (bf16[1,768,128]{2,1,0:T(8,128)(2,1)}, bf16[1,768,128]{2,1,0:T(8,128)(2,1)S(1)}, u32[]{:S(2)}, u32[]{:S(2)}) collective-permute-start(bf16[1,768,128]{2,1,0:T(8,128)(2,1)} %bitcast.13), channel_id=1, source_target_pairs={{0,2},{1,3},{2,0},{3,1},{4,6},{5,7},{6,4},{7,5},{8,10},{9,11},{10,... | collective-permute-start | bytes 589832 | tf_op jit(solution)/shard_map/ppermute | solution.py:28
  14.5 9.1 %collective-permute-start.9 = (bf16[1,768,128]{2,1,0:T(8,128)(2,1)S(1)}, bf16[1,768,128]{2,1,0:T(8,128)(2,1)S(1)}, u32[]{:S(2)}, u32[]{:S(2)}) collective-permute-start(bf16[1,768,128]{2,1,0:T(8,128)(2,1)S(1)} %bitcast.9), channel_id=1, source_target_pairs={{0,2},{1,3},{2,0},{3,1},{4,6},{5,7},{6,4},{7,5},{8,10},{9,11},{10,... | collective-permute-start | bytes 589832 | tf_op jit(solution)/shard_map/ppermute | solution.py:28
  18.9 2.8 %collective-permute-start.7 = (bf16[2,256,128]{2,1,0:T(8,128)(2,1)S(1)}, bf16[2,256,128]{2,1,0:T(8,128)(2,1)S(1)}, u32[]{:S(2)}, u32[]{:S(2)}) collective-permute-start(bf16[2,256,128]{2,1,0:T(8,128)(2,1)S(1)} %get-tuple-element.35.refs_9_.refs_11_), channel_id=1, source_target_pairs={{0,1},{1,0},{2,3},{3,2},{4,5},{5,4},{6,7},{7,6},{8,9},{9,8},{10,11... | collective-permute-start | bytes 393224 | tf_op jit(solution)/shard_map/ppermute | solution.py:28
  19.0 4.6 %collective-permute-start.10 = (bf16[272,128]{1,0:T(8,128)(2,1)S(1)}, bf16[272,128]{1,0:T(8,128)(2,1)S(1)}, u32[]{:S(2)}, u32[]{:S(2)}) collective-permute-start(bf16[272,128]{1,0:T(8,128)(2,1)S(1)} %get-tuple-element.37), channel_id=1, source_target_pairs={{0,4},{1,5},{2,6},{3,7},{4,0},{5,1},{6,2},{7,3},{8,12},{9,13},{10,... | collective-permute-start | bytes 208904 | tf_op jit(solution)/shard_map/ppermute | solution.py:28
  19.1 5.8 %collective-permute-start.12 = (bf16[2,256,128]{2,1,0:T(8,128)(2,1)S(1)}, bf16[2,256,128]{2,1,0:T(8,128)(2,1)S(1)}, u32[]{:S(2)}, u32[]{:S(2)}) collective-permute-start(bf16[2,256,128]{2,1,0:T(8,128)(2,1)S(1)} %get-tuple-element.35.refs_9_.refs_11_), channel_id=1, source_target_pairs={{0,2},{1,3},{2,0},{3,1},{4,6},{5,7},{6,4},{7,5},{8,10},{9,11},{10,... | collective-permute-start | bytes 393224 | tf_op jit(solution)/shard_map/ppermute | solution.py:28
  20.7 0.9 %copy-start.1 = (bf16[272,128]{1,0:T(8,128)(2,1)S(1)}, bf16[272,128]{1,0:T(8,128)(2,1)}, u32[]{:S(2)}) copy-start(bf16[272,128]{1,0:T(8,128)(2,1)} %get-tuple-element.28.refs_1_) | copy-start | bytes 208900
  21.6 3.3 %collective-permute-start = (bf16[1,768,128]{2,1,0:T(8,128)(2,1)S(1)}, bf16[1,768,128]{2,1,0:T(8,128)(2,1)S(1)}, u32[]{:S(2)}, u32[]{:S(2)}) collective-permute-start(bf16[1,768,128]{2,1,0:T(8,128)(2,1)S(1)} %get-tuple-element.29.refs_0_), channel_id=1, source_target_pairs={{0,1},{1,0},{2,3},{3,2},{4,5},{5,4},{6,7},{7,6},{8,9},{9,8},{10,11... | collective-permute-start | bytes 589832 | tf_op jit(solution)/shard_map/ppermute | solution.py:28
  21.7 3.2 %collective-permute-start.2 = (bf16[1,768,128]{2,1,0:T(8,128)(2,1)S(1)}, bf16[1,768,128]{2,1,0:T(8,128)(2,1)S(1)}, u32[]{:S(2)}, u32[]{:S(2)}) collective-permute-start(bf16[1,768,128]{2,1,0:T(8,128)(2,1)S(1)} %collective-permute-done.1.refs_2_), channel_id=1, source_target_pairs={{0,1},{1,0},{2,3},{3,2},{4,5},{5,4},{6,7},{7,6},{8,9},{9,8},{10,11... | collective-permute-start | bytes 589832 | tf_op jit(solution)/shard_map/ppermute | solution.py:28
  23.6 1.4 %collective-permute-start.8 = (bf16[1,768,128]{2,1,0:T(8,128)(2,1)S(1)}, bf16[1,768,128]{2,1,0:T(8,128)(2,1)S(1)}, u32[]{:S(2)}, u32[]{:S(2)}) collective-permute-start(bf16[1,768,128]{2,1,0:T(8,128)(2,1)S(1)} %bitcast.10), channel_id=1, source_target_pairs={{0,1},{1,0},{2,3},{3,2},{4,5},{5,4},{6,7},{7,6},{8,9},{9,8},{10,11... | collective-permute-start | bytes 589832 | tf_op jit(solution)/shard_map/ppermute | solution.py:28
  23.6 1.7 %collective-permute-start.11 = (bf16[1,768,128]{2,1,0:T(8,128)(2,1)S(1)}, bf16[1,768,128]{2,1,0:T(8,128)(2,1)S(1)}, u32[]{:S(2)}, u32[]{:S(2)}) collective-permute-start(bf16[1,768,128]{2,1,0:T(8,128)(2,1)S(1)} %collective-permute-done.9.refs_6_), channel_id=1, source_target_pairs={{0,1},{1,0},{2,3},{3,2},{4,5},{5,4},{6,7},{7,6},{8,9},{9,8},{10,11... | collective-permute-start | bytes 589832 | tf_op jit(solution)/shard_map/ppermute | solution.py:28
  24.9 2.6 %collective-permute-start.13 = (bf16[2,256,128]{2,1,0:T(8,128)(2,1)S(1)}, bf16[2,256,128]{2,1,0:T(8,128)(2,1)S(1)}, u32[]{:S(2)}, u32[]{:S(2)}) collective-permute-start(bf16[2,256,128]{2,1,0:T(8,128)(2,1)S(1)} %collective-permute-done.12.refs_11_.refs_13_), channel_id=1, source_target_pairs={{0,1},{1,0},{2,3},{3,2},{4,5},{5,4},{6,7},{7,6},{8,9},{9,8},{10,11... | collective-permute-start | bytes 393224 | tf_op jit(solution)/shard_map/ppermute | solution.py:28
  27.9 6.1 %collective-permute-start.16 = (bf16[8,16,128]{2,1,0:T(8,128)(2,1)S(1)}, bf16[8,16,128]{2,1,0:T(8,128)(2,1)S(1)}, u32[]{:S(2)}, u32[]{:S(2)}) collective-permute-start(bf16[8,16,128]{2,1,0:T(8,128)(2,1)S(1)} %get-tuple-element.48), channel_id=1, source_target_pairs={{0,12},{1,13},{2,14},{3,15},{4,8},{5,9},{6,10},{7,11},{8,4},{9,5},... | collective-permute-start | bytes 98312 | tf_op jit(solution)/shard_map/ppermute | solution.py:28
  30.1 4.9 %collective-permute-start.15 = (bf16[8,16,128]{2,1,0:T(8,128)(2,1)S(1)}, bf16[8,16,128]{2,1,0:T(8,128)(2,1)S(1)}, u32[]{:S(2)}, u32[]{:S(2)}) collective-permute-start(bf16[8,16,128]{2,1,0:T(8,128)(2,1)S(1)} %get-tuple-element.47), channel_id=1, source_target_pairs={{0,8},{1,9},{2,10},{3,11},{4,12},{5,13},{6,14},{7,15},{8,0},{9,1},... | collective-permute-start | bytes 98312 | tf_op jit(solution)/shard_map/ppermute | solution.py:28
  30.8 4.5 %collective-permute-start.14 = (bf16[8,16,128]{2,1,0:T(8,128)(2,1)S(1)}, bf16[8,16,128]{2,1,0:T(8,128)(2,1)S(1)}, u32[]{:S(2)}, u32[]{:S(2)}) collective-permute-start(bf16[8,16,128]{2,1,0:T(8,128)(2,1)S(1)} %get-tuple-element.46), channel_id=1, source_target_pairs={{0,4},{1,5},{2,6},{3,7},{4,0},{5,1},{6,2},{7,3},{8,12},{9,13},{10,... | collective-permute-start | bytes 98312 | tf_op jit(solution)/shard_map/ppermute | solution.py:28

commit v11 on v9

--- a/solution.py
+++ b/solution.py
@@ -288,8 +288,8 @@
     relays[0] = own
     packs = [local, near, far[0], handed]
     far_beside = swap(after(relays[2], near), 1)
-    beside = [swap(after(relays[0], far_beside), 1), swap(relays[1], 1), far_beside]
-    corner = [swap(across[0], 1), swap(after(across[1], handed), 1), swap(across[2], 1)]
+    beside = [swap(relays[0], 1), swap(relays[1], 1), far_beside]
+    corner = [swap(after(across[0], far_beside), 1), swap(after(across[1], handed), 1), swap(across[2], 1)]
     early = 2 * PLANE
     far_slots = range(early, owners, PLANE)
     order = list(range(early)) + [k + n for n in (0, 1, 2) for k in far_slots]

time: 36 us -> 36 us (level)
  no operation moved by 1% of the time
where the time goes in v11:
time: 36 us; the launch traced here: 35.8 us
  starting transfers between devices  18 us (50%)
  waiting for transfers between devices  9.59 us (27%)
  Pallas kernels  6.62 us (18%)
  local copies, waits for them, and re-layouts  0.89 us (2%)
  other arithmetic  0.65 us (2%)
    ppermute x17, starting transfers between devices, swap(): return lax.ppermute(x, 'bits', [(i, i ^ bit) for i in range(owners)])  18 us
    ppermute x17, waiting for transfers between devices, swap(): return lax.ppermute(x, 'bits', [(i, i ^ bit) for i in range(owners)])  9.59 us
    pallas_call x2, Pallas kernels, sums_of(): pl.pallas_call(functools.partial(front_kernel, count, list(chosen).index(...  3.27 us
    pallas_call x1, Pallas kernels, in_planes(): pl.pallas_call(functools.partial(pack_kernel, planes, pair_prefix.shape[1...  2.68 us
    unnamed x4, local copies, waits for them, and re-layouts  0.89 us
  transfers between devices with their start and end apart: 17, of which 9 were waited for; matrix products, arithmetic and copies ran while one was open for 0% of the time, Pallas kernels for 10%

profile of v11, /device:TPU:0, one launch (start us, length us, event | category | flops | bytes accessed | tf_op | source)
XLA Modules:
  0.0 35.8 jit_solution(4035154163450455148)
XLA Ops:
  0.0 2.7 %pack.1 = (bf16[768,128]{1,0:T(8,128)(2,1)}, bf16[768,128]{1,0:T(8,128)(2,1)}, bf16[528,128]{1,0:T(8,128)(2,1)}, bf16[256,128]{1,0:T(8,128)(2,1)}, bf16[272,128]{1,0:T(8,128)(2,1)}, /*index=5*/bf16[272,128]{1,0:T(8,128)(2,1)}) custom-call(bf16[256,512]{1,0:T(8,128)(2,1)} %bitcast.16, bf16[64,1024]{1,0:T(8,128)(2,1)} %bitcast.17, ...), custom_call_target="tpu_custom_call" | custom-call | flops 1048576 | bytes 4096 | tf_op jit(solution)/shard_map/pack/pallas_call | solution.py:269
  2.7 0.0 copy-start
  2.7 3.1 %collective-permute-start.7 = (bf16[768,128]{1,0:T(8,128)(2,1)}, bf16[768,128]{1,0:T(8,128)(2,1)S(1)}, u32[]{:S(2)}, u32[]{:S(2)}) collective-permute-start(bf16[768,128]{1,0:T(8,128)(2,1)} %get-tuple-element.36), channel_id=1, source_target_pairs={{0,4},{1,5},{2,6},{3,7},{4,0},{5,1},{6,2},{7,3},{8,12},{9,13},{10,... | collective-permute-start | bytes 589832 | tf_op jit(solution)/shard_map/ppermute | solution.py:28
  5.8 2.6 %collective-permute-start.2 = (bf16[528,128]{1,0:T(8,128)(2,1)}, bf16[528,128]{1,0:T(8,128)(2,1)S(1)}, u32[]{:S(2)}, u32[]{:S(2)}) collective-permute-start(bf16[528,128]{1,0:T(8,128)(2,1)} %get-tuple-element.30), channel_id=1, source_target_pairs={{0,8},{1,9},{2,10},{3,11},{4,12},{5,13},{6,14},{7,15},{8,0},{9,1},... | collective-permute-start | bytes 405512 | tf_op jit(solution)/shard_map/ppermute | solution.py:28
  8.4 0.5 %collective-permute-start.4 = (bf16[272,128]{1,0:T(8,128)(2,1)}, bf16[272,128]{1,0:T(8,128)(2,1)S(1)}, u32[]{:S(2)}, u32[]{:S(2)}) collective-permute-start(bf16[272,128]{1,0:T(8,128)(2,1)} %get-tuple-element.33), channel_id=1, source_target_pairs={{0,4},{1,5},{2,6},{3,7},{4,0},{5,1},{6,2},{7,3},{8,12},{9,13},{10,... | collective-permute-start | bytes 208904 | tf_op jit(solution)/shard_map/ppermute | solution.py:28
  8.8 1.4 %collective-permute-start.3 = (bf16[256,128]{1,0:T(8,128)(2,1)}, bf16[256,128]{1,0:T(8,128)(2,1)S(1)}, u32[]{:S(2)}, u32[]{:S(2)}) collective-permute-start(bf16[256,128]{1,0:T(8,128)(2,1)} %get-tuple-element.31), channel_id=1, source_target_pairs={{0,12},{1,13},{2,14},{3,15},{4,8},{5,9},{6,10},{7,11},{8,4},{9,5},... | collective-permute-start | bytes 196616 | tf_op jit(solution)/shard_map/ppermute | solution.py:28
  10.2 1.5 %collective-permute-start.1 = (bf16[1,768,128]{2,1,0:T(8,128)(2,1)}, bf16[1,768,128]{2,1,0:T(8,128)(2,1)S(1)}, u32[]{:S(2)}, u32[]{:S(2)}) collective-permute-start(bf16[1,768,128]{2,1,0:T(8,128)(2,1)} %bitcast.13), channel_id=1, source_target_pairs={{0,2},{1,3},{2,0},{3,1},{4,6},{5,7},{6,4},{7,5},{8,10},{9,11},{10,... | collective-permute-start | bytes 589832 | tf_op jit(solution)/shard_map/ppermute | solution.py:28
  11.7 2.8 %collective-permute-done.7 = bf16[768,128]{1,0:T(8,128)(2,1)S(1)} collective-permute-done((bf16[768,128]{1,0:T(8,128)(2,1)}, bf16[768,128]{1,0:T(8,128)(2,1)S(1)}, u32[]{:S(2)}, u32[]{:S(2)}) %collective-permute-start.7) | collective-permute-done | bytes 196640 | tf_op jit(solution)/shard_map/ppermute | solution.py:28
  14.5 1.7 %collective-permute-start.9 = (bf16[1,768,128]{2,1,0:T(8,128)(2,1)S(1)}, bf16[1,768,128]{2,1,0:T(8,128)(2,1)S(1)}, u32[]{:S(2)}, u32[]{:S(2)}) collective-permute-start(bf16[1,768,128]{2,1,0:T(8,128)(2,1)S(1)} %bitcast.9), channel_id=1, source_target_pairs={{0,2},{1,3},{2,0},{3,1},{4,6},{5,7},{6,4},{7,5},{8,10},{9,11},{10,... | collective-permute-start | bytes 589832 | tf_op jit(solution)/shard_map/ppermute | solution.py:28
  16.2 2.6 %collective-permute-done.3.refs_1_ = bf16[256,128]{1,0:T(8,128)(2,1)S(1)} collective-permute-done((bf16[256,128]{1,0:T(8,128)(2,1)}, bf16[256,128]{1,0:T(8,128)(2,1)S(1)}, u32[]{:S(2)}, u32[]{:S(2)}) %collective-permute-start.3) | collective-permute-done | bytes 65568 | tf_op jit(solution)/shard_map/ppermute | solution.py:28
  18.9 0.0 collective-permute-done.2.refs_0_.refs_9_
  18.9 0.0 collective-permute-done.4.refs_8_
  18.9 0.1 collective-permute-start.5
  19.0 0.1 collective-permute-start.10
  19.1 1.6 %collective-permute-start.12 = (bf16[2,256,128]{2,1,0:T(8,128)(2,1)S(1)}, bf16[2,256,128]{2,1,0:T(8,128)(2,1)S(1)}, u32[]{:S(2)}, u32[]{:S(2)}) collective-permute-start(bf16[2,256,128]{2,1,0:T(8,128)(2,1)S(1)} %get-tuple-element.34.refs_9_.refs_11_), channel_id=1, source_target_pairs={{0,2},{1,3},{2,0},{3,1},{4,6},{5,7},{6,4},{7,5},{8,10},{9,11},{10,... | collective-permute-start | bytes 393224 | tf_op jit(solution)/shard_map/ppermute | solution.py:28
  20.6 0.0 copy-done
  20.7 0.0 copy-start.1
  20.7 0.9 %copy-done.1 = bf16[272,128]{1,0:T(8,128)(2,1)S(1)} copy-done((bf16[272,128]{1,0:T(8,128)(2,1)S(1)}, bf16[272,128]{1,0:T(8,128)(2,1)}, u32[]{:S(2)}) %copy-start.1) | copy-done | bytes 69656
  21.6 0.0 collective-permute-done.1.refs_2_
  21.6 0.1 collective-permute-start
  21.7 0.0 collective-permute-done.5.refs_10_.refs_12_
  21.7 0.4 %collective-permute-start.8 = (bf16[1,768,128]{2,1,0:T(8,128)(2,1)S(1)}, bf16[1,768,128]{2,1,0:T(8,128)(2,1)S(1)}, u32[]{:S(2)}, u32[]{:S(2)}) collective-permute-start(bf16[1,768,128]{2,1,0:T(8,128)(2,1)S(1)} %bitcast.10), channel_id=1, source_target_pairs={{0,1},{1,0},{2,3},{3,2},{4,5},{5,4},{6,7},{7,6},{8,9},{9,8},{10,11... | collective-permute-start | bytes 589832 | tf_op jit(solution)/shard_map/ppermute | solution.py:28
  22.1 1.4 %collective-permute-done.10.refs_10_ = bf16[272,128]{1,0:T(8,128)(2,1)S(1)} collective-permute-done((bf16[272,128]{1,0:T(8,128)(2,1)S(1)}, bf16[272,128]{1,0:T(8,128)(2,1)S(1)}, u32[]{:S(2)}, u32[]{:S(2)}) %collective-permute-start.10) | collective-permute-done | bytes 69664 | tf_op jit(solution)/shard_map/ppermute | solution.py:28
  23.6 0.0 collective-permute-start.6
  23.6 0.0 collective-permute-done.9.refs_6_
  23.6 0.5 %collective-permute-start.11 = (bf16[1,768,128]{2,1,0:T(8,128)(2,1)S(1)}, bf16[1,768,128]{2,1,0:T(8,128)(2,1)S(1)}, u32[]{:S(2)}, u32[]{:S(2)}) collective-permute-start(bf16[1,768,128]{2,1,0:T(8,128)(2,1)S(1)} %collective-permute-done.9.refs_6_), channel_id=1, source_target_pairs={{0,1},{1,0},{2,3},{3,2},{4,5},{5,4},{6,7},{7,6},{8,9},{9,8},{10,11... | collective-permute-start | bytes 589832 | tf_op jit(solution)/shard_map/ppermute | solution.py:28
  24.1 0.8 %collective-permute-done.12.refs_11_.refs_13_ = bf16[2,256,128]{2,1,0:T(8,128)(2,1)S(1)} collective-permute-done((bf16[2,256,128]{2,1,0:T(8,128)(2,1)S(1)}, bf16[2,256,128]{2,1,0:T(8,128)(2,1)S(1)}, u32[]{:S(2)}, u32[]{:S(2)}) %collective-permute-start.12) | collective-permute-done | bytes 131104 | tf_op jit(solution)/shard_map/ppermute | solution.py:28
  24.9 0.0 collective-permute-start.13
  24.9 0.0 collective-permute-done.refs_1_
  24.9 0.0 collective-permute-done.8.refs_5_
  24.9 0.1 collective-permute-done.6.refs_3_
  25.0 0.3 collective-permute-done.11.refs_7_
  25.3 2.1 %front.3 = (bf16[384,512]{1,0:T(8,128)(2,1)S(1)}, f32[384,128]{1,0:T(8,128)S(1)}, f32[384,128]{1,0:T(8,128)S(1)}) custom-call(bf16[1,768,128]{2,1,0:T(8,128)(2,1)S(1)} %get-tuple-element.29.refs_0_, bf16[1,768,128]{2,1,0:T(8,128)(2,1)S(1)} %collective-permute-done.refs_1_, bf16[1,768,128]{2,1,0:T(8,128)(2,1)S(1)} %collective-permute-done.1.refs_2_, ...), custom_call_target="tpu_custom_call" | custom-call | bytes 4096 | tf_op jit(solution)/shard_map/front/pallas_call | solution.py:304
  27.4 0.0 collective-permute-done.13.relay
  27.4 0.4 last.3
  27.8 2.2 %collective-permute-start.16 = (bf16[8,16,128]{2,1,0:T(8,128)(2,1)S(1)}, bf16[8,16,128]{2,1,0:T(8,128)(2,1)S(1)}, u32[]{:S(2)}, u32[]{:S(2)}) collective-permute-start(bf16[8,16,128]{2,1,0:T(8,128)(2,1)S(1)} %get-tuple-element.48), channel_id=1, source_target_pairs={{0,12},{1,13},{2,14},{3,15},{4,8},{5,9},{6,10},{7,11},{8,4},{9,5},... | collective-permute-start | bytes 98312 | tf_op jit(solution)/shard_map/ppermute | solution.py:28
  30.0 0.7 %collective-permute-start.15 = (bf16[8,16,128]{2,1,0:T(8,128)(2,1)S(1)}, bf16[8,16,128]{2,1,0:T(8,128)(2,1)S(1)}, u32[]{:S(2)}, u32[]{:S(2)}) collective-permute-start(bf16[8,16,128]{2,1,0:T(8,128)(2,1)S(1)} %get-tuple-element.47), channel_id=1, source_target_pairs={{0,8},{1,9},{2,10},{3,11},{4,12},{5,13},{6,14},{7,15},{8,0},{9,1},... | collective-permute-start | bytes 98312 | tf_op jit(solution)/shard_map/ppermute | solution.py:28
  30.7 1.5 %collective-permute-start.14 = (bf16[8,16,128]{2,1,0:T(8,128)(2,1)S(1)}, bf16[8,16,128]{2,1,0:T(8,128)(2,1)S(1)}, u32[]{:S(2)}, u32[]{:S(2)}) collective-permute-start(bf16[8,16,128]{2,1,0:T(8,128)(2,1)S(1)} %get-tuple-element.46), channel_id=1, source_target_pairs={{0,4},{1,5},{2,6},{3,7},{4,0},{5,1},{6,2},{7,3},{8,12},{9,13},{10,... | collective-permute-start | bytes 98312 | tf_op jit(solution)/shard_map/ppermute | solution.py:28
  32.2 1.2 %front.2 = (bf16[128,512]{1,0:T(8,128)(2,1)S(1)}, f32[128,128]{1,0:T(8,128)S(1)}, f32[128,128]{1,0:T(8,128)S(1)}) custom-call(bf16[1,768,128]{2,1,0:T(8,128)(2,1)S(1)} %get-tuple-element.29.refs_0_, bf16[1,768,128]{2,1,0:T(8,128)(2,1)S(1)} %collective-permute-done.refs_1_, bf16[1,768,128]{2,1,0:T(8,128)(2,1)S(1)} %collective-permute-done.1.refs_2_, ...), custom_call_target="tpu_custom_call" | custom-call | bytes 4096 | tf_op jit(solution)/shard_map/front/pallas_call | solution.py:304
  33.4 0.3 last.2
  33.7 0.2 collective-permute-done.16
  33.9 1.0 %collective-permute-done.15 = bf16[8,16,128]{2,1,0:T(8,128)(2,1)S(1)} collective-permute-done((bf16[8,16,128]{2,1,0:T(8,128)(2,1)S(1)}, bf16[8,16,128]{2,1,0:T(8,128)(2,1)S(1)}, u32[]{:S(2)}, u32[]{:S(2)}) %collective-permute-start.15) | collective-permute-done | bytes 32800 | tf_op jit(solution)/shard_map/ppermute | solution.py:28
  34.9 0.3 collective-permute-done.14
  35.2 0.6 %convert_add_fusion = f32[8,16,128]{2,1,0:T(8,128)} fusion(bf16[8,16,128]{2,1,0:T(8,128)(2,1)S(1)} %collective-permute-done.16, bf16[8,16,128]{2,1,0:T(8,128)(2,1)S(1)} %collective-permute-done.15, f32[8,16,128]{2,1,0:T(8,128)S(1)} %last.2, bf16[8,16,128]{2,1,0:T(8,128)(2,1)S(1)} %collective-permute-done.14), kind=kLoop, calls=%fused_computation | loop fusion | flops 98304 | bytes 229376 | tf_op jit(solution)/shard_map/add | solution.py:340
  (2 shorter events, 0.0 us)
Async XLA Ops:
  2.7 18.0 %copy-start = (bf16[768,128]{1,0:T(8,128)(2,1)S(1)}, bf16[768,128]{1,0:T(8,128)(2,1)}, u32[]{:S(2)}) copy-start(bf16[768,128]{1,0:T(8,128)(2,1)} %get-tuple-element.27) | copy-start | bytes 589828
  2.7 11.8 %collective-permute-start.7 = (bf16[768,128]{1,0:T(8,128)(2,1)}, bf16[768,128]{1,0:T(8,128)(2,1)S(1)}, u32[]{:S(2)}, u32[]{:S(2)}) collective-permute-start(bf16[768,128]{1,0:T(8,128)(2,1)} %get-tuple-element.36), channel_id=1, source_target_pairs={{0,4},{1,5},{2,6},{3,7},{4,0},{5,1},{6,2},{7,3},{8,12},{9,13},{10,... | collective-permute-start | bytes 589832 | tf_op jit(solution)/shard_map/ppermute | solution.py:28
  5.8 13.1 %collective-permute-start.2 = (bf16[528,128]{1,0:T(8,128)(2,1)}, bf16[528,128]{1,0:T(8,128)(2,1)S(1)}, u32[]{:S(2)}, u32[]{:S(2)}) collective-permute-start(bf16[528,128]{1,0:T(8,128)(2,1)} %get-tuple-element.30), channel_id=1, source_target_pairs={{0,8},{1,9},{2,10},{3,11},{4,12},{5,13},{6,14},{7,15},{8,0},{9,1},... | collective-permute-start | bytes 405512 | tf_op jit(solution)/shard_map/ppermute | solution.py:28
  8.4 10.5 %collective-permute-start.4 = (bf16[272,128]{1,0:T(8,128)(2,1)}, bf16[272,128]{1,0:T(8,128)(2,1)S(1)}, u32[]{:S(2)}, u32[]{:S(2)}) collective-permute-start(bf16[272,128]{1,0:T(8,128)(2,1)} %get-tuple-element.33), channel_id=1, source_target_pairs={{0,4},{1,5},{2,6},{3,7},{4,0},{5,1},{6,2},{7,3},{8,12},{9,13},{10,... | collective-permute-start | bytes 208904 | tf_op jit(solution)/shard_map/ppermute | solution.py:28
  8.8 10.1 %collective-permute-start.3 = (bf16[256,128]{1,0:T(8,128)(2,1)}, bf16[256,128]{1,0:T(8,128)(2,1)S(1)}, u32[]{:S(2)}, u32[]{:S(2)}) collective-permute-start(bf16[256,128]{1,0:T(8,128)(2,1)} %get-tuple-element.31), channel_id=1, source_target_pairs={{0,12},{1,13},{2,14},{3,15},{4,8},{5,9},{6,10},{7,11},{8,4},{9,5},... | collective-permute-start | bytes 196616 | tf_op jit(solution)/shard_map/ppermute | solution.py:28
  10.2 11.4 %collective-permute-start.1 = (bf16[1,768,128]{2,1,0:T(8,128)(2,1)}, bf16[1,768,128]{2,1,0:T(8,128)(2,1)S(1)}, u32[]{:S(2)}, u32[]{:S(2)}) collective-permute-start(bf16[1,768,128]{2,1,0:T(8,128)(2,1)} %bitcast.13), channel_id=1, source_target_pairs={{0,2},{1,3},{2,0},{3,1},{4,6},{5,7},{6,4},{7,5},{8,10},{9,11},{10,... | collective-permute-start | bytes 589832 | tf_op jit(solution)/shard_map/ppermute | solution.py:28
  14.5 9.1 %collective-permute-start.9 = (bf16[1,768,128]{2,1,0:T(8,128)(2,1)S(1)}, bf16[1,768,128]{2,1,0:T(8,128)(2,1)S(1)}, u32[]{:S(2)}, u32[]{:S(2)}) collective-permute-start(bf16[1,768,128]{2,1,0:T(8,128)(2,1)S(1)} %bitcast.9), channel_id=1, source_target_pairs={{0,2},{1,3},{2,0},{3,1},{4,6},{5,7},{6,4},{7,5},{8,10},{9,11},{10,... | collective-permute-start | bytes 589832 | tf_op jit(solution)/shard_map/ppermute | solution.py:28
  18.9 2.8 %collective-permute-start.5 = (bf16[2,256,128]{2,1,0:T(8,128)(2,1)S(1)}, bf16[2,256,128]{2,1,0:T(8,128)(2,1)S(1)}, u32[]{:S(2)}, u32[]{:S(2)}) collective-permute-start(bf16[2,256,128]{2,1,0:T(8,128)(2,1)S(1)} %get-tuple-element.34.refs_9_.refs_11_), channel_id=1, source_target_pairs={{0,1},{1,0},{2,3},{3,2},{4,5},{5,4},{6,7},{7,6},{8,9},{9,8},{10,11... | collective-permute-start | bytes 393224 | tf_op jit(solution)/shard_map/ppermute | solution.py:28
  19.0 4.6 %collective-permute-start.10 = (bf16[272,128]{1,0:T(8,128)(2,1)S(1)}, bf16[272,128]{1,0:T(8,128)(2,1)S(1)}, u32[]{:S(2)}, u32[]{:S(2)}) collective-permute-start(bf16[272,128]{1,0:T(8,128)(2,1)S(1)} %get-tuple-element.37), channel_id=1, source_target_pairs={{0,4},{1,5},{2,6},{3,7},{4,0},{5,1},{6,2},{7,3},{8,12},{9,13},{10,... | collective-permute-start | bytes 208904 | tf_op jit(solution)/shard_map/ppermute | solution.py:28
  19.1 5.8 %collective-permute-start.12 = (bf16[2,256,128]{2,1,0:T(8,128)(2,1)S(1)}, bf16[2,256,128]{2,1,0:T(8,128)(2,1)S(1)}, u32[]{:S(2)}, u32[]{:S(2)}) collective-permute-start(bf16[2,256,128]{2,1,0:T(8,128)(2,1)S(1)} %get-tuple-element.34.refs_9_.refs_11_), channel_id=1, source_target_pairs={{0,2},{1,3},{2,0},{3,1},{4,6},{5,7},{6,4},{7,5},{8,10},{9,11},{10,... | collective-permute-start | bytes 393224 | tf_op jit(solution)/shard_map/ppermute | solution.py:28
  20.7 0.9 %copy-start.1 = (bf16[272,128]{1,0:T(8,128)(2,1)S(1)}, bf16[272,128]{1,0:T(8,128)(2,1)}, u32[]{:S(2)}) copy-start(bf16[272,128]{1,0:T(8,128)(2,1)} %get-tuple-element.28.refs_1_) | copy-start | bytes 208900
  21.6 3.3 %collective-permute-start = (bf16[1,768,128]{2,1,0:T(8,128)(2,1)S(1)}, bf16[1,768,128]{2,1,0:T(8,128)(2,1)S(1)}, u32[]{:S(2)}, u32[]{:S(2)}) collective-permute-start(bf16[1,768,128]{2,1,0:T(8,128)(2,1)S(1)} %get-tuple-element.29.refs_0_), channel_id=1, source_target_pairs={{0,1},{1,0},{2,3},{3,2},{4,5},{5,4},{6,7},{7,6},{8,9},{9,8},{10,11... | collective-permute-start | bytes 589832 | tf_op jit(solution)/shard_map/ppermute | solution.py:28
  21.7 3.2 %collective-permute-start.8 = (bf16[1,768,128]{2,1,0:T(8,128)(2,1)S(1)}, bf16[1,768,128]{2,1,0:T(8,128)(2,1)S(1)}, u32[]{:S(2)}, u32[]{:S(2)}) collective-permute-start(bf16[1,768,128]{2,1,0:T(8,128)(2,1)S(1)} %bitcast.10), channel_id=1, source_target_pairs={{0,1},{1,0},{2,3},{3,2},{4,5},{5,4},{6,7},{7,6},{8,9},{9,8},{10,11... | collective-permute-start | bytes 589832 | tf_op jit(solution)/shard_map/ppermute | solution.py:28
  23.6 1.4 %collective-permute-start.6 = (bf16[1,768,128]{2,1,0:T(8,128)(2,1)S(1)}, bf16[1,768,128]{2,1,0:T(8,128)(2,1)S(1)}, u32[]{:S(2)}, u32[]{:S(2)}) collective-permute-start(bf16[1,768,128]{2,1,0:T(8,128)(2,1)S(1)} %collective-permute-done.1.refs_2_), channel_id=1, source_target_pairs={{0,1},{1,0},{2,3},{3,2},{4,5},{5,4},{6,7},{7,6},{8,9},{9,8},{10,11... | collective-permute-start | bytes 589832 | tf_op jit(solution)/shard_map/ppermute | solution.py:28
  23.6 1.7 %collective-permute-start.11 = (bf16[1,768,128]{2,1,0:T(8,128)(2,1)S(1)}, bf16[1,768,128]{2,1,0:T(8,128)(2,1)S(1)}, u32[]{:S(2)}, u32[]{:S(2)}) collective-permute-start(bf16[1,768,128]{2,1,0:T(8,128)(2,1)S(1)} %collective-permute-done.9.refs_6_), channel_id=1, source_target_pairs={{0,1},{1,0},{2,3},{3,2},{4,5},{5,4},{6,7},{7,6},{8,9},{9,8},{10,11... | collective-permute-start | bytes 589832 | tf_op jit(solution)/shard_map/ppermute | solution.py:28
  24.9 2.5 %collective-permute-start.13 = (bf16[2,256,128]{2,1,0:T(8,128)(2,1)S(1)}, bf16[2,256,128]{2,1,0:T(8,128)(2,1)S(1)}, u32[]{:S(2)}, u32[]{:S(2)}) collective-permute-start(bf16[2,256,128]{2,1,0:T(8,128)(2,1)S(1)} %collective-permute-done.12.refs_11_.refs_13_), channel_id=1, source_target_pairs={{0,1},{1,0},{2,3},{3,2},{4,5},{5,4},{6,7},{7,6},{8,9},{9,8},{10,11... | collective-permute-start | bytes 393224 | tf_op jit(solution)/shard_map/ppermute | solution.py:28
  27.8 6.1 %collective-permute-start.16 = (bf16[8,16,128]{2,1,0:T(8,128)(2,1)S(1)}, bf16[8,16,128]{2,1,0:T(8,128)(2,1)S(1)}, u32[]{:S(2)}, u32[]{:S(2)}) collective-permute-start(bf16[8,16,128]{2,1,0:T(8,128)(2,1)S(1)} %get-tuple-element.48), channel_id=1, source_target_pairs={{0,12},{1,13},{2,14},{3,15},{4,8},{5,9},{6,10},{7,11},{8,4},{9,5},... | collective-permute-start | bytes 98312 | tf_op jit(solution)/shard_map/ppermute | solution.py:28
  30.0 4.9 %collective-permute-start.15 = (bf16[8,16,128]{2,1,0:T(8,128)(2,1)S(1)}, bf16[8,16,128]{2,1,0:T(8,128)(2,1)S(1)}, u32[]{:S(2)}, u32[]{:S(2)}) collective-permute-start(bf16[8,16,128]{2,1,0:T(8,128)(2,1)S(1)} %get-tuple-element.47), channel_id=1, source_target_pairs={{0,8},{1,9},{2,10},{3,11},{4,12},{5,13},{6,14},{7,15},{8,0},{9,1},... | collective-permute-start | bytes 98312 | tf_op jit(solution)/shard_map/ppermute | solution.py:28
  30.7 4.5 %collective-permute-start.14 = (bf16[8,16,128]{2,1,0:T(8,128)(2,1)S(1)}, bf16[8,16,128]{2,1,0:T(8,128)(2,1)S(1)}, u32[]{:S(2)}, u32[]{:S(2)}) collective-permute-start(bf16[8,16,128]{2,1,0:T(8,128)(2,1)S(1)} %get-tuple-element.46), channel_id=1, source_target_pairs={{0,4},{1,5},{2,6},{3,7},{4,0},{5,1},{6,2},{7,3},{8,12},{9,13},{10,... | collective-permute-start | bytes 98312 | tf_op jit(solution)/shard_map/ppermute | solution.py:28
